TPU v7x, 32 devices: a whole 2x2x4 slice. The times are simulated.
32 devices in a mesh: sector: 4 (over y, core), inner: 8 (over z, x).
Axes of the slice: x: 2, y: 2, z: 4, core: 2. Of those that a mesh axis runs over, the one named last changes fastest.
Arguments:
- density: float32 [128, 64, 8192], P('inner', None, 'sector'), may hold values from -6 to 6
- source_sector: int32 [8, 4, 16], P('inner'), may hold values from 0 to 3, as said below
- source_tile: int32 [8, 4, 16], P('inner'), may hold values from 0 to 15
- matrix_id: int32 [8, 4, 16], P('inner'), may hold values from 0 to 31
- cubic_weights: float32 [32, 128, 128], replicated, may hold values from -0.6 to 1.5, as said below
- bin_cells: int32 [4, 8], P('sector'), may hold values from 1 to 512, 2048 in all within a row
- wave_level: float32 [4, 8], P('sector'), may hold values from 0.15 to 1
- energy_rate: float32 [128, 64], replicated, may hold values from 0.01 to 0.12
- pitch_rate: float32 [128, 64], replicated, may hold values from 0.01 to 0.12
Outputs:
- advanced: float32 [128, 64, 8192], P('inner', None, 'sector')
Inputs may be any that keep to these rules, and one draw needn't show every extreme that they name: `source_sector`: for every energy block and destination sector, at most 6 of its 16 tiles depart from any one sector, exactly 6 depart from one sector, and that sector lies one to three sectors below the destination, cyclically. `cubic_weights`: every row of every matrix sums to one.
All inputs are finite; a program needn't handle non-finite values.
Results may differ from a plain program's by a relative error of at most 0.000096.
Values sent between devices are 32-bit elements; how exact they have to be, the bound alone decides.
No kernel may reach another device: no remote copies, remote signals or barrier semaphores. Data moves between devices by JAX's collectives and lax.ppermute only.
A program may use at most 128 MiB of HBM per device.

v0:
```python
import jax
import jax.numpy as jnp
from jax import lax
from jax.sharding import PartitionSpec as P

PASSES = 12


def order_within(sources):
    tile_count = sources.shape[1]
    same = sources[:, :, None] == sources[:, None, :]
    earlier = jnp.arange(tile_count)[None, :] < jnp.arange(tile_count)[:, None]
    return jnp.sum((same & earlier[None]).astype(jnp.int32), axis=2)


def drift_step(density, source_sector, source_tile, matrix_id, cubic_weights):
    sectors = lax.axis_size("sector")
    sector_here = lax.axis_index("sector")
    energies, pitches, cell_count = density.shape
    tile_len = cubic_weights.shape[1]
    tile_count = cell_count // tile_len
    slot_count = max(2, (3 * tile_count + 2 * sectors - 1) // (2 * sectors))
    sources = source_sector[0]
    picked_tiles = source_tile[0]
    matrix_ids = matrix_id[0]
    tile_ranks = order_within(sources)
    slot_rank = jnp.arange(slot_count, dtype=jnp.int32)
    matched = (sources[:, None, :] == sector_here) & (
        tile_ranks[:, None, :] == slot_rank[None, :, None]
    )
    chosen = jnp.sum(jnp.where(matched, picked_tiles[:, None, :], 0), axis=2).reshape(-1)
    filled = jnp.any(matched, axis=2).reshape(-1).astype(jnp.float32)
    blocks = density.reshape(energies, pitches, tile_count, tile_len)
    outgoing = jnp.take(blocks, chosen, axis=2) * filled[None, None, :, None]
    incoming = lax.all_to_all(outgoing, "sector", split_axis=2, concat_axis=2, tiled=True)
    own_sources = sources[sector_here]
    own_ranks = tile_ranks[sector_here]
    own_ids = matrix_ids[sector_here]
    where_from = own_sources * slot_count + own_ranks
    departing = jnp.take(incoming, where_from, axis=2)
    matrices = jnp.take(cubic_weights, own_ids, axis=0)
    drifted = jnp.einsum("eptj,tij->epti", departing, matrices, precision=lax.Precision.HIGHEST)
    return drifted.reshape(energies, pitches, cell_count)


def one_pass(field, rate_cell, energy_rate, pitch_rate):
    flux_e = energy_rate[:-1, :, None] * (field[1:] - field[:-1])
    flux_p = pitch_rate[:, :-1, None] * (field[:, 1:] - field[:, :-1])
    change_e = jnp.pad(flux_e, ((0, 1), (0, 0), (0, 0))) - jnp.pad(flux_e, ((1, 0), (0, 0), (0, 0)))
    change_p = jnp.pad(flux_p, ((0, 0), (0, 1), (0, 0))) - jnp.pad(flux_p, ((0, 0), (1, 0), (0, 0)))
    return field + rate_cell[None, None, :] * (change_e + change_p)


def shards(
    density,
    source_sector,
    source_tile,
    matrix_id,
    cubic_weights,
    bin_cells,
    wave_level,
    energy_rate,
    pitch_rate,
):
    first = drift_step(density, source_sector, source_tile, matrix_id, cubic_weights)
    inner_count = lax.axis_size("inner")
    inner_here = lax.axis_index("inner")
    cell_count = first.shape[2]
    lengths = bin_cells[0]
    per_device = cell_count // inner_count
    owner_cells = jnp.full((inner_count,), per_device, jnp.int32)
    owner_ends = jnp.cumsum(owner_cells)
    owner_starts = owner_ends - owner_cells
    offsets = jnp.arange(per_device, dtype=jnp.int32)
    cell_index = owner_starts[:, None] + offsets[None, :]
    valid = (offsets[None, :] < owner_cells[:, None]).reshape(-1).astype(jnp.float32)
    clipped = jnp.minimum(cell_index, cell_count - 1).reshape(-1)
    packed = jnp.take(first, clipped, axis=2) * valid[None, None, :]
    cellwise = lax.all_to_all(packed, "inner", split_axis=2, concat_axis=0, tiled=True)
    bin_ends = jnp.cumsum(lengths)
    global_cells = owner_starts[inner_here] + offsets
    is_live = (offsets < owner_cells[inner_here]).astype(jnp.float32)
    bin_of = jnp.sum((bin_ends[None, :] <= global_cells[:, None]).astype(jnp.int32), axis=1)
    onehot = bin_of[:, None] == jnp.arange(inner_count, dtype=jnp.int32)[None, :]
    cell_level = jnp.sum(jnp.where(onehot, wave_level[0][None, :], 0.0), axis=1) * is_live

    def loop_body(step, current):
        return one_pass(current, cell_level, energy_rate, pitch_rate)

    diffused = lax.fori_loop(0, PASSES, loop_body, cellwise)
    returned = lax.all_to_all(diffused, "inner", split_axis=0, concat_axis=2, tiled=True)
    every_cell = jnp.arange(cell_count, dtype=jnp.int32)
    owner_index = jnp.sum((owner_ends[None, :] <= every_cell[:, None]).astype(jnp.int32), axis=1)
    offset = every_cell - owner_starts[owner_index]
    position = owner_index * per_device + offset
    restored = jnp.take(returned, position, axis=2)
    return drift_step(restored, source_sector, source_tile, matrix_id, cubic_weights)


def solution(mesh):
    return jax.shard_map(
        shards,
        mesh=mesh,
        in_specs=(
            P("inner", None, "sector"),
            P("inner", None, None),
            P("inner", None, None),
            P("inner", None, None),
            P(),
            P("sector", None),
            P("sector", None),
            P(),
            P(),
        ),
        out_specs=P("inner", None, "sector"),
        check_vma=False,
    )
```

profile of v0, /device:TPU:25, one launch (start us, length us, event | category | flops | bytes accessed | tf_op | source)
XLA Modules:
  0.0 1388.7 jit_solution(8755569406440947074)
XLA Ops:
  3.1 8.0 copy_bitcast_fusion.1
  11.3 10.5 gather_fusion.1
  21.7 12.3 bitcast_multiply_fusion.2
  34.0 7.1 all-to-all-start
  43.4 135.0 %all-to-all-done = f32[16,64,24,128]{3,1,0,2:T(8,128)} async-done(((f32[16,64,24,128]{3,1,0,2:T(8,128)}), f32[16,64,24,128]{3,1,0,2:T(8,128)}, u32[]{:S(2)}, u32[]{:S(2)}) %all-to-all-start) | async-done | bytes 12582944 | tf_op jit(solution)/shard_map/all_to_all | solution.py:35
  178.4 11.8 copy.39
  190.2 9.1 gather_fusion.2
  199.2 4.4 broadcast_select_fusion.2
  203.7 9.8 fusion.2
  213.5 12.7 copy.51
  226.2 24.6 %gather_fusion.3 = f32[2048,16,64]{2,1,0:T(8,128)} fusion(f32[16,64,2048]{1,0,2:T(8,128)} %bitcast.105, s32[2048]{0:T(1024)S(1)} %fusion.11), kind=kCustom, calls=%fused_computation.3.clone | custom fusion | bytes 16785408 | tf_op jit(solution)/shard_map/jit(_take)/gather | solution.py:78
  250.7 12.4 fusion.22
  263.2 15.4 %reshape.283 = f32[8,1,262144]{2,1,0:T(1,128)} reshape(f32[2048,16,64]{2,1,0:T(8,128)} %fusion.22) | data formatting | bytes 16777216
  278.6 5.9 all-to-all-start.1
  286.3 180.5 %all-to-all-done.1 = f32[8,1,262144]{2,1,0:T(1,128)} async-done(((f32[8,1,262144]{2,1,0:T(1,128)}), f32[8,1,262144]{2,1,0:T(1,128)}, u32[]{:S(2)}, u32[]{:S(2)}) %all-to-all-start.1) | async-done | bytes 8388640 | tf_op jit(solution)/shard_map/all_to_all | solution.py:79
  467.3 26.3 %reduce.2 = f32[8,262144]{1,0:T(8,128)} reduce(f32[8,1,262144]{2,1,0:T(1,128)} %all-to-all-done.1, f32[]{:T(128)} %broadcast.330), dimensions={1}, to_apply=%all_to_all.33.reduce_sub_computation | reduce | bytes 16777220 | tf_op jit(solution)/shard_map/all_to_all | solution.py:79
  493.6 15.6 %reshape.284 = f32[2048,16,64]{2,1,0:T(8,128)} reshape(f32[8,262144]{1,0:T(8,128)} %reduce.2) | data formatting | bytes 16777216
  509.2 13.9 %copy.43 = f32[8,16,64,256]{3,2,1,0:T(8,128)} copy(f32[8,16,64,256]{2,1,3,0:T(8,128)} %bitcast.103) | data formatting | bytes 16777216 | tf_op jit(solution)/shard_map/all_to_all | solution.py:79
  523.1 404.3 %while.12 = (s32[]{:T(128)}, f32[128,64,256]{2,1,0:T(8,128)}, f32[256]{0:T(256)S(1)}, f32[128,64]{1,0:T(8,128)S(1)}, f32[128,64]{1,0:T(8,128)S(1)}, /*index=5*/s32[]{:T(128)}) while((s32[]{:T(128)}, f32[128,64,256]{2,1,0:T(8,128)}, f32[256]{0:T(256)S(1)}, f32[128,64]{1,0:T(8,128)S(1)}, f32[128,64]{1,0:T(8,128)S(1)}, ...), condition=%wide.region_7.12_spmd, body=%wide.region_6.11_spmd.sunk | while | flops 18776064 | bytes 108331384 | solution.py:90
  523.5 10.1 subtract_multiply_fusion.4
  533.6 4.3 subtract_multiply_fusion.5
  537.9 19.3 %multiply_add_fusion.2 = f32[128,64,256]{2,1,0:T(8,128)} fusion(f32[128,64,256]{2,1,0:T(8,128)} %get-tuple-element.156, f32[128,63,256]{2,1,0:T(8,128)} %subtract_multiply_fusion.4, f32[127,64,256]{2,1,0:T(8,128)} %subtract_multiply_fusion.5, f32[256]{0:T(256)S(1)} %get-tuple-element.163), kind=kLoop, calls=%fused_computation.7.clone.1 | loop fusion | flops 10485760 | bytes 33358848 | tf_op jit(solution)/shard_map/while/body/eval_jaxpr/add | solution.py:51
  557.2 10.1 subtract_multiply_fusion.4
  567.3 4.3 subtract_multiply_fusion.5
  571.6 19.3 %multiply_add_fusion.2 = f32[128,64,256]{2,1,0:T(8,128)} fusion(f32[128,64,256]{2,1,0:T(8,128)} %get-tuple-element.156, f32[128,63,256]{2,1,0:T(8,128)} %subtract_multiply_fusion.4, f32[127,64,256]{2,1,0:T(8,128)} %subtract_multiply_fusion.5, f32[256]{0:T(256)S(1)} %get-tuple-element.163), kind=kLoop, calls=%fused_computation.7.clone.1 | loop fusion | flops 10485760 | bytes 33358848 | tf_op jit(solution)/shard_map/while/body/eval_jaxpr/add | solution.py:51
  590.9 10.1 subtract_multiply_fusion.4
  601.0 4.3 subtract_multiply_fusion.5
  605.3 19.3 %multiply_add_fusion.2 = f32[128,64,256]{2,1,0:T(8,128)} fusion(f32[128,64,256]{2,1,0:T(8,128)} %get-tuple-element.156, f32[128,63,256]{2,1,0:T(8,128)} %subtract_multiply_fusion.4, f32[127,64,256]{2,1,0:T(8,128)} %subtract_multiply_fusion.5, f32[256]{0:T(256)S(1)} %get-tuple-element.163), kind=kLoop, calls=%fused_computation.7.clone.1 | loop fusion | flops 10485760 | bytes 33358848 | tf_op jit(solution)/shard_map/while/body/eval_jaxpr/add | solution.py:51
  624.5 10.1 subtract_multiply_fusion.4
  634.6 4.3 subtract_multiply_fusion.5
  638.9 19.3 %multiply_add_fusion.2 = f32[128,64,256]{2,1,0:T(8,128)} fusion(f32[128,64,256]{2,1,0:T(8,128)} %get-tuple-element.156, f32[128,63,256]{2,1,0:T(8,128)} %subtract_multiply_fusion.4, f32[127,64,256]{2,1,0:T(8,128)} %subtract_multiply_fusion.5, f32[256]{0:T(256)S(1)} %get-tuple-element.163), kind=kLoop, calls=%fused_computation.7.clone.1 | loop fusion | flops 10485760 | bytes 33358848 | tf_op jit(solution)/shard_map/while/body/eval_jaxpr/add | solution.py:51
  658.2 10.1 subtract_multiply_fusion.4
  668.3 4.3 subtract_multiply_fusion.5
  672.6 19.3 %multiply_add_fusion.2 = f32[128,64,256]{2,1,0:T(8,128)} fusion(f32[128,64,256]{2,1,0:T(8,128)} %get-tuple-element.156, f32[128,63,256]{2,1,0:T(8,128)} %subtract_multiply_fusion.4, f32[127,64,256]{2,1,0:T(8,128)} %subtract_multiply_fusion.5, f32[256]{0:T(256)S(1)} %get-tuple-element.163), kind=kLoop, calls=%fused_computation.7.clone.1 | loop fusion | flops 10485760 | bytes 33358848 | tf_op jit(solution)/shard_map/while/body/eval_jaxpr/add | solution.py:51
  691.8 10.1 subtract_multiply_fusion.4
  701.9 4.3 subtract_multiply_fusion.5
  706.2 19.3 %multiply_add_fusion.2 = f32[128,64,256]{2,1,0:T(8,128)} fusion(f32[128,64,256]{2,1,0:T(8,128)} %get-tuple-element.156, f32[128,63,256]{2,1,0:T(8,128)} %subtract_multiply_fusion.4, f32[127,64,256]{2,1,0:T(8,128)} %subtract_multiply_fusion.5, f32[256]{0:T(256)S(1)} %get-tuple-element.163), kind=kLoop, calls=%fused_computation.7.clone.1 | loop fusion | flops 10485760 | bytes 33358848 | tf_op jit(solution)/shard_map/while/body/eval_jaxpr/add | solution.py:51
  725.5 10.1 subtract_multiply_fusion.4
  739.9 19.3 %multiply_add_fusion.2 = f32[128,64,256]{2,1,0:T(8,128)} fusion(f32[128,64,256]{2,1,0:T(8,128)} %get-tuple-element.156, f32[128,63,256]{2,1,0:T(8,128)} %subtract_multiply_fusion.4, f32[127,64,256]{2,1,0:T(8,128)} %subtract_multiply_fusion.5, f32[256]{0:T(256)S(1)} %get-tuple-element.163), kind=kLoop, calls=%fused_computation.7.clone.1 | loop fusion | flops 10485760 | bytes 33358848 | tf_op jit(solution)/shard_map/while/body/eval_jaxpr/add | solution.py:51
  759.2 10.1 subtract_multiply_fusion.4
  773.6 19.3 %multiply_add_fusion.2 = f32[128,64,256]{2,1,0:T(8,128)} fusion(f32[128,64,256]{2,1,0:T(8,128)} %get-tuple-element.156, f32[128,63,256]{2,1,0:T(8,128)} %subtract_multiply_fusion.4, f32[127,64,256]{2,1,0:T(8,128)} %subtract_multiply_fusion.5, f32[256]{0:T(256)S(1)} %get-tuple-element.163), kind=kLoop, calls=%fused_computation.7.clone.1 | loop fusion | flops 10485760 | bytes 33358848 | tf_op jit(solution)/shard_map/while/body/eval_jaxpr/add | solution.py:51
  792.8 10.1 subtract_multiply_fusion.4
  807.2 19.3 %multiply_add_fusion.2 = f32[128,64,256]{2,1,0:T(8,128)} fusion(f32[128,64,256]{2,1,0:T(8,128)} %get-tuple-element.156, f32[128,63,256]{2,1,0:T(8,128)} %subtract_multiply_fusion.4, f32[127,64,256]{2,1,0:T(8,128)} %subtract_multiply_fusion.5, f32[256]{0:T(256)S(1)} %get-tuple-element.163), kind=kLoop, calls=%fused_computation.7.clone.1 | loop fusion | flops 10485760 | bytes 33358848 | tf_op jit(solution)/shard_map/while/body/eval_jaxpr/add | solution.py:51
  826.5 10.1 subtract_multiply_fusion.4
  840.9 19.3 %multiply_add_fusion.2 = f32[128,64,256]{2,1,0:T(8,128)} fusion(f32[128,64,256]{2,1,0:T(8,128)} %get-tuple-element.156, f32[128,63,256]{2,1,0:T(8,128)} %subtract_multiply_fusion.4, f32[127,64,256]{2,1,0:T(8,128)} %subtract_multiply_fusion.5, f32[256]{0:T(256)S(1)} %get-tuple-element.163), kind=kLoop, calls=%fused_computation.7.clone.1 | loop fusion | flops 10485760 | bytes 33358848 | tf_op jit(solution)/shard_map/while/body/eval_jaxpr/add | solution.py:51
  860.2 10.1 subtract_multiply_fusion.4
  874.6 19.3 %multiply_add_fusion.2 = f32[128,64,256]{2,1,0:T(8,128)} fusion(f32[128,64,256]{2,1,0:T(8,128)} %get-tuple-element.156, f32[128,63,256]{2,1,0:T(8,128)} %subtract_multiply_fusion.4, f32[127,64,256]{2,1,0:T(8,128)} %subtract_multiply_fusion.5, f32[256]{0:T(256)S(1)} %get-tuple-element.163), kind=kLoop, calls=%fused_computation.7.clone.1 | loop fusion | flops 10485760 | bytes 33358848 | tf_op jit(solution)/shard_map/while/body/eval_jaxpr/add | solution.py:51
  893.8 10.1 subtract_multiply_fusion.4
  908.2 19.3 %multiply_add_fusion.2 = f32[128,64,256]{2,1,0:T(8,128)} fusion(f32[128,64,256]{2,1,0:T(8,128)} %get-tuple-element.156, f32[128,63,256]{2,1,0:T(8,128)} %subtract_multiply_fusion.4, f32[127,64,256]{2,1,0:T(8,128)} %subtract_multiply_fusion.5, f32[256]{0:T(256)S(1)} %get-tuple-element.163), kind=kLoop, calls=%fused_computation.7.clone.1 | loop fusion | flops 10485760 | bytes 33358848 | tf_op jit(solution)/shard_map/while/body/eval_jaxpr/add | solution.py:51
  927.5 4.9 all-to-all-start.2
  932.6 4.5 compare_select_fusion.1
  938.4 176.3 %all-to-all-done.2 = f32[128,64,256]{2,1,0:T(8,128)} async-done(((f32[128,64,256]{2,1,0:T(8,128)}), f32[128,64,256]{2,1,0:T(8,128)}, u32[]{:S(2)}, u32[]{:S(2)}) %all-to-all-start.2) | async-done | bytes 8388640 | tf_op jit(solution)/shard_map/all_to_all | solution.py:91
  1114.7 14.5 %copy.54 = f32[16,64,8,256]{1,0,3,2:T(8,128)} copy(f32[16,64,8,256]{3,1,0,2:T(8,128)} %bitcast.46) | data formatting | bytes 16777216 | tf_op jit(solution)/shard_map/all_to_all | solution.py:91
  1129.2 24.6 %gather_fusion.4 = f32[2048,16,64]{2,1,0:T(8,128)} fusion(f32[16,64,2048]{1,0,2:T(8,128)} %bitcast.106, s32[2048]{0:T(1024)S(1)} %broadcast_clamp_fusion), kind=kCustom, calls=%fused_computation.6.clone | custom fusion | bytes 16785408 | tf_op jit(solution)/shard_map/jit(_take)/gather | solution.py:96
  1153.8 13.2 broadcast_select_fusion
  1167.0 12.7 copy.48
  1179.7 10.6 gather_fusion.5
  1190.4 12.3 bitcast_multiply_fusion.1
  1202.7 147.0 %all_to_all.46 = f32[16,64,24,128]{3,1,0,2:T(8,128)} all-to-all(f32[16,64,24,128]{3,1,0,2:T(8,128)} %bitcast_multiply_fusion.1), channel_id=1, replica_groups=mesh['sector'=4,'inner'=8] {'sector'}, dimensions={2} | all-to-all | bytes 25165824 | tf_op jit(solution)/shard_map/all_to_all | solution.py:35
  1349.7 11.9 copy.49
  1361.5 9.2 gather_fusion.6
  1370.7 4.5 broadcast_select_fusion.1
  1375.3 8.7 fusion
  1383.9 4.6 copy.63
  (142 shorter events, 35.1 us)
Async XLA Ops:
  0.0 42.0 %copy-start = (f32[32,128,128]{2,1,0:T(8,128)S(1)}, f32[32,128,128]{2,1,0:T(8,128)}, u32[]{:S(2)}) copy-start(f32[32,128,128]{2,1,0:T(8,128)} %param.23) | copy-start | bytes 6291460
  3.1 18.7 %copy-start.14 = (pred[24]{0:T(512)(128)(4,1)}, pred[24]{0:T(512)(128)(4,1)S(1)}, u32[]{:S(2)}) copy-start(pred[24]{0:T(512)(128)(4,1)S(1)} %compare_and_fusion.3) | copy-start | bytes 76
  11.1 10.7 copy-start.7
  11.3 10.5 copy-start.8
  34.0 144.4 %all-to-all-start = ((f32[16,64,24,128]{3,1,0,2:T(8,128)}), f32[16,64,24,128]{3,1,0,2:T(8,128)}, u32[]{:S(2)}, u32[]{:S(2)}) async-start(f32[16,64,24,128]{3,1,0,2:T(8,128)} %bitcast_multiply_fusion.2), calls=%async_computation | async-start | bytes 25165824 | tf_op jit(solution)/shard_map/all_to_all | solution.py:35
  41.9 161.7 %copy-start.12 = (pred[16]{0:T(512)(128)(4,1)}, pred[16]{0:T(512)(128)(4,1)S(1)}, u32[]{:S(2)}) copy-start(pred[16]{0:T(512)(128)(4,1)S(1)} %get-tuple-element.105) | copy-start | bytes 52
  42.6 161.1 %copy-start.2 = (f32[16,128,128]{2,1,0:T(8,128)}, f32[16,128,128]{2,1,0:T(8,128)S(1)}, u32[]{:S(2)}) copy-start(f32[16,128,128]{2,1,0:T(8,128)S(1)} %gather_fusion) | copy-start | bytes 3145732
  43.4 155.9 %copy-start.10 = (pred[16]{0:T(512)(128)(4,1)}, pred[16]{0:T(512)(128)(4,1)S(1)}, u32[]{:S(2)}) copy-start(pred[16]{0:T(512)(128)(4,1)S(1)} %get-tuple-element.107) | copy-start | bytes 52
  43.4 146.8 %copy-start.6 = (s32[1024]{0:T(1024)}, s32[1024]{0:T(1024)S(1)}, u32[]{:S(2)}) copy-start(s32[1024]{0:T(1024)S(1)} %pad_clamp_fusion) | copy-start | bytes 12292
  278.6 5.9 copy-start.17
  278.6 6.1 copy-start.4
  278.6 6.2 copy-start.5
  278.6 7.7 copy-start.16
  278.6 188.2 %all-to-all-start.1 = ((f32[8,1,262144]{2,1,0:T(1,128)}), f32[8,1,262144]{2,1,0:T(1,128)}, u32[]{:S(2)}, u32[]{:S(2)}) async-start(f32[8,1,262144]{2,1,0:T(1,128)} %reshape.283), calls=%async_computation.1 | async-start | bytes 16777216 | tf_op jit(solution)/shard_map/all_to_all | solution.py:79
  523.5 10.1 slice-start
  523.5 10.1 slice-start.1
  557.2 10.1 slice-start
  557.2 10.1 slice-start.1
  590.9 10.1 slice-start
  590.9 10.1 slice-start.1
  624.5 10.1 slice-start
  624.5 10.1 slice-start.1
  658.2 10.1 slice-start
  658.2 10.1 slice-start.1
  691.8 10.1 slice-start
  691.8 10.1 slice-start.1
  725.5 10.1 slice-start
  725.5 10.1 slice-start.1
  759.2 10.1 slice-start
  759.2 10.1 slice-start.1
  792.8 10.1 slice-start
  792.8 10.1 slice-start.1
  826.5 10.1 slice-start
  826.5 10.1 slice-start.1
  860.2 10.1 slice-start
  860.2 10.1 slice-start.1
  893.8 10.1 slice-start
  893.8 10.1 slice-start.1
  927.5 187.2 %all-to-all-start.2 = ((f32[128,64,256]{2,1,0:T(8,128)}), f32[128,64,256]{2,1,0:T(8,128)}, u32[]{:S(2)}, u32[]{:S(2)}) async-start(f32[128,64,256]{2,1,0:T(8,128)} %get-tuple-element.74), calls=%async_computation.2 | async-start | bytes 16777216 | tf_op jit(solution)/shard_map/all_to_all | solution.py:91
  1179.7 10.7 copy-start.9
  1179.7 10.7 copy-start.15
  1361.5 9.2 copy-start.11
  1370.7 4.5 copy-start.3
  1370.7 4.6 copy-start.13
  1383.9 4.6 copy-start.1
where the time goes:
time: 1400 us; the launch traced here: 1390 us
  other arithmetic  501 us (36%)
  waiting for transfers between devices  492 us (35%)
  local copies, waits for them, and re-layouts  212 us (15%)
  blocking collectives  147 us (10%)
  matrix products  18.4 us (1%)
  starting transfers between devices  17.9 us (1%)
    add x12, other arithmetic, one_pass(): return field + rate_cell[None, None, :] * (change_e + change_p)  231 us
    all_to_all x1, waiting for transfers between devices, shards(): lax.all_to_all(packed, 'inner', split_axis=2, concat_axis=0, tiled=True)  180 us
    all_to_all x1, waiting for transfers between devices, shards(): lax.all_to_all(diffused, 'inner', split_axis=0, concat_axis=2, tiled=True)  176 us
    all_to_all x1, blocking collectives, drift_step(): lax.all_to_all(outgoing, 'sector', split_axis=2, concat_axis=2, tiled=True)  147 us
    all_to_all x1, waiting for transfers between devices, drift_step(): lax.all_to_all(outgoing, 'sector', split_axis=2, concat_axis=2, tiled=True)  135 us
    mul x12, other arithmetic, one_pass(): flux_p = pitch_rate[:, :-1, None] * (field[:, 1:] - field[:, :-1])  121 us
    mul x12, other arithmetic, one_pass(): flux_e = energy_rate[:-1, :, None] * (field[1:] - field[:-1])  51.5 us
    unnamed x41, local copies, waits for them, and re-layouts  31.1 us
  transfers between devices with their start and end apart: 3, of which 3 were waited for; matrix products, arithmetic and copies ran while one was open for 1% of the time, Pallas kernels for 0%

commit v1 on v0

--- a/solution.py
+++ b/solution.py
@@ -1,9 +1,493 @@
+import functools
+
 import jax
 import jax.numpy as jnp
 from jax import lax
+from jax.experimental import pallas as pl
+from jax.experimental.pallas import tpu as pltpu
 from jax.sharding import PartitionSpec as P
 
 PASSES = 12
+CHUNKS = 4
+VMEM_LIMIT = 58 * 1024 * 1024
+ANY = pl.BlockSpec(memory_space=pl.ANY)
+SMEM = pl.BlockSpec(memory_space=pltpu.SMEM)
+VMEM = pl.BlockSpec(memory_space=pltpu.VMEM)
+F32 = jnp.float32
+BF16 = jnp.bfloat16
+
+
+def params():
+    return pltpu.CompilerParams(vmem_limit_bytes=VMEM_LIMIT)
+
+
+def cost(flops, bytes_accessed):
+    return pl.CostEstimate(flops=flops, bytes_accessed=bytes_accessed, transcendentals=0)
+
+
+def weights_kernel(mid_ref, w_ref, out_ref, raw, sems):
+    tiles, side = raw.shape[0], raw.shape[1]
+    me = lax.axis_index("sector")
+
+    def copy(t):
+        return pltpu.make_async_copy(w_ref.at[mid_ref[0, me, t]], raw.at[t], sems.at[t])
+
+    @pl.loop(0, tiles)
+    def _(t):
+        copy(t).start()
+
+    @pl.loop(0, tiles)
+    def _(t):
+        copy(t).wait()
+        turned = jnp.transpose(raw[t])
+        high = turned.astype(BF16)
+        low = (turned - high.astype(F32)).astype(BF16)
+        out_ref[t, :side, :side] = high
+        out_ref[t, side:, :side] = high
+        out_ref[t, :side, side:] = low
+        out_ref[t, side:, side:] = jnp.zeros((side, side), BF16)
+
+
+def split_weights(matrix_id, cubic_weights):
+    tiles, side = matrix_id.shape[2], cubic_weights.shape[1]
+    return pl.pallas_call(
+        weights_kernel,
+        out_shape=jax.ShapeDtypeStruct((tiles, 2 * side, 2 * side), BF16),
+        in_specs=[SMEM, ANY],
+        out_specs=VMEM,
+        scratch_shapes=[
+            pltpu.VMEM((tiles, side, side), F32),
+            pltpu.SemaphoreType.DMA((tiles,)),
+        ],
+        compiler_params=params(),
+        cost_estimate=cost(tiles * side * side * 8, tiles * side * side * 12),
+        name="split_weights",
+    )(matrix_id, cubic_weights)
+
+
+def pack_kernel(find, n_arrays, sec_ref, til_ref, *refs):
+    sectors, tiles = sec_ref.shape[1], sec_ref.shape[2]
+    sends, sems = refs[-sectors:-1], refs[-1]
+    pieces = find(*refs[:n_arrays])
+    me = lax.axis_index("sector")
+    counts = []
+    for d in range(1, sectors):
+        dest = me ^ d
+
+        def body(t, count, d=d, dest=dest):
+            hit = sec_ref[0, dest, t] == me
+
+            @pl.when(hit)
+            def _():
+                for guard, piece in pieces(til_ref[0, dest, t]):
+
+                    @pl.when(guard)
+                    def _():
+                        pltpu.make_async_copy(piece(), sends[d - 1].at[count], sems.at[d - 1, count]).start()
+
+            return count + hit.astype(jnp.int32)
+
+        counts.append(lax.fori_loop(0, tiles, body, jnp.int32(0)))
+    for d in range(1, sectors):
+
+        @pl.loop(0, counts[d - 1])
+        def _(slot, d=d):
+            there = sends[d - 1].at[slot]
+            pltpu.make_async_copy(there, there, sems.at[d - 1, slot]).wait()
+
+
+def pack(find, cap, source_sector, source_tile, arrays, piece, after=()):
+    sectors = source_sector.shape[1]
+    send = jax.ShapeDtypeStruct((cap,) + piece, F32)
+    size = 4 * cap * (sectors - 1) * piece[0] * piece[1] * piece[2]
+    return pl.pallas_call(
+        functools.partial(pack_kernel, find, len(arrays)),
+        out_shape=[send] * (sectors - 1),
+        in_specs=[SMEM, SMEM] + [ANY] * (len(arrays) + len(after)),
+        out_specs=[ANY] * (sectors - 1),
+        scratch_shapes=[pltpu.SemaphoreType.DMA((sectors - 1, cap))],
+        compiler_params=params(),
+        cost_estimate=cost(0, 2 * size),
+        name="pack_tiles",
+    )(source_sector, source_tile, *arrays, *after)
+
+
+def sector_exchange(sends):
+    sectors = lax.axis_size("sector")
+    return [
+        lax.ppermute(send, "sector", [(s, s ^ (d + 1)) for s in range(sectors)])
+        for d, send in enumerate(sends)
+    ]
+
+
+def drift_kernel(find, place, n_local, sec_ref, til_ref, w_ref, *refs):
+    sectors, tiles = sec_ref.shape[1], sec_ref.shape[2]
+    local, recvs = refs[:n_local], refs[n_local : n_local + sectors - 1]
+    outs = refs[n_local + sectors - 1 : -4]
+    taken, made, in_sems, out_sems = refs[-4:]
+    pieces = find(*local)
+    put = place(*outs)
+    me = lax.axis_index("sector")
+    rows, side = taken.shape[1] * taken.shape[2], taken.shape[3]
+
+    def fetch(t, counts):
+        d = sec_ref[0, me, t] ^ me
+
+        @pl.when(d == 0)
+        def _():
+            for guard, piece in pieces(til_ref[0, me, t]):
+
+                @pl.when(guard)
+                def _():
+                    pltpu.make_async_copy(piece(), taken.at[t], in_sems.at[t]).start()
+
+        for other in range(1, sectors):
+
+            @pl.when(d == other)
+            def _(other=other):
+                pltpu.make_async_copy(
+                    recvs[other - 1].at[counts[other - 1]], taken.at[t], in_sems.at[t]
+                ).start()
+
+        return tuple(c + (d == i + 1).astype(jnp.int32) for i, c in enumerate(counts))
+
+    lax.fori_loop(0, tiles, fetch, (jnp.int32(0),) * (sectors - 1))
+
+    @pl.loop(0, tiles)
+    def _(t):
+        pltpu.make_async_copy(taken.at[t], taken.at[t], in_sems.at[t]).wait()
+        value = taken[t].reshape(rows, side)
+        high = value.astype(BF16)
+        low = (value - high.astype(F32)).astype(BF16)
+        both = jnp.dot(jnp.concatenate([high, low], axis=1), w_ref[t], preferred_element_type=F32)
+        made[t] = (both[:, :side] + both[:, side:]).reshape(taken.shape[1:])
+        for guard, there in put(t):
+
+            @pl.when(guard)
+            def _():
+                pltpu.make_async_copy(made.at[t], there(), out_sems.at[t]).start()
+
+    @pl.loop(0, tiles)
+    def _(t):
+        pltpu.make_async_copy(made.at[t], made.at[t], out_sems.at[t]).wait()
+
+
+def drift(find, place, tables, weights, local, recvs, outs, piece, carried=None):
+    source_sector, source_tile = tables
+    sectors, tiles = source_sector.shape[1], source_sector.shape[2]
+    n_local = len(local)
+    rows, side = piece[0] * piece[1], piece[2]
+    ins = [source_sector, source_tile, weights, *local, *recvs]
+    specs = [SMEM, SMEM, VMEM] + [ANY] * (n_local + sectors - 1)
+    aliases = {}
+    body = functools.partial(drift_kernel, find, place, n_local)
+    if carried is not None:
+        aliases = {len(ins): 0}
+        ins.append(carried)
+        specs.append(ANY)
+        at = len(ins) - 1
+
+        def body(*refs):
+            drift_kernel(find, place, n_local, *refs[:at], *refs[at + 1 :])
+
+    return pl.pallas_call(
+        body,
+        out_shape=outs,
+        in_specs=specs,
+        out_specs=[ANY] * len(outs),
+        scratch_shapes=[
+            pltpu.VMEM((tiles,) + piece, F32),
+            pltpu.VMEM((tiles,) + piece, F32),
+            pltpu.SemaphoreType.DMA((tiles,)),
+            pltpu.SemaphoreType.DMA((tiles,)),
+        ],
+        input_output_aliases=aliases,
+        compiler_params=params(),
+        cost_estimate=cost(tiles * rows * side * side * 8, tiles * rows * side * 8 + weights.size * 2),
+        name="drift_chunk",
+    )(*ins)
+
+
+def diffusion_kernel(
+    chunks, halo_chunks, rate_ref, a_ref, b_ref, *refs
+):
+    n_in = 2 * chunks + 2 * halo_chunks
+    ins, keep, sends = refs[:n_in], refs[n_in], refs[n_in + 1 : n_in + 1 + chunks]
+    field, work, done, in_sems, out_sems = refs[n_in + 1 + chunks :]
+    tiles, step = ins[0].shape[0], ins[0].shape[1]
+    frame, pitches, side = work.shape
+    halo = halo_chunks * step
+    block = chunks * step
+    vregs = pitches // 8
+    flip = lax.axis_index("inner") % 2
+    order = (
+        list(range(chunks))
+        + [2 * chunks - 1 - k for k in range(chunks)]
+        + [2 * chunks + k for k in range(halo_chunks)]
+        + [-1 - k for k in range(halo_chunks)]
+    )
+
+    def fetch(g, slot):
+        copies = []
+        for i, position in enumerate(order):
+            straight = (position + halo_chunks) * step
+            mirrored = (2 * chunks - 1 - position + halo_chunks) * step
+            at = jnp.where(flip == 0, straight, mirrored)
+            copies.append(
+                pltpu.make_async_copy(
+                    ins[i].at[g], field.at[slot, pl.ds(at, step)], in_sems.at[slot, i]
+                )
+            )
+        return copies
+
+    def store(g, slot):
+        copies = [
+            pltpu.make_async_copy(
+                done.at[slot, pl.ds(flip * block, block)], keep.at[g], out_sems.at[slot, chunks]
+            )
+        ]
+        for k in range(chunks):
+            copies.append(
+                pltpu.make_async_copy(
+                    done.at[slot, pl.ds((1 - flip) * block + k * step, step)],
+                    sends[k].at[g],
+                    out_sems.at[slot, k],
+                )
+            )
+        return copies
+
+    for copy in fetch(0, 0):
+        copy.start()
+
+    @pl.loop(0, tiles)
+    def _(g):
+        slot = g % 2
+
+        @pl.when(g + 1 < tiles)
+        def _():
+            for copy in fetch(g + 1, 1 - slot):
+                copy.start()
+
+        for copy in fetch(g, slot):
+            copy.wait()
+
+        @pl.when(g >= 2)
+        def _():
+            for copy in store(g - 2, slot):
+                copy.wait()
+
+        rate = rate_ref[g]
+
+        def read_work(e):
+            return [work[e, 8 * v : 8 * v + 8, :] for v in range(vregs)]
+
+        def write_work(e, rows):
+            for v in range(vregs):
+                work[e, 8 * v : 8 * v + 8, :] = rows[v]
+
+        def read_field(e):
+            return [field[slot, e, pl.ds(v, 8, stride=vregs), :] for v in range(vregs)]
+
+        def write_done(e, rows):
+            for v in range(vregs):
+                done[slot, e - halo, pl.ds(v, 8, stride=vregs), :] = rows[v]
+
+        def sweep(first, count, read, write):
+            def energy(e, here, below):
+                after = read(e + 1)
+                above = [
+                    a_ref[e, 8 * v : 8 * v + 8, :] * (after[v] - here[v]) for v in range(vregs)
+                ]
+                nearby = here[1:] + [pltpu.roll(here[0], 7, 0)]
+                pitch = [
+                    b_ref[e, 8 * v : 8 * v + 8, :] * (nearby[v] - here[v]) for v in range(vregs)
+                ]
+                before = [pltpu.roll(pitch[-1], 1, 0)] + pitch[:-1]
+                write(
+                    e,
+                    [
+                        here[v] + rate * ((above[v] - below[v]) + (pitch[v] - before[v]))
+                        for v in range(vregs)
+                    ],
+                )
+                return after, above
+
+            edge = read(first - 1)
+            here = read(first)
+            below = [
+                a_ref[first - 1, 8 * v : 8 * v + 8, :] * (here[v] - edge[v]) for v in range(vregs)
+            ]
+
+            def two(i, carry):
+                here, below = list(carry[:vregs]), list(carry[vregs:])
+                e = first + 2 * i
+                here, below = energy(e, here, below)
+                here, below = energy(e + 1, here, below)
+                return (*here, *below)
+
+            lax.fori_loop(0, count // 2, two, (*here, *below))
+
+        sweep(1, frame - 2, read_field, write_work)
+
+        @pl.loop(1, PASSES - 1)
+        def _(n):
+            sweep(n + 1, frame - 2 - 2 * n, read_work, write_work)
+
+        sweep(PASSES, frame - 2 * PASSES, read_work, write_done)
+
+        for copy in store(g, slot):
+            copy.start()
+
+    for g in range(max(0, tiles - 2), tiles):
+        for copy in store(g, g % 2):
+            copy.wait()
+
+
+def diffuse(rate, a, b, own, got, own_halo, got_halo):
+    chunks, halo_chunks = len(own), len(own_halo)
+    tiles, step, pitches, side = own[0].shape
+    frame = a.shape[0]
+    block = chunks * step
+    n_in = 2 * (chunks + halo_chunks)
+    keep = jax.ShapeDtypeStruct((tiles, block, pitches, side), F32)
+    send = jax.ShapeDtypeStruct((tiles, step, pitches, side), F32)
+    size = tiles * frame * pitches * side
+    out = pl.pallas_call(
+        functools.partial(diffusion_kernel, chunks, halo_chunks),
+        out_shape=[keep] + [send] * chunks,
+        in_specs=[VMEM] * 3 + [ANY] * n_in,
+        out_specs=[ANY] * (1 + chunks),
+        scratch_shapes=[
+            pltpu.VMEM((2, frame, pitches, side), F32),
+            pltpu.VMEM((frame, pitches, side), F32),
+            pltpu.VMEM((2, 2 * block, pitches, side), F32),
+            pltpu.SemaphoreType.DMA((2, n_in)),
+            pltpu.SemaphoreType.DMA((2, chunks + 1)),
+        ],
+        compiler_params=params(),
+        cost_estimate=cost(size * PASSES * 10, size * 8),
+        name="diffuse_tiles",
+    )(rate, a, b, *own, *got, *own_halo, *got_halo)
+    return out[0], out[1:]
+
+
+def across_lanes(window, side):
+    frame, pitches = window.shape
+    turned = window.reshape(frame, 8, pitches // 8).transpose(0, 2, 1).reshape(frame, pitches)
+    return jnp.broadcast_to(turned[:, :, None], (frame, pitches, side))
+
+
+def paired_shards(
+    density,
+    source_sector,
+    source_tile,
+    matrix_id,
+    cubic_weights,
+    bin_cells,
+    wave_level,
+    energy_rate,
+    pitch_rate,
+):
+    sectors, inner = lax.axis_size("sector"), lax.axis_size("inner")
+    inner_here = lax.axis_index("inner")
+    flip, group = inner_here % 2, inner_here // 2
+    block, pitches, cell_count = density.shape
+    side = cubic_weights.shape[1]
+    tiles = cell_count // side
+    half = tiles // 2
+    step = block // CHUNKS
+    halo_chunks = PASSES // step
+    cap = slots(tiles, sectors)
+    tables = (source_sector, source_tile)
+    piece = (step, pitches, side)
+    part = jax.ShapeDtypeStruct((half,) + piece, F32)
+    yes = None
+
+    weights = split_weights(matrix_id, cubic_weights)
+
+    def at_lanes(t):
+        return pl.ds(pl.multiple_of(t * side, side), side)
+
+    def side_here():
+        return lax.axis_index("inner") % 2
+
+    swap = [(i, i ^ 1) for i in range(inner)]
+    own_pairs, got_pairs = [], []
+    for i in range(inner):
+        for pairs, shift in ((own_pairs, -2 if i % 2 == 0 else 2), (got_pairs, 2 if i % 2 == 0 else -2)):
+            if 0 <= i + shift < inner:
+                pairs.append((i, i + shift))
+
+    own, got, own_halo, got_halo = [], [], [], []
+    for k in range(CHUNKS):
+
+        def find(field, k=k):
+            here = side_here()
+            first = here * (block - step * (k + 1)) + (1 - here) * (step * k)
+            return lambda t: [(t >= 0, lambda: field.at[pl.ds(first, step), :, at_lanes(t)])]
+
+        def place(kept, sent):
+            here = side_here()
+            mine = lambda t: (t // half) == here
+            return lambda t: [
+                (mine(t), lambda: kept.at[t % half]),
+                (jnp.logical_not(mine(t)), lambda: sent.at[t % half]),
+            ]
+
+        after = own[k - 2 : k - 1] if k >= 2 else ()
+        recvs = sector_exchange(pack(find, cap, *tables, [density], piece, after))
+        kept, sent = drift(find, place, tables, weights, [density], recvs, [part, part], piece)
+        swapped = lax.ppermute(sent, "inner", swap)
+        own.append(kept)
+        got.append(swapped)
+        if k < halo_chunks:
+            own_halo.append(lax.ppermute(kept, "inner", own_pairs))
+            got_halo.append(lax.ppermute(swapped, "inner", got_pairs))
+
+    energies = energy_rate.shape[0]
+    frame = 2 * block + 2 * PASSES
+    energy_pad = jnp.pad(energy_rate[: energies - 1], ((PASSES, PASSES + 1), (0, 0)))
+    pitch_pad = jnp.pad(pitch_rate[:, : pitches - 1], ((PASSES, PASSES), (0, 1)))
+    first_energy = group * 2 * block
+    a = across_lanes(lax.dynamic_slice_in_dim(energy_pad, first_energy, frame, 0), side)
+    b = across_lanes(lax.dynamic_slice_in_dim(pitch_pad, first_energy, frame, 0), side)
+    bin_ends = jnp.cumsum(bin_cells[0])
+    cells = flip * (half * side) + jnp.arange(half * side, dtype=jnp.int32)
+    bin_of = jnp.sum((bin_ends[None, :] <= cells[:, None]).astype(jnp.int32), axis=1)
+    bins = jnp.arange(bin_ends.shape[0], dtype=jnp.int32)
+    level = jnp.sum(jnp.where(bin_of[:, None] == bins[None, :], wave_level[0][None, :], 0.0), axis=1)
+    rate = jnp.broadcast_to(level.reshape(half, 1, side), (half, 8, side))
+
+    kept, sends = diffuse(rate, a, b, own, got, own_halo, got_halo)
+
+    outs, backs = [], []
+    for k in range(CHUNKS):
+        send = sends[k]
+        if backs:
+            send, backs[-1] = lax.optimization_barrier((send, backs[-1]))
+        backs.append(lax.ppermute(send, "inner", swap))
+    for k in range(CHUNKS):
+        back = backs[k]
+
+        def find(mine, theirs, k=k):
+            here = side_here()
+            return lambda t: [
+                ((t // half) == here, lambda: mine.at[t % half, pl.ds(step * k, step)]),
+                ((t // half) != here, lambda: theirs.at[t % half]),
+            ]
+
+        def place(result, k=k):
+            return lambda t: [(t >= 0, lambda: result.at[pl.ds(step * k, step), :, at_lanes(t)])]
+
+        recvs = sector_exchange(pack(find, cap, *tables, [kept, back], piece))
+        whole = [jax.ShapeDtypeStruct(density.shape, F32)]
+        carried = outs[-1] if outs else None
+        outs += drift(find, place, tables, weights, [kept, back], recvs, whole, piece, carried)
+    return outs[-1]
+
+
+def slots(tiles, sectors):
+    return max(2, (3 * tiles + 2 * sectors - 1) // (2 * sectors))
 
 
 def order_within(sources):
@@ -97,21 +581,44 @@
     return drift_step(restored, source_sector, source_tile, matrix_id, cubic_weights)
 
 
+def pairs_fit(mesh, energies, pitches, cells, side):
+    sectors, inner = mesh.shape["sector"], mesh.shape["inner"]
+    block = energies // inner
+    tiles = cells // sectors // side
+    return (
+        sectors & (sectors - 1) == 0
+        and inner % 2 == 0
+        and tiles % 2 == 0
+        and pitches % 16 == 0
+        and side % 128 == 0
+        and block >= PASSES
+        and block % CHUNKS == 0
+        and PASSES % (block // CHUNKS) == 0
+    )
+
+
 def solution(mesh):
-    return jax.shard_map(
-        shards,
-        mesh=mesh,
-        in_specs=(
-            P("inner", None, "sector"),
-            P("inner", None, None),
-            P("inner", None, None),
-            P("inner", None, None),
-            P(),
-            P("sector", None),
-            P("sector", None),
-            P(),
-            P(),
-        ),
-        out_specs=P("inner", None, "sector"),
-        check_vma=False,
+    specs = (
+        P("inner", None, "sector"),
+        P("inner", None, None),
+        P("inner", None, None),
+        P("inner", None, None),
+        P(),
+        P("sector", None),
+        P("sector", None),
+        P(),
+        P(),
     )
+
+    def whole(*arrays):
+        energies, pitches, cells = arrays[0].shape
+        fits = pairs_fit(mesh, energies, pitches, cells, arrays[4].shape[1])
+        return jax.shard_map(
+            paired_shards if fits else shards,
+            mesh=mesh,
+            in_specs=specs,
+            out_specs=P("inner", None, "sector"),
+            check_vma=False,
+        )(*arrays)
+
+    return whole

time: 1400 us -> 901 us (0.64)
  Pallas kernels: 0 us -> 706 us
  other arithmetic: 501 us -> 0.35 us
  waiting for transfers between devices: 492 us -> 156 us
  local copies, waits for them, and re-layouts: 212 us -> 9.01 us
  blocking collectives: 147 us -> 0 us
  matrix products: 18.4 us -> 0 us
    pallas_call x0 -> x18, Pallas kernels: none -> 706 us  [the longest x8 588 us: pack(): pl.pallas_call(functools.partial(pack_kernel, find, len(arrays)), out_sha...]
    all_to_all x3 -> x0, waiting for transfers between devices: 492 us -> none  [the longest x1 180 us: shards(): lax.all_to_all(packed, 'inner', split_axis=2, concat_axis=0, tiled=True)]
    add x13 -> x1, other arithmetic: 232 us -> 0.01 us  [paired_shards(): cells = flip * (half * side) + jnp.arange(half * side, dtype=jnp.int32)]
    mul x27 -> x0, other arithmetic: 197 us -> none  [the longest x12 121 us: one_pass(): flux_p = pitch_rate[:, :-1, None] * (field[:, 1:] - field[:, :-1])]
    ppermute x0 -> x38, waiting for transfers between devices: none -> 156 us  [the longest x4 50.8 us: paired_shards(): swapped = lax.ppermute(sent, 'inner', swap)]
    all_to_all x1 -> x0, blocking collectives: 147 us -> none  [drift_step(): lax.all_to_all(outgoing, 'sector', split_axis=2, concat_axis=2, tiled=True)]
    gather x8 -> x0, local copies, waits for them, and re-layouts: 89.8 us -> none  [the longest x1 24.6 us: shards(): restored = jnp.take(returned, position, axis=2)]
    all_to_all x5 -> x0, local copies, waits for them, and re-layouts: 52.6 us -> none  [the longest x2 23.7 us: drift_step(): lax.all_to_all(outgoing, 'sector', split_axis=2, concat_axis=2, tiled=True)]
  transfers between devices with their start and end apart: 3 -> 38, of which waited for: 3 -> 10; matrix products, arithmetic and copies ran while one was open for 1% -> 0% of each run, Pallas kernels for 0% -> 63%
where the time goes in v1:
time: 901 us; the launch traced here: 898 us
  Pallas kernels  706 us (78%)
  waiting for transfers between devices  156 us (17%)
  starting transfers between devices  26 us (3%)
  local copies, waits for them, and re-layouts  9.01 us (1%)
    pallas_call x8, Pallas kernels, pack(): pl.pallas_call(functools.partial(pack_kernel, find, len(arrays)), out_sha...  588 us
    pallas_call x1, Pallas kernels, diffuse(): pl.pallas_call(functools.partial(diffusion_kernel, chunks, halo_chunks),...  60.1 us
    pallas_call x8, Pallas kernels, drift(): pl.pallas_call(body, out_shape=outs, in_specs=specs, out_specs=[ANY] * le...  52.5 us
    ppermute x4, waiting for transfers between devices, paired_shards(): swapped = lax.ppermute(sent, 'inner', swap)  50.8 us
    ppermute x4, waiting for transfers between devices, paired_shards(): backs.append(lax.ppermute(send, 'inner', swap))  46.2 us
    ppermute x24, waiting for transfers between devices, sector_exchange(): lax.ppermute(send, 'sector', [(s, s ^ d + 1) for s in range(sectors)])  29.5 us
  transfers between devices with their start and end apart: 38, of which 10 were waited for; matrix products, arithmetic and copies ran while one was open for 0% of the time, Pallas kernels for 63%

profile of v1, /device:TPU:25, one launch (start us, length us, event | category | flops | bytes accessed | tf_op | source)
XLA Modules:
  0.0 897.9 jit_solution(8511209797497572077)
XLA Ops:
  0.0 73.5 %pack_tiles.8 = (f32[6,4,64,128]{3,2,1,0:T(8,128)}, f32[6,4,64,128]{3,2,1,0:T(8,128)}, f32[6,4,64,128]{3,2,1,0:T(8,128)}) custom-call(s32[1,4,16]{2,1,0:T(4,128)} %refs_0_.21, s32[1,4,16]{2,1,0:T(4,128)} %refs_1_.5, f32[16,64,2048]{2,1,0:T(8,128)} %refs_0_.18), custom_call_target="tpu_custom_call" | custom-call | bytes 4718592 | tf_op jit(solution)/shard_map/pack_tiles/pallas_call | solution.py:103
  73.6 0.1 collective-permute-start.1
  73.7 2.1 collective-permute-start.2
  75.7 73.5 %pack_tiles.9 = (f32[6,4,64,128]{3,2,1,0:T(8,128)}, f32[6,4,64,128]{3,2,1,0:T(8,128)}, f32[6,4,64,128]{3,2,1,0:T(8,128)}) custom-call(s32[1,4,16]{2,1,0:T(4,128)} %refs_0_.21, s32[1,4,16]{2,1,0:T(4,128)} %refs_1_.5, f32[16,64,2048]{2,1,0:T(8,128)} %refs_0_.18), custom_call_target="tpu_custom_call" | custom-call | bytes 4718592 | tf_op jit(solution)/shard_map/pack_tiles/pallas_call | solution.py:103
  149.4 2.0 collective-permute-start.5
  151.4 4.7 split_weights.1.w_ref.refs_2_
  156.2 0.9 copy-done.22
  157.1 0.9 copy-done.23
  157.9 6.6 drift_chunk.8
  164.5 73.5 %pack_tiles.10 = (f32[6,4,64,128]{3,2,1,0:T(8,128)}, f32[6,4,64,128]{3,2,1,0:T(8,128)}, f32[6,4,64,128]{3,2,1,0:T(8,128)}) custom-call(s32[1,4,16]{2,1,0:T(4,128)} %refs_0_.21, s32[1,4,16]{2,1,0:T(4,128)} %refs_1_.5, f32[16,64,2048]{2,1,0:T(8,128)} %refs_0_.18, f32[8,4,64,128]{3,2,1,0:T(8,128)} %get-tuple-element.51.refs_1_.refs_0_), custom_call_target="tpu_custom_call" | custom-call | bytes 4718592 | tf_op jit(solution)/shard_map/pack_tiles/pallas_call | solution.py:103
  238.2 2.0 collective-permute-start.8
  240.3 0.9 copy-done.19
  241.1 0.9 copy-done.20
  242.0 6.6 drift_chunk.9
  248.6 73.6 %pack_tiles.11 = (f32[6,4,64,128]{3,2,1,0:T(8,128)}, f32[6,4,64,128]{3,2,1,0:T(8,128)}, f32[6,4,64,128]{3,2,1,0:T(8,128)}) custom-call(s32[1,4,16]{2,1,0:T(4,128)} %refs_0_.21, s32[1,4,16]{2,1,0:T(4,128)} %refs_1_.5, f32[16,64,2048]{2,1,0:T(8,128)} %refs_0_.18, f32[8,4,64,128]{3,2,1,0:T(8,128)} %get-tuple-element.55.refs_1_), custom_call_target="tpu_custom_call" | custom-call | bytes 4718592 | tf_op jit(solution)/shard_map/pack_tiles/pallas_call | solution.py:103
  322.2 0.1 collective-permute-start.10
  322.3 0.1 collective-permute-start.11
  322.4 1.8 collective-permute-start.9
  324.1 1.4 collective-permute-start.17
  325.5 1.4 collective-permute-start.16
  326.9 6.6 drift_chunk.10
  333.5 8.0 collective-permute-done.10.refs_2_
  341.5 6.8 collective-permute-done.11.refs_3_
  348.4 1.5 collective-permute-start.14
  349.9 6.5 drift_chunk.11
  356.4 1.4 collective-permute-start.18
  357.8 12.9 %collective-permute-done.16.refs_8_ = f32[8,4,64,128]{3,2,1,0:T(8,128)S(1)} collective-permute-done((f32[8,4,64,128]{3,2,1,0:T(8,128)S(1)}, f32[8,4,64,128]{3,2,1,0:T(8,128)S(1)}, u32[]{:S(2)}, u32[]{:S(2)}) %collective-permute-start.16) | collective-permute-done | bytes 1048608 | tf_op jit(solution)/shard_map/ppermute | solution.py:444
  370.7 1.0 copy-done.7
  371.6 1.3 collective-permute-start.20
  372.9 14.2 %collective-permute-done.12.refs_4_ = f32[8,4,64,128]{3,2,1,0:T(8,128)} collective-permute-done((f32[8,4,64,128]{3,2,1,0:T(8,128)}, f32[8,4,64,128]{3,2,1,0:T(8,128)}, u32[]{:S(2)}, u32[]{:S(2)}) %collective-permute-start.12) | collective-permute-done | bytes 1048608 | tf_op jit(solution)/shard_map/ppermute | solution.py:440
  387.1 1.3 collective-permute-start.19
  388.4 21.2 %collective-permute-done.14.refs_6_ = f32[8,4,64,128]{3,2,1,0:T(8,128)} collective-permute-done((f32[8,4,64,128]{3,2,1,0:T(8,128)}, f32[8,4,64,128]{3,2,1,0:T(8,128)}, u32[]{:S(2)}, u32[]{:S(2)}) %collective-permute-start.14) | collective-permute-done | bytes 1048608 | tf_op jit(solution)/shard_map/ppermute | solution.py:440
  409.6 1.3 collective-permute-start.21
  410.9 0.1 fusion
  411.0 0.1 copy.18
  411.1 0.1 copy.20
  411.2 0.2 reduce-window.8
  411.4 0.1 convert_reduce_fusion
  411.5 0.1 select_reduce_fusion
  411.6 15.4 %collective-permute-done.15.refs_7_ = f32[8,4,64,128]{3,2,1,0:T(8,128)S(1)} collective-permute-done((f32[8,4,64,128]{3,2,1,0:T(8,128)}, f32[8,4,64,128]{3,2,1,0:T(8,128)S(1)}, u32[]{:S(2)}, u32[]{:S(2)}) %collective-permute-start.15) | collective-permute-done | bytes 1048608 | tf_op jit(solution)/shard_map/ppermute | solution.py:440
  427.0 16.9 %collective-permute-done.21.refs_13_ = f32[8,4,64,128]{3,2,1,0:T(8,128)} collective-permute-done((f32[8,4,64,128]{3,2,1,0:T(8,128)}, f32[8,4,64,128]{3,2,1,0:T(8,128)}, u32[]{:S(2)}, u32[]{:S(2)}) %collective-permute-start.21) | collective-permute-done | bytes 1048608 | tf_op jit(solution)/shard_map/ppermute | solution.py:445
  443.9 1.8 broadcast_in_dim.45.a_ref
  445.7 1.8 broadcast_in_dim.47.b_ref
  447.5 0.6 broadcast_in_dim.43.rate_ref
  448.1 60.1 %diffuse_tiles.1 = (f32[8,16,64,128]{3,2,1,0:T(8,128)}, f32[8,4,64,128]{3,2,1,0:T(8,128)}, f32[8,4,64,128]{3,2,1,0:T(8,128)}, f32[8,4,64,128]{3,2,1,0:T(8,128)}, f32[8,4,64,128]{3,2,1,0:T(8,128)}) custom-call(f32[8,8,128]{2,1,0:T(8,128)} %broadcast_in_dim.43.rate_ref, f32[56,64,128]{2,1,0:T(8,128)} %broadcast_in_dim.45.a_ref, ...), custom_call_target="tpu_custom_call" | custom-call | flops 440401920 | bytes 29360128 | tf_op jit(solution)/shard_map/diffuse_tiles/pallas_call | solution.py:355
  508.3 0.1 collective-permute-start.22
  508.4 23.5 %collective-permute-done.22.refs_1_ = f32[8,4,64,128]{3,2,1,0:T(8,128)S(1)} collective-permute-done((f32[8,4,64,128]{3,2,1,0:T(8,128)}, f32[8,4,64,128]{3,2,1,0:T(8,128)S(1)}, u32[]{:S(2)}, u32[]{:S(2)}) %collective-permute-start.22) | collective-permute-done | bytes 1048608 | tf_op jit(solution)/shard_map/ppermute | solution.py:468
  532.0 22.7 %collective-permute-done.23.refs_1_.refs_4_ = f32[8,4,64,128]{3,2,1,0:T(8,128)S(1)} collective-permute-done((f32[8,4,64,128]{3,2,1,0:T(8,128)}, f32[8,4,64,128]{3,2,1,0:T(8,128)S(1)}, u32[]{:S(2)}, u32[]{:S(2)}) %collective-permute-start.23) | collective-permute-done | bytes 1048608 | tf_op jit(solution)/shard_map/ppermute | solution.py:468
  554.6 73.5 %pack_tiles.15 = (f32[6,4,64,128]{3,2,1,0:T(8,128)}, f32[6,4,64,128]{3,2,1,0:T(8,128)}, f32[6,4,64,128]{3,2,1,0:T(8,128)}) custom-call(s32[1,4,16]{2,1,0:T(4,128)} %refs_0_.21, s32[1,4,16]{2,1,0:T(4,128)} %refs_1_.5, f32[8,16,64,128]{3,2,1,0:T(8,128)} %get-tuple-element.68.refs_0_.refs_3_, f32[8,4,64,128]{3,2,1,0:T(8,128)} %copy-done.3), custom_call_target="tpu_custom_call" | custom-call | bytes 4718592 | tf_op jit(solution)/shard_map/pack_tiles/pallas_call | solution.py:103
  628.3 2.1 collective-permute-start.37
  630.4 73.5 %pack_tiles.14 = (f32[6,4,64,128]{3,2,1,0:T(8,128)}, f32[6,4,64,128]{3,2,1,0:T(8,128)}, f32[6,4,64,128]{3,2,1,0:T(8,128)}) custom-call(s32[1,4,16]{2,1,0:T(4,128)} %refs_0_.21, s32[1,4,16]{2,1,0:T(4,128)} %refs_1_.5, f32[8,16,64,128]{3,2,1,0:T(8,128)} %get-tuple-element.68.refs_0_.refs_3_, f32[8,4,64,128]{3,2,1,0:T(8,128)} %copy-done.4), custom_call_target="tpu_custom_call" | custom-call | bytes 4718592 | tf_op jit(solution)/shard_map/pack_tiles/pallas_call | solution.py:103
  704.0 73.5 %pack_tiles.13 = (f32[6,4,64,128]{3,2,1,0:T(8,128)}, f32[6,4,64,128]{3,2,1,0:T(8,128)}, f32[6,4,64,128]{3,2,1,0:T(8,128)}) custom-call(s32[1,4,16]{2,1,0:T(4,128)} %refs_0_.21, s32[1,4,16]{2,1,0:T(4,128)} %refs_1_.5, f32[8,16,64,128]{3,2,1,0:T(8,128)} %get-tuple-element.68.refs_0_.refs_3_, f32[8,4,64,128]{3,2,1,0:T(8,128)} %copy-done.2), custom_call_target="tpu_custom_call" | custom-call | bytes 4718592 | tf_op jit(solution)/shard_map/pack_tiles/pallas_call | solution.py:103
  777.6 0.1 collective-permute-start.34
  777.7 1.7 collective-permute-start.29
  779.5 0.1 collective-permute-start.30
  779.6 1.6 collective-permute-start.31
  781.2 73.5 %pack_tiles.12 = (f32[6,4,64,128]{3,2,1,0:T(8,128)}, f32[6,4,64,128]{3,2,1,0:T(8,128)}, f32[6,4,64,128]{3,2,1,0:T(8,128)}) custom-call(s32[1,4,16]{2,1,0:T(4,128)} %refs_0_.21, s32[1,4,16]{2,1,0:T(4,128)} %refs_1_.5, f32[8,16,64,128]{3,2,1,0:T(8,128)} %get-tuple-element.68.refs_0_.refs_3_, f32[8,4,64,128]{3,2,1,0:T(8,128)} %copy-done.5), custom_call_target="tpu_custom_call" | custom-call | bytes 4718592 | tf_op jit(solution)/shard_map/pack_tiles/pallas_call | solution.py:103
  854.8 0.1 collective-permute-start.27
  854.9 2.0 collective-permute-start.28
  857.0 6.6 drift_chunk.12.refs_8_
  863.6 6.6 drift_chunk.13.refs_8_
  870.2 6.6 drift_chunk.14.refs_8_
  876.8 14.6 %collective-permute-done.28.refs_7_ = f32[6,4,64,128]{3,2,1,0:T(8,128)} collective-permute-done((f32[6,4,64,128]{3,2,1,0:T(8,128)}, f32[6,4,64,128]{3,2,1,0:T(8,128)}, u32[]{:S(2)}, u32[]{:S(2)}) %collective-permute-start.28) | collective-permute-done | bytes 786464 | tf_op jit(solution)/shard_map/ppermute | solution.py:118
  891.3 6.6 drift_chunk.15
  (98 shorter events, 0.9 us)
Async XLA Ops:
  73.5 75.9 %collective-permute-start = (f32[6,4,64,128]{3,2,1,0:T(8,128)}, f32[6,4,64,128]{3,2,1,0:T(8,128)S(1)}, u32[]{:S(2)}, u32[]{:S(2)}) collective-permute-start(f32[6,4,64,128]{3,2,1,0:T(8,128)} %get-tuple-element.48), channel_id=1, source_target_pairs={{0,8},{8,0},{16,24},{24,16},{1,9},{9,1},{17,25},{25,17},{2,10},{10... | collective-permute-start | bytes 2359304 | tf_op jit(solution)/shard_map/ppermute | solution.py:118
  73.6 82.6 %collective-permute-start.1 = (f32[6,4,64,128]{3,2,1,0:T(8,128)}, f32[6,4,64,128]{3,2,1,0:T(8,128)S(1)}, u32[]{:S(2)}, u32[]{:S(2)}) collective-permute-start(f32[6,4,64,128]{3,2,1,0:T(8,128)} %get-tuple-element.49), channel_id=1, source_target_pairs={{0,16},{8,24},{16,0},{24,8},{1,17},{9,25},{17,1},{25,9},{2,18},{10... | collective-permute-start | bytes 2359304 | tf_op jit(solution)/shard_map/ppermute | solution.py:118
  73.7 82.5 %collective-permute-start.2 = (f32[6,4,64,128]{3,2,1,0:T(8,128)}, f32[6,4,64,128]{3,2,1,0:T(8,128)S(1)}, u32[]{:S(2)}, u32[]{:S(2)}) collective-permute-start(f32[6,4,64,128]{3,2,1,0:T(8,128)} %get-tuple-element.50), channel_id=1, source_target_pairs={{0,24},{8,16},{16,8},{24,0},{1,25},{9,17},{17,9},{25,1},{2,26},{10... | collective-permute-start | bytes 2359304 | tf_op jit(solution)/shard_map/ppermute | solution.py:118
  149.2 89.0 %collective-permute-start.3 = (f32[6,4,64,128]{3,2,1,0:T(8,128)}, f32[6,4,64,128]{3,2,1,0:T(8,128)S(1)}, u32[]{:S(2)}, u32[]{:S(2)}) collective-permute-start(f32[6,4,64,128]{3,2,1,0:T(8,128)} %get-tuple-element.52), channel_id=1, source_target_pairs={{0,8},{8,0},{16,24},{24,16},{1,9},{9,1},{17,25},{25,17},{2,10},{10... | collective-permute-start | bytes 2359304 | tf_op jit(solution)/shard_map/ppermute | solution.py:118
  149.3 90.9 %collective-permute-start.4 = (f32[6,4,64,128]{3,2,1,0:T(8,128)}, f32[6,4,64,128]{3,2,1,0:T(8,128)S(1)}, u32[]{:S(2)}, u32[]{:S(2)}) collective-permute-start(f32[6,4,64,128]{3,2,1,0:T(8,128)} %get-tuple-element.53), channel_id=1, source_target_pairs={{0,16},{8,24},{16,0},{24,8},{1,17},{9,25},{17,1},{25,9},{2,18},{10... | collective-permute-start | bytes 2359304 | tf_op jit(solution)/shard_map/ppermute | solution.py:118
  149.4 6.8 copy-start.21
  149.4 90.8 %collective-permute-start.5 = (f32[6,4,64,128]{3,2,1,0:T(8,128)}, f32[6,4,64,128]{3,2,1,0:T(8,128)S(1)}, u32[]{:S(2)}, u32[]{:S(2)}) collective-permute-start(f32[6,4,64,128]{3,2,1,0:T(8,128)} %get-tuple-element.54), channel_id=1, source_target_pairs={{0,24},{8,16},{16,8},{24,0},{1,25},{9,17},{17,9},{25,1},{2,26},{10... | collective-permute-start | bytes 2359304 | tf_op jit(solution)/shard_map/ppermute | solution.py:118
  156.2 0.9 copy-start.22
  238.0 84.4 %collective-permute-start.6 = (f32[6,4,64,128]{3,2,1,0:T(8,128)}, f32[6,4,64,128]{3,2,1,0:T(8,128)S(1)}, u32[]{:S(2)}, u32[]{:S(2)}) collective-permute-start(f32[6,4,64,128]{3,2,1,0:T(8,128)} %get-tuple-element.56), channel_id=1, source_target_pairs={{0,8},{8,0},{16,24},{24,16},{1,9},{9,1},{17,25},{25,17},{2,10},{10... | collective-permute-start | bytes 2359304 | tf_op jit(solution)/shard_map/ppermute | solution.py:118
  238.1 86.0 %collective-permute-start.7 = (f32[6,4,64,128]{3,2,1,0:T(8,128)}, f32[6,4,64,128]{3,2,1,0:T(8,128)S(1)}, u32[]{:S(2)}, u32[]{:S(2)}) collective-permute-start(f32[6,4,64,128]{3,2,1,0:T(8,128)} %get-tuple-element.57), channel_id=1, source_target_pairs={{0,16},{8,24},{16,0},{24,8},{1,17},{9,25},{17,1},{25,9},{2,18},{10... | collective-permute-start | bytes 2359304 | tf_op jit(solution)/shard_map/ppermute | solution.py:118
  238.2 2.1 copy-start.18
  238.2 87.3 %copy-start = (f32[8,4,64,128]{3,2,1,0:T(8,128)S(1)}, f32[8,4,64,128]{3,2,1,0:T(8,128)}, u32[]{:S(2)}) copy-start(f32[8,4,64,128]{3,2,1,0:T(8,128)} %get-tuple-element.51.refs_1_.refs_0_) | copy-start | bytes 3145732
  238.2 87.3 %collective-permute-start.8 = (f32[6,4,64,128]{3,2,1,0:T(8,128)}, f32[6,4,64,128]{3,2,1,0:T(8,128)}, u32[]{:S(2)}, u32[]{:S(2)}) collective-permute-start(f32[6,4,64,128]{3,2,1,0:T(8,128)} %get-tuple-element.58), channel_id=1, source_target_pairs={{0,24},{8,16},{16,8},{24,0},{1,25},{9,17},{17,9},{25,1},{2,26},{10... | collective-permute-start | bytes 2359304 | tf_op jit(solution)/shard_map/ppermute | solution.py:118
  240.2 0.9 copy-start.19
  248.6 75.6 %copy-start.1 = (f32[8,4,64,128]{3,2,1,0:T(8,128)S(1)}, f32[8,4,64,128]{3,2,1,0:T(8,128)}, u32[]{:S(2)}) copy-start(f32[8,4,64,128]{3,2,1,0:T(8,128)} %get-tuple-element.55.refs_1_) | copy-start | bytes 3145732
  322.2 19.3 %collective-permute-start.10 = (f32[6,4,64,128]{3,2,1,0:T(8,128)}, f32[6,4,64,128]{3,2,1,0:T(8,128)}, u32[]{:S(2)}, u32[]{:S(2)}) collective-permute-start(f32[6,4,64,128]{3,2,1,0:T(8,128)} %get-tuple-element.61), channel_id=1, source_target_pairs={{0,16},{8,24},{16,0},{24,8},{1,17},{9,25},{17,1},{25,9},{2,18},{10... | collective-permute-start | bytes 2359304 | tf_op jit(solution)/shard_map/ppermute | solution.py:118
  322.3 26.1 %collective-permute-start.11 = (f32[6,4,64,128]{3,2,1,0:T(8,128)}, f32[6,4,64,128]{3,2,1,0:T(8,128)}, u32[]{:S(2)}, u32[]{:S(2)}) collective-permute-start(f32[6,4,64,128]{3,2,1,0:T(8,128)} %get-tuple-element.62), channel_id=1, source_target_pairs={{0,24},{8,16},{16,8},{24,0},{1,25},{9,17},{17,9},{25,1},{2,26},{10... | collective-permute-start | bytes 2359304 | tf_op jit(solution)/shard_map/ppermute | solution.py:118
  322.4 4.5 copy-start.16
  322.4 26.0 %collective-permute-start.9 = (f32[6,4,64,128]{3,2,1,0:T(8,128)}, f32[6,4,64,128]{3,2,1,0:T(8,128)}, u32[]{:S(2)}, u32[]{:S(2)}) collective-permute-start(f32[6,4,64,128]{3,2,1,0:T(8,128)} %get-tuple-element.60), channel_id=1, source_target_pairs={{0,8},{8,0},{16,24},{24,16},{1,9},{9,1},{17,25},{25,17},{2,10},{10... | collective-permute-start | bytes 2359304 | tf_op jit(solution)/shard_map/ppermute | solution.py:118
  324.1 2.8 copy-start.17
  324.1 32.3 %collective-permute-start.17 = (f32[8,4,64,128]{3,2,1,0:T(8,128)S(1)}, f32[8,4,64,128]{3,2,1,0:T(8,128)S(1)}, u32[]{:S(2)}, u32[]{:S(2)}) collective-permute-start(f32[8,4,64,128]{3,2,1,0:T(8,128)S(1)} %copy-done.1), channel_id=1, source_target_pairs={{1,3},{2,0},{3,5},{4,2},{5,7},{6,4},{9,11},{10,8},{11,13},{12,10},... | collective-permute-start | bytes 3145736 | tf_op jit(solution)/shard_map/ppermute | solution.py:444
  325.5 45.1 %collective-permute-start.16 = (f32[8,4,64,128]{3,2,1,0:T(8,128)S(1)}, f32[8,4,64,128]{3,2,1,0:T(8,128)S(1)}, u32[]{:S(2)}, u32[]{:S(2)}) collective-permute-start(f32[8,4,64,128]{3,2,1,0:T(8,128)S(1)} %copy-done), channel_id=1, source_target_pairs={{1,3},{2,0},{3,5},{4,2},{5,7},{6,4},{9,11},{10,8},{11,13},{12,10},... | collective-permute-start | bytes 3145736 | tf_op jit(solution)/shard_map/ppermute | solution.py:444
  333.5 77.4 %copy-start.24 = (f32[128,64]{0,1:T(8,128)S(1)}, f32[128,64]{0,1:T(8,128)}, u32[]{:S(2)}) copy-start(f32[128,64]{0,1:T(8,128)} %param.16) | copy-start | bytes 98308
  333.5 77.4 %copy-start.25 = (f32[128,64]{0,1:T(8,128)S(1)}, f32[128,64]{0,1:T(8,128)}, u32[]{:S(2)}) copy-start(f32[128,64]{0,1:T(8,128)} %param.17) | copy-start | bytes 98308
  333.5 77.7 %copy-start.27 = (s32[1,8]{1,0:T(1,128)S(1)}, s32[1,8]{1,0:T(1,128)}, u32[]{:S(2)}) copy-start(s32[1,8]{1,0:T(1,128)} %param.14) | copy-start | bytes 100
  333.5 78.0 %copy-start.26 = (f32[1,8]{1,0:T(1,128)S(1)}, f32[1,8]{1,0:T(1,128)}, u32[]{:S(2)}) copy-start(f32[1,8]{1,0:T(1,128)} %param.15) | copy-start | bytes 100
  341.5 30.1 %collective-permute-start.13 = (f32[8,4,64,128]{3,2,1,0:T(8,128)}, f32[8,4,64,128]{3,2,1,0:T(8,128)}, u32[]{:S(2)}, u32[]{:S(2)}) collective-permute-start(f32[8,4,64,128]{3,2,1,0:T(8,128)} %get-tuple-element.65), channel_id=1, source_target_pairs={{0,1},{1,0},{2,3},{3,2},{4,5},{5,4},{6,7},{7,6},{8,9},{9,8},{10,11... | collective-permute-start | bytes 3145736 | tf_op jit(solution)/shard_map/ppermute | solution.py:440
  348.4 38.7 %collective-permute-start.12 = (f32[8,4,64,128]{3,2,1,0:T(8,128)}, f32[8,4,64,128]{3,2,1,0:T(8,128)}, u32[]{:S(2)}, u32[]{:S(2)}) collective-permute-start(f32[8,4,64,128]{3,2,1,0:T(8,128)} %get-tuple-element.64), channel_id=1, source_target_pairs={{0,1},{1,0},{2,3},{3,2},{4,5},{5,4},{6,7},{7,6},{8,9},{9,8},{10,11... | collective-permute-start | bytes 3145736 | tf_op jit(solution)/shard_map/ppermute | solution.py:440
  348.4 61.2 %collective-permute-start.14 = (f32[8,4,64,128]{3,2,1,0:T(8,128)}, f32[8,4,64,128]{3,2,1,0:T(8,128)}, u32[]{:S(2)}, u32[]{:S(2)}) collective-permute-start(f32[8,4,64,128]{3,2,1,0:T(8,128)} %get-tuple-element.66), channel_id=1, source_target_pairs={{0,1},{1,0},{2,3},{3,2},{4,5},{5,4},{6,7},{7,6},{8,9},{9,8},{10,11... | collective-permute-start | bytes 3145736 | tf_op jit(solution)/shard_map/ppermute | solution.py:440
  356.4 91.7 %copy-start.6 = (f32[8,4,64,128]{3,2,1,0:T(8,128)}, f32[8,4,64,128]{3,2,1,0:T(8,128)S(1)}, u32[]{:S(2)}) copy-start(f32[8,4,64,128]{3,2,1,0:T(8,128)S(1)} %collective-permute-done.17.refs_9_) | copy-start | bytes 3145732
  356.4 55.1 %collective-permute-start.18 = (f32[8,4,64,128]{3,2,1,0:T(8,128)}, f32[8,4,64,128]{3,2,1,0:T(8,128)S(1)}, u32[]{:S(2)}, u32[]{:S(2)}) collective-permute-start(f32[8,4,64,128]{3,2,1,0:T(8,128)} %get-tuple-element.59.refs_2_), channel_id=1, source_target_pairs={{1,3},{2,0},{3,5},{4,2},{5,7},{6,4},{9,11},{10,8},{11,13},{12,10},... | collective-permute-start | bytes 3145736 | tf_op jit(solution)/shard_map/ppermute | solution.py:444
  370.7 1.0 copy-start.7
  371.6 55.4 %collective-permute-start.15 = (f32[8,4,64,128]{3,2,1,0:T(8,128)}, f32[8,4,64,128]{3,2,1,0:T(8,128)S(1)}, u32[]{:S(2)}, u32[]{:S(2)}) collective-permute-start(f32[8,4,64,128]{3,2,1,0:T(8,128)} %get-tuple-element.67), channel_id=1, source_target_pairs={{0,1},{1,0},{2,3},{3,2},{4,5},{5,4},{6,7},{7,6},{8,9},{9,8},{10,11... | collective-permute-start | bytes 3145736 | tf_op jit(solution)/shard_map/ppermute | solution.py:440
  371.6 55.4 %collective-permute-start.20 = (f32[8,4,64,128]{3,2,1,0:T(8,128)}, f32[8,4,64,128]{3,2,1,0:T(8,128)}, u32[]{:S(2)}, u32[]{:S(2)}) collective-permute-start(f32[8,4,64,128]{3,2,1,0:T(8,128)} %collective-permute-done.13.refs_5_), channel_id=1, source_target_pairs={{0,2},{2,4},{3,1},{4,6},{5,3},{7,5},{8,10},{10,12},{11,9},{12,14},... | collective-permute-start | bytes 3145736 | tf_op jit(solution)/shard_map/ppermute | solution.py:445
  387.1 39.9 %collective-permute-start.19 = (f32[8,4,64,128]{3,2,1,0:T(8,128)}, f32[8,4,64,128]{3,2,1,0:T(8,128)}, u32[]{:S(2)}, u32[]{:S(2)}) collective-permute-start(f32[8,4,64,128]{3,2,1,0:T(8,128)} %collective-permute-done.12.refs_4_), channel_id=1, source_target_pairs={{0,2},{2,4},{3,1},{4,6},{5,3},{7,5},{8,10},{10,12},{11,9},{12,14},... | collective-permute-start | bytes 3145736 | tf_op jit(solution)/shard_map/ppermute | solution.py:445
  409.6 34.3 %collective-permute-start.21 = (f32[8,4,64,128]{3,2,1,0:T(8,128)}, f32[8,4,64,128]{3,2,1,0:T(8,128)}, u32[]{:S(2)}, u32[]{:S(2)}) collective-permute-start(f32[8,4,64,128]{3,2,1,0:T(8,128)} %collective-permute-done.14.refs_6_), channel_id=1, source_target_pairs={{0,2},{2,4},{3,1},{4,6},{5,3},{7,5},{8,10},{10,12},{11,9},{12,14},... | collective-permute-start | bytes 3145736 | tf_op jit(solution)/shard_map/ppermute | solution.py:445
  411.6 36.6 %copy-start.8 = (f32[8,4,64,128]{3,2,1,0:T(8,128)}, f32[8,4,64,128]{3,2,1,0:T(8,128)S(1)}, u32[]{:S(2)}) copy-start(f32[8,4,64,128]{3,2,1,0:T(8,128)S(1)} %collective-permute-done.18.refs_10_) | copy-start | bytes 3145732
  427.0 21.2 %copy-start.9 = (f32[8,4,64,128]{3,2,1,0:T(8,128)}, f32[8,4,64,128]{3,2,1,0:T(8,128)S(1)}, u32[]{:S(2)}) copy-start(f32[8,4,64,128]{3,2,1,0:T(8,128)S(1)} %collective-permute-done.15.refs_7_) | copy-start | bytes 3145732
  508.3 23.7 %collective-permute-start.22 = (f32[8,4,64,128]{3,2,1,0:T(8,128)}, f32[8,4,64,128]{3,2,1,0:T(8,128)S(1)}, u32[]{:S(2)}, u32[]{:S(2)}) collective-permute-start(f32[8,4,64,128]{3,2,1,0:T(8,128)} %get-tuple-element.72), channel_id=1, source_target_pairs={{0,1},{1,0},{2,3},{3,2},{4,5},{5,4},{6,7},{7,6},{8,9},{9,8},{10,11... | collective-permute-start | bytes 3145736 | tf_op jit(solution)/shard_map/ppermute | solution.py:468
  532.0 22.7 %copy-start.3 = (f32[8,4,64,128]{3,2,1,0:T(8,128)}, f32[8,4,64,128]{3,2,1,0:T(8,128)S(1)}, u32[]{:S(2)}) copy-start(f32[8,4,64,128]{3,2,1,0:T(8,128)S(1)} %collective-permute-done.22.refs_1_) | copy-start | bytes 3145732
  532.0 22.7 %collective-permute-start.23 = (f32[8,4,64,128]{3,2,1,0:T(8,128)}, f32[8,4,64,128]{3,2,1,0:T(8,128)S(1)}, u32[]{:S(2)}, u32[]{:S(2)}) collective-permute-start(f32[8,4,64,128]{3,2,1,0:T(8,128)} %get-tuple-element.73), channel_id=1, source_target_pairs={{0,1},{1,0},{2,3},{3,2},{4,5},{5,4},{6,7},{7,6},{8,9},{9,8},{10,11... | collective-permute-start | bytes 3145736 | tf_op jit(solution)/shard_map/ppermute | solution.py:468
  554.6 75.8 %copy-start.4 = (f32[8,4,64,128]{3,2,1,0:T(8,128)}, f32[8,4,64,128]{3,2,1,0:T(8,128)S(1)}, u32[]{:S(2)}) copy-start(f32[8,4,64,128]{3,2,1,0:T(8,128)S(1)} %collective-permute-done.23.refs_1_.refs_4_) | copy-start | bytes 3145732
  554.6 75.7 %collective-permute-start.24 = (f32[8,4,64,128]{3,2,1,0:T(8,128)}, f32[8,4,64,128]{3,2,1,0:T(8,128)S(1)}, u32[]{:S(2)}, u32[]{:S(2)}) collective-permute-start(f32[8,4,64,128]{3,2,1,0:T(8,128)} %get-tuple-element.74), channel_id=1, source_target_pairs={{0,1},{1,0},{2,3},{3,2},{4,5},{5,4},{6,7},{7,6},{8,9},{9,8},{10,11... | collective-permute-start | bytes 3145736 | tf_op jit(solution)/shard_map/ppermute | solution.py:468
  628.2 149.4 %collective-permute-start.35 = (f32[6,4,64,128]{3,2,1,0:T(8,128)}, f32[6,4,64,128]{3,2,1,0:T(8,128)S(1)}, u32[]{:S(2)}, u32[]{:S(2)}) collective-permute-start(f32[6,4,64,128]{3,2,1,0:T(8,128)} %get-tuple-element.88), channel_id=1, source_target_pairs={{0,8},{8,0},{16,24},{24,16},{1,9},{9,1},{17,25},{25,17},{2,10},{10... | collective-permute-start | bytes 2359304 | tf_op jit(solution)/shard_map/ppermute | solution.py:118
  628.2 149.4 %collective-permute-start.36 = (f32[6,4,64,128]{3,2,1,0:T(8,128)}, f32[6,4,64,128]{3,2,1,0:T(8,128)S(1)}, u32[]{:S(2)}, u32[]{:S(2)}) collective-permute-start(f32[6,4,64,128]{3,2,1,0:T(8,128)} %get-tuple-element.89), channel_id=1, source_target_pairs={{0,16},{8,24},{16,0},{24,8},{1,17},{9,25},{17,1},{25,9},{2,18},{10... | collective-permute-start | bytes 2359304 | tf_op jit(solution)/shard_map/ppermute | solution.py:118
  628.3 149.4 %collective-permute-start.37 = (f32[6,4,64,128]{3,2,1,0:T(8,128)}, f32[6,4,64,128]{3,2,1,0:T(8,128)S(1)}, u32[]{:S(2)}, u32[]{:S(2)}) collective-permute-start(f32[6,4,64,128]{3,2,1,0:T(8,128)} %get-tuple-element.90), channel_id=1, source_target_pairs={{0,24},{8,16},{16,8},{24,0},{1,25},{9,17},{17,9},{25,1},{2,26},{10... | collective-permute-start | bytes 2359304 | tf_op jit(solution)/shard_map/ppermute | solution.py:118
  630.4 73.6 %copy-start.2 = (f32[8,4,64,128]{3,2,1,0:T(8,128)}, f32[8,4,64,128]{3,2,1,0:T(8,128)S(1)}, u32[]{:S(2)}) copy-start(f32[8,4,64,128]{3,2,1,0:T(8,128)S(1)} %collective-permute-done.24.refs_1_.refs_4_) | copy-start | bytes 3145732
  630.4 149.2 %collective-permute-start.25 = (f32[8,4,64,128]{3,2,1,0:T(8,128)}, f32[8,4,64,128]{3,2,1,0:T(8,128)S(1)}, u32[]{:S(2)}, u32[]{:S(2)}) collective-permute-start(f32[8,4,64,128]{3,2,1,0:T(8,128)} %get-tuple-element.75), channel_id=1, source_target_pairs={{0,1},{1,0},{2,3},{3,2},{4,5},{5,4},{6,7},{7,6},{8,9},{9,8},{10,11... | collective-permute-start | bytes 3145736 | tf_op jit(solution)/shard_map/ppermute | solution.py:468
  703.9 75.6 %collective-permute-start.32 = (f32[6,4,64,128]{3,2,1,0:T(8,128)}, f32[6,4,64,128]{3,2,1,0:T(8,128)S(1)}, u32[]{:S(2)}, u32[]{:S(2)}) collective-permute-start(f32[6,4,64,128]{3,2,1,0:T(8,128)} %get-tuple-element.84), channel_id=1, source_target_pairs={{0,8},{8,0},{16,24},{24,16},{1,9},{9,1},{17,25},{25,17},{2,10},{10... | collective-permute-start | bytes 2359304 | tf_op jit(solution)/shard_map/ppermute | solution.py:118
  777.5 79.4 %copy-start.10 = (f32[6,4,64,128]{3,2,1,0:T(8,128)}, f32[6,4,64,128]{3,2,1,0:T(8,128)S(1)}, u32[]{:S(2)}) copy-start(f32[6,4,64,128]{3,2,1,0:T(8,128)S(1)} %collective-permute-done.35.refs_2_) | copy-start | bytes 2359300
  777.5 77.2 %collective-permute-start.33 = (f32[6,4,64,128]{3,2,1,0:T(8,128)}, f32[6,4,64,128]{3,2,1,0:T(8,128)S(1)}, u32[]{:S(2)}, u32[]{:S(2)}) collective-permute-start(f32[6,4,64,128]{3,2,1,0:T(8,128)} %get-tuple-element.85), channel_id=1, source_target_pairs={{0,16},{8,24},{16,0},{24,8},{1,17},{9,25},{17,1},{25,9},{2,18},{10... | collective-permute-start | bytes 2359304 | tf_op jit(solution)/shard_map/ppermute | solution.py:118
  777.6 79.3 %copy-start.11 = (f32[6,4,64,128]{3,2,1,0:T(8,128)}, f32[6,4,64,128]{3,2,1,0:T(8,128)S(1)}, u32[]{:S(2)}) copy-start(f32[6,4,64,128]{3,2,1,0:T(8,128)S(1)} %collective-permute-done.36.refs_3_) | copy-start | bytes 2359300
  777.6 77.2 %collective-permute-start.34 = (f32[6,4,64,128]{3,2,1,0:T(8,128)}, f32[6,4,64,128]{3,2,1,0:T(8,128)}, u32[]{:S(2)}, u32[]{:S(2)}) collective-permute-start(f32[6,4,64,128]{3,2,1,0:T(8,128)} %get-tuple-element.86), channel_id=1, source_target_pairs={{0,24},{8,16},{16,8},{24,0},{1,25},{9,17},{17,9},{25,1},{2,26},{10... | collective-permute-start | bytes 2359304 | tf_op jit(solution)/shard_map/ppermute | solution.py:118
  777.7 79.2 %copy-start.12 = (f32[6,4,64,128]{3,2,1,0:T(8,128)}, f32[6,4,64,128]{3,2,1,0:T(8,128)S(1)}, u32[]{:S(2)}) copy-start(f32[6,4,64,128]{3,2,1,0:T(8,128)S(1)} %collective-permute-done.37.refs_4_) | copy-start | bytes 2359300
  777.7 77.2 %collective-permute-start.29 = (f32[6,4,64,128]{3,2,1,0:T(8,128)}, f32[6,4,64,128]{3,2,1,0:T(8,128)}, u32[]{:S(2)}, u32[]{:S(2)}) collective-permute-start(f32[6,4,64,128]{3,2,1,0:T(8,128)} %get-tuple-element.80), channel_id=1, source_target_pairs={{0,8},{8,0},{16,24},{24,16},{1,9},{9,1},{17,25},{25,17},{2,10},{10... | collective-permute-start | bytes 2359304 | tf_op jit(solution)/shard_map/ppermute | solution.py:118
  779.5 84.1 %copy-start.13 = (f32[6,4,64,128]{3,2,1,0:T(8,128)}, f32[6,4,64,128]{3,2,1,0:T(8,128)S(1)}, u32[]{:S(2)}) copy-start(f32[6,4,64,128]{3,2,1,0:T(8,128)S(1)} %collective-permute-done.32.refs_5_) | copy-start | bytes 2359300
  779.5 90.7 %collective-permute-start.30 = (f32[6,4,64,128]{3,2,1,0:T(8,128)}, f32[6,4,64,128]{3,2,1,0:T(8,128)}, u32[]{:S(2)}, u32[]{:S(2)}) collective-permute-start(f32[6,4,64,128]{3,2,1,0:T(8,128)} %get-tuple-element.81), channel_id=1, source_target_pairs={{0,16},{8,24},{16,0},{24,8},{1,17},{9,25},{17,1},{25,9},{2,18},{10... | collective-permute-start | bytes 2359304 | tf_op jit(solution)/shard_map/ppermute | solution.py:118
  779.6 1.6 copy-start.5
  779.6 90.5 %collective-permute-start.31 = (f32[6,4,64,128]{3,2,1,0:T(8,128)}, f32[6,4,64,128]{3,2,1,0:T(8,128)}, u32[]{:S(2)}, u32[]{:S(2)}) collective-permute-start(f32[6,4,64,128]{3,2,1,0:T(8,128)} %get-tuple-element.82), channel_id=1, source_target_pairs={{0,24},{8,16},{16,8},{24,0},{1,25},{9,17},{17,9},{25,1},{2,26},{10... | collective-permute-start | bytes 2359304 | tf_op jit(solution)/shard_map/ppermute | solution.py:118
  854.7 8.8 copy-start.14
  854.7 22.0 %collective-permute-start.26 = (f32[6,4,64,128]{3,2,1,0:T(8,128)}, f32[6,4,64,128]{3,2,1,0:T(8,128)S(1)}, u32[]{:S(2)}, u32[]{:S(2)}) collective-permute-start(f32[6,4,64,128]{3,2,1,0:T(8,128)} %get-tuple-element.76), channel_id=1, source_target_pairs={{0,8},{8,0},{16,24},{24,16},{1,9},{9,1},{17,25},{25,17},{2,10},{10... | collective-permute-start | bytes 2359304 | tf_op jit(solution)/shard_map/ppermute | solution.py:118
  854.8 21.9 %collective-permute-start.27 = (f32[6,4,64,128]{3,2,1,0:T(8,128)}, f32[6,4,64,128]{3,2,1,0:T(8,128)}, u32[]{:S(2)}, u32[]{:S(2)}) collective-permute-start(f32[6,4,64,128]{3,2,1,0:T(8,128)} %get-tuple-element.77), channel_id=1, source_target_pairs={{0,16},{8,24},{16,0},{24,8},{1,17},{9,25},{17,1},{25,9},{2,18},{10... | collective-permute-start | bytes 2359304 | tf_op jit(solution)/shard_map/ppermute | solution.py:118
  854.9 36.4 %collective-permute-start.28 = (f32[6,4,64,128]{3,2,1,0:T(8,128)}, f32[6,4,64,128]{3,2,1,0:T(8,128)}, u32[]{:S(2)}, u32[]{:S(2)}) collective-permute-start(f32[6,4,64,128]{3,2,1,0:T(8,128)} %get-tuple-element.78), channel_id=1, source_target_pairs={{0,24},{8,16},{16,8},{24,0},{1,25},{9,17},{17,9},{25,1},{2,26},{10... | collective-permute-start | bytes 2359304 | tf_op jit(solution)/shard_map/ppermute | solution.py:118
  876.8 14.6 %copy-start.15 = (f32[6,4,64,128]{3,2,1,0:T(8,128)}, f32[6,4,64,128]{3,2,1,0:T(8,128)S(1)}, u32[]{:S(2)}) copy-start(f32[6,4,64,128]{3,2,1,0:T(8,128)S(1)} %collective-permute-done.26.refs_5_) | copy-start | bytes 2359300
  (2 other events, 1.7 us)

commit v2 on v1

--- a/solution.py
+++ b/solution.py
@@ -8,9 +8,8 @@
 from jax.sharding import PartitionSpec as P
 
 PASSES = 12
-CHUNKS = 4
-VMEM_LIMIT = 58 * 1024 * 1024
-ANY = pl.BlockSpec(memory_space=pl.ANY)
+VMEM_LIMIT = 63 * 1024 * 1024
+ANY = pl.BlockSpec(memory_space=pltpu.HBM)
 SMEM = pl.BlockSpec(memory_space=pltpu.SMEM)
 VMEM = pl.BlockSpec(memory_space=pltpu.VMEM)
 F32 = jnp.float32
@@ -21,8 +20,8 @@
     return pltpu.CompilerParams(vmem_limit_bytes=VMEM_LIMIT)
 
 
-def cost(flops, bytes_accessed):
-    return pl.CostEstimate(flops=flops, bytes_accessed=bytes_accessed, transcendentals=0)
+def cost():
+    return pl.CostEstimate(flops=0, bytes_accessed=1024, transcendentals=0)
 
 
 def weights_kernel(mid_ref, w_ref, out_ref, raw, sems):
@@ -60,21 +59,21 @@
             pltpu.SemaphoreType.DMA((tiles,)),
         ],
         compiler_params=params(),
-        cost_estimate=cost(tiles * side * side * 8, tiles * side * side * 12),
+        cost_estimate=cost(),
         name="split_weights",
     )(matrix_id, cubic_weights)
 
 
-def pack_kernel(find, n_arrays, sec_ref, til_ref, *refs):
-    sectors, tiles = sec_ref.shape[1], sec_ref.shape[2]
-    sends, sems = refs[-sectors:-1], refs[-1]
+def pack_kernel(find, n_arrays, offsets, sec_ref, til_ref, *refs):
+    tiles, n = sec_ref.shape[2], len(offsets)
+    sends, room, in_sems, out_sems = refs[-n - 3 : -3], *refs[-3:]
     pieces = find(*refs[:n_arrays])
     me = lax.axis_index("sector")
     counts = []
-    for d in range(1, sectors):
+    for i, d in enumerate(offsets):
         dest = me ^ d
 
-        def body(t, count, d=d, dest=dest):
+        def body(t, count, i=i, dest=dest):
             hit = sec_ref[0, dest, t] == me
 
             @pl.when(hit)
@@ -83,52 +82,69 @@
 
                     @pl.when(guard)
                     def _():
-                        pltpu.make_async_copy(piece(), sends[d - 1].at[count], sems.at[d - 1, count]).start()
+                        pltpu.make_async_copy(piece(), room.at[i, count], in_sems.at[i, count]).start()
 
             return count + hit.astype(jnp.int32)
 
         counts.append(lax.fori_loop(0, tiles, body, jnp.int32(0)))
-    for d in range(1, sectors):
-
-        @pl.loop(0, counts[d - 1])
-        def _(slot, d=d):
-            there = sends[d - 1].at[slot]
-            pltpu.make_async_copy(there, there, sems.at[d - 1, slot]).wait()
-
-
-def pack(find, cap, source_sector, source_tile, arrays, piece, after=()):
-    sectors = source_sector.shape[1]
+    for i in range(n):
+
+        @pl.loop(0, counts[i])
+        def _(slot, i=i):
+            here = room.at[i, slot]
+            pltpu.make_async_copy(here, here, in_sems.at[i, slot]).wait()
+            pltpu.make_async_copy(here, sends[i].at[slot], out_sems.at[i, slot]).start()
+
+    for i in range(n):
+
+        @pl.loop(0, counts[i])
+        def _(slot, i=i):
+            here = room.at[i, slot]
+            pltpu.make_async_copy(here, sends[i].at[slot], out_sems.at[i, slot]).wait()
+
+
+def pack(find, offsets, cap, tables, arrays, piece, after=()):
+    n = len(offsets)
     send = jax.ShapeDtypeStruct((cap,) + piece, F32)
-    size = 4 * cap * (sectors - 1) * piece[0] * piece[1] * piece[2]
     return pl.pallas_call(
-        functools.partial(pack_kernel, find, len(arrays)),
-        out_shape=[send] * (sectors - 1),
+        functools.partial(pack_kernel, find, len(arrays), tuple(offsets)),
+        out_shape=[send] * n,
         in_specs=[SMEM, SMEM] + [ANY] * (len(arrays) + len(after)),
-        out_specs=[ANY] * (sectors - 1),
-        scratch_shapes=[pltpu.SemaphoreType.DMA((sectors - 1, cap))],
+        out_specs=[ANY] * n,
+        scratch_shapes=[
+            pltpu.VMEM((n, cap) + piece, F32),
+            pltpu.SemaphoreType.DMA((n, cap)),
+            pltpu.SemaphoreType.DMA((n, cap)),
+        ],
         compiler_params=params(),
-        cost_estimate=cost(0, 2 * size),
+        cost_estimate=cost(),
         name="pack_tiles",
-    )(source_sector, source_tile, *arrays, *after)
-
-
-def sector_exchange(sends):
+    )(*tables, *arrays, *after)
+
+
+def sector_exchange(sends, offsets):
     sectors = lax.axis_size("sector")
     return [
-        lax.ppermute(send, "sector", [(s, s ^ (d + 1)) for s in range(sectors)])
-        for d, send in enumerate(sends)
+        lax.ppermute(send, "sector", [(s, s ^ d) for s in range(sectors)])
+        for d, send in zip(offsets, sends)
     ]
 
 
-def drift_kernel(find, place, n_local, sec_ref, til_ref, w_ref, *refs):
+def in_turn(later, earlier):
+    both = lax.optimization_barrier((*later, *earlier))
+    return list(both[: len(later)]), list(both[len(later) :])
+
+
+def drift_kernel(find, place, receive, n_local, n_extra, sec_ref, til_ref, w_ref, *refs):
     sectors, tiles = sec_ref.shape[1], sec_ref.shape[2]
     local, recvs = refs[:n_local], refs[n_local : n_local + sectors - 1]
-    outs = refs[n_local + sectors - 1 : -4]
-    taken, made, in_sems, out_sems = refs[-4:]
+    outs = refs[n_local + sectors - 1 + n_extra : -5]
+    token, taken, made, in_sems, out_sems = refs[-5:]
     pieces = find(*local)
     put = place(*outs)
     me = lax.axis_index("sector")
     rows, side = taken.shape[1] * taken.shape[2], taken.shape[3]
+    token[...] = jnp.zeros(token.shape, F32)
 
     def fetch(t, counts):
         d = sec_ref[0, me, t] ^ me
@@ -145,9 +161,8 @@
 
             @pl.when(d == other)
             def _(other=other):
-                pltpu.make_async_copy(
-                    recvs[other - 1].at[counts[other - 1]], taken.at[t], in_sems.at[t]
-                ).start()
+                came = receive(recvs[other - 1], other, counts[other - 1])
+                pltpu.make_async_copy(came, taken.at[t], in_sems.at[t]).start()
 
         return tuple(c + (d == i + 1).astype(jnp.int32) for i, c in enumerate(counts))
 
@@ -172,67 +187,51 @@
         pltpu.make_async_copy(made.at[t], made.at[t], out_sems.at[t]).wait()
 
 
-def drift(find, place, tables, weights, local, recvs, outs, piece, carried=None):
-    source_sector, source_tile = tables
-    sectors, tiles = source_sector.shape[1], source_sector.shape[2]
+def drift(find, place, receive, tables, weights, local, recvs, outs, piece, carried=()):
+    sectors, tiles = tables[0].shape[1], tables[0].shape[2]
     n_local = len(local)
-    rows, side = piece[0] * piece[1], piece[2]
-    ins = [source_sector, source_tile, weights, *local, *recvs]
-    specs = [SMEM, SMEM, VMEM] + [ANY] * (n_local + sectors - 1)
-    aliases = {}
-    body = functools.partial(drift_kernel, find, place, n_local)
-    if carried is not None:
-        aliases = {len(ins): 0}
-        ins.append(carried)
-        specs.append(ANY)
-        at = len(ins) - 1
-
-        def body(*refs):
-            drift_kernel(find, place, n_local, *refs[:at], *refs[at + 1 :])
-
+    ins = [*tables, weights, *local, *recvs, *carried]
     return pl.pallas_call(
-        body,
-        out_shape=outs,
-        in_specs=specs,
-        out_specs=[ANY] * len(outs),
+        functools.partial(drift_kernel, find, place, receive, n_local, len(carried)),
+        out_shape=[*outs, jax.ShapeDtypeStruct((8, 128), F32)],
+        in_specs=[SMEM, SMEM, VMEM] + [ANY] * (len(ins) - 3),
+        out_specs=[ANY] * len(outs) + [VMEM],
         scratch_shapes=[
             pltpu.VMEM((tiles,) + piece, F32),
             pltpu.VMEM((tiles,) + piece, F32),
             pltpu.SemaphoreType.DMA((tiles,)),
             pltpu.SemaphoreType.DMA((tiles,)),
         ],
-        input_output_aliases=aliases,
+        input_output_aliases={len(ins) - 1: 0} if carried else {},
         compiler_params=params(),
-        cost_estimate=cost(tiles * rows * side * side * 8, tiles * rows * side * 8 + weights.size * 2),
+        cost_estimate=cost(),
         name="drift_chunk",
     )(*ins)
 
 
-def diffusion_kernel(
-    chunks, halo_chunks, rate_ref, a_ref, b_ref, *refs
-):
-    n_in = 2 * chunks + 2 * halo_chunks
-    ins, keep, sends = refs[:n_in], refs[n_in], refs[n_in + 1 : n_in + 1 + chunks]
-    field, work, done, in_sems, out_sems = refs[n_in + 1 + chunks :]
-    tiles, step = ins[0].shape[0], ins[0].shape[1]
+def diffusion_kernel(n_own, n_halo, n_send, rate_ref, a_ref, b_ref, *refs):
+    n_in = 2 * n_own + 2 * n_halo
+    ins, keep, sends = refs[:n_in], refs[n_in], refs[n_in + 1 : n_in + 1 + n_send]
+    field, work, ra_ref, rb_ref, done, in_sems, out_sems = refs[n_in + 1 + n_send :]
+    tiles, block = keep.shape[0], keep.shape[1]
     frame, pitches, side = work.shape
-    halo = halo_chunks * step
-    block = chunks * step
+    halo = (frame - 2 * block) // 2
     vregs = pitches // 8
     flip = lax.axis_index("inner") % 2
-    order = (
-        list(range(chunks))
-        + [2 * chunks - 1 - k for k in range(chunks)]
-        + [2 * chunks + k for k in range(halo_chunks)]
-        + [-1 - k for k in range(halo_chunks)]
-    )
+    places, start = [], 0
+    for i in range(n_own):
+        step = ins[i].shape[1]
+        places.append((i, step, halo + start))
+        places.append((n_own + i, step, halo + 2 * block - start - step))
+        if i < n_halo:
+            places.append((2 * n_own + i, step, halo + 2 * block + start))
+            places.append((2 * n_own + n_halo + i, step, halo - start - step))
+        start += step
 
     def fetch(g, slot):
         copies = []
-        for i, position in enumerate(order):
-            straight = (position + halo_chunks) * step
-            mirrored = (2 * chunks - 1 - position + halo_chunks) * step
-            at = jnp.where(flip == 0, straight, mirrored)
+        for i, step, place in places:
+            at = jnp.where(flip == 0, place, frame - place - step)
             copies.append(
                 pltpu.make_async_copy(
                     ins[i].at[g], field.at[slot, pl.ds(at, step)], in_sems.at[slot, i]
@@ -243,17 +242,18 @@
     def store(g, slot):
         copies = [
             pltpu.make_async_copy(
-                done.at[slot, pl.ds(flip * block, block)], keep.at[g], out_sems.at[slot, chunks]
+                done.at[slot, pl.ds(flip * block, block)], keep.at[g], out_sems.at[slot, n_send]
             )
         ]
-        for k in range(chunks):
+        first = (1 - flip) * block
+        for k in range(n_send):
+            step = sends[k].shape[1]
             copies.append(
                 pltpu.make_async_copy(
-                    done.at[slot, pl.ds((1 - flip) * block + k * step, step)],
-                    sends[k].at[g],
-                    out_sems.at[slot, k],
+                    done.at[slot, pl.ds(first, step)], sends[k].at[g], out_sems.at[slot, k]
                 )
             )
+            first = first + step
         return copies
 
     for copy in fetch(0, 0):
@@ -278,13 +278,16 @@
 
         rate = rate_ref[g]
 
-        def read_work(e):
-            return [work[e, 8 * v : 8 * v + 8, :] for v in range(vregs)]
+        def rows_of(ref, e):
+            return [ref[e, 8 * v : 8 * v + 8, :] for v in range(vregs)]
 
         def write_work(e, rows):
             for v in range(vregs):
                 work[e, 8 * v : 8 * v + 8, :] = rows[v]
 
+        def read_work(e):
+            return rows_of(work, e)
+
         def read_field(e):
             return [field[slot, e, pl.ds(v, 8, stride=vregs), :] for v in range(vregs)]
 
@@ -292,48 +295,63 @@
             for v in range(vregs):
                 done[slot, e - halo, pl.ds(v, 8, stride=vregs), :] = rows[v]
 
-        def sweep(first, count, read, write):
+        def scaled(e):
+            ra = [rate * x for x in rows_of(a_ref, e)]
+            rb = [rate * x for x in rows_of(b_ref, e)]
+            for v in range(vregs):
+                ra_ref[e, 8 * v : 8 * v + 8, :] = ra[v]
+                rb_ref[e, 8 * v : 8 * v + 8, :] = rb[v]
+            return ra, rb
+
+        def ready(e):
+            return rows_of(ra_ref, e), rows_of(rb_ref, e)
+
+        def sweep(first, count, read, write, rates, wide):
             def energy(e, here, below):
                 after = read(e + 1)
-                above = [
-                    a_ref[e, 8 * v : 8 * v + 8, :] * (after[v] - here[v]) for v in range(vregs)
-                ]
+                ra, rb = rates(e)
+                above = [ra[v] * (after[v] - here[v]) for v in range(vregs)]
                 nearby = here[1:] + [pltpu.roll(here[0], 7, 0)]
-                pitch = [
-                    b_ref[e, 8 * v : 8 * v + 8, :] * (nearby[v] - here[v]) for v in range(vregs)
-                ]
+                pitch = [rb[v] * (nearby[v] - here[v]) for v in range(vregs)]
                 before = [pltpu.roll(pitch[-1], 1, 0)] + pitch[:-1]
                 write(
                     e,
                     [
-                        here[v] + rate * ((above[v] - below[v]) + (pitch[v] - before[v]))
+                        here[v] + ((above[v] - below[v]) + (pitch[v] - before[v]))
                         for v in range(vregs)
                     ],
                 )
                 return after, above
 
+            def several(e, carry, n):
+                here, below = list(carry[:vregs]), list(carry[vregs:])
+                for i in range(n):
+                    here, below = energy(e + i, here, below)
+                return (*here, *below)
+
             edge = read(first - 1)
             here = read(first)
-            below = [
-                a_ref[first - 1, 8 * v : 8 * v + 8, :] * (here[v] - edge[v]) for v in range(vregs)
-            ]
-
-            def two(i, carry):
-                here, below = list(carry[:vregs]), list(carry[vregs:])
-                e = first + 2 * i
-                here, below = energy(e, here, below)
-                here, below = energy(e + 1, here, below)
-                return (*here, *below)
-
-            lax.fori_loop(0, count // 2, two, (*here, *below))
-
-        sweep(1, frame - 2, read_field, write_work)
+            ra = rates(first - 1)[0]
+            below = [ra[v] * (here[v] - edge[v]) for v in range(vregs)]
+            carry = lax.fori_loop(
+                0,
+                count // wide,
+                lambda i, carry: several(first + wide * i, carry, wide),
+                (*here, *below),
+            )
+            for left in range(2, wide, 2):
+
+                @pl.when(count % wide == left)
+                def _(left=left):
+                    several(first + count - left, carry, left)
+
+        sweep(1, frame - 2, read_field, write_work, scaled, 2)
 
         @pl.loop(1, PASSES - 1)
         def _(n):
-            sweep(n + 1, frame - 2 - 2 * n, read_work, write_work)
-
-        sweep(PASSES, frame - 2 * PASSES, read_work, write_done)
+            sweep(n + 1, frame - 2 - 2 * n, read_work, write_work, ready, 4)
+
+        sweep(PASSES, frame - 2 * PASSES, read_work, write_done, ready, 4)
 
         for copy in store(g, slot):
             copy.start()
@@ -343,31 +361,31 @@
             copy.wait()
 
 
-def diffuse(rate, a, b, own, got, own_halo, got_halo):
-    chunks, halo_chunks = len(own), len(own_halo)
-    tiles, step, pitches, side = own[0].shape
+def diffuse(rate, a, b, own, got, own_halo, got_halo, steps):
+    tiles, _, pitches, side = own[0].shape
     frame = a.shape[0]
-    block = chunks * step
-    n_in = 2 * (chunks + halo_chunks)
-    keep = jax.ShapeDtypeStruct((tiles, block, pitches, side), F32)
-    send = jax.ShapeDtypeStruct((tiles, step, pitches, side), F32)
-    size = tiles * frame * pitches * side
+    block = sum(steps)
+    ins = [*own, *got, *own_halo, *got_halo]
     out = pl.pallas_call(
-        functools.partial(diffusion_kernel, chunks, halo_chunks),
-        out_shape=[keep] + [send] * chunks,
-        in_specs=[VMEM] * 3 + [ANY] * n_in,
-        out_specs=[ANY] * (1 + chunks),
+        functools.partial(diffusion_kernel, len(own), len(own_halo), len(steps)),
+        out_shape=[
+            jax.ShapeDtypeStruct((tiles, step, pitches, side), F32) for step in (block, *steps)
+        ],
+        in_specs=[VMEM] * 3 + [ANY] * len(ins),
+        out_specs=[ANY] * (1 + len(steps)),
         scratch_shapes=[
             pltpu.VMEM((2, frame, pitches, side), F32),
             pltpu.VMEM((frame, pitches, side), F32),
+            pltpu.VMEM((frame, pitches, side), F32),
+            pltpu.VMEM((frame, pitches, side), F32),
             pltpu.VMEM((2, 2 * block, pitches, side), F32),
-            pltpu.SemaphoreType.DMA((2, n_in)),
-            pltpu.SemaphoreType.DMA((2, chunks + 1)),
+            pltpu.SemaphoreType.DMA((2, len(ins))),
+            pltpu.SemaphoreType.DMA((2, len(steps) + 1)),
         ],
         compiler_params=params(),
-        cost_estimate=cost(size * PASSES * 10, size * 8),
+        cost_estimate=cost(),
         name="diffuse_tiles",
-    )(rate, a, b, *own, *got, *own_halo, *got_halo)
+    )(rate, a, b, *ins)
     return out[0], out[1:]
 
 
@@ -395,13 +413,13 @@
     side = cubic_weights.shape[1]
     tiles = cell_count // side
     half = tiles // 2
-    step = block // CHUNKS
-    halo_chunks = PASSES // step
+    quarter = block // 4
+    halo_chunks = PASSES // quarter
+    first_steps = (quarter,) * 4
+    last_steps = (quarter // 2, quarter - quarter // 4, quarter, quarter, quarter - quarter // 4)
     cap = slots(tiles, sectors)
     tables = (source_sector, source_tile)
-    piece = (step, pitches, side)
-    part = jax.ShapeDtypeStruct((half,) + piece, F32)
-    yes = None
+    near, far = [1], list(range(2, sectors))
 
     weights = split_weights(matrix_id, cubic_weights)
 
@@ -419,12 +437,23 @@
                 pairs.append((i, i + shift))
 
     own, got, own_halo, got_halo = [], [], [], []
-    for k in range(CHUNKS):
-
-        def find(field, k=k):
+    packed = []
+    start = 0
+    for k, step in enumerate(first_steps):
+
+        def first_of(start=start, step=step):
             here = side_here()
-            first = here * (block - step * (k + 1)) + (1 - here) * (step * k)
+            return here * (block - start - step) + (1 - here) * start
+
+        def find(field, first_of=first_of, step=step):
+            first = first_of()
             return lambda t: [(t >= 0, lambda: field.at[pl.ds(first, step), :, at_lanes(t)])]
+
+        def find_all(field):
+            return lambda t: [(t >= 0, lambda: field.at[:, :, at_lanes(t)])]
+
+        def receive(came, other, slot, first_of=first_of, step=step):
+            return came.at[slot, pl.ds(first_of(), step)] if other == 1 else came.at[slot]
 
         def place(kept, sent):
             here = side_here()
@@ -434,15 +463,41 @@
                 (jnp.logical_not(mine(t)), lambda: sent.at[t % half]),
             ]
 
-        after = own[k - 2 : k - 1] if k >= 2 else ()
-        recvs = sector_exchange(pack(find, cap, *tables, [density], piece, after))
-        kept, sent = drift(find, place, tables, weights, [density], recvs, [part, part], piece)
-        swapped = lax.ppermute(sent, "inner", swap)
+        packed.append((start, step, find, receive, place))
+        start += step
+
+    def pack_first(k, after):
+        start, step, find, _, _ = packed[k]
+        return pack(find, far, cap, tables, [density], (step, pitches, side), after)
+
+    sends = pack_first(0, ())
+    recvs = sector_exchange(sends, far)
+    beside = pack(find_all, near, cap, tables, [density], (block, pitches, side), (sends[0],))
+    beside = sector_exchange(beside, near)
+    token = sends[0]
+    crossing = []
+    for k, (start, step, find, receive, place) in enumerate(packed):
+        if k + 1 < len(packed):
+            later = pack_first(k + 1, (token,))
+            later, recvs = in_turn(later, recvs)
+            coming = sector_exchange(later, far)
+        if k >= 2:
+            recvs, _ = in_turn(recvs, crossing[k - 2])
+        part = jax.ShapeDtypeStruct((half, step, pitches, side), F32)
+        piece = (step, pitches, side)
+        kept, sent, token = drift(
+            find, place, receive, tables, weights, [density], beside + recvs, [part, part], piece
+        )
+        recvs = coming
         own.append(kept)
-        got.append(swapped)
+        got.append(lax.ppermute(sent, "inner", swap))
+        crossing.append(got[-1:])
         if k < halo_chunks:
             own_halo.append(lax.ppermute(kept, "inner", own_pairs))
-            got_halo.append(lax.ppermute(swapped, "inner", got_pairs))
+            crossing[-1] += own_halo[-1:]
+        if 0 < k <= halo_chunks:
+            got_halo.append(lax.ppermute(got[k - 1], "inner", got_pairs))
+            crossing[-1] += got_halo[-1:]
 
     energies = energy_rate.shape[0]
     frame = 2 * block + 2 * PASSES
@@ -458,32 +513,53 @@
     level = jnp.sum(jnp.where(bin_of[:, None] == bins[None, :], wave_level[0][None, :], 0.0), axis=1)
     rate = jnp.broadcast_to(level.reshape(half, 1, side), (half, 8, side))
 
-    kept, sends = diffuse(rate, a, b, own, got, own_halo, got_halo)
-
-    outs, backs = [], []
-    for k in range(CHUNKS):
-        send = sends[k]
-        if backs:
-            send, backs[-1] = lax.optimization_barrier((send, backs[-1]))
-        backs.append(lax.ppermute(send, "inner", swap))
-    for k in range(CHUNKS):
-        back = backs[k]
-
-        def find(mine, theirs, k=k):
+    kept, sends = diffuse(rate, a, b, own, got, own_halo, got_halo, last_steps)
+
+    returns, ready, out, start = sends, [], (), 0
+    for k, step in enumerate(last_steps):
+
+        def find(mine, theirs, start=start, step=step):
             here = side_here()
             return lambda t: [
-                ((t // half) == here, lambda: mine.at[t % half, pl.ds(step * k, step)]),
+                ((t // half) == here, lambda: mine.at[t % half, pl.ds(start, step)]),
                 ((t // half) != here, lambda: theirs.at[t % half]),
             ]
 
-        def place(result, k=k):
-            return lambda t: [(t >= 0, lambda: result.at[pl.ds(step * k, step), :, at_lanes(t)])]
-
-        recvs = sector_exchange(pack(find, cap, *tables, [kept, back], piece))
-        whole = [jax.ShapeDtypeStruct(density.shape, F32)]
-        carried = outs[-1] if outs else None
-        outs += drift(find, place, tables, weights, [kept, back], recvs, whole, piece, carried)
-    return outs[-1]
+        def place(result, start=start, step=step):
+            return lambda t: [(t >= 0, lambda: result.at[pl.ds(start, step), :, at_lanes(t)])]
+
+        ready.append((find, place, (step, pitches, side)))
+        start += step
+
+    def receive_slot(came, other, slot):
+        return came.at[slot]
+
+    def pack_last(k, after):
+        find, _, piece = ready[k]
+        sends = pack(find, near + far, cap, tables, [kept, backs[k]], piece, after)
+        return sends[:1], sends[1:]
+
+    whole = [jax.ShapeDtypeStruct(density.shape, F32)]
+    backs = [lax.ppermute(returns[0], "inner", swap)]
+    (last,), _ = in_turn([returns[1]], [backs[0]])
+    backs.append(lax.ppermute(last, "inner", swap))
+    sends, far_sends = pack_last(0, ())
+    recvs = sector_exchange(far_sends, far)
+    beside = sector_exchange(sends, near)
+    token = kept
+    for k, (find, place, piece) in enumerate(ready):
+        if k + 1 < len(ready):
+            sends, far_sends = pack_last(k + 1, (token,))
+            far_sends, recvs = in_turn(far_sends, recvs)
+            coming = sector_exchange(far_sends, far), sector_exchange(sends, near)
+        if k + 2 < len(ready):
+            (last,), _ = in_turn([returns[k + 2]], [backs[k + 1], *recvs])
+            backs.append(lax.ppermute(last, "inner", swap))
+        *out, token = drift(
+            find, place, receive_slot, tables, weights, [kept, backs[k]], beside + recvs, whole, piece, out
+        )
+        recvs, beside = coming
+    return out[0]
 
 
 def slots(tiles, sectors):
@@ -591,9 +667,8 @@
         and tiles % 2 == 0
         and pitches % 16 == 0
         and side % 128 == 0
-        and block >= PASSES
-        and block % CHUNKS == 0
-        and PASSES % (block // CHUNKS) == 0
+        and block % 16 == 0
+        and 4 * PASSES == 3 * block
     )
 
 

time: 901 us -> 435 us (0.48)
  Pallas kernels: 706 us -> 155 us
  waiting for transfers between devices: 156 us -> 226 us
  starting transfers between devices: 26 us -> 42.4 us
    pallas_call x17 -> x20, Pallas kernels: 701 us -> 150 us  [the longest x9 63.6 us: drift(): pl.pallas_call(functools.partial(drift_kernel, find, place, receive, n_lo...]
    ppermute x35 -> x36, waiting for transfers between devices: 143 us -> 226 us  [the longest x24 146 us: sector_exchange(): lax.ppermute(send, 'sector', [(s, s ^ d) for s in range(sectors)])]
    ppermute x3, waiting for transfers between devices: 12.9 us -> 0.01 us  [paired_shards(): own_halo.append(lax.ppermute(kept, 'inner', own_pairs))]
    ppermute x35 -> x36, starting transfers between devices: 21.9 us -> 34.3 us  [the longest x24 22.2 us: sector_exchange(): lax.ppermute(send, 'sector', [(s, s ^ d) for s in range(sectors)])]
  transfers between devices with their start and end apart: 38 -> 39, of which waited for: 10 -> 22; matrix products, arithmetic and copies ran while one was open for 0% -> 0% of each run, Pallas kernels for 63% -> 21%
where the time goes in v2:
time: 435 us; the launch traced here: 432 us
  waiting for transfers between devices  226 us (52%)
  Pallas kernels  155 us (36%)
  starting transfers between devices  42.4 us (10%)
  local copies, waits for them, and re-layouts  7.9 us (2%)
    ppermute x24, waiting for transfers between devices, sector_exchange(): lax.ppermute(send, 'sector', [(s, s ^ d) for s in range(sectors)])  146 us
    pallas_call x9, Pallas kernels, drift(): pl.pallas_call(functools.partial(drift_kernel, find, place, receive, n_lo...  63.6 us
    pallas_call x1, Pallas kernels, diffuse(): pl.pallas_call(functools.partial(diffusion_kernel, len(own), len(own_halo...  52.4 us
    ppermute x4, waiting for transfers between devices, paired_shards(): backs.append(lax.ppermute(last, 'inner', swap))  41.8 us
    pallas_call x10, Pallas kernels, pack(): pl.pallas_call(functools.partial(pack_kernel, find, len(arrays), tuple(of...  34.1 us
    ppermute x4, waiting for transfers between devices, paired_shards(): got.append(lax.ppermute(sent, 'inner', swap))  22.6 us
    ppermute x24, starting transfers between devices, sector_exchange(): lax.ppermute(send, 'sector', [(s, s ^ d) for s in range(sectors)])  22.2 us
    ppermute x1, waiting for transfers between devices, paired_shards(): backs = [lax.ppermute(returns[0], 'inner', swap)]  13.3 us
  transfers between devices with their start and end apart: 39, of which 22 were waited for; matrix products, arithmetic and copies ran while one was open for 0% of the time, Pallas kernels for 21%

profile of v2, /device:TPU:25, one launch (start us, length us, event | category | flops | bytes accessed | tf_op | source)
XLA Modules:
  0.0 432.1 jit_solution(3799885153612454512)
XLA Ops:
  0.0 3.1 pack_tiles.10
  3.1 3.2 pack_tiles.11
  7.2 1.6 collective-permute-start.2
  8.9 3.1 pack_tiles.12
  12.0 15.3 %collective-permute-done.2.refs_3_ = f32[6,4,64,128]{3,2,1,0:T(8,128)} collective-permute-done((f32[6,4,64,128]{3,2,1,0:T(8,128)}, f32[6,4,64,128]{3,2,1,0:T(8,128)}, u32[]{:S(2)}, u32[]{:S(2)}) %collective-permute-start.2) | collective-permute-done | bytes 786464 | tf_op jit(solution)/shard_map/ppermute | solution.py:128
  27.3 16.6 %collective-permute-done.1.refs_2_ = f32[6,4,64,128]{3,2,1,0:T(8,128)} collective-permute-done((f32[6,4,64,128]{3,2,1,0:T(8,128)S(1)}, f32[6,4,64,128]{3,2,1,0:T(8,128)}, u32[]{:S(2)}, u32[]{:S(2)}) %collective-permute-start.1) | collective-permute-done | bytes 786464 | tf_op jit(solution)/shard_map/ppermute | solution.py:128
  43.8 1.1 collective-permute-start.3
  45.0 1.2 collective-permute-start.4
  46.2 4.7 %split_weights.1.w_ref = bf16[16,256,256]{2,1,0:T(8,128)(2,1)} custom-call(s32[1,4,16]{2,1,0:T(4,128)} %mid_ref.1, f32[32,128,128]{2,1,0:T(8,128)} %w_ref.1), custom_call_target="tpu_custom_call" | custom-call | bytes 1024 | tf_op jit(solution)/shard_map/split_weights/pallas_call | solution.py:52
  50.9 7.2 %drift_chunk.9 = (f32[8,4,64,128]{3,2,1,0:T(8,128)}, f32[8,4,64,128]{3,2,1,0:T(8,128)}, f32[8,128]{1,0:T(8,128)}) custom-call(s32[1,4,16]{2,1,0:T(4,128)} %sec_ref.37, s32[1,4,16]{2,1,0:T(4,128)} %til_ref.37, bf16[16,256,256]{2,1,0:T(8,128)(2,1)} %split_weights.1.w_ref, f32[16,64,2048]{2,1,0:T(8,128)} %refs_0_.17, ...), custom_call_target="tpu_custom_call" | custom-call | bytes 1024 | tf_op jit(solution)/shard_map/drift_chunk/pallas_call | solution.py:194
  58.1 1.4 collective-permute-start.7
  59.4 2.9 collective-permute-start.8
  62.3 3.1 pack_tiles.13
  65.4 15.1 %collective-permute-done.4.refs_3_ = f32[6,4,64,128]{3,2,1,0:T(8,128)} collective-permute-done((f32[6,4,64,128]{3,2,1,0:T(8,128)}, f32[6,4,64,128]{3,2,1,0:T(8,128)}, u32[]{:S(2)}, u32[]{:S(2)}) %collective-permute-start.4) | collective-permute-done | bytes 786464 | tf_op jit(solution)/shard_map/ppermute | solution.py:128
  80.6 1.1 collective-permute-start.5
  81.7 7.2 %drift_chunk.10 = (f32[8,4,64,128]{3,2,1,0:T(8,128)}, f32[8,4,64,128]{3,2,1,0:T(8,128)}, f32[8,128]{1,0:T(8,128)}) custom-call(s32[1,4,16]{2,1,0:T(4,128)} %sec_ref.37, s32[1,4,16]{2,1,0:T(4,128)} %til_ref.37, bf16[16,256,256]{2,1,0:T(8,128)(2,1)} %split_weights.1.w_ref, f32[16,64,2048]{2,1,0:T(8,128)} %refs_0_.17, ...), custom_call_target="tpu_custom_call" | custom-call | bytes 1024 | tf_op jit(solution)/shard_map/drift_chunk/pallas_call | solution.py:194
  89.7 3.1 pack_tiles.14
  92.8 7.6 %collective-permute-done.5.refs_2_ = f32[6,4,64,128]{3,2,1,0:T(8,128)} collective-permute-done((f32[6,4,64,128]{3,2,1,0:T(8,128)}, f32[6,4,64,128]{3,2,1,0:T(8,128)}, u32[]{:S(2)}, u32[]{:S(2)}) %collective-permute-start.5) | collective-permute-done | bytes 786464 | tf_op jit(solution)/shard_map/ppermute | solution.py:128
  100.4 2.8 collective-permute-start.12
  103.2 13.7 %collective-permute-done.6.refs_3_ = f32[6,4,64,128]{3,2,1,0:T(8,128)} collective-permute-done((f32[6,4,64,128]{3,2,1,0:T(8,128)}, f32[6,4,64,128]{3,2,1,0:T(8,128)}, u32[]{:S(2)}, u32[]{:S(2)}) %collective-permute-start.6) | collective-permute-done | bytes 786464 | tf_op jit(solution)/shard_map/ppermute | solution.py:128
  116.9 1.3 collective-permute-start.13
  118.2 7.2 %drift_chunk.11 = (f32[8,4,64,128]{3,2,1,0:T(8,128)}, f32[8,4,64,128]{3,2,1,0:T(8,128)}, f32[8,128]{1,0:T(8,128)}) custom-call(s32[1,4,16]{2,1,0:T(4,128)} %sec_ref.37, s32[1,4,16]{2,1,0:T(4,128)} %til_ref.37, bf16[16,256,256]{2,1,0:T(8,128)(2,1)} %split_weights.1.w_ref, f32[16,64,2048]{2,1,0:T(8,128)} %refs_0_.17, ...), custom_call_target="tpu_custom_call" | custom-call | bytes 1024 | tf_op jit(solution)/shard_map/drift_chunk/pallas_call | solution.py:194
  125.4 2.9 collective-permute-start.14
  128.6 2.4 collective-permute-start.10
  131.1 2.4 collective-permute-start.16
  133.5 13.0 %collective-permute-done.9.refs_2_ = f32[6,4,64,128]{3,2,1,0:T(8,128)S(1)} collective-permute-done((f32[6,4,64,128]{3,2,1,0:T(8,128)}, f32[6,4,64,128]{3,2,1,0:T(8,128)S(1)}, u32[]{:S(2)}, u32[]{:S(2)}) %collective-permute-start.9) | collective-permute-done | bytes 786464 | tf_op jit(solution)/shard_map/ppermute | solution.py:128
  146.5 1.3 collective-permute-start.17
  147.8 17.3 %collective-permute-done.10.refs_3_ = f32[6,4,64,128]{3,2,1,0:T(8,128)} collective-permute-done((f32[6,4,64,128]{3,2,1,0:T(8,128)}, f32[6,4,64,128]{3,2,1,0:T(8,128)}, u32[]{:S(2)}, u32[]{:S(2)}) %collective-permute-start.10) | collective-permute-done | bytes 786464 | tf_op jit(solution)/shard_map/ppermute | solution.py:128
  165.0 7.1 %drift_chunk.12 = (f32[8,4,64,128]{3,2,1,0:T(8,128)}, f32[8,4,64,128]{3,2,1,0:T(8,128)}, f32[8,128]{1,0:T(8,128)}) custom-call(s32[1,4,16]{2,1,0:T(4,128)} %sec_ref.37, s32[1,4,16]{2,1,0:T(4,128)} %til_ref.37, bf16[16,256,256]{2,1,0:T(8,128)(2,1)} %split_weights.1.w_ref, f32[16,64,2048]{2,1,0:T(8,128)} %refs_0_.17, ...), custom_call_target="tpu_custom_call" | custom-call | bytes 1024 | tf_op jit(solution)/shard_map/drift_chunk/pallas_call | solution.py:194
  172.3 1.3 collective-permute-start.18
  174.3 22.6 %collective-permute-done.15.refs_7_ = f32[8,4,64,128]{3,2,1,0:T(8,128)} collective-permute-done((f32[8,4,64,128]{3,2,1,0:T(8,128)}, f32[8,4,64,128]{3,2,1,0:T(8,128)}, u32[]{:S(2)}, u32[]{:S(2)}) %collective-permute-start.15) | collective-permute-done | bytes 1048608 | tf_op jit(solution)/shard_map/ppermute | solution.py:493
  196.9 2.3 collective-permute-done.18.refs_13_
  199.9 1.9 broadcast_in_dim.47.b_ref
  201.7 1.8 broadcast_in_dim.45.a_ref
  203.5 52.4 %diffuse_tiles.1 = (f32[8,16,64,128]{3,2,1,0:T(8,128)}, f32[8,2,64,128]{3,2,1,0:T(8,128)}, f32[8,3,64,128]{3,2,1,0:T(8,128)}, f32[8,4,64,128]{3,2,1,0:T(8,128)},...) custom-call(f32[8,8,128]{2,1,0:T(8,128)} %broadcast_in_dim.43.rate_ref, f32[56,64,128]{2,1,0:T(8,128)} %broadcast_in_dim.45.a_ref, ...), custom_call_target="tpu_custom_call" | custom-call | bytes 1024 | tf_op jit(solution)/shard_map/diffuse_tiles/pallas_call | solution.py:369
  255.9 13.3 %collective-permute-done.19.refs_1_ = f32[8,2,64,128]{3,2,1,0:T(8,128)S(1)} collective-permute-done((f32[8,2,64,128]{3,2,1,0:T(8,128)}, f32[8,2,64,128]{3,2,1,0:T(8,128)S(1)}, u32[]{:S(2)}, u32[]{:S(2)}) %collective-permute-start.19) | collective-permute-done | bytes 524320 | tf_op jit(solution)/shard_map/ppermute | solution.py:543
  270.4 3.6 pack_tiles.16
  274.5 2.3 collective-permute-start.22
  276.8 11.4 %collective-permute-done.20.refs_1_ = f32[8,3,64,128]{3,2,1,0:T(8,128)S(1)} collective-permute-done((f32[8,3,64,128]{3,2,1,0:T(8,128)}, f32[8,3,64,128]{3,2,1,0:T(8,128)S(1)}, u32[]{:S(2)}, u32[]{:S(2)}) %collective-permute-start.20) | collective-permute-done | bytes 786464 | tf_op jit(solution)/shard_map/ppermute | solution.py:545
  288.2 0.9 copy-done
  289.1 3.7 pack_tiles.15
  293.6 1.2 collective-permute-start.23
  295.3 1.9 collective-permute-start.26
  297.3 1.9 collective-permute-done.24.refs_2_
  300.0 6.7 %drift_chunk.13 = (f32[16,64,2048]{2,1,0:T(8,128)}, f32[8,128]{1,0:T(8,128)}) custom-call(s32[1,4,16]{2,1,0:T(4,128)} %sec_ref.37, s32[1,4,16]{2,1,0:T(4,128)} %til_ref.37, bf16[16,256,256]{2,1,0:T(8,128)(2,1)} %split_weights.1.w_ref, f32[8,16,64,128]{3,2,1,0:T(8,128)} %get-tuple-element.122.refs_0_.refs_2_, f32[8,2,64,128]{3,2,1,0:T(8,128)} %copy-done.3, ...), custom_call_target="tpu_custom_call" | custom-call | bytes 1024 | tf_op jit(solution)/shard_map/drift_chunk/pallas_call | solution.py:194
  306.6 10.6 %collective-permute-done.23.refs_1_ = f32[8,4,64,128]{3,2,1,0:T(8,128)} collective-permute-done((f32[8,4,64,128]{3,2,1,0:T(8,128)}, f32[8,4,64,128]{3,2,1,0:T(8,128)}, u32[]{:S(2)}, u32[]{:S(2)}) %collective-permute-start.23) | collective-permute-done | bytes 1048608 | tf_op jit(solution)/shard_map/ppermute | solution.py:557
  317.2 3.8 pack_tiles.17
  321.0 1.8 collective-permute-done.26.refs_4_
  322.8 1.1 collective-permute-start.27
  324.5 2.7 collective-permute-start.30
  327.8 1.8 collective-permute-done.28.refs_2_
  329.6 7.0 %drift_chunk.14 = (f32[16,64,2048]{2,1,0:T(8,128)}, f32[8,128]{1,0:T(8,128)}) custom-call(s32[1,4,16]{2,1,0:T(4,128)} %sec_ref.37, s32[1,4,16]{2,1,0:T(4,128)} %til_ref.37, bf16[16,256,256]{2,1,0:T(8,128)(2,1)} %split_weights.1.w_ref, f32[8,16,64,128]{3,2,1,0:T(8,128)} %get-tuple-element.122.refs_0_.refs_2_, ...), custom_call_target="tpu_custom_call", output_to_operand_aliasing={{0}: (8, {})} | custom-call | bytes 1024 | tf_op jit(solution)/shard_map/drift_chunk/pallas_call | solution.py:194
  336.6 9.8 %collective-permute-done.27.refs_1_ = f32[8,4,64,128]{3,2,1,0:T(8,128)} collective-permute-done((f32[8,4,64,128]{3,2,1,0:T(8,128)}, f32[8,4,64,128]{3,2,1,0:T(8,128)}, u32[]{:S(2)}, u32[]{:S(2)}) %collective-permute-start.27) | collective-permute-done | bytes 1048608 | tf_op jit(solution)/shard_map/ppermute | solution.py:557
  346.4 3.8 pack_tiles.18
  350.2 10.1 %collective-permute-done.30.refs_4_ = f32[6,4,64,128]{3,2,1,0:T(8,128)} collective-permute-done((f32[6,4,64,128]{3,2,1,0:T(8,128)}, f32[6,4,64,128]{3,2,1,0:T(8,128)}, u32[]{:S(2)}, u32[]{:S(2)}) %collective-permute-start.30) | collective-permute-done | bytes 786464 | tf_op jit(solution)/shard_map/ppermute | solution.py:128
  362.5 7.2 %drift_chunk.15 = (f32[16,64,2048]{2,1,0:T(8,128)}, f32[8,128]{1,0:T(8,128)}) custom-call(s32[1,4,16]{2,1,0:T(4,128)} %sec_ref.37, s32[1,4,16]{2,1,0:T(4,128)} %til_ref.37, bf16[16,256,256]{2,1,0:T(8,128)(2,1)} %split_weights.1.w_ref, f32[8,16,64,128]{3,2,1,0:T(8,128)} %get-tuple-element.122.refs_0_.refs_2_, ...), custom_call_target="tpu_custom_call", output_to_operand_aliasing={{0}: (8, {})} | custom-call | bytes 1024 | tf_op jit(solution)/shard_map/drift_chunk/pallas_call | solution.py:194
  369.7 10.1 %collective-permute-done.31.refs_1_ = f32[8,3,64,128]{3,2,1,0:T(8,128)S(1)} collective-permute-done((f32[8,3,64,128]{3,2,1,0:T(8,128)}, f32[8,3,64,128]{3,2,1,0:T(8,128)S(1)}, u32[]{:S(2)}, u32[]{:S(2)}) %collective-permute-start.31) | collective-permute-done | bytes 786464 | tf_op jit(solution)/shard_map/ppermute | solution.py:557
  380.7 3.8 pack_tiles.19
  384.5 12.6 %collective-permute-done.35.refs_4_ = f32[6,4,64,128]{3,2,1,0:T(8,128)} collective-permute-done((f32[6,4,64,128]{3,2,1,0:T(8,128)}, f32[6,4,64,128]{3,2,1,0:T(8,128)}, u32[]{:S(2)}, u32[]{:S(2)}) %collective-permute-start.35) | collective-permute-done | bytes 786464 | tf_op jit(solution)/shard_map/ppermute | solution.py:128
  397.9 1.4 collective-permute-start.37
  399.3 7.2 %drift_chunk.16 = (f32[16,64,2048]{2,1,0:T(8,128)}, f32[8,128]{1,0:T(8,128)}) custom-call(s32[1,4,16]{2,1,0:T(4,128)} %sec_ref.37, s32[1,4,16]{2,1,0:T(4,128)} %til_ref.37, bf16[16,256,256]{2,1,0:T(8,128)(2,1)} %split_weights.1.w_ref, f32[8,16,64,128]{3,2,1,0:T(8,128)} %get-tuple-element.122.refs_0_.refs_2_, ...), custom_call_target="tpu_custom_call", output_to_operand_aliasing={{0}: (8, {})} | custom-call | bytes 1024 | tf_op jit(solution)/shard_map/drift_chunk/pallas_call | solution.py:194
  406.4 5.1 %collective-permute-done.36.refs_3_ = f32[6,3,64,128]{3,2,1,0:T(8,128)S(1)} collective-permute-done((f32[6,3,64,128]{3,2,1,0:T(8,128)}, f32[6,3,64,128]{3,2,1,0:T(8,128)S(1)}, u32[]{:S(2)}, u32[]{:S(2)}) %collective-permute-start.36) | collective-permute-done | bytes 589856 | tf_op jit(solution)/shard_map/ppermute | solution.py:128
  411.6 13.5 %collective-permute-done.37.refs_4_ = f32[6,3,64,128]{3,2,1,0:T(8,128)} collective-permute-done((f32[6,3,64,128]{3,2,1,0:T(8,128)}, f32[6,3,64,128]{3,2,1,0:T(8,128)}, u32[]{:S(2)}, u32[]{:S(2)}) %collective-permute-start.37) | collective-permute-done | bytes 589856 | tf_op jit(solution)/shard_map/ppermute | solution.py:128
  425.1 7.0 %drift_chunk.17 = (f32[16,64,2048]{2,1,0:T(8,128)}, f32[8,128]{1,0:T(8,128)}) custom-call(s32[1,4,16]{2,1,0:T(4,128)} %sec_ref.37, s32[1,4,16]{2,1,0:T(4,128)} %til_ref.37, bf16[16,256,256]{2,1,0:T(8,128)(2,1)} %split_weights.1.w_ref, f32[8,16,64,128]{3,2,1,0:T(8,128)} %get-tuple-element.122.refs_0_.refs_2_, ...), custom_call_target="tpu_custom_call", output_to_operand_aliasing={{0}: (8, {})} | custom-call | bytes 1024 | tf_op jit(solution)/shard_map/drift_chunk/pallas_call | solution.py:194
  (75 shorter events, 12.5 us)
Async XLA Ops:
  3.1 5.7 %copy-start.2 = (f32[6,4,64,128]{3,2,1,0:T(8,128)S(1)}, f32[6,4,64,128]{3,2,1,0:T(8,128)}, u32[]{:S(2)}) copy-start(f32[6,4,64,128]{3,2,1,0:T(8,128)} %get-tuple-element.88.refs_1_) | copy-start | bytes 2359300
  6.3 44.6 %collective-permute-start = (f32[6,16,64,128]{3,2,1,0:T(8,128)}, f32[6,16,64,128]{3,2,1,0:T(8,128)}, u32[]{:S(2)}, u32[]{:S(2)}) collective-permute-start(f32[6,16,64,128]{3,2,1,0:T(8,128)} %pack_tiles.11), channel_id=1, source_target_pairs={{0,8},{8,0},{16,24},{24,16},{1,9},{9,1},{17,25},{25,17},{2,10},{10... | collective-permute-start | bytes 9437192 | tf_op jit(solution)/shard_map/ppermute | solution.py:128
  7.2 20.1 %collective-permute-start.2 = (f32[6,4,64,128]{3,2,1,0:T(8,128)}, f32[6,4,64,128]{3,2,1,0:T(8,128)}, u32[]{:S(2)}, u32[]{:S(2)}) collective-permute-start(f32[6,4,64,128]{3,2,1,0:T(8,128)} %get-tuple-element.91), channel_id=1, source_target_pairs={{0,24},{8,16},{16,8},{24,0},{1,25},{9,17},{17,9},{25,1},{2,26},{10... | collective-permute-start | bytes 2359304 | tf_op jit(solution)/shard_map/ppermute | solution.py:128
  8.8 35.0 %collective-permute-start.1 = (f32[6,4,64,128]{3,2,1,0:T(8,128)S(1)}, f32[6,4,64,128]{3,2,1,0:T(8,128)}, u32[]{:S(2)}, u32[]{:S(2)}) collective-permute-start(f32[6,4,64,128]{3,2,1,0:T(8,128)S(1)} %copy-done.2), channel_id=1, source_target_pairs={{0,16},{8,24},{16,0},{24,8},{1,17},{9,25},{17,1},{25,9},{2,18},{10... | collective-permute-start | bytes 2359304 | tf_op jit(solution)/shard_map/ppermute | solution.py:128
  43.8 21.6 %collective-permute-start.3 = (f32[6,4,64,128]{3,2,1,0:T(8,128)}, f32[6,4,64,128]{3,2,1,0:T(8,128)S(1)}, u32[]{:S(2)}, u32[]{:S(2)}) collective-permute-start(f32[6,4,64,128]{3,2,1,0:T(8,128)} %get-tuple-element.98), channel_id=1, source_target_pairs={{0,16},{8,24},{16,0},{24,8},{1,17},{9,25},{17,1},{25,9},{2,18},{10... | collective-permute-start | bytes 2359304 | tf_op jit(solution)/shard_map/ppermute | solution.py:128
  45.0 35.6 %collective-permute-start.4 = (f32[6,4,64,128]{3,2,1,0:T(8,128)}, f32[6,4,64,128]{3,2,1,0:T(8,128)}, u32[]{:S(2)}, u32[]{:S(2)}) collective-permute-start(f32[6,4,64,128]{3,2,1,0:T(8,128)} %get-tuple-element.99), channel_id=1, source_target_pairs={{0,24},{8,16},{16,8},{24,0},{1,25},{9,17},{17,9},{25,1},{2,26},{10... | collective-permute-start | bytes 2359304 | tf_op jit(solution)/shard_map/ppermute | solution.py:128
  58.1 58.8 %collective-permute-start.7 = (f32[8,4,64,128]{3,2,1,0:T(8,128)}, f32[8,4,64,128]{3,2,1,0:T(8,128)}, u32[]{:S(2)}, u32[]{:S(2)}) collective-permute-start(f32[8,4,64,128]{3,2,1,0:T(8,128)} %get-tuple-element.110), channel_id=1, source_target_pairs={{0,1},{1,0},{2,3},{3,2},{4,5},{5,4},{6,7},{7,6},{8,9},{9,8},{10,11... | collective-permute-start | bytes 3145736 | tf_op jit(solution)/shard_map/ppermute | solution.py:493
  59.4 58.8 %collective-permute-start.8 = (f32[8,4,64,128]{3,2,1,0:T(8,128)}, f32[8,4,64,128]{3,2,1,0:T(8,128)}, u32[]{:S(2)}, u32[]{:S(2)}) collective-permute-start(f32[8,4,64,128]{3,2,1,0:T(8,128)} %get-tuple-element.94.refs_0_), channel_id=1, source_target_pairs={{1,3},{2,0},{3,5},{4,2},{5,7},{6,4},{9,11},{10,8},{11,13},{12,10},... | collective-permute-start | bytes 3145736 | tf_op jit(solution)/shard_map/ppermute | solution.py:496
  65.4 16.3 %copy-start.5 = (f32[6,4,64,128]{3,2,1,0:T(8,128)}, f32[6,4,64,128]{3,2,1,0:T(8,128)S(1)}, u32[]{:S(2)}) copy-start(f32[6,4,64,128]{3,2,1,0:T(8,128)S(1)} %collective-permute-done.3.refs_2_) | copy-start | bytes 2359300
  80.6 19.9 %collective-permute-start.5 = (f32[6,4,64,128]{3,2,1,0:T(8,128)}, f32[6,4,64,128]{3,2,1,0:T(8,128)}, u32[]{:S(2)}, u32[]{:S(2)}) collective-permute-start(f32[6,4,64,128]{3,2,1,0:T(8,128)} %get-tuple-element.106), channel_id=1, source_target_pairs={{0,16},{8,24},{16,0},{24,8},{1,17},{9,25},{17,1},{25,9},{2,18},{10... | collective-permute-start | bytes 2359304 | tf_op jit(solution)/shard_map/ppermute | solution.py:128
  81.7 35.2 %collective-permute-start.6 = (f32[6,4,64,128]{3,2,1,0:T(8,128)}, f32[6,4,64,128]{3,2,1,0:T(8,128)}, u32[]{:S(2)}, u32[]{:S(2)}) collective-permute-start(f32[6,4,64,128]{3,2,1,0:T(8,128)} %get-tuple-element.107), channel_id=1, source_target_pairs={{0,24},{8,16},{16,8},{24,0},{1,25},{9,17},{17,9},{25,1},{2,26},{10... | collective-permute-start | bytes 2359304 | tf_op jit(solution)/shard_map/ppermute | solution.py:128
  88.9 39.7 %collective-permute-start.11 = (f32[8,4,64,128]{3,2,1,0:T(8,128)}, f32[8,4,64,128]{3,2,1,0:T(8,128)}, u32[]{:S(2)}, u32[]{:S(2)}) collective-permute-start(f32[8,4,64,128]{3,2,1,0:T(8,128)} %get-tuple-element.116), channel_id=1, source_target_pairs={{0,1},{1,0},{2,3},{3,2},{4,5},{5,4},{6,7},{7,6},{8,9},{9,8},{10,11... | collective-permute-start | bytes 3145736 | tf_op jit(solution)/shard_map/ppermute | solution.py:493
  100.4 30.6 %collective-permute-start.12 = (f32[8,4,64,128]{3,2,1,0:T(8,128)}, f32[8,4,64,128]{3,2,1,0:T(8,128)}, u32[]{:S(2)}, u32[]{:S(2)}) collective-permute-start(f32[8,4,64,128]{3,2,1,0:T(8,128)} %get-tuple-element.102.refs_1_), channel_id=1, source_target_pairs={{1,3},{2,0},{3,5},{4,2},{5,7},{6,4},{9,11},{10,8},{11,13},{12,10},... | collective-permute-start | bytes 3145736 | tf_op jit(solution)/shard_map/ppermute | solution.py:496
  116.9 48.1 %collective-permute-start.13 = (f32[8,4,64,128]{3,2,1,0:T(8,128)}, f32[8,4,64,128]{3,2,1,0:T(8,128)}, u32[]{:S(2)}, u32[]{:S(2)}) collective-permute-start(f32[8,4,64,128]{3,2,1,0:T(8,128)} %collective-permute-done.7.refs_4_), channel_id=1, source_target_pairs={{0,2},{2,4},{3,1},{4,6},{5,3},{7,5},{8,10},{10,12},{11,9},{12,14},... | collective-permute-start | bytes 3145736 | tf_op jit(solution)/shard_map/ppermute | solution.py:499
  125.4 46.9 %collective-permute-start.14 = (f32[8,4,64,128]{3,2,1,0:T(8,128)}, f32[8,4,64,128]{3,2,1,0:T(8,128)}, u32[]{:S(2)}, u32[]{:S(2)}) collective-permute-start(f32[8,4,64,128]{3,2,1,0:T(8,128)} %get-tuple-element.120), channel_id=1, source_target_pairs={{0,1},{1,0},{2,3},{3,2},{4,5},{5,4},{6,7},{7,6},{8,9},{9,8},{10,11... | collective-permute-start | bytes 3145736 | tf_op jit(solution)/shard_map/ppermute | solution.py:493
  128.3 18.2 %collective-permute-start.9 = (f32[6,4,64,128]{3,2,1,0:T(8,128)}, f32[6,4,64,128]{3,2,1,0:T(8,128)S(1)}, u32[]{:S(2)}, u32[]{:S(2)}) collective-permute-start(f32[6,4,64,128]{3,2,1,0:T(8,128)} %get-tuple-element.114), channel_id=1, source_target_pairs={{0,16},{8,24},{16,0},{24,8},{1,17},{9,25},{17,1},{25,9},{2,18},{10... | collective-permute-start | bytes 2359304 | tf_op jit(solution)/shard_map/ppermute | solution.py:128
  128.6 36.4 %collective-permute-start.10 = (f32[6,4,64,128]{3,2,1,0:T(8,128)}, f32[6,4,64,128]{3,2,1,0:T(8,128)}, u32[]{:S(2)}, u32[]{:S(2)}) collective-permute-start(f32[6,4,64,128]{3,2,1,0:T(8,128)} %get-tuple-element.115), channel_id=1, source_target_pairs={{0,24},{8,16},{16,8},{24,0},{1,25},{9,17},{17,9},{25,1},{2,26},{10... | collective-permute-start | bytes 2359304 | tf_op jit(solution)/shard_map/ppermute | solution.py:128
  131.1 42.5 %copy-start.13 = (s32[1,8]{1,0:T(1,128)S(1)}, s32[1,8]{1,0:T(1,128)}, u32[]{:S(2)}) copy-start(s32[1,8]{1,0:T(1,128)} %param.14) | copy-start | bytes 100
  131.1 42.7 %copy-start.10 = (f32[128,64]{0,1:T(8,128)S(1)}, f32[128,64]{0,1:T(8,128)}, u32[]{:S(2)}) copy-start(f32[128,64]{0,1:T(8,128)} %param.16) | copy-start | bytes 98308
  131.1 42.7 %copy-start.11 = (f32[128,64]{0,1:T(8,128)S(1)}, f32[128,64]{0,1:T(8,128)}, u32[]{:S(2)}) copy-start(f32[128,64]{0,1:T(8,128)} %param.17) | copy-start | bytes 98308
  131.1 43.1 %copy-start.12 = (f32[1,8]{1,0:T(1,128)S(1)}, f32[1,8]{1,0:T(1,128)}, u32[]{:S(2)}) copy-start(f32[1,8]{1,0:T(1,128)} %param.15) | copy-start | bytes 100
  131.1 43.2 %collective-permute-start.16 = (f32[8,4,64,128]{3,2,1,0:T(8,128)}, f32[8,4,64,128]{3,2,1,0:T(8,128)}, u32[]{:S(2)}, u32[]{:S(2)}) collective-permute-start(f32[8,4,64,128]{3,2,1,0:T(8,128)} %get-tuple-element.113.refs_2_), channel_id=1, source_target_pairs={{1,3},{2,0},{3,5},{4,2},{5,7},{6,4},{9,11},{10,8},{11,13},{12,10},... | collective-permute-start | bytes 3145736 | tf_op jit(solution)/shard_map/ppermute | solution.py:496
  146.5 18.5 %copy-start.6 = (f32[6,4,64,128]{3,2,1,0:T(8,128)}, f32[6,4,64,128]{3,2,1,0:T(8,128)S(1)}, u32[]{:S(2)}) copy-start(f32[6,4,64,128]{3,2,1,0:T(8,128)S(1)} %collective-permute-done.9.refs_2_) | copy-start | bytes 2359300
  146.5 27.8 %collective-permute-start.17 = (f32[8,4,64,128]{3,2,1,0:T(8,128)}, f32[8,4,64,128]{3,2,1,0:T(8,128)}, u32[]{:S(2)}, u32[]{:S(2)}) collective-permute-start(f32[8,4,64,128]{3,2,1,0:T(8,128)} %collective-permute-done.11.refs_5_), channel_id=1, source_target_pairs={{0,2},{2,4},{3,1},{4,6},{5,3},{7,5},{8,10},{10,12},{11,9},{12,14},... | collective-permute-start | bytes 3145736 | tf_op jit(solution)/shard_map/ppermute | solution.py:499
  172.2 24.7 %collective-permute-start.15 = (f32[8,4,64,128]{3,2,1,0:T(8,128)}, f32[8,4,64,128]{3,2,1,0:T(8,128)}, u32[]{:S(2)}, u32[]{:S(2)}) collective-permute-start(f32[8,4,64,128]{3,2,1,0:T(8,128)} %get-tuple-element.121), channel_id=1, source_target_pairs={{0,1},{1,0},{2,3},{3,2},{4,5},{5,4},{6,7},{7,6},{8,9},{9,8},{10,11... | collective-permute-start | bytes 3145736 | tf_op jit(solution)/shard_map/ppermute | solution.py:493
  172.3 27.0 %collective-permute-start.18 = (f32[8,4,64,128]{3,2,1,0:T(8,128)}, f32[8,4,64,128]{3,2,1,0:T(8,128)}, u32[]{:S(2)}, u32[]{:S(2)}) collective-permute-start(f32[8,4,64,128]{3,2,1,0:T(8,128)} %collective-permute-done.14.refs_6_), channel_id=1, source_target_pairs={{0,2},{2,4},{3,1},{4,6},{5,3},{7,5},{8,10},{10,12},{11,9},{12,14},... | collective-permute-start | bytes 3145736 | tf_op jit(solution)/shard_map/ppermute | solution.py:499
  255.9 13.4 %collective-permute-start.19 = (f32[8,2,64,128]{3,2,1,0:T(8,128)}, f32[8,2,64,128]{3,2,1,0:T(8,128)S(1)}, u32[]{:S(2)}, u32[]{:S(2)}) collective-permute-start(f32[8,2,64,128]{3,2,1,0:T(8,128)} %get-tuple-element.127), channel_id=1, source_target_pairs={{0,1},{1,0},{2,3},{3,2},{4,5},{5,4},{6,7},{7,6},{8,9},{9,8},{10,11... | collective-permute-start | bytes 1572872 | tf_op jit(solution)/shard_map/ppermute | solution.py:543
  269.3 0.8 copy-start.3
  270.1 18.1 %collective-permute-start.20 = (f32[8,3,64,128]{3,2,1,0:T(8,128)}, f32[8,3,64,128]{3,2,1,0:T(8,128)S(1)}, u32[]{:S(2)}, u32[]{:S(2)}) collective-permute-start(f32[8,3,64,128]{3,2,1,0:T(8,128)} %get-tuple-element.128), channel_id=1, source_target_pairs={{0,1},{1,0},{2,3},{3,2},{4,5},{5,4},{6,7},{7,6},{8,9},{9,8},{10,11... | collective-permute-start | bytes 2359304 | tf_op jit(solution)/shard_map/ppermute | solution.py:545
  273.9 18.9 %collective-permute-start.21 = (f32[6,2,64,128]{3,2,1,0:T(8,128)}, f32[6,2,64,128]{3,2,1,0:T(8,128)}, u32[]{:S(2)}, u32[]{:S(2)}) collective-permute-start(f32[6,2,64,128]{3,2,1,0:T(8,128)} %get-tuple-element.131), channel_id=1, source_target_pairs={{0,16},{8,24},{16,0},{24,8},{1,17},{9,25},{17,1},{25,9},{2,18},{10... | collective-permute-start | bytes 1179656 | tf_op jit(solution)/shard_map/ppermute | solution.py:128
  274.5 19.1 %collective-permute-start.22 = (f32[6,2,64,128]{3,2,1,0:T(8,128)}, f32[6,2,64,128]{3,2,1,0:T(8,128)}, u32[]{:S(2)}, u32[]{:S(2)}) collective-permute-start(f32[6,2,64,128]{3,2,1,0:T(8,128)} %get-tuple-element.132), channel_id=1, source_target_pairs={{0,24},{8,16},{16,8},{24,0},{1,25},{9,17},{17,9},{25,1},{2,26},{10... | collective-permute-start | bytes 1179656 | tf_op jit(solution)/shard_map/ppermute | solution.py:128
  288.2 0.9 copy-start
  293.6 23.6 %collective-permute-start.23 = (f32[8,4,64,128]{3,2,1,0:T(8,128)}, f32[8,4,64,128]{3,2,1,0:T(8,128)}, u32[]{:S(2)}, u32[]{:S(2)}) collective-permute-start(f32[8,4,64,128]{3,2,1,0:T(8,128)} %get-tuple-element.135), channel_id=1, source_target_pairs={{0,1},{1,0},{2,3},{3,2},{4,5},{5,4},{6,7},{7,6},{8,9},{9,8},{10,11... | collective-permute-start | bytes 3145736 | tf_op jit(solution)/shard_map/ppermute | solution.py:557
  294.8 26.2 %collective-permute-start.25 = (f32[6,3,64,128]{3,2,1,0:T(8,128)}, f32[6,3,64,128]{3,2,1,0:T(8,128)S(1)}, u32[]{:S(2)}, u32[]{:S(2)}) collective-permute-start(f32[6,3,64,128]{3,2,1,0:T(8,128)} %get-tuple-element.140), channel_id=1, source_target_pairs={{0,16},{8,24},{16,0},{24,8},{1,17},{9,25},{17,1},{25,9},{2,18},{10... | collective-permute-start | bytes 1769480 | tf_op jit(solution)/shard_map/ppermute | solution.py:128
  295.3 27.4 %collective-permute-start.26 = (f32[6,3,64,128]{3,2,1,0:T(8,128)}, f32[6,3,64,128]{3,2,1,0:T(8,128)}, u32[]{:S(2)}, u32[]{:S(2)}) collective-permute-start(f32[6,3,64,128]{3,2,1,0:T(8,128)} %get-tuple-element.141), channel_id=1, source_target_pairs={{0,24},{8,16},{16,8},{24,0},{1,25},{9,17},{17,9},{25,1},{2,26},{10... | collective-permute-start | bytes 1769480 | tf_op jit(solution)/shard_map/ppermute | solution.py:128
  297.3 1.9 collective-permute-start.24
  299.2 0.8 copy-start.9
  321.0 1.8 copy-start.7
  322.8 23.6 %collective-permute-start.27 = (f32[8,4,64,128]{3,2,1,0:T(8,128)}, f32[8,4,64,128]{3,2,1,0:T(8,128)}, u32[]{:S(2)}, u32[]{:S(2)}) collective-permute-start(f32[8,4,64,128]{3,2,1,0:T(8,128)} %get-tuple-element.144), channel_id=1, source_target_pairs={{0,1},{1,0},{2,3},{3,2},{4,5},{5,4},{6,7},{7,6},{8,9},{9,8},{10,11... | collective-permute-start | bytes 3145736 | tf_op jit(solution)/shard_map/ppermute | solution.py:557
  323.8 26.3 %collective-permute-start.29 = (f32[6,4,64,128]{3,2,1,0:T(8,128)}, f32[6,4,64,128]{3,2,1,0:T(8,128)S(1)}, u32[]{:S(2)}, u32[]{:S(2)}) collective-permute-start(f32[6,4,64,128]{3,2,1,0:T(8,128)} %get-tuple-element.150), channel_id=1, source_target_pairs={{0,16},{8,24},{16,0},{24,8},{1,17},{9,25},{17,1},{25,9},{2,18},{10... | collective-permute-start | bytes 2359304 | tf_op jit(solution)/shard_map/ppermute | solution.py:128
  324.5 35.7 %collective-permute-start.30 = (f32[6,4,64,128]{3,2,1,0:T(8,128)}, f32[6,4,64,128]{3,2,1,0:T(8,128)}, u32[]{:S(2)}, u32[]{:S(2)}) collective-permute-start(f32[6,4,64,128]{3,2,1,0:T(8,128)} %get-tuple-element.151), channel_id=1, source_target_pairs={{0,24},{8,16},{16,8},{24,0},{1,25},{9,17},{17,9},{25,1},{2,26},{10... | collective-permute-start | bytes 2359304 | tf_op jit(solution)/shard_map/ppermute | solution.py:128
  327.2 2.3 collective-permute-start.28
  327.3 35.3 %collective-permute-start.32 = (f32[6,4,64,128]{3,2,1,0:T(8,128)}, f32[6,4,64,128]{3,2,1,0:T(8,128)}, u32[]{:S(2)}, u32[]{:S(2)}) collective-permute-start(f32[6,4,64,128]{3,2,1,0:T(8,128)} %get-tuple-element.155), channel_id=1, source_target_pairs={{0,8},{8,0},{16,24},{24,16},{1,9},{9,1},{17,25},{25,17},{2,10},{10... | collective-permute-start | bytes 2359304 | tf_op jit(solution)/shard_map/ppermute | solution.py:128
  350.2 10.1 %copy-start.4 = (f32[6,4,64,128]{3,2,1,0:T(8,128)}, f32[6,4,64,128]{3,2,1,0:T(8,128)S(1)}, u32[]{:S(2)}) copy-start(f32[6,4,64,128]{3,2,1,0:T(8,128)S(1)} %collective-permute-done.29.refs_3_) | copy-start | bytes 2359300
  360.3 19.5 %collective-permute-start.31 = (f32[8,3,64,128]{3,2,1,0:T(8,128)}, f32[8,3,64,128]{3,2,1,0:T(8,128)S(1)}, u32[]{:S(2)}, u32[]{:S(2)}) collective-permute-start(f32[8,3,64,128]{3,2,1,0:T(8,128)} %get-tuple-element.154), channel_id=1, source_target_pairs={{0,1},{1,0},{2,3},{3,2},{4,5},{5,4},{6,7},{7,6},{8,9},{9,8},{10,11... | collective-permute-start | bytes 2359304 | tf_op jit(solution)/shard_map/ppermute | solution.py:557
  360.7 23.8 %collective-permute-start.34 = (f32[6,4,64,128]{3,2,1,0:T(8,128)}, f32[6,4,64,128]{3,2,1,0:T(8,128)}, u32[]{:S(2)}, u32[]{:S(2)}) collective-permute-start(f32[6,4,64,128]{3,2,1,0:T(8,128)} %get-tuple-element.161), channel_id=1, source_target_pairs={{0,16},{8,24},{16,0},{24,8},{1,17},{9,25},{17,1},{25,9},{2,18},{10... | collective-permute-start | bytes 2359304 | tf_op jit(solution)/shard_map/ppermute | solution.py:128
  361.3 35.8 %collective-permute-start.35 = (f32[6,4,64,128]{3,2,1,0:T(8,128)}, f32[6,4,64,128]{3,2,1,0:T(8,128)}, u32[]{:S(2)}, u32[]{:S(2)}) collective-permute-start(f32[6,4,64,128]{3,2,1,0:T(8,128)} %get-tuple-element.162), channel_id=1, source_target_pairs={{0,24},{8,16},{16,8},{24,0},{1,25},{9,17},{17,9},{25,1},{2,26},{10... | collective-permute-start | bytes 2359304 | tf_op jit(solution)/shard_map/ppermute | solution.py:128
  361.7 37.6 %collective-permute-start.38 = (f32[6,4,64,128]{3,2,1,0:T(8,128)}, f32[6,4,64,128]{3,2,1,0:T(8,128)}, u32[]{:S(2)}, u32[]{:S(2)}) collective-permute-start(f32[6,4,64,128]{3,2,1,0:T(8,128)} %get-tuple-element.165), channel_id=1, source_target_pairs={{0,8},{8,0},{16,24},{24,16},{1,9},{9,1},{17,25},{25,17},{2,10},{10... | collective-permute-start | bytes 2359304 | tf_op jit(solution)/shard_map/ppermute | solution.py:128
  379.8 0.9 copy-start.1
  397.0 14.5 %collective-permute-start.36 = (f32[6,3,64,128]{3,2,1,0:T(8,128)}, f32[6,3,64,128]{3,2,1,0:T(8,128)S(1)}, u32[]{:S(2)}, u32[]{:S(2)}) collective-permute-start(f32[6,3,64,128]{3,2,1,0:T(8,128)} %get-tuple-element.163), channel_id=1, source_target_pairs={{0,16},{8,24},{16,0},{24,8},{1,17},{9,25},{17,1},{25,9},{2,18},{10... | collective-permute-start | bytes 1769480 | tf_op jit(solution)/shard_map/ppermute | solution.py:128
  397.9 27.2 %collective-permute-start.37 = (f32[6,3,64,128]{3,2,1,0:T(8,128)}, f32[6,3,64,128]{3,2,1,0:T(8,128)}, u32[]{:S(2)}, u32[]{:S(2)}) collective-permute-start(f32[6,3,64,128]{3,2,1,0:T(8,128)} %get-tuple-element.164), channel_id=1, source_target_pairs={{0,24},{8,16},{16,8},{24,0},{1,25},{9,17},{17,9},{25,1},{2,26},{10... | collective-permute-start | bytes 1769480 | tf_op jit(solution)/shard_map/ppermute | solution.py:128
  399.3 25.8 %collective-permute-start.33 = (f32[6,3,64,128]{3,2,1,0:T(8,128)}, f32[6,3,64,128]{3,2,1,0:T(8,128)}, u32[]{:S(2)}, u32[]{:S(2)}) collective-permute-start(f32[6,3,64,128]{3,2,1,0:T(8,128)} %get-tuple-element.158), channel_id=1, source_target_pairs={{0,8},{8,0},{16,24},{24,16},{1,9},{9,1},{17,25},{25,17},{2,10},{10... | collective-permute-start | bytes 1769480 | tf_op jit(solution)/shard_map/ppermute | solution.py:128
  411.5 13.5 %copy-start.8 = (f32[6,3,64,128]{3,2,1,0:T(8,128)}, f32[6,3,64,128]{3,2,1,0:T(8,128)S(1)}, u32[]{:S(2)}) copy-start(f32[6,3,64,128]{3,2,1,0:T(8,128)S(1)} %collective-permute-done.36.refs_3_) | copy-start | bytes 1769476

commit v3 on v2

--- a/solution.py
+++ b/solution.py
@@ -8,7 +8,7 @@
 from jax.sharding import PartitionSpec as P
 
 PASSES = 12
-VMEM_LIMIT = 63 * 1024 * 1024
+VMEM_LIMIT = 64 * 1024 * 1024 - 128 * 1024
 ANY = pl.BlockSpec(memory_space=pltpu.HBM)
 SMEM = pl.BlockSpec(memory_space=pltpu.SMEM)
 VMEM = pl.BlockSpec(memory_space=pltpu.VMEM)
@@ -64,16 +64,17 @@
     )(matrix_id, cubic_weights)
 
 
-def pack_kernel(find, n_arrays, offsets, sec_ref, til_ref, *refs):
+def pack_kernel(offsets, finds, n_arrays, sec_ref, til_ref, *refs):
     tiles, n = sec_ref.shape[2], len(offsets)
-    sends, room, in_sems, out_sems = refs[-n - 3 : -3], *refs[-3:]
-    pieces = find(*refs[:n_arrays])
+    sends, rooms = refs[-2 * n - 2 : -n - 2], refs[-n - 2 : -2]
+    in_sems, out_sems = refs[-2:]
     me = lax.axis_index("sector")
     counts = []
     for i, d in enumerate(offsets):
         dest = me ^ d
-
-        def body(t, count, i=i, dest=dest):
+        pieces = finds[i](*refs[:n_arrays])
+
+        def body(t, count, i=i, dest=dest, pieces=pieces):
             hit = sec_ref[0, dest, t] == me
 
             @pl.when(hit)
@@ -82,7 +83,7 @@
 
                     @pl.when(guard)
                     def _():
-                        pltpu.make_async_copy(piece(), room.at[i, count], in_sems.at[i, count]).start()
+                        pltpu.make_async_copy(piece(), rooms[i].at[count], in_sems.at[i, count]).start()
 
             return count + hit.astype(jnp.int32)
 
@@ -91,7 +92,7 @@
 
         @pl.loop(0, counts[i])
         def _(slot, i=i):
-            here = room.at[i, slot]
+            here = rooms[i].at[slot]
             pltpu.make_async_copy(here, here, in_sems.at[i, slot]).wait()
             pltpu.make_async_copy(here, sends[i].at[slot], out_sems.at[i, slot]).start()
 
@@ -99,20 +100,19 @@
 
         @pl.loop(0, counts[i])
         def _(slot, i=i):
-            here = room.at[i, slot]
-            pltpu.make_async_copy(here, sends[i].at[slot], out_sems.at[i, slot]).wait()
-
-
-def pack(find, offsets, cap, tables, arrays, piece, after=()):
-    n = len(offsets)
-    send = jax.ShapeDtypeStruct((cap,) + piece, F32)
+            pltpu.make_async_copy(rooms[i].at[slot], sends[i].at[slot], out_sems.at[i, slot]).wait()
+
+
+def pack(groups, cap, tables, arrays, after=()):
+    n = len(groups)
+    offsets, finds, shapes = zip(*groups)
     return pl.pallas_call(
-        functools.partial(pack_kernel, find, len(arrays), tuple(offsets)),
-        out_shape=[send] * n,
+        functools.partial(pack_kernel, offsets, finds, len(arrays)),
+        out_shape=[jax.ShapeDtypeStruct((cap,) + shape, F32) for shape in shapes],
         in_specs=[SMEM, SMEM] + [ANY] * (len(arrays) + len(after)),
         out_specs=[ANY] * n,
         scratch_shapes=[
-            pltpu.VMEM((n, cap) + piece, F32),
+            *[pltpu.VMEM((cap,) + shape, F32) for shape in shapes],
             pltpu.SemaphoreType.DMA((n, cap)),
             pltpu.SemaphoreType.DMA((n, cap)),
         ],
@@ -187,12 +187,13 @@
         pltpu.make_async_copy(made.at[t], made.at[t], out_sems.at[t]).wait()
 
 
-def drift(find, place, receive, tables, weights, local, recvs, outs, piece, carried=()):
+def drift(find, place, receive, tables, weights, local, recvs, outs, piece, after=(), carried=()):
     sectors, tiles = tables[0].shape[1], tables[0].shape[2]
     n_local = len(local)
-    ins = [*tables, weights, *local, *recvs, *carried]
+    ins = [*tables, weights, *local, *recvs, *after, *carried]
+    n_extra = len(after) + len(carried)
     return pl.pallas_call(
-        functools.partial(drift_kernel, find, place, receive, n_local, len(carried)),
+        functools.partial(drift_kernel, find, place, receive, n_local, n_extra),
         out_shape=[*outs, jax.ShapeDtypeStruct((8, 128), F32)],
         in_specs=[SMEM, SMEM, VMEM] + [ANY] * (len(ins) - 3),
         out_specs=[ANY] * len(outs) + [VMEM],
@@ -415,89 +416,13 @@
     half = tiles // 2
     quarter = block // 4
     halo_chunks = PASSES // quarter
-    first_steps = (quarter,) * 4
-    last_steps = (quarter // 2, quarter - quarter // 4, quarter, quarter, quarter - quarter // 4)
+    first_steps = (quarter, quarter, quarter, quarter // 2, quarter - quarter // 2)
+    last_steps = (quarter // 2, quarter, quarter, quarter - quarter // 4, block - 3 * quarter - quarter // 2 + quarter // 4)
     cap = slots(tiles, sectors)
     tables = (source_sector, source_tile)
     near, far = [1], list(range(2, sectors))
 
     weights = split_weights(matrix_id, cubic_weights)
-
-    def at_lanes(t):
-        return pl.ds(pl.multiple_of(t * side, side), side)
-
-    def side_here():
-        return lax.axis_index("inner") % 2
-
-    swap = [(i, i ^ 1) for i in range(inner)]
-    own_pairs, got_pairs = [], []
-    for i in range(inner):
-        for pairs, shift in ((own_pairs, -2 if i % 2 == 0 else 2), (got_pairs, 2 if i % 2 == 0 else -2)):
-            if 0 <= i + shift < inner:
-                pairs.append((i, i + shift))
-
-    own, got, own_halo, got_halo = [], [], [], []
-    packed = []
-    start = 0
-    for k, step in enumerate(first_steps):
-
-        def first_of(start=start, step=step):
-            here = side_here()
-            return here * (block - start - step) + (1 - here) * start
-
-        def find(field, first_of=first_of, step=step):
-            first = first_of()
-            return lambda t: [(t >= 0, lambda: field.at[pl.ds(first, step), :, at_lanes(t)])]
-
-        def find_all(field):
-            return lambda t: [(t >= 0, lambda: field.at[:, :, at_lanes(t)])]
-
-        def receive(came, other, slot, first_of=first_of, step=step):
-            return came.at[slot, pl.ds(first_of(), step)] if other == 1 else came.at[slot]
-
-        def place(kept, sent):
-            here = side_here()
-            mine = lambda t: (t // half) == here
-            return lambda t: [
-                (mine(t), lambda: kept.at[t % half]),
-                (jnp.logical_not(mine(t)), lambda: sent.at[t % half]),
-            ]
-
-        packed.append((start, step, find, receive, place))
-        start += step
-
-    def pack_first(k, after):
-        start, step, find, _, _ = packed[k]
-        return pack(find, far, cap, tables, [density], (step, pitches, side), after)
-
-    sends = pack_first(0, ())
-    recvs = sector_exchange(sends, far)
-    beside = pack(find_all, near, cap, tables, [density], (block, pitches, side), (sends[0],))
-    beside = sector_exchange(beside, near)
-    token = sends[0]
-    crossing = []
-    for k, (start, step, find, receive, place) in enumerate(packed):
-        if k + 1 < len(packed):
-            later = pack_first(k + 1, (token,))
-            later, recvs = in_turn(later, recvs)
-            coming = sector_exchange(later, far)
-        if k >= 2:
-            recvs, _ = in_turn(recvs, crossing[k - 2])
-        part = jax.ShapeDtypeStruct((half, step, pitches, side), F32)
-        piece = (step, pitches, side)
-        kept, sent, token = drift(
-            find, place, receive, tables, weights, [density], beside + recvs, [part, part], piece
-        )
-        recvs = coming
-        own.append(kept)
-        got.append(lax.ppermute(sent, "inner", swap))
-        crossing.append(got[-1:])
-        if k < halo_chunks:
-            own_halo.append(lax.ppermute(kept, "inner", own_pairs))
-            crossing[-1] += own_halo[-1:]
-        if 0 < k <= halo_chunks:
-            got_halo.append(lax.ppermute(got[k - 1], "inner", got_pairs))
-            crossing[-1] += got_halo[-1:]
 
     energies = energy_rate.shape[0]
     frame = 2 * block + 2 * PASSES
@@ -513,6 +438,87 @@
     level = jnp.sum(jnp.where(bin_of[:, None] == bins[None, :], wave_level[0][None, :], 0.0), axis=1)
     rate = jnp.broadcast_to(level.reshape(half, 1, side), (half, 8, side))
 
+    def at_lanes(t):
+        return pl.ds(pl.multiple_of(t * side, side), side)
+
+    def side_here():
+        return lax.axis_index("inner") % 2
+
+    swap = [(i, i ^ 1) for i in range(inner)]
+    own_pairs, got_pairs = [], []
+    for i in range(inner):
+        for pairs, shift in ((own_pairs, -2 if i % 2 == 0 else 2), (got_pairs, 2 if i % 2 == 0 else -2)):
+            if 0 <= i + shift < inner:
+                pairs.append((i, i + shift))
+
+    own, got, own_halo, got_halo = [], [], [], []
+    packed = []
+    start = 0
+    for k, step in enumerate(first_steps):
+
+        def first_of(start=start, step=step):
+            here = side_here()
+            return here * (block - start - step) + (1 - here) * start
+
+        def find(field, first_of=first_of, step=step):
+            first = first_of()
+            return lambda t: [(t >= 0, lambda: field.at[pl.ds(first, step), :, at_lanes(t)])]
+
+        def find_all(field):
+            return lambda t: [(t >= 0, lambda: field.at[:, :, at_lanes(t)])]
+
+        def receive(came, other, slot, first_of=first_of, step=step):
+            return came.at[slot, pl.ds(first_of(), step)] if other == 1 else came.at[slot]
+
+        def place(kept, sent):
+            here = side_here()
+            mine = lambda t: (t // half) == here
+            return lambda t: [
+                (mine(t), lambda: kept.at[t % half]),
+                (jnp.logical_not(mine(t)), lambda: sent.at[t % half]),
+            ]
+
+        packed.append((start, step, find, receive, place))
+        start += step
+
+    def pack_first(k, after):
+        start, step, find, _, _ = packed[k]
+        groups = [(d, find, (step, pitches, side)) for d in far]
+        if k == 0:
+            groups += [(d, find_all, (block, pitches, side)) for d in near]
+        return pack(groups, cap, tables, [density], after)
+
+    sends = pack_first(0, ())
+    recvs = sector_exchange(sends[:-1], far)
+    beside = sector_exchange(sends[-1:], near)
+    token = sends[0]
+    crossing = []
+    for k, (start, step, find, receive, place) in enumerate(packed):
+        if k + 1 < len(packed):
+            later = pack_first(k + 1, (token,))
+            later, recvs = in_turn(later, recvs)
+            coming = sector_exchange(later, far)
+        if k == 1:
+            recvs, (rate, a, b) = in_turn(recvs, [rate, a, b])
+        after = ()
+        if k > 0:
+            after = [token, *(crossing[k - 2] if k == 2 else ()), *got_halo[: k - 2][-1:]]
+        part = jax.ShapeDtypeStruct((half, step, pitches, side), F32)
+        piece = (step, pitches, side)
+        kept, sent, token = drift(
+            find, place, receive, tables, weights, [density], beside + recvs, [part, part], piece, after
+        )
+        recvs = coming
+        own.append(kept)
+        got.append(lax.ppermute(sent, "inner", swap))
+        crossing.append(got[-1:])
+        if k < halo_chunks:
+            own_halo.append(lax.ppermute(kept, "inner", own_pairs))
+            crossing[-1] += own_halo[-1:]
+        if 0 < k <= halo_chunks:
+            got_halo.append(lax.ppermute(got[k - 1], "inner", got_pairs))
+            crossing[-1] += got_halo[-1:]
+
     kept, sends = diffuse(rate, a, b, own, got, own_halo, got_halo, last_steps)
 
     returns, ready, out, start = sends, [], (), 0
@@ -536,12 +542,12 @@
 
     def pack_last(k, after):
         find, _, piece = ready[k]
-        sends = pack(find, near + far, cap, tables, [kept, backs[k]], piece, after)
+        sends = pack([(d, find, piece) for d in near + far], cap, tables, [kept, backs[k]], after)
         return sends[:1], sends[1:]
 
     whole = [jax.ShapeDtypeStruct(density.shape, F32)]
     backs = [lax.ppermute(returns[0], "inner", swap)]
-    (last,), _ = in_turn([returns[1]], [backs[0]])
+    (last,), (backs[0],) = in_turn([returns[1]], [backs[0]])
     backs.append(lax.ppermute(last, "inner", swap))
     sends, far_sends = pack_last(0, ())
     recvs = sector_exchange(far_sends, far)
@@ -553,10 +559,10 @@
             far_sends, recvs = in_turn(far_sends, recvs)
             coming = sector_exchange(far_sends, far), sector_exchange(sends, near)
         if k + 2 < len(ready):
-            (last,), _ = in_turn([returns[k + 2]], [backs[k + 1], *recvs])
+            (last,), (backs[k + 1], *recvs) = in_turn([returns[k + 2]], [backs[k + 1], *recvs])
             backs.append(lax.ppermute(last, "inner", swap))
         *out, token = drift(
-            find, place, receive_slot, tables, weights, [kept, backs[k]], beside + recvs, whole, piece, out
+            find, place, receive_slot, tables, weights, [kept, backs[k]], beside + recvs, whole, piece, (), out
         )
         recvs, beside = coming
     return out[0]

time: 435 us -> 435 us (level)
  waiting for transfers between devices: 226 us -> 208 us
  starting transfers between devices: 42.4 us -> 52.2 us
  Pallas kernels: 155 us -> 163 us
    ppermute x4 -> x5, waiting for transfers between devices: 22.6 us -> 3.95 us  [paired_shards(): got.append(lax.ppermute(sent, 'inner', swap))]
    ppermute x3, waiting for transfers between devices: 0.01 us -> 12.9 us  [paired_shards(): own_halo.append(lax.ppermute(kept, 'inner', own_pairs))]
    ppermute x24 -> x26, waiting for transfers between devices: 146 us -> 138 us  [sector_exchange(): lax.ppermute(send, 'sector', [(s, s ^ d) for s in range(sectors)])]
    pallas_call x9 -> x10, Pallas kernels: 63.6 us -> 69.7 us  [drift(): pl.pallas_call(functools.partial(drift_kernel, find, place, receive, n_lo...]
    ppermute x3, starting transfers between devices: 8.11 us -> 13.2 us  [paired_shards(): own_halo.append(lax.ppermute(kept, 'inner', own_pairs))]
    ppermute x24 -> x26, starting transfers between devices: 22.2 us -> 23.7 us  [sector_exchange(): lax.ppermute(send, 'sector', [(s, s ^ d) for s in range(sectors)])]
  transfers between devices with their start and end apart: 39 -> 42, of which waited for: 22 -> 22; matrix products, arithmetic and copies ran while one was open for 0% -> 2% of each run, Pallas kernels for 21% -> 23%
where the time goes in v3:
time: 435 us; the launch traced here: 431 us
  waiting for transfers between devices  208 us (48%)
  Pallas kernels  163 us (37%)
  starting transfers between devices  52.2 us (12%)
  local copies, waits for them, and re-layouts  5.25 us (1%)
    ppermute x26, waiting for transfers between devices, sector_exchange(): lax.ppermute(send, 'sector', [(s, s ^ d) for s in range(sectors)])  138 us
    pallas_call x10, Pallas kernels, drift(): pl.pallas_call(functools.partial(drift_kernel, find, place, receive, n_lo...  69.7 us
    pallas_call x1, Pallas kernels, diffuse(): pl.pallas_call(functools.partial(diffusion_kernel, len(own), len(own_halo...  52.4 us
    ppermute x4, waiting for transfers between devices, paired_shards(): backs.append(lax.ppermute(last, 'inner', swap))  41.2 us
    pallas_call x10, Pallas kernels, pack(): pl.pallas_call(functools.partial(pack_kernel, offsets, finds, len(arrays)...  36.5 us
    ppermute x26, starting transfers between devices, sector_exchange(): lax.ppermute(send, 'sector', [(s, s ^ d) for s in range(sectors)])  23.7 us
    ppermute x3, starting transfers between devices, paired_shards(): own_halo.append(lax.ppermute(kept, 'inner', own_pairs))  13.2 us
    ppermute x3, waiting for transfers between devices, paired_shards(): own_halo.append(lax.ppermute(kept, 'inner', own_pairs))  12.9 us
  transfers between devices with their start and end apart: 42, of which 22 were waited for; matrix products, arithmetic and copies ran while one was open for 2% of the time, Pallas kernels for 23%

profile of v3, /device:TPU:25, one launch (start us, length us, event | category | flops | bytes accessed | tf_op | source)
XLA Modules:
  0.0 430.8 jit_solution(10834007499499445010)
XLA Ops:
  0.0 5.2 %pack_tiles.10 = (f32[6,4,64,128]{3,2,1,0:T(8,128)}, f32[6,4,64,128]{3,2,1,0:T(8,128)}, f32[6,16,64,128]{3,2,1,0:T(8,128)}) custom-call(s32[1,4,16]{2,1,0:T(4,128)} %sec_ref.39, s32[1,4,16]{2,1,0:T(4,128)} %til_ref.39, f32[16,64,2048]{2,1,0:T(8,128)} %refs_0_.19), custom_call_target="tpu_custom_call" | custom-call | bytes 1024 | tf_op jit(solution)/shard_map/pack_tiles/pallas_call | solution.py:109
  7.2 3.2 pack_tiles.11
  10.3 15.2 %collective-permute-done.2.refs_3_ = f32[6,4,64,128]{3,2,1,0:T(8,128)} collective-permute-done((f32[6,4,64,128]{3,2,1,0:T(8,128)}, f32[6,4,64,128]{3,2,1,0:T(8,128)}, u32[]{:S(2)}, u32[]{:S(2)}) %collective-permute-start.2) | collective-permute-done | bytes 786464 | tf_op jit(solution)/shard_map/ppermute | solution.py:128
  25.6 16.6 %collective-permute-done.1.refs_2_ = f32[6,4,64,128]{3,2,1,0:T(8,128)} collective-permute-done((f32[6,4,64,128]{3,2,1,0:T(8,128)}, f32[6,4,64,128]{3,2,1,0:T(8,128)}, u32[]{:S(2)}, u32[]{:S(2)}) %collective-permute-start.1) | collective-permute-done | bytes 786464 | tf_op jit(solution)/shard_map/ppermute | solution.py:128
  42.4 2.0 collective-permute-start.4
  44.5 4.7 %split_weights.1.w_ref = bf16[16,256,256]{2,1,0:T(8,128)(2,1)} custom-call(s32[1,4,16]{2,1,0:T(4,128)} %mid_ref.1, f32[32,128,128]{2,1,0:T(8,128)} %w_ref.1), custom_call_target="tpu_custom_call" | custom-call | bytes 1024 | tf_op jit(solution)/shard_map/split_weights/pallas_call | solution.py:52
  49.2 7.2 %drift_chunk.10 = (f32[8,4,64,128]{3,2,1,0:T(8,128)}, f32[8,4,64,128]{3,2,1,0:T(8,128)}, f32[8,128]{1,0:T(8,128)}) custom-call(s32[1,4,16]{2,1,0:T(4,128)} %sec_ref.39, s32[1,4,16]{2,1,0:T(4,128)} %til_ref.39, bf16[16,256,256]{2,1,0:T(8,128)(2,1)} %split_weights.1.w_ref, f32[16,64,2048]{2,1,0:T(8,128)} %refs_0_.19, ...), custom_call_target="tpu_custom_call" | custom-call | bytes 1024 | tf_op jit(solution)/shard_map/drift_chunk/pallas_call | solution.py:195
  57.3 3.6 collective-permute-start.8
  61.7 3.2 pack_tiles.12
  64.9 14.0 %collective-permute-done.4.refs_3_ = f32[6,4,64,128]{3,2,1,0:T(8,128)} collective-permute-done((f32[6,4,64,128]{3,2,1,0:T(8,128)}, f32[6,4,64,128]{3,2,1,0:T(8,128)}, u32[]{:S(2)}, u32[]{:S(2)}) %collective-permute-start.4) | collective-permute-done | bytes 786464 | tf_op jit(solution)/shard_map/ppermute | solution.py:128
  82.2 1.9 broadcast_in_dim.47.b_ref
  84.1 1.8 broadcast_in_dim.45.a_ref
  85.8 7.1 %drift_chunk.11 = (f32[8,4,64,128]{3,2,1,0:T(8,128)}, f32[8,4,64,128]{3,2,1,0:T(8,128)}, f32[8,128]{1,0:T(8,128)}) custom-call(s32[1,4,16]{2,1,0:T(4,128)} %sec_ref.39, s32[1,4,16]{2,1,0:T(4,128)} %til_ref.39, bf16[16,256,256]{2,1,0:T(8,128)(2,1)} %split_weights.1.w_ref, f32[16,64,2048]{2,1,0:T(8,128)} %refs_0_.19, ...), custom_call_target="tpu_custom_call" | custom-call | bytes 1024 | tf_op jit(solution)/shard_map/drift_chunk/pallas_call | solution.py:195
  93.0 1.8 collective-permute-start.14
  94.8 3.0 pack_tiles.13
  97.7 1.0 collective-permute-done.5.refs_2_
  98.8 16.3 %collective-permute-done.6.refs_3_ = f32[6,4,64,128]{3,2,1,0:T(8,128)} collective-permute-done((f32[6,4,64,128]{3,2,1,0:T(8,128)}, f32[6,4,64,128]{3,2,1,0:T(8,128)}, u32[]{:S(2)}, u32[]{:S(2)}) %collective-permute-start.6) | collective-permute-done | bytes 786464 | tf_op jit(solution)/shard_map/ppermute | solution.py:128
  115.0 7.1 %drift_chunk.12 = (f32[8,4,64,128]{3,2,1,0:T(8,128)}, f32[8,4,64,128]{3,2,1,0:T(8,128)}, f32[8,128]{1,0:T(8,128)}) custom-call(s32[1,4,16]{2,1,0:T(4,128)} %sec_ref.39, s32[1,4,16]{2,1,0:T(4,128)} %til_ref.39, bf16[16,256,256]{2,1,0:T(8,128)(2,1)} %split_weights.1.w_ref, f32[16,64,2048]{2,1,0:T(8,128)} %refs_0_.19, ...), custom_call_target="tpu_custom_call" | custom-call | bytes 1024 | tf_op jit(solution)/shard_map/drift_chunk/pallas_call | solution.py:195
  122.2 1.8 collective-permute-start.16
  124.0 1.3 collective-permute-start.11
  126.2 1.3 collective-permute-start.10
  127.5 1.3 collective-permute-start.15
  128.8 3.0 pack_tiles.14
  131.8 4.0 collective-permute-done.9.refs_2_
  135.7 9.4 %collective-permute-done.10.refs_3_ = f32[6,2,64,128]{3,2,1,0:T(8,128)} collective-permute-done((f32[6,2,64,128]{3,2,1,0:T(8,128)}, f32[6,2,64,128]{3,2,1,0:T(8,128)}, u32[]{:S(2)}, u32[]{:S(2)}) %collective-permute-start.10) | collective-permute-done | bytes 393248 | tf_op jit(solution)/shard_map/ppermute | solution.py:128
  146.1 5.0 %collective-permute-start.19 = (f32[8,4,64,128]{3,2,1,0:T(8,128)}, f32[8,4,64,128]{3,2,1,0:T(8,128)}, u32[]{:S(2)}, u32[]{:S(2)}) collective-permute-start(f32[8,4,64,128]{3,2,1,0:T(8,128)} %get-tuple-element.130.refs_1_), channel_id=1, source_target_pairs={{1,3},{2,0},{3,5},{4,2},{5,7},{6,4},{9,11},{10,8},{11,13},{12,10},... | collective-permute-start | bytes 3145736 | tf_op jit(solution)/shard_map/ppermute | solution.py:516
  151.0 5.4 %collective-permute-done.12.refs_2_ = f32[6,2,64,128]{3,2,1,0:T(8,128)} collective-permute-done((f32[6,2,64,128]{3,2,1,0:T(8,128)}, f32[6,2,64,128]{3,2,1,0:T(8,128)}, u32[]{:S(2)}, u32[]{:S(2)}) %collective-permute-start.12) | collective-permute-done | bytes 393248 | tf_op jit(solution)/shard_map/ppermute | solution.py:128
  156.5 4.7 %collective-permute-start.20 = (f32[8,4,64,128]{3,2,1,0:T(8,128)}, f32[8,4,64,128]{3,2,1,0:T(8,128)}, u32[]{:S(2)}, u32[]{:S(2)}) collective-permute-start(f32[8,4,64,128]{3,2,1,0:T(8,128)} %get-tuple-element.139.refs_2_), channel_id=1, source_target_pairs={{1,3},{2,0},{3,5},{4,2},{5,7},{6,4},{9,11},{10,8},{11,13},{12,10},... | collective-permute-start | bytes 3145736 | tf_op jit(solution)/shard_map/ppermute | solution.py:516
  161.2 1.3 collective-permute-start.21
  162.9 6.7 %drift_chunk.13 = (f32[8,2,64,128]{3,2,1,0:T(8,128)}, f32[8,2,64,128]{3,2,1,0:T(8,128)}, f32[8,128]{1,0:T(8,128)}) custom-call(s32[1,4,16]{2,1,0:T(4,128)} %sec_ref.39, s32[1,4,16]{2,1,0:T(4,128)} %til_ref.39, bf16[16,256,256]{2,1,0:T(8,128)(2,1)} %split_weights.1.w_ref, f32[16,64,2048]{2,1,0:T(8,128)} %refs_0_.19, ...), custom_call_target="tpu_custom_call" | custom-call | bytes 1024 | tf_op jit(solution)/shard_map/drift_chunk/pallas_call | solution.py:195
  169.6 4.6 %collective-permute-done.13.refs_3_ = f32[6,2,64,128]{3,2,1,0:T(8,128)} collective-permute-done((f32[6,2,64,128]{3,2,1,0:T(8,128)}, f32[6,2,64,128]{3,2,1,0:T(8,128)}, u32[]{:S(2)}, u32[]{:S(2)}) %collective-permute-start.13) | collective-permute-done | bytes 393248 | tf_op jit(solution)/shard_map/ppermute | solution.py:128
  174.2 1.5 collective-permute-start.17
  175.7 6.6 %drift_chunk.14 = (f32[8,2,64,128]{3,2,1,0:T(8,128)}, f32[8,2,64,128]{3,2,1,0:T(8,128)}, f32[8,128]{1,0:T(8,128)}) custom-call(s32[1,4,16]{2,1,0:T(4,128)} %sec_ref.39, s32[1,4,16]{2,1,0:T(4,128)} %til_ref.39, bf16[16,256,256]{2,1,0:T(8,128)(2,1)} %split_weights.1.w_ref, f32[16,64,2048]{2,1,0:T(8,128)} %refs_0_.19, ...), custom_call_target="tpu_custom_call" | custom-call | bytes 1024 | tf_op jit(solution)/shard_map/drift_chunk/pallas_call | solution.py:195
  182.4 12.9 %collective-permute-done.20.refs_12_ = f32[8,4,64,128]{3,2,1,0:T(8,128)} collective-permute-done((f32[8,4,64,128]{3,2,1,0:T(8,128)}, f32[8,4,64,128]{3,2,1,0:T(8,128)}, u32[]{:S(2)}, u32[]{:S(2)}) %collective-permute-start.20) | collective-permute-done | bytes 1048608 | tf_op jit(solution)/shard_map/ppermute | solution.py:516
  195.3 3.9 collective-permute-done.18.refs_9_
  199.3 52.4 %diffuse_tiles.1 = (f32[8,16,64,128]{3,2,1,0:T(8,128)}, f32[8,2,64,128]{3,2,1,0:T(8,128)}, f32[8,4,64,128]{3,2,1,0:T(8,128)}, f32[8,4,64,128]{3,2,1,0:T(8,128)},...) custom-call(f32[8,8,128]{2,1,0:T(8,128)} %broadcast_in_dim.43.rate_ref, f32[56,64,128]{2,1,0:T(8,128)} %broadcast_in_dim.45.a_ref, ...), custom_call_target="tpu_custom_call" | custom-call | bytes 1024 | tf_op jit(solution)/shard_map/diffuse_tiles/pallas_call | solution.py:370
  251.6 1.4 collective-permute-start.22
  253.1 11.6 %collective-permute-done.22.refs_1_ = f32[8,2,64,128]{3,2,1,0:T(8,128)} collective-permute-done((f32[8,2,64,128]{3,2,1,0:T(8,128)}, f32[8,2,64,128]{3,2,1,0:T(8,128)}, u32[]{:S(2)}, u32[]{:S(2)}) %collective-permute-start.22) | collective-permute-done | bytes 524320 | tf_op jit(solution)/shard_map/ppermute | solution.py:549
  264.6 1.2 collective-permute-start.23
  265.8 3.6 pack_tiles.16
  270.2 3.0 collective-permute-start.25
  273.3 14.6 %collective-permute-done.23.refs_1_ = f32[8,4,64,128]{3,2,1,0:T(8,128)} collective-permute-done((f32[8,4,64,128]{3,2,1,0:T(8,128)}, f32[8,4,64,128]{3,2,1,0:T(8,128)}, u32[]{:S(2)}, u32[]{:S(2)}) %collective-permute-start.23) | collective-permute-done | bytes 1048608 | tf_op jit(solution)/shard_map/ppermute | solution.py:551
  287.9 3.9 pack_tiles.15
  291.8 1.1 collective-permute-start.26
  293.6 3.9 collective-permute-start.29
  298.1 1.6 collective-permute-done.27.refs_2_
  299.6 6.7 %drift_chunk.15 = (f32[16,64,2048]{2,1,0:T(8,128)}, f32[8,128]{1,0:T(8,128)}) custom-call(s32[1,4,16]{2,1,0:T(4,128)} %sec_ref.39, s32[1,4,16]{2,1,0:T(4,128)} %til_ref.39, bf16[16,256,256]{2,1,0:T(8,128)(2,1)} %split_weights.1.w_ref, f32[8,16,64,128]{3,2,1,0:T(8,128)} %get-tuple-element.156.refs_0_.refs_2_, ...), custom_call_target="tpu_custom_call" | custom-call | bytes 1024 | tf_op jit(solution)/shard_map/drift_chunk/pallas_call | solution.py:195
  306.3 8.1 %collective-permute-done.26.refs_1_ = f32[8,4,64,128]{3,2,1,0:T(8,128)} collective-permute-done((f32[8,4,64,128]{3,2,1,0:T(8,128)}, f32[8,4,64,128]{3,2,1,0:T(8,128)}, u32[]{:S(2)}, u32[]{:S(2)}) %collective-permute-start.26) | collective-permute-done | bytes 1048608 | tf_op jit(solution)/shard_map/ppermute | solution.py:563
  314.4 3.9 pack_tiles.17
  318.3 11.0 %collective-permute-done.29.refs_4_ = f32[6,4,64,128]{3,2,1,0:T(8,128)} collective-permute-done((f32[6,4,64,128]{3,2,1,0:T(8,128)}, f32[6,4,64,128]{3,2,1,0:T(8,128)}, u32[]{:S(2)}, u32[]{:S(2)}) %collective-permute-start.29) | collective-permute-done | bytes 786464 | tf_op jit(solution)/shard_map/ppermute | solution.py:128
  331.6 7.1 %drift_chunk.16 = (f32[16,64,2048]{2,1,0:T(8,128)}, f32[8,128]{1,0:T(8,128)}) custom-call(s32[1,4,16]{2,1,0:T(4,128)} %sec_ref.39, s32[1,4,16]{2,1,0:T(4,128)} %til_ref.39, bf16[16,256,256]{2,1,0:T(8,128)(2,1)} %split_weights.1.w_ref, f32[8,16,64,128]{3,2,1,0:T(8,128)} %get-tuple-element.156.refs_0_.refs_2_, ...), custom_call_target="tpu_custom_call", output_to_operand_aliasing={{0}: (8, {})} | custom-call | bytes 1024 | tf_op jit(solution)/shard_map/drift_chunk/pallas_call | solution.py:195
  338.8 10.1 %collective-permute-done.30.refs_1_ = f32[8,3,64,128]{3,2,1,0:T(8,128)} collective-permute-done((f32[8,3,64,128]{3,2,1,0:T(8,128)}, f32[8,3,64,128]{3,2,1,0:T(8,128)}, u32[]{:S(2)}, u32[]{:S(2)}) %collective-permute-start.30) | collective-permute-done | bytes 786464 | tf_op jit(solution)/shard_map/ppermute | solution.py:563
  348.9 3.8 pack_tiles.18
  352.7 13.5 %collective-permute-done.33.refs_4_ = f32[6,4,64,128]{3,2,1,0:T(8,128)} collective-permute-done((f32[6,4,64,128]{3,2,1,0:T(8,128)}, f32[6,4,64,128]{3,2,1,0:T(8,128)}, u32[]{:S(2)}, u32[]{:S(2)}) %collective-permute-start.33) | collective-permute-done | bytes 786464 | tf_op jit(solution)/shard_map/ppermute | solution.py:128
  366.3 1.2 collective-permute-start.34
  368.1 1.7 collective-permute-start.38
  369.8 7.1 %drift_chunk.17 = (f32[16,64,2048]{2,1,0:T(8,128)}, f32[8,128]{1,0:T(8,128)}) custom-call(s32[1,4,16]{2,1,0:T(4,128)} %sec_ref.39, s32[1,4,16]{2,1,0:T(4,128)} %til_ref.39, bf16[16,256,256]{2,1,0:T(8,128)(2,1)} %split_weights.1.w_ref, f32[8,16,64,128]{3,2,1,0:T(8,128)} %get-tuple-element.156.refs_0_.refs_2_, ...), custom_call_target="tpu_custom_call", output_to_operand_aliasing={{0}: (8, {})} | custom-call | bytes 1024 | tf_op jit(solution)/shard_map/drift_chunk/pallas_call | solution.py:195
  377.0 8.3 %collective-permute-done.34.refs_1_ = f32[8,3,64,128]{3,2,1,0:T(8,128)} collective-permute-done((f32[8,3,64,128]{3,2,1,0:T(8,128)}, f32[8,3,64,128]{3,2,1,0:T(8,128)}, u32[]{:S(2)}, u32[]{:S(2)}) %collective-permute-start.34) | collective-permute-done | bytes 786464 | tf_op jit(solution)/shard_map/ppermute | solution.py:563
  385.3 3.8 pack_tiles.19
  389.1 6.4 %collective-permute-done.38.refs_4_ = f32[6,3,64,128]{3,2,1,0:T(8,128)} collective-permute-done((f32[6,3,64,128]{3,2,1,0:T(8,128)}, f32[6,3,64,128]{3,2,1,0:T(8,128)}, u32[]{:S(2)}, u32[]{:S(2)}) %collective-permute-start.38) | collective-permute-done | bytes 589856 | tf_op jit(solution)/shard_map/ppermute | solution.py:128
  397.4 7.0 %drift_chunk.18 = (f32[16,64,2048]{2,1,0:T(8,128)}, f32[8,128]{1,0:T(8,128)}) custom-call(s32[1,4,16]{2,1,0:T(4,128)} %sec_ref.39, s32[1,4,16]{2,1,0:T(4,128)} %til_ref.39, bf16[16,256,256]{2,1,0:T(8,128)(2,1)} %split_weights.1.w_ref, f32[8,16,64,128]{3,2,1,0:T(8,128)} %get-tuple-element.156.refs_0_.refs_2_, ...), custom_call_target="tpu_custom_call", output_to_operand_aliasing={{0}: (8, {})} | custom-call | bytes 1024 | tf_op jit(solution)/shard_map/drift_chunk/pallas_call | solution.py:195
  404.4 6.8 %collective-permute-done.39.refs_3_ = f32[6,3,64,128]{3,2,1,0:T(8,128)} collective-permute-done((f32[6,3,64,128]{3,2,1,0:T(8,128)}, f32[6,3,64,128]{3,2,1,0:T(8,128)}, u32[]{:S(2)}, u32[]{:S(2)}) %collective-permute-start.39) | collective-permute-done | bytes 589856 | tf_op jit(solution)/shard_map/ppermute | solution.py:128
  411.2 12.6 %collective-permute-done.40.refs_4_ = f32[6,3,64,128]{3,2,1,0:T(8,128)} collective-permute-done((f32[6,3,64,128]{3,2,1,0:T(8,128)}, f32[6,3,64,128]{3,2,1,0:T(8,128)}, u32[]{:S(2)}, u32[]{:S(2)}) %collective-permute-start.40) | collective-permute-done | bytes 589856 | tf_op jit(solution)/shard_map/ppermute | solution.py:128
  423.8 7.0 %drift_chunk.19 = (f32[16,64,2048]{2,1,0:T(8,128)}, f32[8,128]{1,0:T(8,128)}) custom-call(s32[1,4,16]{2,1,0:T(4,128)} %sec_ref.39, s32[1,4,16]{2,1,0:T(4,128)} %til_ref.39, bf16[16,256,256]{2,1,0:T(8,128)(2,1)} %split_weights.1.w_ref, f32[8,16,64,128]{3,2,1,0:T(8,128)} %get-tuple-element.156.refs_0_.refs_2_, ...), custom_call_target="tpu_custom_call", output_to_operand_aliasing={{0}: (8, {})} | custom-call | bytes 1024 | tf_op jit(solution)/shard_map/drift_chunk/pallas_call | solution.py:195
  (54 shorter events, 16.6 us)
Async XLA Ops:
  5.2 44.0 %collective-permute-start = (f32[6,16,64,128]{3,2,1,0:T(8,128)}, f32[6,16,64,128]{3,2,1,0:T(8,128)}, u32[]{:S(2)}, u32[]{:S(2)}) collective-permute-start(f32[6,16,64,128]{3,2,1,0:T(8,128)} %get-tuple-element.110), channel_id=1, source_target_pairs={{0,8},{8,0},{16,24},{24,16},{1,9},{9,1},{17,25},{25,17},{2,10},{10... | collective-permute-start | bytes 9437192 | tf_op jit(solution)/shard_map/ppermute | solution.py:128
  5.4 20.2 %collective-permute-start.2 = (f32[6,4,64,128]{3,2,1,0:T(8,128)}, f32[6,4,64,128]{3,2,1,0:T(8,128)}, u32[]{:S(2)}, u32[]{:S(2)}) collective-permute-start(f32[6,4,64,128]{3,2,1,0:T(8,128)} %get-tuple-element.114), channel_id=1, source_target_pairs={{0,24},{8,16},{16,8},{24,0},{1,25},{9,17},{17,9},{25,1},{2,26},{10... | collective-permute-start | bytes 2359304 | tf_op jit(solution)/shard_map/ppermute | solution.py:128
  6.2 35.9 %collective-permute-start.1 = (f32[6,4,64,128]{3,2,1,0:T(8,128)}, f32[6,4,64,128]{3,2,1,0:T(8,128)}, u32[]{:S(2)}, u32[]{:S(2)}) collective-permute-start(f32[6,4,64,128]{3,2,1,0:T(8,128)} %get-tuple-element.111.refs_1_), channel_id=1, source_target_pairs={{0,16},{8,24},{16,0},{24,8},{1,17},{9,25},{17,1},{25,9},{2,18},{10... | collective-permute-start | bytes 2359304 | tf_op jit(solution)/shard_map/ppermute | solution.py:128
  42.2 22.7 %collective-permute-start.3 = (f32[6,4,64,128]{3,2,1,0:T(8,128)}, f32[6,4,64,128]{3,2,1,0:T(8,128)}, u32[]{:S(2)}, u32[]{:S(2)}) collective-permute-start(f32[6,4,64,128]{3,2,1,0:T(8,128)} %get-tuple-element.120), channel_id=1, source_target_pairs={{0,16},{8,24},{16,0},{24,8},{1,17},{9,25},{17,1},{25,9},{2,18},{10... | collective-permute-start | bytes 2359304 | tf_op jit(solution)/shard_map/ppermute | solution.py:128
  42.4 36.5 %collective-permute-start.4 = (f32[6,4,64,128]{3,2,1,0:T(8,128)}, f32[6,4,64,128]{3,2,1,0:T(8,128)}, u32[]{:S(2)}, u32[]{:S(2)}) collective-permute-start(f32[6,4,64,128]{3,2,1,0:T(8,128)} %get-tuple-element.121), channel_id=1, source_target_pairs={{0,24},{8,16},{16,8},{24,0},{1,25},{9,17},{17,9},{25,1},{2,26},{10... | collective-permute-start | bytes 2359304 | tf_op jit(solution)/shard_map/ppermute | solution.py:128
  56.4 58.6 %collective-permute-start.7 = (f32[8,4,64,128]{3,2,1,0:T(8,128)}, f32[8,4,64,128]{3,2,1,0:T(8,128)}, u32[]{:S(2)}, u32[]{:S(2)}) collective-permute-start(f32[8,4,64,128]{3,2,1,0:T(8,128)} %get-tuple-element.138), channel_id=1, source_target_pairs={{0,1},{1,0},{2,3},{3,2},{4,5},{5,4},{6,7},{7,6},{8,9},{9,8},{10,11... | collective-permute-start | bytes 3145736 | tf_op jit(solution)/shard_map/ppermute | solution.py:513
  57.3 57.7 %collective-permute-start.8 = (f32[8,4,64,128]{3,2,1,0:T(8,128)}, f32[8,4,64,128]{3,2,1,0:T(8,128)}, u32[]{:S(2)}, u32[]{:S(2)}) collective-permute-start(f32[8,4,64,128]{3,2,1,0:T(8,128)} %get-tuple-element.127.refs_0_), channel_id=1, source_target_pairs={{1,3},{2,0},{3,5},{4,2},{5,7},{6,4},{9,11},{10,8},{11,13},{12,10},... | collective-permute-start | bytes 3145736 | tf_op jit(solution)/shard_map/ppermute | solution.py:516
  78.9 19.9 %collective-permute-start.5 = (f32[6,4,64,128]{3,2,1,0:T(8,128)}, f32[6,4,64,128]{3,2,1,0:T(8,128)}, u32[]{:S(2)}, u32[]{:S(2)}) collective-permute-start(f32[6,4,64,128]{3,2,1,0:T(8,128)} %get-tuple-element.134), channel_id=1, source_target_pairs={{0,16},{8,24},{16,0},{24,8},{1,17},{9,25},{17,1},{25,9},{2,18},{10... | collective-permute-start | bytes 2359304 | tf_op jit(solution)/shard_map/ppermute | solution.py:128
  79.1 35.9 %collective-permute-start.6 = (f32[6,4,64,128]{3,2,1,0:T(8,128)}, f32[6,4,64,128]{3,2,1,0:T(8,128)}, u32[]{:S(2)}, u32[]{:S(2)}) collective-permute-start(f32[6,4,64,128]{3,2,1,0:T(8,128)} %get-tuple-element.135), channel_id=1, source_target_pairs={{0,24},{8,16},{16,8},{24,0},{1,25},{9,17},{17,9},{25,1},{2,26},{10... | collective-permute-start | bytes 2359304 | tf_op jit(solution)/shard_map/ppermute | solution.py:128
  93.0 34.5 %collective-permute-start.14 = (f32[8,4,64,128]{3,2,1,0:T(8,128)}, f32[8,4,64,128]{3,2,1,0:T(8,128)}, u32[]{:S(2)}, u32[]{:S(2)}) collective-permute-start(f32[8,4,64,128]{3,2,1,0:T(8,128)} %get-tuple-element.151), channel_id=1, source_target_pairs={{0,1},{1,0},{2,3},{3,2},{4,5},{5,4},{6,7},{7,6},{8,9},{9,8},{10,11... | collective-permute-start | bytes 3145736 | tf_op jit(solution)/shard_map/ppermute | solution.py:513
  122.2 39.0 %collective-permute-start.16 = (f32[8,4,64,128]{3,2,1,0:T(8,128)}, f32[8,4,64,128]{3,2,1,0:T(8,128)}, u32[]{:S(2)}, u32[]{:S(2)}) collective-permute-start(f32[8,4,64,128]{3,2,1,0:T(8,128)} %get-tuple-element.153), channel_id=1, source_target_pairs={{0,1},{1,0},{2,3},{3,2},{4,5},{5,4},{6,7},{7,6},{8,9},{9,8},{10,11... | collective-permute-start | bytes 3145736 | tf_op jit(solution)/shard_map/ppermute | solution.py:513
  124.0 38.5 %collective-permute-start.11 = (f32[8,4,64,128]{3,2,1,0:T(8,128)}, f32[8,4,64,128]{3,2,1,0:T(8,128)}, u32[]{:S(2)}, u32[]{:S(2)}) collective-permute-start(f32[8,4,64,128]{3,2,1,0:T(8,128)} %collective-permute-done.7.refs_5_), channel_id=1, source_target_pairs={{0,2},{2,4},{3,1},{4,6},{5,3},{7,5},{8,10},{10,12},{11,9},{12,14},... | collective-permute-start | bytes 3145736 | tf_op jit(solution)/shard_map/ppermute | solution.py:519
  125.2 10.5 %collective-permute-start.9 = (f32[6,2,64,128]{3,2,1,0:T(8,128)}, f32[6,2,64,128]{3,2,1,0:T(8,128)}, u32[]{:S(2)}, u32[]{:S(2)}) collective-permute-start(f32[6,2,64,128]{3,2,1,0:T(8,128)} %get-tuple-element.143), channel_id=1, source_target_pairs={{0,16},{8,24},{16,0},{24,8},{1,17},{9,25},{17,1},{25,9},{2,18},{10... | collective-permute-start | bytes 1179656 | tf_op jit(solution)/shard_map/ppermute | solution.py:128
  126.2 19.0 %collective-permute-start.10 = (f32[6,2,64,128]{3,2,1,0:T(8,128)}, f32[6,2,64,128]{3,2,1,0:T(8,128)}, u32[]{:S(2)}, u32[]{:S(2)}) collective-permute-start(f32[6,2,64,128]{3,2,1,0:T(8,128)} %get-tuple-element.144), channel_id=1, source_target_pairs={{0,24},{8,16},{16,8},{24,0},{1,25},{9,17},{17,9},{25,1},{2,26},{10... | collective-permute-start | bytes 1179656 | tf_op jit(solution)/shard_map/ppermute | solution.py:128
  127.5 48.2 %collective-permute-start.15 = (f32[8,4,64,128]{3,2,1,0:T(8,128)}, f32[8,4,64,128]{3,2,1,0:T(8,128)}, u32[]{:S(2)}, u32[]{:S(2)}) collective-permute-start(f32[8,4,64,128]{3,2,1,0:T(8,128)} %collective-permute-done.14.refs_6_), channel_id=1, source_target_pairs={{0,2},{2,4},{3,1},{4,6},{5,3},{7,5},{8,10},{10,12},{11,9},{12,14},... | collective-permute-start | bytes 3145736 | tf_op jit(solution)/shard_map/ppermute | solution.py:519
  145.2 11.3 %collective-permute-start.12 = (f32[6,2,64,128]{3,2,1,0:T(8,128)}, f32[6,2,64,128]{3,2,1,0:T(8,128)}, u32[]{:S(2)}, u32[]{:S(2)}) collective-permute-start(f32[6,2,64,128]{3,2,1,0:T(8,128)} %get-tuple-element.148), channel_id=1, source_target_pairs={{0,16},{8,24},{16,0},{24,8},{1,17},{9,25},{17,1},{25,9},{2,18},{10... | collective-permute-start | bytes 1179656 | tf_op jit(solution)/shard_map/ppermute | solution.py:128
  146.1 36.3 %collective-permute-start.19 = (f32[8,4,64,128]{3,2,1,0:T(8,128)}, f32[8,4,64,128]{3,2,1,0:T(8,128)}, u32[]{:S(2)}, u32[]{:S(2)}) collective-permute-start(f32[8,4,64,128]{3,2,1,0:T(8,128)} %get-tuple-element.130.refs_1_), channel_id=1, source_target_pairs={{1,3},{2,0},{3,5},{4,2},{5,7},{6,4},{9,11},{10,8},{11,13},{12,10},... | collective-permute-start | bytes 3145736 | tf_op jit(solution)/shard_map/ppermute | solution.py:516
  156.5 38.8 %collective-permute-start.20 = (f32[8,4,64,128]{3,2,1,0:T(8,128)}, f32[8,4,64,128]{3,2,1,0:T(8,128)}, u32[]{:S(2)}, u32[]{:S(2)}) collective-permute-start(f32[8,4,64,128]{3,2,1,0:T(8,128)} %get-tuple-element.139.refs_2_), channel_id=1, source_target_pairs={{1,3},{2,0},{3,5},{4,2},{5,7},{6,4},{9,11},{10,8},{11,13},{12,10},... | collective-permute-start | bytes 3145736 | tf_op jit(solution)/shard_map/ppermute | solution.py:516
  161.2 38.1 %collective-permute-start.21 = (f32[8,4,64,128]{3,2,1,0:T(8,128)}, f32[8,4,64,128]{3,2,1,0:T(8,128)}, u32[]{:S(2)}, u32[]{:S(2)}) collective-permute-start(f32[8,4,64,128]{3,2,1,0:T(8,128)} %collective-permute-done.16.refs_7_), channel_id=1, source_target_pairs={{0,2},{2,4},{3,1},{4,6},{5,3},{7,5},{8,10},{10,12},{11,9},{12,14},... | collective-permute-start | bytes 3145736 | tf_op jit(solution)/shard_map/ppermute | solution.py:519
  162.5 11.7 %collective-permute-start.13 = (f32[6,2,64,128]{3,2,1,0:T(8,128)}, f32[6,2,64,128]{3,2,1,0:T(8,128)}, u32[]{:S(2)}, u32[]{:S(2)}) collective-permute-start(f32[6,2,64,128]{3,2,1,0:T(8,128)} %get-tuple-element.149), channel_id=1, source_target_pairs={{0,24},{8,16},{16,8},{24,0},{1,25},{9,17},{17,9},{25,1},{2,26},{10... | collective-permute-start | bytes 1179656 | tf_op jit(solution)/shard_map/ppermute | solution.py:128
  174.2 21.2 %collective-permute-start.17 = (f32[8,2,64,128]{3,2,1,0:T(8,128)}, f32[8,2,64,128]{3,2,1,0:T(8,128)}, u32[]{:S(2)}, u32[]{:S(2)}) collective-permute-start(f32[8,2,64,128]{3,2,1,0:T(8,128)} %get-tuple-element.154), channel_id=1, source_target_pairs={{0,1},{1,0},{2,3},{3,2},{4,5},{5,4},{6,7},{7,6},{8,9},{9,8},{10,11... | collective-permute-start | bytes 1572872 | tf_op jit(solution)/shard_map/ppermute | solution.py:513
  182.3 16.9 %collective-permute-start.18 = (f32[8,2,64,128]{3,2,1,0:T(8,128)}, f32[8,2,64,128]{3,2,1,0:T(8,128)}, u32[]{:S(2)}, u32[]{:S(2)}) collective-permute-start(f32[8,2,64,128]{3,2,1,0:T(8,128)} %get-tuple-element.155), channel_id=1, source_target_pairs={{0,1},{1,0},{2,3},{3,2},{4,5},{5,4},{6,7},{7,6},{8,9},{9,8},{10,11... | collective-permute-start | bytes 1572872 | tf_op jit(solution)/shard_map/ppermute | solution.py:513
  251.6 13.0 %collective-permute-start.22 = (f32[8,2,64,128]{3,2,1,0:T(8,128)}, f32[8,2,64,128]{3,2,1,0:T(8,128)}, u32[]{:S(2)}, u32[]{:S(2)}) collective-permute-start(f32[8,2,64,128]{3,2,1,0:T(8,128)} %get-tuple-element.161), channel_id=1, source_target_pairs={{0,1},{1,0},{2,3},{3,2},{4,5},{5,4},{6,7},{7,6},{8,9},{9,8},{10,11... | collective-permute-start | bytes 1572872 | tf_op jit(solution)/shard_map/ppermute | solution.py:549
  264.6 23.2 %collective-permute-start.23 = (f32[8,4,64,128]{3,2,1,0:T(8,128)}, f32[8,4,64,128]{3,2,1,0:T(8,128)}, u32[]{:S(2)}, u32[]{:S(2)}) collective-permute-start(f32[8,4,64,128]{3,2,1,0:T(8,128)} %get-tuple-element.162), channel_id=1, source_target_pairs={{0,1},{1,0},{2,3},{3,2},{4,5},{5,4},{6,7},{7,6},{8,9},{9,8},{10,11... | collective-permute-start | bytes 3145736 | tf_op jit(solution)/shard_map/ppermute | solution.py:551
  269.5 22.3 %collective-permute-start.24 = (f32[6,2,64,128]{3,2,1,0:T(8,128)}, f32[6,2,64,128]{3,2,1,0:T(8,128)}, u32[]{:S(2)}, u32[]{:S(2)}) collective-permute-start(f32[6,2,64,128]{3,2,1,0:T(8,128)} %get-tuple-element.166), channel_id=1, source_target_pairs={{0,16},{8,24},{16,0},{24,8},{1,17},{9,25},{17,1},{25,9},{2,18},{10... | collective-permute-start | bytes 1179656 | tf_op jit(solution)/shard_map/ppermute | solution.py:128
  270.2 21.6 %collective-permute-start.25 = (f32[6,2,64,128]{3,2,1,0:T(8,128)}, f32[6,2,64,128]{3,2,1,0:T(8,128)}, u32[]{:S(2)}, u32[]{:S(2)}) collective-permute-start(f32[6,2,64,128]{3,2,1,0:T(8,128)} %get-tuple-element.167), channel_id=1, source_target_pairs={{0,24},{8,16},{16,8},{24,0},{1,25},{9,17},{17,9},{25,1},{2,26},{10... | collective-permute-start | bytes 1179656 | tf_op jit(solution)/shard_map/ppermute | solution.py:128
  291.8 22.6 %collective-permute-start.26 = (f32[8,4,64,128]{3,2,1,0:T(8,128)}, f32[8,4,64,128]{3,2,1,0:T(8,128)}, u32[]{:S(2)}, u32[]{:S(2)}) collective-permute-start(f32[8,4,64,128]{3,2,1,0:T(8,128)} %get-tuple-element.170), channel_id=1, source_target_pairs={{0,1},{1,0},{2,3},{3,2},{4,5},{5,4},{6,7},{7,6},{8,9},{9,8},{10,11... | collective-permute-start | bytes 3145736 | tf_op jit(solution)/shard_map/ppermute | solution.py:563
  292.9 25.4 %collective-permute-start.28 = (f32[6,4,64,128]{3,2,1,0:T(8,128)}, f32[6,4,64,128]{3,2,1,0:T(8,128)}, u32[]{:S(2)}, u32[]{:S(2)}) collective-permute-start(f32[6,4,64,128]{3,2,1,0:T(8,128)} %get-tuple-element.177), channel_id=1, source_target_pairs={{0,16},{8,24},{16,0},{24,8},{1,17},{9,25},{17,1},{25,9},{2,18},{10... | collective-permute-start | bytes 2359304 | tf_op jit(solution)/shard_map/ppermute | solution.py:128
  293.6 35.7 %collective-permute-start.29 = (f32[6,4,64,128]{3,2,1,0:T(8,128)}, f32[6,4,64,128]{3,2,1,0:T(8,128)}, u32[]{:S(2)}, u32[]{:S(2)}) collective-permute-start(f32[6,4,64,128]{3,2,1,0:T(8,128)} %get-tuple-element.178), channel_id=1, source_target_pairs={{0,24},{8,16},{16,8},{24,0},{1,25},{9,17},{17,9},{25,1},{2,26},{10... | collective-permute-start | bytes 2359304 | tf_op jit(solution)/shard_map/ppermute | solution.py:128
  297.5 2.1 collective-permute-start.27
  297.6 34.1 %collective-permute-start.31 = (f32[6,4,64,128]{3,2,1,0:T(8,128)}, f32[6,4,64,128]{3,2,1,0:T(8,128)}, u32[]{:S(2)}, u32[]{:S(2)}) collective-permute-start(f32[6,4,64,128]{3,2,1,0:T(8,128)} %get-tuple-element.183), channel_id=1, source_target_pairs={{0,8},{8,0},{16,24},{24,16},{1,9},{9,1},{17,25},{25,17},{2,10},{10... | collective-permute-start | bytes 2359304 | tf_op jit(solution)/shard_map/ppermute | solution.py:128
  329.3 19.6 %collective-permute-start.30 = (f32[8,3,64,128]{3,2,1,0:T(8,128)}, f32[8,3,64,128]{3,2,1,0:T(8,128)}, u32[]{:S(2)}, u32[]{:S(2)}) collective-permute-start(f32[8,3,64,128]{3,2,1,0:T(8,128)} %get-tuple-element.181), channel_id=1, source_target_pairs={{0,1},{1,0},{2,3},{3,2},{4,5},{5,4},{6,7},{7,6},{8,9},{9,8},{10,11... | collective-permute-start | bytes 2359304 | tf_op jit(solution)/shard_map/ppermute | solution.py:563
  329.8 22.9 %collective-permute-start.32 = (f32[6,4,64,128]{3,2,1,0:T(8,128)}, f32[6,4,64,128]{3,2,1,0:T(8,128)}, u32[]{:S(2)}, u32[]{:S(2)}) collective-permute-start(f32[6,4,64,128]{3,2,1,0:T(8,128)} %get-tuple-element.190), channel_id=1, source_target_pairs={{0,16},{8,24},{16,0},{24,8},{1,17},{9,25},{17,1},{25,9},{2,18},{10... | collective-permute-start | bytes 2359304 | tf_op jit(solution)/shard_map/ppermute | solution.py:128
  330.8 35.5 %collective-permute-start.33 = (f32[6,4,64,128]{3,2,1,0:T(8,128)}, f32[6,4,64,128]{3,2,1,0:T(8,128)}, u32[]{:S(2)}, u32[]{:S(2)}) collective-permute-start(f32[6,4,64,128]{3,2,1,0:T(8,128)} %get-tuple-element.191), channel_id=1, source_target_pairs={{0,24},{8,16},{16,8},{24,0},{1,25},{9,17},{17,9},{25,1},{2,26},{10... | collective-permute-start | bytes 2359304 | tf_op jit(solution)/shard_map/ppermute | solution.py:128
  331.2 38.6 %collective-permute-start.35 = (f32[6,4,64,128]{3,2,1,0:T(8,128)}, f32[6,4,64,128]{3,2,1,0:T(8,128)}, u32[]{:S(2)}, u32[]{:S(2)}) collective-permute-start(f32[6,4,64,128]{3,2,1,0:T(8,128)} %get-tuple-element.196), channel_id=1, source_target_pairs={{0,8},{8,0},{16,24},{24,16},{1,9},{9,1},{17,25},{25,17},{2,10},{10... | collective-permute-start | bytes 2359304 | tf_op jit(solution)/shard_map/ppermute | solution.py:128
  366.3 19.0 %collective-permute-start.34 = (f32[8,3,64,128]{3,2,1,0:T(8,128)}, f32[8,3,64,128]{3,2,1,0:T(8,128)}, u32[]{:S(2)}, u32[]{:S(2)}) collective-permute-start(f32[8,3,64,128]{3,2,1,0:T(8,128)} %get-tuple-element.194), channel_id=1, source_target_pairs={{0,1},{1,0},{2,3},{3,2},{4,5},{5,4},{6,7},{7,6},{8,9},{9,8},{10,11... | collective-permute-start | bytes 2359304 | tf_op jit(solution)/shard_map/ppermute | solution.py:563
  367.5 21.6 %collective-permute-start.37 = (f32[6,3,64,128]{3,2,1,0:T(8,128)}, f32[6,3,64,128]{3,2,1,0:T(8,128)}, u32[]{:S(2)}, u32[]{:S(2)}) collective-permute-start(f32[6,3,64,128]{3,2,1,0:T(8,128)} %get-tuple-element.204), channel_id=1, source_target_pairs={{0,16},{8,24},{16,0},{24,8},{1,17},{9,25},{17,1},{25,9},{2,18},{10... | collective-permute-start | bytes 1769480 | tf_op jit(solution)/shard_map/ppermute | solution.py:128
  368.1 27.4 %collective-permute-start.38 = (f32[6,3,64,128]{3,2,1,0:T(8,128)}, f32[6,3,64,128]{3,2,1,0:T(8,128)}, u32[]{:S(2)}, u32[]{:S(2)}) collective-permute-start(f32[6,3,64,128]{3,2,1,0:T(8,128)} %get-tuple-element.205), channel_id=1, source_target_pairs={{0,24},{8,16},{16,8},{24,0},{1,25},{9,17},{17,9},{25,1},{2,26},{10... | collective-permute-start | bytes 1769480 | tf_op jit(solution)/shard_map/ppermute | solution.py:128
  369.8 27.6 %collective-permute-start.41 = (f32[6,3,64,128]{3,2,1,0:T(8,128)}, f32[6,3,64,128]{3,2,1,0:T(8,128)}, u32[]{:S(2)}, u32[]{:S(2)}) collective-permute-start(f32[6,3,64,128]{3,2,1,0:T(8,128)} %get-tuple-element.209), channel_id=1, source_target_pairs={{0,8},{8,0},{16,24},{24,16},{1,9},{9,1},{17,25},{25,17},{2,10},{10... | collective-permute-start | bytes 1769480 | tf_op jit(solution)/shard_map/ppermute | solution.py:128
  395.5 15.7 %collective-permute-start.39 = (f32[6,3,64,128]{3,2,1,0:T(8,128)}, f32[6,3,64,128]{3,2,1,0:T(8,128)}, u32[]{:S(2)}, u32[]{:S(2)}) collective-permute-start(f32[6,3,64,128]{3,2,1,0:T(8,128)} %get-tuple-element.206), channel_id=1, source_target_pairs={{0,16},{8,24},{16,0},{24,8},{1,17},{9,25},{17,1},{25,9},{2,18},{10... | collective-permute-start | bytes 1769480 | tf_op jit(solution)/shard_map/ppermute | solution.py:128
  396.1 27.7 %collective-permute-start.40 = (f32[6,3,64,128]{3,2,1,0:T(8,128)}, f32[6,3,64,128]{3,2,1,0:T(8,128)}, u32[]{:S(2)}, u32[]{:S(2)}) collective-permute-start(f32[6,3,64,128]{3,2,1,0:T(8,128)} %get-tuple-element.207), channel_id=1, source_target_pairs={{0,24},{8,16},{16,8},{24,0},{1,25},{9,17},{17,9},{25,1},{2,26},{10... | collective-permute-start | bytes 1769480 | tf_op jit(solution)/shard_map/ppermute | solution.py:128
  396.7 27.1 %collective-permute-start.36 = (f32[6,3,64,128]{3,2,1,0:T(8,128)}, f32[6,3,64,128]{3,2,1,0:T(8,128)}, u32[]{:S(2)}, u32[]{:S(2)}) collective-permute-start(f32[6,3,64,128]{3,2,1,0:T(8,128)} %get-tuple-element.201), channel_id=1, source_target_pairs={{0,8},{8,0},{16,24},{24,16},{1,9},{9,1},{17,25},{25,17},{2,10},{10... | collective-permute-start | bytes 1769480 | tf_op jit(solution)/shard_map/ppermute | solution.py:128

commit v4 on v3

--- a/solution.py
+++ b/solution.py
@@ -64,18 +64,16 @@
     )(matrix_id, cubic_weights)
 
 
-def pack_kernel(offsets, finds, n_arrays, sec_ref, til_ref, *refs):
-    tiles, n = sec_ref.shape[2], len(offsets)
-    sends, rooms = refs[-2 * n - 2 : -n - 2], refs[-n - 2 : -2]
-    in_sems, out_sems = refs[-2:]
+def pack_kernel(find, n_arrays, sec_ref, til_ref, *refs):
+    sectors, tiles = sec_ref.shape[1], sec_ref.shape[2]
+    send, room, in_sems, out_sems = refs[-4:]
+    pieces = find(*refs[:n_arrays])
     me = lax.axis_index("sector")
     counts = []
-    for i, d in enumerate(offsets):
-        dest = me ^ d
-        pieces = finds[i](*refs[:n_arrays])
-
-        def body(t, count, i=i, dest=dest, pieces=pieces):
-            hit = sec_ref[0, dest, t] == me
+    for dest in range(sectors):
+
+        def body(t, count, dest=dest):
+            hit = jnp.logical_and(sec_ref[0, dest, t] == me, me != dest)
 
             @pl.when(hit)
             def _():
@@ -83,38 +81,40 @@
 
                     @pl.when(guard)
                     def _():
-                        pltpu.make_async_copy(piece(), rooms[i].at[count], in_sems.at[i, count]).start()
+                        pltpu.make_async_copy(
+                            piece(), room.at[dest, count], in_sems.at[dest, count]
+                        ).start()
 
             return count + hit.astype(jnp.int32)
 
         counts.append(lax.fori_loop(0, tiles, body, jnp.int32(0)))
-    for i in range(n):
-
-        @pl.loop(0, counts[i])
-        def _(slot, i=i):
-            here = rooms[i].at[slot]
-            pltpu.make_async_copy(here, here, in_sems.at[i, slot]).wait()
-            pltpu.make_async_copy(here, sends[i].at[slot], out_sems.at[i, slot]).start()
-
-    for i in range(n):
-
-        @pl.loop(0, counts[i])
-        def _(slot, i=i):
-            pltpu.make_async_copy(rooms[i].at[slot], sends[i].at[slot], out_sems.at[i, slot]).wait()
-
-
-def pack(groups, cap, tables, arrays, after=()):
-    n = len(groups)
-    offsets, finds, shapes = zip(*groups)
+    for dest in range(sectors):
+
+        @pl.loop(0, counts[dest])
+        def _(slot, dest=dest):
+            here, there = room.at[dest, slot], send.at[dest, slot]
+            pltpu.make_async_copy(here, here, in_sems.at[dest, slot]).wait()
+            pltpu.make_async_copy(here, there, out_sems.at[dest, slot]).start()
+
+    for dest in range(sectors):
+
+        @pl.loop(0, counts[dest])
+        def _(slot, dest=dest):
+            here, there = room.at[dest, slot], send.at[dest, slot]
+            pltpu.make_async_copy(here, there, out_sems.at[dest, slot]).wait()
+
+
+def pack(find, cap, tables, arrays, piece, after=()):
+    sectors = tables[0].shape[1]
     return pl.pallas_call(
-        functools.partial(pack_kernel, offsets, finds, len(arrays)),
-        out_shape=[jax.ShapeDtypeStruct((cap,) + shape, F32) for shape in shapes],
+        functools.partial(pack_kernel, find, len(arrays)),
+        out_shape=jax.ShapeDtypeStruct((sectors, cap) + piece, F32),
         in_specs=[SMEM, SMEM] + [ANY] * (len(arrays) + len(after)),
-        out_specs=[ANY] * n,
+        out_specs=ANY,
         scratch_shapes=[
-            *[pltpu.VMEM((cap,) + shape, F32) for shape in shapes],
-            pltpu.SemaphoreType.DMA((n, cap)),
-            pltpu.SemaphoreType.DMA((n, cap)),
+            pltpu.VMEM((sectors, cap) + piece, F32),
+            pltpu.SemaphoreType.DMA((sectors, cap)),
+            pltpu.SemaphoreType.DMA((sectors, cap)),
         ],
         compiler_params=params(),
         cost_estimate=cost(),
@@ -122,12 +122,8 @@
     )(*tables, *arrays, *after)
 
 
-def sector_exchange(sends, offsets):
-    sectors = lax.axis_size("sector")
-    return [
-        lax.ppermute(send, "sector", [(s, s ^ d) for s in range(sectors)])
-        for d, send in zip(offsets, sends)
-    ]
+def sector_exchange(send):
+    return lax.all_to_all(send, "sector", split_axis=0, concat_axis=0, tiled=True)
 
 
 def in_turn(later, earlier):
@@ -135,10 +131,10 @@
     return list(both[: len(later)]), list(both[len(later) :])
 
 
-def drift_kernel(find, place, receive, n_local, n_extra, sec_ref, til_ref, w_ref, *refs):
+def drift_kernel(find, place, n_local, n_extra, sec_ref, til_ref, w_ref, *refs):
     sectors, tiles = sec_ref.shape[1], sec_ref.shape[2]
-    local, recvs = refs[:n_local], refs[n_local : n_local + sectors - 1]
-    outs = refs[n_local + sectors - 1 + n_extra : -5]
+    local, came = refs[:n_local], refs[n_local]
+    outs = refs[n_local + 1 + n_extra : -5]
     token, taken, made, in_sems, out_sems = refs[-5:]
     pieces = find(*local)
     put = place(*outs)
@@ -147,9 +143,9 @@
     token[...] = jnp.zeros(token.shape, F32)
 
     def fetch(t, counts):
-        d = sec_ref[0, me, t] ^ me
-
-        @pl.when(d == 0)
+        source = sec_ref[0, me, t]
+
+        @pl.when(source == me)
         def _():
             for guard, piece in pieces(til_ref[0, me, t]):
 
@@ -157,16 +153,17 @@
                 def _():
                     pltpu.make_async_copy(piece(), taken.at[t], in_sems.at[t]).start()
 
-        for other in range(1, sectors):
-
-            @pl.when(d == other)
-            def _(other=other):
-                came = receive(recvs[other - 1], other, counts[other - 1])
-                pltpu.make_async_copy(came, taken.at[t], in_sems.at[t]).start()
-
-        return tuple(c + (d == i + 1).astype(jnp.int32) for i, c in enumerate(counts))
-
-    lax.fori_loop(0, tiles, fetch, (jnp.int32(0),) * (sectors - 1))
+        slot = jnp.int32(0)
+        for s in range(sectors):
+            slot = jnp.where(source == s, counts[s], slot)
+
+        @pl.when(source != me)
+        def _():
+            pltpu.make_async_copy(came.at[source, slot], taken.at[t], in_sems.at[t]).start()
+
+        return tuple(c + (source == s).astype(jnp.int32) for s, c in enumerate(counts))
+
+    lax.fori_loop(0, tiles, fetch, (jnp.int32(0),) * sectors)
 
     @pl.loop(0, tiles)
     def _(t):
@@ -187,13 +184,13 @@
         pltpu.make_async_copy(made.at[t], made.at[t], out_sems.at[t]).wait()
 
 
-def drift(find, place, receive, tables, weights, local, recvs, outs, piece, after=(), carried=()):
-    sectors, tiles = tables[0].shape[1], tables[0].shape[2]
+def drift(find, place, tables, weights, local, came, outs, piece, after=(), carried=()):
+    tiles = tables[0].shape[2]
     n_local = len(local)
-    ins = [*tables, weights, *local, *recvs, *after, *carried]
+    ins = [*tables, weights, *local, came, *after, *carried]
     n_extra = len(after) + len(carried)
     return pl.pallas_call(
-        functools.partial(drift_kernel, find, place, receive, n_local, n_extra),
+        functools.partial(drift_kernel, find, place, n_local, n_extra),
         out_shape=[*outs, jax.ShapeDtypeStruct((8, 128), F32)],
         in_specs=[SMEM, SMEM, VMEM] + [ANY] * (len(ins) - 3),
         out_specs=[ANY] * len(outs) + [VMEM],
@@ -420,7 +417,6 @@
     last_steps = (quarter // 2, quarter, quarter, quarter - quarter // 4, block - 3 * quarter - quarter // 2 + quarter // 4)
     cap = slots(tiles, sectors)
     tables = (source_sector, source_tile)
-    near, far = [1], list(range(2, sectors))
 
     weights = split_weights(matrix_id, cubic_weights)
 
@@ -464,12 +460,6 @@
             first = first_of()
             return lambda t: [(t >= 0, lambda: field.at[pl.ds(first, step), :, at_lanes(t)])]
 
-        def find_all(field):
-            return lambda t: [(t >= 0, lambda: field.at[:, :, at_lanes(t)])]
-
-        def receive(came, other, slot, first_of=first_of, step=step):
-            return came.at[slot, pl.ds(first_of(), step)] if other == 1 else came.at[slot]
-
         def place(kept, sent):
             here = side_here()
             mine = lambda t: (t // half) == here
@@ -478,37 +468,33 @@
                 (jnp.logical_not(mine(t)), lambda: sent.at[t % half]),
             ]
 
-        packed.append((start, step, find, receive, place))
+        packed.append((start, step, find, place))
         start += step
 
     def pack_first(k, after):
-        start, step, find, _, _ = packed[k]
-        groups = [(d, find, (step, pitches, side)) for d in far]
-        if k == 0:
-            groups += [(d, find_all, (block, pitches, side)) for d in near]
-        return pack(groups, cap, tables, [density], after)
-
-    sends = pack_first(0, ())
-    recvs = sector_exchange(sends[:-1], far)
-    beside = sector_exchange(sends[-1:], near)
-    token = sends[0]
+        _, step, find, _ = packed[k]
+        return pack(find, cap, tables, [density], (step, pitches, side), after)
+
+    send = pack_first(0, ())
+    came = sector_exchange(send)
+    token = send
     crossing = []
-    for k, (start, step, find, receive, place) in enumerate(packed):
+    for k, (start, step, find, place) in enumerate(packed):
         if k + 1 < len(packed):
             later = pack_first(k + 1, (token,))
-            later, recvs = in_turn(later, recvs)
-            coming = sector_exchange(later, far)
+            (later,), (came,) = in_turn([later], [came])
+            coming = sector_exchange(later)
         if k == 1:
-            recvs, (rate, a, b) = in_turn(recvs, [rate, a, b])
+            (came,), (rate, a, b) = in_turn([came], [rate, a, b])
         after = ()
         if k > 0:
             after = [token, *(crossing[k - 2] if k == 2 else ()), *got_halo[: k - 2][-1:]]
         part = jax.ShapeDtypeStruct((half, step, pitches, side), F32)
         piece = (step, pitches, side)
         kept, sent, token = drift(
-            find, place, receive, tables, weights, [density], beside + recvs, [part, part], piece, after
+            find, place, tables, weights, [density], came, [part, part], piece, after
         )
-        recvs = coming
+        came = coming
         own.append(kept)
         got.append(lax.ppermute(sent, "inner", swap))
         crossing.append(got[-1:])
@@ -537,34 +523,28 @@
         ready.append((find, place, (step, pitches, side)))
         start += step
 
-    def receive_slot(came, other, slot):
-        return came.at[slot]
-
     def pack_last(k, after):
         find, _, piece = ready[k]
-        sends = pack([(d, find, piece) for d in near + far], cap, tables, [kept, backs[k]], after)
-        return sends[:1], sends[1:]
+        return pack(find, cap, tables, [kept, backs[k]], piece, after)
 
     whole = [jax.ShapeDtypeStruct(density.shape, F32)]
     backs = [lax.ppermute(returns[0], "inner", swap)]
     (last,), (backs[0],) = in_turn([returns[1]], [backs[0]])
     backs.append(lax.ppermute(last, "inner", swap))
-    sends, far_sends = pack_last(0, ())
-    recvs = sector_exchange(far_sends, far)
-    beside = sector_exchange(sends, near)
+    came = sector_exchange(pack_last(0, ()))
     token = kept
     for k, (find, place, piece) in enumerate(ready):
         if k + 1 < len(ready):
-            sends, far_sends = pack_last(k + 1, (token,))
-            far_sends, recvs = in_turn(far_sends, recvs)
-            coming = sector_exchange(far_sends, far), sector_exchange(sends, near)
+            send = pack_last(k + 1, (token,))
+            (send,), (came,) = in_turn([send], [came])
+            coming = sector_exchange(send)
         if k + 2 < len(ready):
-            (last,), (backs[k + 1], *recvs) = in_turn([returns[k + 2]], [backs[k + 1], *recvs])
+            (last,), (backs[k + 1],) = in_turn([returns[k + 2]], [backs[k + 1]])
             backs.append(lax.ppermute(last, "inner", swap))
         *out, token = drift(
-            find, place, receive_slot, tables, weights, [kept, backs[k]], beside + recvs, whole, piece, (), out
+            find, place, tables, weights, [kept, backs[k]], came, whole, piece, (), out
         )
-        recvs, beside = coming
+        came = coming
     return out[0]
 
 

time: 435 us -> 495 us (1.14)
  waiting for transfers between devices: 208 us -> 246 us
  starting transfers between devices: 52.2 us -> 73.7 us
    ppermute x26 -> x0, waiting for transfers between devices: 138 us -> none  [sector_exchange(): lax.ppermute(send, 'sector', [(s, s ^ d) for s in range(sectors)])]
    all_to_all x0 -> x10, waiting for transfers between devices: none -> 120 us  [sector_exchange(): lax.all_to_all(send, 'sector', split_axis=0, concat_axis=0, tiled=True)]
    all_to_all x0 -> x10, starting transfers between devices: none -> 54.6 us  [sector_exchange(): lax.all_to_all(send, 'sector', split_axis=0, concat_axis=0, tiled=True)]
    ppermute x3, waiting for transfers between devices: 0.01 us -> 33.9 us  [paired_shards(): got_halo.append(lax.ppermute(got[k - 1], 'inner', got_pairs))]
    ppermute x4, waiting for transfers between devices: 41.2 us -> 67.3 us  [paired_shards(): backs.append(lax.ppermute(last, 'inner', swap))]
    ppermute x26 -> x0, starting transfers between devices: 23.7 us -> none  [sector_exchange(): lax.ppermute(send, 'sector', [(s, s ^ d) for s in range(sectors)])]
    ppermute x3, waiting for transfers between devices: 12.9 us -> 0.01 us  [paired_shards(): own_halo.append(lax.ppermute(kept, 'inner', own_pairs))]
    ppermute x5, waiting for transfers between devices: 3.95 us -> 11.3 us  [paired_shards(): got.append(lax.ppermute(sent, 'inner', swap))]
  transfers between devices with their start and end apart: 42 -> 26, of which waited for: 22 -> 17; matrix products, arithmetic and copies ran while one was open for 2% -> 1% of each run, Pallas kernels for 23% -> 20%
where the time goes in v4:
time: 495 us; the launch traced here: 491 us
  waiting for transfers between devices  246 us (50%)
  Pallas kernels  167 us (34%)
  starting transfers between devices  73.7 us (15%)
    all_to_all x10, waiting for transfers between devices, sector_exchange(): lax.all_to_all(send, 'sector', split_axis=0, concat_axis=0, tiled=True)  120 us
    pallas_call x10, Pallas kernels, drift(): pl.pallas_call(functools.partial(drift_kernel, find, place, n_local, n_ex...  69.8 us
    ppermute x4, waiting for transfers between devices, paired_shards(): backs.append(lax.ppermute(last, 'inner', swap))  67.3 us
    all_to_all x10, starting transfers between devices, sector_exchange(): lax.all_to_all(send, 'sector', split_axis=0, concat_axis=0, tiled=True)  54.6 us
    pallas_call x1, Pallas kernels, diffuse(): pl.pallas_call(functools.partial(diffusion_kernel, len(own), len(own_halo...  52.4 us
    pallas_call x10, Pallas kernels, pack(): pl.pallas_call(functools.partial(pack_kernel, find, len(arrays)), out_sha...  39.9 us
    ppermute x3, waiting for transfers between devices, paired_shards(): got_halo.append(lax.ppermute(got[k - 1], 'inner', got_pairs))  33.9 us
    ppermute x1, waiting for transfers between devices, paired_shards(): backs = [lax.ppermute(returns[0], 'inner', swap)]  12.9 us
  transfers between devices with their start and end apart: 26, of which 17 were waited for; matrix products, arithmetic and copies ran while one was open for 1% of the time, Pallas kernels for 20%

profile of v4, /device:TPU:25, one launch (start us, length us, event | category | flops | bytes accessed | tf_op | source)
XLA Modules:
  0.0 491.5 jit_solution(17889688329796384383)
XLA Ops:
  0.0 3.8 pack_tiles.10.refs_1_
  3.8 5.3 %all-to-all-start = ((f32[4,6,4,64,128]{4,3,2,1,0:T(8,128)}), f32[4,6,4,64,128]{4,3,2,1,0:T(8,128)}, u32[]{:S(2)}, u32[]{:S(2)}) async-start(f32[4,6,4,64,128]{4,3,2,1,0:T(8,128)} %pack_tiles.10.refs_1_), calls=%async_computation | async-start | bytes 6291456 | tf_op jit(solution)/shard_map/all_to_all | solution.py:126
  9.1 3.8 pack_tiles.11
  13.0 32.3 %all-to-all-done.refs_1_ = f32[4,6,4,64,128]{4,3,2,1,0:T(8,128)} async-done(((f32[4,6,4,64,128]{4,3,2,1,0:T(8,128)}), f32[4,6,4,64,128]{4,3,2,1,0:T(8,128)}, u32[]{:S(2)}, u32[]{:S(2)}) %all-to-all-start) | async-done | bytes 3145760 | tf_op jit(solution)/shard_map/all_to_all | solution.py:126
  45.3 5.5 %all-to-all-start.1 = ((f32[4,6,4,64,128]{4,3,2,1,0:T(8,128)}), f32[4,6,4,64,128]{4,3,2,1,0:T(8,128)}, u32[]{:S(2)}, u32[]{:S(2)}) async-start(f32[4,6,4,64,128]{4,3,2,1,0:T(8,128)} %pack_tiles.11), calls=%async_computation.1 | async-start | bytes 6291456 | tf_op jit(solution)/shard_map/all_to_all | solution.py:126
  50.7 4.7 split_weights.1.w_ref
  55.5 7.1 %drift_chunk.10 = (f32[8,4,64,128]{3,2,1,0:T(8,128)}, f32[8,4,64,128]{3,2,1,0:T(8,128)}, f32[8,128]{1,0:T(8,128)}) custom-call(s32[1,4,16]{2,1,0:T(4,128)} %sec_ref.39, s32[1,4,16]{2,1,0:T(4,128)} %til_ref.39, bf16[16,256,256]{2,1,0:T(8,128)(2,1)} %split_weights.1.w_ref, f32[16,64,2048]{2,1,0:T(8,128)} %refs_0_.19, f32[4,6,4,64,128]{4,3,2,1,0:T(8,128)} %all-to-all-done.refs_1_), custom_call_target="tpu_custom_call" | custom-call | bytes 1024 | tf_op jit(solution)/shard_map/drift_chunk/pallas_call | solution.py:192
  62.6 3.8 pack_tiles.12
  66.5 20.4 %all-to-all-done.1.refs_1_ = f32[4,6,4,64,128]{4,3,2,1,0:T(8,128)} async-done(((f32[4,6,4,64,128]{4,3,2,1,0:T(8,128)}), f32[4,6,4,64,128]{4,3,2,1,0:T(8,128)}, u32[]{:S(2)}, u32[]{:S(2)}) %all-to-all-start.1) | async-done | bytes 3145760 | tf_op jit(solution)/shard_map/all_to_all | solution.py:126
  86.9 5.5 %all-to-all-start.2 = ((f32[4,6,4,64,128]{4,3,2,1,0:T(8,128)}), f32[4,6,4,64,128]{4,3,2,1,0:T(8,128)}, u32[]{:S(2)}, u32[]{:S(2)}) async-start(f32[4,6,4,64,128]{4,3,2,1,0:T(8,128)} %pack_tiles.12), calls=%async_computation.2 | async-start | bytes 6291456 | tf_op jit(solution)/shard_map/all_to_all | solution.py:126
  92.4 0.1 fusion
  92.5 1.2 collective-permute-start
  93.8 3.1 collective-permute-start.1
  96.9 0.2 reduce-window.8
  97.4 0.6 broadcast_in_dim.43.rate_ref
  98.0 1.8 broadcast_in_dim.47.b_ref
  99.9 1.9 broadcast_in_dim.45.a_ref
  101.7 7.2 %drift_chunk.11 = (f32[8,4,64,128]{3,2,1,0:T(8,128)}, f32[8,4,64,128]{3,2,1,0:T(8,128)}, f32[8,128]{1,0:T(8,128)}) custom-call(s32[1,4,16]{2,1,0:T(4,128)} %sec_ref.39, s32[1,4,16]{2,1,0:T(4,128)} %til_ref.39, bf16[16,256,256]{2,1,0:T(8,128)(2,1)} %split_weights.1.w_ref, f32[16,64,2048]{2,1,0:T(8,128)} %refs_0_.19, ...), custom_call_target="tpu_custom_call" | custom-call | bytes 1024 | tf_op jit(solution)/shard_map/drift_chunk/pallas_call | solution.py:192
  108.9 3.6 pack_tiles.13
  112.5 16.1 %all-to-all-done.2.refs_1_ = f32[4,6,4,64,128]{4,3,2,1,0:T(8,128)} async-done(((f32[4,6,4,64,128]{4,3,2,1,0:T(8,128)}), f32[4,6,4,64,128]{4,3,2,1,0:T(8,128)}, u32[]{:S(2)}, u32[]{:S(2)}) %all-to-all-start.2) | async-done | bytes 3145760 | tf_op jit(solution)/shard_map/all_to_all | solution.py:126
  128.6 5.2 %all-to-all-start.3 = ((f32[4,6,2,64,128]{4,3,2,1,0:T(8,128)}), f32[4,6,2,64,128]{4,3,2,1,0:T(8,128)}, u32[]{:S(2)}, u32[]{:S(2)}) async-start(f32[4,6,2,64,128]{4,3,2,1,0:T(8,128)} %pack_tiles.13), calls=%async_computation.3 | async-start | bytes 3145728 | tf_op jit(solution)/shard_map/all_to_all | solution.py:126
  133.8 1.2 collective-permute-start.3
  134.9 7.1 %drift_chunk.12 = (f32[8,4,64,128]{3,2,1,0:T(8,128)}, f32[8,4,64,128]{3,2,1,0:T(8,128)}, f32[8,128]{1,0:T(8,128)}) custom-call(s32[1,4,16]{2,1,0:T(4,128)} %sec_ref.39, s32[1,4,16]{2,1,0:T(4,128)} %til_ref.39, bf16[16,256,256]{2,1,0:T(8,128)(2,1)} %split_weights.1.w_ref, f32[16,64,2048]{2,1,0:T(8,128)} %refs_0_.19, ...), custom_call_target="tpu_custom_call" | custom-call | bytes 1024 | tf_op jit(solution)/shard_map/drift_chunk/pallas_call | solution.py:192
  142.1 0.4 collective-permute-start.5
  142.5 3.6 pack_tiles.14
  146.1 7.0 %all-to-all-done.3.refs_1_ = f32[4,6,2,64,128]{4,3,2,1,0:T(8,128)} async-done(((f32[4,6,2,64,128]{4,3,2,1,0:T(8,128)}), f32[4,6,2,64,128]{4,3,2,1,0:T(8,128)}, u32[]{:S(2)}, u32[]{:S(2)}) %all-to-all-start.3) | async-done | bytes 1572896 | tf_op jit(solution)/shard_map/all_to_all | solution.py:126
  153.1 5.2 %all-to-all-start.4 = ((f32[4,6,2,64,128]{4,3,2,1,0:T(8,128)}), f32[4,6,2,64,128]{4,3,2,1,0:T(8,128)}, u32[]{:S(2)}, u32[]{:S(2)}) async-start(f32[4,6,2,64,128]{4,3,2,1,0:T(8,128)} %pack_tiles.14), calls=%async_computation.4 | async-start | bytes 3145728 | tf_op jit(solution)/shard_map/all_to_all | solution.py:126
  158.3 1.3 collective-permute-start.2
  159.6 1.3 collective-permute-start.4
  160.9 5.6 %collective-permute-start.8 = (f32[8,4,64,128]{3,2,1,0:T(8,128)}, f32[8,4,64,128]{3,2,1,0:T(8,128)}, u32[]{:S(2)}, u32[]{:S(2)}) collective-permute-start(f32[8,4,64,128]{3,2,1,0:T(8,128)} %get-tuple-element.70.refs_1_), channel_id=1, source_target_pairs={{1,3},{2,0},{3,5},{4,2},{5,7},{6,4},{9,11},{10,8},{11,13},{12,10},... | collective-permute-start | bytes 3145736 | tf_op jit(solution)/shard_map/ppermute | solution.py:502
  166.5 3.3 collective-permute-start.9
  169.8 11.3 %collective-permute-done.5.refs_7_ = f32[8,4,64,128]{3,2,1,0:T(8,128)} collective-permute-done((f32[8,4,64,128]{3,2,1,0:T(8,128)}, f32[8,4,64,128]{3,2,1,0:T(8,128)}, u32[]{:S(2)}, u32[]{:S(2)}) %collective-permute-start.5) | collective-permute-done | bytes 1048608 | tf_op jit(solution)/shard_map/ppermute | solution.py:499
  181.2 1.3 collective-permute-start.10
  182.5 2.7 collective-permute-done.2.refs_3_.refs_13_
  185.2 6.7 %drift_chunk.13 = (f32[8,2,64,128]{3,2,1,0:T(8,128)}, f32[8,2,64,128]{3,2,1,0:T(8,128)}, f32[8,128]{1,0:T(8,128)}) custom-call(s32[1,4,16]{2,1,0:T(4,128)} %sec_ref.39, s32[1,4,16]{2,1,0:T(4,128)} %til_ref.39, bf16[16,256,256]{2,1,0:T(8,128)(2,1)} %split_weights.1.w_ref, f32[16,64,2048]{2,1,0:T(8,128)} %refs_0_.19, ...), custom_call_target="tpu_custom_call" | custom-call | bytes 1024 | tf_op jit(solution)/shard_map/drift_chunk/pallas_call | solution.py:192
  191.9 0.3 collective-permute-start.6
  192.2 15.5 %collective-permute-done.4.refs_3_.refs_14_ = f32[8,4,64,128]{3,2,1,0:T(8,128)} collective-permute-done((f32[8,4,64,128]{3,2,1,0:T(8,128)}, f32[8,4,64,128]{3,2,1,0:T(8,128)}, u32[]{:S(2)}, u32[]{:S(2)}) %collective-permute-start.4) | collective-permute-done | bytes 1048608 | tf_op jit(solution)/shard_map/ppermute | solution.py:505
  207.7 6.7 %drift_chunk.14 = (f32[8,2,64,128]{3,2,1,0:T(8,128)}, f32[8,2,64,128]{3,2,1,0:T(8,128)}, f32[8,128]{1,0:T(8,128)}) custom-call(s32[1,4,16]{2,1,0:T(4,128)} %sec_ref.39, s32[1,4,16]{2,1,0:T(4,128)} %til_ref.39, bf16[16,256,256]{2,1,0:T(8,128)(2,1)} %split_weights.1.w_ref, f32[16,64,2048]{2,1,0:T(8,128)} %refs_0_.19, ...), custom_call_target="tpu_custom_call" | custom-call | bytes 1024 | tf_op jit(solution)/shard_map/drift_chunk/pallas_call | solution.py:192
  214.5 15.7 %collective-permute-done.10.refs_15_ = f32[8,4,64,128]{3,2,1,0:T(8,128)} collective-permute-done((f32[8,4,64,128]{3,2,1,0:T(8,128)}, f32[8,4,64,128]{3,2,1,0:T(8,128)}, u32[]{:S(2)}, u32[]{:S(2)}) %collective-permute-start.10) | collective-permute-done | bytes 1048608 | tf_op jit(solution)/shard_map/ppermute | solution.py:505
  230.1 52.4 %diffuse_tiles.1 = (f32[8,16,64,128]{3,2,1,0:T(8,128)}, f32[8,2,64,128]{3,2,1,0:T(8,128)}, f32[8,4,64,128]{3,2,1,0:T(8,128)}, f32[8,4,64,128]{3,2,1,0:T(8,128)},...) custom-call(f32[8,8,128]{2,1,0:T(8,128)} %broadcast_in_dim.43.rate_ref, f32[56,64,128]{2,1,0:T(8,128)} %broadcast_in_dim.45.a_ref, ...), custom_call_target="tpu_custom_call" | custom-call | bytes 1024 | tf_op jit(solution)/shard_map/diffuse_tiles/pallas_call | solution.py:367
  282.6 12.9 %collective-permute-done.11.refs_1_ = f32[8,2,64,128]{3,2,1,0:T(8,128)} collective-permute-done((f32[8,2,64,128]{3,2,1,0:T(8,128)}, f32[8,2,64,128]{3,2,1,0:T(8,128)}, u32[]{:S(2)}, u32[]{:S(2)}) %collective-permute-start.11) | collective-permute-done | bytes 524320 | tf_op jit(solution)/shard_map/ppermute | solution.py:531
  295.5 4.1 pack_tiles.16
  299.6 6.2 %all-to-all-start.5 = ((f32[4,6,2,64,128]{4,3,2,1,0:T(8,128)}), f32[4,6,2,64,128]{4,3,2,1,0:T(8,128)}, u32[]{:S(2)}, u32[]{:S(2)}) async-start(f32[4,6,2,64,128]{4,3,2,1,0:T(8,128)} %pack_tiles.16), calls=%async_computation.5 | async-start | bytes 3145728 | tf_op jit(solution)/shard_map/all_to_all | solution.py:126
  305.8 24.7 %collective-permute-done.12.refs_1_ = f32[8,4,64,128]{3,2,1,0:T(8,128)} collective-permute-done((f32[8,4,64,128]{3,2,1,0:T(8,128)S(1)}, f32[8,4,64,128]{3,2,1,0:T(8,128)}, u32[]{:S(2)}, u32[]{:S(2)}) %collective-permute-start.12) | collective-permute-done | bytes 1048608 | tf_op jit(solution)/shard_map/ppermute | solution.py:533
  330.5 4.3 pack_tiles.15
  334.8 5.6 %all-to-all-start.6 = ((f32[4,6,4,64,128]{4,3,2,1,0:T(8,128)}), f32[4,6,4,64,128]{4,3,2,1,0:T(8,128)}, u32[]{:S(2)}, u32[]{:S(2)}) async-start(f32[4,6,4,64,128]{4,3,2,1,0:T(8,128)} %pack_tiles.15), calls=%async_computation.6 | async-start | bytes 6291456 | tf_op jit(solution)/shard_map/all_to_all | solution.py:126
  340.4 6.7 %drift_chunk.15 = (f32[16,64,2048]{2,1,0:T(8,128)}, f32[8,128]{1,0:T(8,128)}) custom-call(s32[1,4,16]{2,1,0:T(4,128)} %sec_ref.39, s32[1,4,16]{2,1,0:T(4,128)} %til_ref.39, bf16[16,256,256]{2,1,0:T(8,128)(2,1)} %split_weights.1.w_ref, f32[8,16,64,128]{3,2,1,0:T(8,128)} %get-tuple-element.87.refs_0_.refs_2_, ...), custom_call_target="tpu_custom_call" | custom-call | bytes 1024 | tf_op jit(solution)/shard_map/drift_chunk/pallas_call | solution.py:192
  347.1 18.3 %collective-permute-done.13.refs_1_ = f32[8,4,64,128]{3,2,1,0:T(8,128)} collective-permute-done((f32[8,4,64,128]{3,2,1,0:T(8,128)}, f32[8,4,64,128]{3,2,1,0:T(8,128)}, u32[]{:S(2)}, u32[]{:S(2)}) %collective-permute-start.13) | collective-permute-done | bytes 1048608 | tf_op jit(solution)/shard_map/ppermute | solution.py:543
  365.4 4.3 pack_tiles.17
  369.6 6.9 %all-to-all-done.6.refs_2_ = f32[4,6,4,64,128]{4,3,2,1,0:T(8,128)} async-done(((f32[4,6,4,64,128]{4,3,2,1,0:T(8,128)}), f32[4,6,4,64,128]{4,3,2,1,0:T(8,128)}, u32[]{:S(2)}, u32[]{:S(2)}) %all-to-all-start.6) | async-done | bytes 3145760 | tf_op jit(solution)/shard_map/all_to_all | solution.py:126
  376.6 5.6 %all-to-all-start.7 = ((f32[4,6,4,64,128]{4,3,2,1,0:T(8,128)}), f32[4,6,4,64,128]{4,3,2,1,0:T(8,128)}, u32[]{:S(2)}, u32[]{:S(2)}) async-start(f32[4,6,4,64,128]{4,3,2,1,0:T(8,128)} %pack_tiles.17), calls=%async_computation.7 | async-start | bytes 6291456 | tf_op jit(solution)/shard_map/all_to_all | solution.py:126
  382.2 7.2 %drift_chunk.16 = (f32[16,64,2048]{2,1,0:T(8,128)}, f32[8,128]{1,0:T(8,128)}) custom-call(s32[1,4,16]{2,1,0:T(4,128)} %sec_ref.39, s32[1,4,16]{2,1,0:T(4,128)} %til_ref.39, bf16[16,256,256]{2,1,0:T(8,128)(2,1)} %split_weights.1.w_ref, f32[8,16,64,128]{3,2,1,0:T(8,128)} %get-tuple-element.87.refs_0_.refs_2_, ...), custom_call_target="tpu_custom_call", output_to_operand_aliasing={{0}: (6, {})} | custom-call | bytes 1024 | tf_op jit(solution)/shard_map/drift_chunk/pallas_call | solution.py:192
  389.3 12.2 %collective-permute-done.14.refs_1_ = f32[8,3,64,128]{3,2,1,0:T(8,128)} collective-permute-done((f32[8,3,64,128]{3,2,1,0:T(8,128)}, f32[8,3,64,128]{3,2,1,0:T(8,128)}, u32[]{:S(2)}, u32[]{:S(2)}) %collective-permute-start.14) | collective-permute-done | bytes 786464 | tf_op jit(solution)/shard_map/ppermute | solution.py:543
  401.5 4.3 pack_tiles.18
  405.7 12.6 %all-to-all-done.7.refs_2_ = f32[4,6,4,64,128]{4,3,2,1,0:T(8,128)} async-done(((f32[4,6,4,64,128]{4,3,2,1,0:T(8,128)}), f32[4,6,4,64,128]{4,3,2,1,0:T(8,128)}, u32[]{:S(2)}, u32[]{:S(2)}) %all-to-all-start.7) | async-done | bytes 3145760 | tf_op jit(solution)/shard_map/all_to_all | solution.py:126
  418.3 5.3 %all-to-all-start.8 = ((f32[4,6,3,64,128]{4,3,2,1,0:T(8,128)}), f32[4,6,3,64,128]{4,3,2,1,0:T(8,128)}, u32[]{:S(2)}, u32[]{:S(2)}) async-start(f32[4,6,3,64,128]{4,3,2,1,0:T(8,128)} %pack_tiles.18), calls=%async_computation.8 | async-start | bytes 4718592 | tf_op jit(solution)/shard_map/all_to_all | solution.py:126
  423.7 7.2 %drift_chunk.17 = (f32[16,64,2048]{2,1,0:T(8,128)}, f32[8,128]{1,0:T(8,128)}) custom-call(s32[1,4,16]{2,1,0:T(4,128)} %sec_ref.39, s32[1,4,16]{2,1,0:T(4,128)} %til_ref.39, bf16[16,256,256]{2,1,0:T(8,128)(2,1)} %split_weights.1.w_ref, f32[8,16,64,128]{3,2,1,0:T(8,128)} %get-tuple-element.87.refs_0_.refs_2_, ...), custom_call_target="tpu_custom_call", output_to_operand_aliasing={{0}: (6, {})} | custom-call | bytes 1024 | tf_op jit(solution)/shard_map/drift_chunk/pallas_call | solution.py:192
  430.8 12.2 %collective-permute-done.15.refs_1_ = f32[8,3,64,128]{3,2,1,0:T(8,128)} collective-permute-done((f32[8,3,64,128]{3,2,1,0:T(8,128)}, f32[8,3,64,128]{3,2,1,0:T(8,128)}, u32[]{:S(2)}, u32[]{:S(2)}) %collective-permute-start.15) | collective-permute-done | bytes 786464 | tf_op jit(solution)/shard_map/ppermute | solution.py:543
  443.0 4.2 pack_tiles.19
  447.2 4.2 all-to-all-done.8.refs_2_
  451.4 5.3 %all-to-all-start.9 = ((f32[4,6,3,64,128]{4,3,2,1,0:T(8,128)}), f32[4,6,3,64,128]{4,3,2,1,0:T(8,128)}, u32[]{:S(2)}, u32[]{:S(2)}) async-start(f32[4,6,3,64,128]{4,3,2,1,0:T(8,128)} %pack_tiles.19), calls=%async_computation.9 | async-start | bytes 4718592 | tf_op jit(solution)/shard_map/all_to_all | solution.py:126
  456.7 7.0 %drift_chunk.18 = (f32[16,64,2048]{2,1,0:T(8,128)}, f32[8,128]{1,0:T(8,128)}) custom-call(s32[1,4,16]{2,1,0:T(4,128)} %sec_ref.39, s32[1,4,16]{2,1,0:T(4,128)} %til_ref.39, bf16[16,256,256]{2,1,0:T(8,128)(2,1)} %split_weights.1.w_ref, f32[8,16,64,128]{3,2,1,0:T(8,128)} %get-tuple-element.87.refs_0_.refs_2_, ...), custom_call_target="tpu_custom_call", output_to_operand_aliasing={{0}: (6, {})} | custom-call | bytes 1024 | tf_op jit(solution)/shard_map/drift_chunk/pallas_call | solution.py:192
  463.7 20.7 %all-to-all-done.9.refs_2_ = f32[4,6,3,64,128]{4,3,2,1,0:T(8,128)} async-done(((f32[4,6,3,64,128]{4,3,2,1,0:T(8,128)}), f32[4,6,3,64,128]{4,3,2,1,0:T(8,128)}, u32[]{:S(2)}, u32[]{:S(2)}) %all-to-all-start.9) | async-done | bytes 2359328 | tf_op jit(solution)/shard_map/all_to_all | solution.py:126
  484.5 7.0 %drift_chunk.19 = (f32[16,64,2048]{2,1,0:T(8,128)}, f32[8,128]{1,0:T(8,128)}) custom-call(s32[1,4,16]{2,1,0:T(4,128)} %sec_ref.39, s32[1,4,16]{2,1,0:T(4,128)} %til_ref.39, bf16[16,256,256]{2,1,0:T(8,128)(2,1)} %split_weights.1.w_ref, f32[8,16,64,128]{3,2,1,0:T(8,128)} %get-tuple-element.87.refs_0_.refs_2_, ...), custom_call_target="tpu_custom_call", output_to_operand_aliasing={{0}: (6, {})} | custom-call | bytes 1024 | tf_op jit(solution)/shard_map/drift_chunk/pallas_call | solution.py:192
  (32 shorter events, 0.5 us)
Async XLA Ops:
  3.8 41.4 %all-to-all-start = ((f32[4,6,4,64,128]{4,3,2,1,0:T(8,128)}), f32[4,6,4,64,128]{4,3,2,1,0:T(8,128)}, u32[]{:S(2)}, u32[]{:S(2)}) async-start(f32[4,6,4,64,128]{4,3,2,1,0:T(8,128)} %pack_tiles.10.refs_1_), calls=%async_computation | async-start | bytes 6291456 | tf_op jit(solution)/shard_map/all_to_all | solution.py:126
  45.3 41.6 %all-to-all-start.1 = ((f32[4,6,4,64,128]{4,3,2,1,0:T(8,128)}), f32[4,6,4,64,128]{4,3,2,1,0:T(8,128)}, u32[]{:S(2)}, u32[]{:S(2)}) async-start(f32[4,6,4,64,128]{4,3,2,1,0:T(8,128)} %pack_tiles.11), calls=%async_computation.1 | async-start | bytes 6291456 | tf_op jit(solution)/shard_map/all_to_all | solution.py:126
  66.5 26.0 %copy-start = (f32[128,64]{0,1:T(8,128)S(1)}, f32[128,64]{0,1:T(8,128)}, u32[]{:S(2)}) copy-start(f32[128,64]{0,1:T(8,128)} %param.16) | copy-start | bytes 98308
  66.5 25.9 %copy-start.1 = (f32[128,64]{0,1:T(8,128)S(1)}, f32[128,64]{0,1:T(8,128)}, u32[]{:S(2)}) copy-start(f32[128,64]{0,1:T(8,128)} %param.17) | copy-start | bytes 98308
  66.5 30.4 %copy-start.4 = (s32[1,8]{1,0:T(1,128)S(1)}, s32[1,8]{1,0:T(1,128)}, u32[]{:S(2)}) copy-start(s32[1,8]{1,0:T(1,128)} %param.14) | copy-start | bytes 100
  66.5 30.8 %copy-start.2 = (f32[1,8]{1,0:T(1,128)S(1)}, f32[1,8]{1,0:T(1,128)}, u32[]{:S(2)}) copy-start(f32[1,8]{1,0:T(1,128)} %param.15) | copy-start | bytes 100
  86.9 41.7 %all-to-all-start.2 = ((f32[4,6,4,64,128]{4,3,2,1,0:T(8,128)}), f32[4,6,4,64,128]{4,3,2,1,0:T(8,128)}, u32[]{:S(2)}, u32[]{:S(2)}) async-start(f32[4,6,4,64,128]{4,3,2,1,0:T(8,128)} %pack_tiles.12), calls=%async_computation.2 | async-start | bytes 6291456 | tf_op jit(solution)/shard_map/all_to_all | solution.py:126
  92.5 42.4 %collective-permute-start = (f32[8,4,64,128]{3,2,1,0:T(8,128)}, f32[8,4,64,128]{3,2,1,0:T(8,128)}, u32[]{:S(2)}, u32[]{:S(2)}) collective-permute-start(f32[8,4,64,128]{3,2,1,0:T(8,128)} %get-tuple-element.74), channel_id=1, source_target_pairs={{0,1},{1,0},{2,3},{3,2},{4,5},{5,4},{6,7},{7,6},{8,9},{9,8},{10,11... | collective-permute-start | bytes 3145736 | tf_op jit(solution)/shard_map/ppermute | solution.py:499
  93.8 41.2 %collective-permute-start.1 = (f32[8,4,64,128]{3,2,1,0:T(8,128)}, f32[8,4,64,128]{3,2,1,0:T(8,128)}, u32[]{:S(2)}, u32[]{:S(2)}) collective-permute-start(f32[8,4,64,128]{3,2,1,0:T(8,128)} %get-tuple-element.68.refs_0_), channel_id=1, source_target_pairs={{1,3},{2,0},{3,5},{4,2},{5,7},{6,4},{9,11},{10,8},{11,13},{12,10},... | collective-permute-start | bytes 3145736 | tf_op jit(solution)/shard_map/ppermute | solution.py:502
  128.6 24.5 %all-to-all-start.3 = ((f32[4,6,2,64,128]{4,3,2,1,0:T(8,128)}), f32[4,6,2,64,128]{4,3,2,1,0:T(8,128)}, u32[]{:S(2)}, u32[]{:S(2)}) async-start(f32[4,6,2,64,128]{4,3,2,1,0:T(8,128)} %pack_tiles.13), calls=%async_computation.3 | async-start | bytes 3145728 | tf_op jit(solution)/shard_map/all_to_all | solution.py:126
  133.8 25.8 %collective-permute-start.3 = (f32[8,4,64,128]{3,2,1,0:T(8,128)}, f32[8,4,64,128]{3,2,1,0:T(8,128)}, u32[]{:S(2)}, u32[]{:S(2)}) collective-permute-start(f32[8,4,64,128]{3,2,1,0:T(8,128)} %get-tuple-element.82), channel_id=1, source_target_pairs={{0,1},{1,0},{2,3},{3,2},{4,5},{5,4},{6,7},{7,6},{8,9},{9,8},{10,11... | collective-permute-start | bytes 3145736 | tf_op jit(solution)/shard_map/ppermute | solution.py:499
  142.1 39.1 %collective-permute-start.5 = (f32[8,4,64,128]{3,2,1,0:T(8,128)}, f32[8,4,64,128]{3,2,1,0:T(8,128)}, u32[]{:S(2)}, u32[]{:S(2)}) collective-permute-start(f32[8,4,64,128]{3,2,1,0:T(8,128)} %get-tuple-element.84), channel_id=1, source_target_pairs={{0,1},{1,0},{2,3},{3,2},{4,5},{5,4},{6,7},{7,6},{8,9},{9,8},{10,11... | collective-permute-start | bytes 3145736 | tf_op jit(solution)/shard_map/ppermute | solution.py:499
  153.1 54.6 %all-to-all-start.4 = ((f32[4,6,2,64,128]{4,3,2,1,0:T(8,128)}), f32[4,6,2,64,128]{4,3,2,1,0:T(8,128)}, u32[]{:S(2)}, u32[]{:S(2)}) async-start(f32[4,6,2,64,128]{4,3,2,1,0:T(8,128)} %pack_tiles.14), calls=%async_computation.4 | async-start | bytes 3145728 | tf_op jit(solution)/shard_map/all_to_all | solution.py:126
  158.3 26.9 %collective-permute-start.2 = (f32[8,4,64,128]{3,2,1,0:T(8,128)}, f32[8,4,64,128]{3,2,1,0:T(8,128)}, u32[]{:S(2)}, u32[]{:S(2)}) collective-permute-start(f32[8,4,64,128]{3,2,1,0:T(8,128)} %collective-permute-done.refs_3_.refs_5_), channel_id=1, source_target_pairs={{0,2},{2,4},{3,1},{4,6},{5,3},{7,5},{8,10},{10,12},{11,9},{12,14},... | collective-permute-start | bytes 3145736 | tf_op jit(solution)/shard_map/ppermute | solution.py:505
  159.6 48.1 %collective-permute-start.4 = (f32[8,4,64,128]{3,2,1,0:T(8,128)}, f32[8,4,64,128]{3,2,1,0:T(8,128)}, u32[]{:S(2)}, u32[]{:S(2)}) collective-permute-start(f32[8,4,64,128]{3,2,1,0:T(8,128)} %collective-permute-done.3.refs_6_), channel_id=1, source_target_pairs={{0,2},{2,4},{3,1},{4,6},{5,3},{7,5},{8,10},{10,12},{11,9},{12,14},... | collective-permute-start | bytes 3145736 | tf_op jit(solution)/shard_map/ppermute | solution.py:505
  160.9 53.6 %collective-permute-start.8 = (f32[8,4,64,128]{3,2,1,0:T(8,128)}, f32[8,4,64,128]{3,2,1,0:T(8,128)}, u32[]{:S(2)}, u32[]{:S(2)}) collective-permute-start(f32[8,4,64,128]{3,2,1,0:T(8,128)} %get-tuple-element.70.refs_1_), channel_id=1, source_target_pairs={{1,3},{2,0},{3,5},{4,2},{5,7},{6,4},{9,11},{10,8},{11,13},{12,10},... | collective-permute-start | bytes 3145736 | tf_op jit(solution)/shard_map/ppermute | solution.py:502
  166.5 47.9 %collective-permute-start.9 = (f32[8,4,64,128]{3,2,1,0:T(8,128)}, f32[8,4,64,128]{3,2,1,0:T(8,128)}, u32[]{:S(2)}, u32[]{:S(2)}) collective-permute-start(f32[8,4,64,128]{3,2,1,0:T(8,128)} %get-tuple-element.75.refs_2_), channel_id=1, source_target_pairs={{1,3},{2,0},{3,5},{4,2},{5,7},{6,4},{9,11},{10,8},{11,13},{12,10},... | collective-permute-start | bytes 3145736 | tf_op jit(solution)/shard_map/ppermute | solution.py:502
  181.2 49.0 %collective-permute-start.10 = (f32[8,4,64,128]{3,2,1,0:T(8,128)}, f32[8,4,64,128]{3,2,1,0:T(8,128)}, u32[]{:S(2)}, u32[]{:S(2)}) collective-permute-start(f32[8,4,64,128]{3,2,1,0:T(8,128)} %collective-permute-done.5.refs_7_), channel_id=1, source_target_pairs={{0,2},{2,4},{3,1},{4,6},{5,3},{7,5},{8,10},{10,12},{11,9},{12,14},... | collective-permute-start | bytes 3145736 | tf_op jit(solution)/shard_map/ppermute | solution.py:505
  191.9 22.6 %collective-permute-start.6 = (f32[8,2,64,128]{3,2,1,0:T(8,128)}, f32[8,2,64,128]{3,2,1,0:T(8,128)}, u32[]{:S(2)}, u32[]{:S(2)}) collective-permute-start(f32[8,2,64,128]{3,2,1,0:T(8,128)} %get-tuple-element.85), channel_id=1, source_target_pairs={{0,1},{1,0},{2,3},{3,2},{4,5},{5,4},{6,7},{7,6},{8,9},{9,8},{10,11... | collective-permute-start | bytes 1572872 | tf_op jit(solution)/shard_map/ppermute | solution.py:499
  214.3 15.8 %collective-permute-start.7 = (f32[8,2,64,128]{3,2,1,0:T(8,128)}, f32[8,2,64,128]{3,2,1,0:T(8,128)}, u32[]{:S(2)}, u32[]{:S(2)}) collective-permute-start(f32[8,2,64,128]{3,2,1,0:T(8,128)} %get-tuple-element.86), channel_id=1, source_target_pairs={{0,1},{1,0},{2,3},{3,2},{4,5},{5,4},{6,7},{7,6},{8,9},{9,8},{10,11... | collective-permute-start | bytes 1572872 | tf_op jit(solution)/shard_map/ppermute | solution.py:499
  282.5 13.0 %collective-permute-start.11 = (f32[8,2,64,128]{3,2,1,0:T(8,128)}, f32[8,2,64,128]{3,2,1,0:T(8,128)}, u32[]{:S(2)}, u32[]{:S(2)}) collective-permute-start(f32[8,2,64,128]{3,2,1,0:T(8,128)} %get-tuple-element.92), channel_id=1, source_target_pairs={{0,1},{1,0},{2,3},{3,2},{4,5},{5,4},{6,7},{7,6},{8,9},{9,8},{10,11... | collective-permute-start | bytes 1572872 | tf_op jit(solution)/shard_map/ppermute | solution.py:531
  299.6 6.2 %copy-start.3 = (f32[8,4,64,128]{3,2,1,0:T(8,128)S(1)}, f32[8,4,64,128]{3,2,1,0:T(8,128)}, u32[]{:S(2)}) copy-start(f32[8,4,64,128]{3,2,1,0:T(8,128)} %get-tuple-element.93) | copy-start | bytes 3145732
  299.6 35.2 %all-to-all-start.5 = ((f32[4,6,2,64,128]{4,3,2,1,0:T(8,128)}), f32[4,6,2,64,128]{4,3,2,1,0:T(8,128)}, u32[]{:S(2)}, u32[]{:S(2)}) async-start(f32[4,6,2,64,128]{4,3,2,1,0:T(8,128)} %pack_tiles.16), calls=%async_computation.5 | async-start | bytes 3145728 | tf_op jit(solution)/shard_map/all_to_all | solution.py:126
  305.8 24.7 %collective-permute-start.12 = (f32[8,4,64,128]{3,2,1,0:T(8,128)S(1)}, f32[8,4,64,128]{3,2,1,0:T(8,128)}, u32[]{:S(2)}, u32[]{:S(2)}) collective-permute-start(f32[8,4,64,128]{3,2,1,0:T(8,128)S(1)} %copy-done.3), channel_id=1, source_target_pairs={{0,1},{1,0},{2,3},{3,2},{4,5},{5,4},{6,7},{7,6},{8,9},{9,8},{10,11... | collective-permute-start | bytes 3145736 | tf_op jit(solution)/shard_map/ppermute | solution.py:533
  334.8 41.8 %all-to-all-start.6 = ((f32[4,6,4,64,128]{4,3,2,1,0:T(8,128)}), f32[4,6,4,64,128]{4,3,2,1,0:T(8,128)}, u32[]{:S(2)}, u32[]{:S(2)}) async-start(f32[4,6,4,64,128]{4,3,2,1,0:T(8,128)} %pack_tiles.15), calls=%async_computation.6 | async-start | bytes 6291456 | tf_op jit(solution)/shard_map/all_to_all | solution.py:126
  340.4 24.9 %collective-permute-start.13 = (f32[8,4,64,128]{3,2,1,0:T(8,128)}, f32[8,4,64,128]{3,2,1,0:T(8,128)}, u32[]{:S(2)}, u32[]{:S(2)}) collective-permute-start(f32[8,4,64,128]{3,2,1,0:T(8,128)} %get-tuple-element.94), channel_id=1, source_target_pairs={{0,1},{1,0},{2,3},{3,2},{4,5},{5,4},{6,7},{7,6},{8,9},{9,8},{10,11... | collective-permute-start | bytes 3145736 | tf_op jit(solution)/shard_map/ppermute | solution.py:543
  376.6 41.7 %all-to-all-start.7 = ((f32[4,6,4,64,128]{4,3,2,1,0:T(8,128)}), f32[4,6,4,64,128]{4,3,2,1,0:T(8,128)}, u32[]{:S(2)}, u32[]{:S(2)}) async-start(f32[4,6,4,64,128]{4,3,2,1,0:T(8,128)} %pack_tiles.17), calls=%async_computation.7 | async-start | bytes 6291456 | tf_op jit(solution)/shard_map/all_to_all | solution.py:126
  382.2 19.3 %collective-permute-start.14 = (f32[8,3,64,128]{3,2,1,0:T(8,128)}, f32[8,3,64,128]{3,2,1,0:T(8,128)}, u32[]{:S(2)}, u32[]{:S(2)}) collective-permute-start(f32[8,3,64,128]{3,2,1,0:T(8,128)} %get-tuple-element.95), channel_id=1, source_target_pairs={{0,1},{1,0},{2,3},{3,2},{4,5},{5,4},{6,7},{7,6},{8,9},{9,8},{10,11... | collective-permute-start | bytes 2359304 | tf_op jit(solution)/shard_map/ppermute | solution.py:543
  418.3 33.1 %all-to-all-start.8 = ((f32[4,6,3,64,128]{4,3,2,1,0:T(8,128)}), f32[4,6,3,64,128]{4,3,2,1,0:T(8,128)}, u32[]{:S(2)}, u32[]{:S(2)}) async-start(f32[4,6,3,64,128]{4,3,2,1,0:T(8,128)} %pack_tiles.18), calls=%async_computation.8 | async-start | bytes 4718592 | tf_op jit(solution)/shard_map/all_to_all | solution.py:126
  423.7 19.3 %collective-permute-start.15 = (f32[8,3,64,128]{3,2,1,0:T(8,128)}, f32[8,3,64,128]{3,2,1,0:T(8,128)}, u32[]{:S(2)}, u32[]{:S(2)}) collective-permute-start(f32[8,3,64,128]{3,2,1,0:T(8,128)} %get-tuple-element.96), channel_id=1, source_target_pairs={{0,1},{1,0},{2,3},{3,2},{4,5},{5,4},{6,7},{7,6},{8,9},{9,8},{10,11... | collective-permute-start | bytes 2359304 | tf_op jit(solution)/shard_map/ppermute | solution.py:543
  451.4 33.1 %all-to-all-start.9 = ((f32[4,6,3,64,128]{4,3,2,1,0:T(8,128)}), f32[4,6,3,64,128]{4,3,2,1,0:T(8,128)}, u32[]{:S(2)}, u32[]{:S(2)}) async-start(f32[4,6,3,64,128]{4,3,2,1,0:T(8,128)} %pack_tiles.19), calls=%async_computation.9 | async-start | bytes 4718592 | tf_op jit(solution)/shard_map/all_to_all | solution.py:126

commit v5 on v3

--- a/solution.py
+++ b/solution.py
@@ -128,6 +128,13 @@
         lax.ppermute(send, "sector", [(s, s ^ d) for s in range(sectors)])
         for d, send in zip(offsets, sends)
     ]
+
+
+def queue(came, sends, offsets):
+    sends = list(sends)
+    for i, send in enumerate(sends):
+        (sends[i],), (came[-1][i],) = in_turn([send], [came[-1][i]])
+    came.append(sector_exchange(sends, offsets))
 
 
 def in_turn(later, earlier):
@@ -489,35 +496,36 @@
         return pack(groups, cap, tables, [density], after)
 
     sends = pack_first(0, ())
-    recvs = sector_exchange(sends[:-1], far)
     beside = sector_exchange(sends[-1:], near)
-    token = sends[0]
-    crossing = []
+    came = [sector_exchange(sends[:-1], far)]
+    after_pack, token = sends[0], None
     for k, (start, step, find, receive, place) in enumerate(packed):
         if k + 1 < len(packed):
-            later = pack_first(k + 1, (token,))
-            later, recvs = in_turn(later, recvs)
-            coming = sector_exchange(later, far)
+            queue(came, pack_first(k + 1, (after_pack,)), far)
+            after_pack = came[k][0]
         if k == 1:
-            recvs, (rate, a, b) = in_turn(recvs, [rate, a, b])
-        after = ()
-        if k > 0:
-            after = [token, *(crossing[k - 2] if k == 2 else ()), *got_halo[: k - 2][-1:]]
+            came[k], (rate, a, b) = in_turn(came[k], [rate, a, b])
         part = jax.ShapeDtypeStruct((half, step, pitches, side), F32)
         piece = (step, pitches, side)
+        after = () if token is None else (token,)
         kept, sent, token = drift(
-            find, place, receive, tables, weights, [density], beside + recvs, [part, part], piece, after
+            find, place, receive, tables, weights, [density], beside + came[k], [part, part], piece, after
         )
-        recvs = coming
         own.append(kept)
+        if k + 1 < len(packed):
+            (sent, kept), (came[k + 1][0],) = in_turn([sent, kept], [came[k + 1][0]])
+        if k > 0:
+            (sent,), (got[k - 1],) = in_turn([sent], [got[k - 1]])
         got.append(lax.ppermute(sent, "inner", swap))
-        crossing.append(got[-1:])
+        if 0 < k <= halo_chunks:
+            forward = got[k - 1]
+            if k > 1:
+                (forward,), (got_halo[k - 2],) = in_turn([forward], [got_halo[k - 2]])
+            got_halo.append(lax.ppermute(forward, "inner", got_pairs))
         if k < halo_chunks:
+            if k > 0:
+                (kept,), (own_halo[k - 1],) = in_turn([kept], [own_halo[k - 1]])
             own_halo.append(lax.ppermute(kept, "inner", own_pairs))
-            crossing[-1] += own_halo[-1:]
-        if 0 < k <= halo_chunks:
-            got_halo.append(lax.ppermute(got[k - 1], "inner", got_pairs))
-            crossing[-1] += got_halo[-1:]
 
     kept, sends = diffuse(rate, a, b, own, got, own_halo, got_halo, last_steps)
 
@@ -550,21 +558,22 @@
     (last,), (backs[0],) = in_turn([returns[1]], [backs[0]])
     backs.append(lax.ppermute(last, "inner", swap))
     sends, far_sends = pack_last(0, ())
-    recvs = sector_exchange(far_sends, far)
+    came = [sector_exchange(far_sends, far)]
     beside = sector_exchange(sends, near)
-    token = kept
+    token = None
     for k, (find, place, piece) in enumerate(ready):
+        after = [] if token is None else [token]
         if k + 1 < len(ready):
-            sends, far_sends = pack_last(k + 1, (token,))
-            far_sends, recvs = in_turn(far_sends, recvs)
-            coming = sector_exchange(far_sends, far), sector_exchange(sends, near)
+            sends, far_sends = pack_last(k + 1, after)
+            queue(came, far_sends, far)
+            beside_next = sector_exchange(sends, near)
         if k + 2 < len(ready):
-            (last,), (backs[k + 1], *recvs) = in_turn([returns[k + 2]], [backs[k + 1], *recvs])
+            (last,), (backs[k + 1], *came[k]) = in_turn([returns[k + 2]], [backs[k + 1], *came[k]])
             backs.append(lax.ppermute(last, "inner", swap))
         *out, token = drift(
-            find, place, receive_slot, tables, weights, [kept, backs[k]], beside + recvs, whole, piece, (), out
+            find, place, receive_slot, tables, weights, [kept, backs[k]], beside + came[k], whole, piece, after, out
         )
-        recvs, beside = coming
+        beside = beside_next
     return out[0]
 
 

time: 435 us -> 427 us (0.982)
  waiting for transfers between devices: 208 us -> 199 us
    ppermute x3, waiting for transfers between devices: 12.9 us -> 0.01 us  [paired_shards(): own_halo.append(lax.ppermute(kept, 'inner', own_pairs))]
    ppermute x5, waiting for transfers between devices: 3.95 us -> 12.5 us  [paired_shards(): got.append(lax.ppermute(sent, 'inner', swap))]
    ppermute x26, starting transfers between devices: 23.7 us -> 29.1 us  [sector_exchange(): lax.ppermute(send, 'sector', [(s, s ^ d) for s in range(sectors)])]
  transfers between devices with their start and end apart: 42 -> 42, of which waited for: 22 -> 21; matrix products, arithmetic and copies ran while one was open for 2% -> 1% of each run, Pallas kernels for 23% -> 23%
where the time goes in v5:
time: 427 us; the launch traced here: 423 us
  waiting for transfers between devices  199 us (47%)
  Pallas kernels  162 us (38%)
  starting transfers between devices  55.4 us (13%)
  local copies, waits for them, and re-layouts  4.51 us (1%)
    ppermute x26, waiting for transfers between devices, sector_exchange(): lax.ppermute(send, 'sector', [(s, s ^ d) for s in range(sectors)])  135 us
    pallas_call x10, Pallas kernels, drift(): pl.pallas_call(functools.partial(drift_kernel, find, place, receive, n_lo...  69.7 us
    pallas_call x1, Pallas kernels, diffuse(): pl.pallas_call(functools.partial(diffusion_kernel, len(own), len(own_halo...  52.4 us
    ppermute x4, waiting for transfers between devices, paired_shards(): backs.append(lax.ppermute(last, 'inner', swap))  39.7 us
    pallas_call x10, Pallas kernels, pack(): pl.pallas_call(functools.partial(pack_kernel, offsets, finds, len(arrays)...  35.6 us
    ppermute x26, starting transfers between devices, sector_exchange(): lax.ppermute(send, 'sector', [(s, s ^ d) for s in range(sectors)])  29.1 us
    ppermute x5, waiting for transfers between devices, paired_shards(): got.append(lax.ppermute(sent, 'inner', swap))  12.5 us
    ppermute x3, starting transfers between devices, paired_shards(): own_halo.append(lax.ppermute(kept, 'inner', own_pairs))  12.3 us
  transfers between devices with their start and end apart: 42, of which 21 were waited for; matrix products, arithmetic and copies ran while one was open for 1% of the time, Pallas kernels for 23%

profile of v5, /device:TPU:25, one launch (start us, length us, event | category | flops | bytes accessed | tf_op | source)
XLA Modules:
  0.0 423.4 jit_solution(9031787119266830103)
XLA Ops:
  0.0 4.8 %pack_tiles.10 = (f32[6,4,64,128]{3,2,1,0:T(8,128)}, f32[6,4,64,128]{3,2,1,0:T(8,128)}, f32[6,16,64,128]{3,2,1,0:T(8,128)}) custom-call(s32[1,4,16]{2,1,0:T(4,128)} %sec_ref.39, s32[1,4,16]{2,1,0:T(4,128)} %til_ref.39, f32[16,64,2048]{2,1,0:T(8,128)} %refs_0_.19), custom_call_target="tpu_custom_call" | custom-call | bytes 1024 | tf_op jit(solution)/shard_map/pack_tiles/pallas_call | solution.py:109
  4.9 1.9 collective-permute-start
  7.0 3.2 pack_tiles.11
  10.2 14.6 %collective-permute-done.refs_1_.refs_2_ = f32[6,4,64,128]{3,2,1,0:T(8,128)} collective-permute-done((f32[6,4,64,128]{3,2,1,0:T(8,128)}, f32[6,4,64,128]{3,2,1,0:T(8,128)}, u32[]{:S(2)}, u32[]{:S(2)}) %collective-permute-start) | collective-permute-done | bytes 786464 | tf_op jit(solution)/shard_map/ppermute | solution.py:128
  24.8 1.5 collective-permute-start.3
  26.3 4.7 %split_weights.1.w_ref = bf16[16,256,256]{2,1,0:T(8,128)(2,1)} custom-call(s32[1,4,16]{2,1,0:T(4,128)} %mid_ref.1, f32[32,128,128]{2,1,0:T(8,128)} %w_ref.1), custom_call_target="tpu_custom_call" | custom-call | bytes 1024 | tf_op jit(solution)/shard_map/split_weights/pallas_call | solution.py:52
  31.0 11.2 %collective-permute-done.2.refs_3_ = f32[6,4,64,128]{3,2,1,0:T(8,128)} collective-permute-done((f32[6,4,64,128]{3,2,1,0:T(8,128)}, f32[6,4,64,128]{3,2,1,0:T(8,128)}, u32[]{:S(2)}, u32[]{:S(2)}) %collective-permute-start.2) | collective-permute-done | bytes 786464 | tf_op jit(solution)/shard_map/ppermute | solution.py:128
  42.2 7.1 %drift_chunk.10 = (f32[8,4,64,128]{3,2,1,0:T(8,128)}, f32[8,4,64,128]{3,2,1,0:T(8,128)}, f32[8,128]{1,0:T(8,128)}) custom-call(s32[1,4,16]{2,1,0:T(4,128)} %sec_ref.39, s32[1,4,16]{2,1,0:T(4,128)} %til_ref.39, bf16[16,256,256]{2,1,0:T(8,128)(2,1)} %split_weights.1.w_ref, f32[16,64,2048]{2,1,0:T(8,128)} %refs_0_.19, ...), custom_call_target="tpu_custom_call" | custom-call | bytes 1024 | tf_op jit(solution)/shard_map/drift_chunk/pallas_call | solution.py:202
  49.4 9.1 %collective-permute-done.3.refs_2_.refs_1_ = f32[6,4,64,128]{3,2,1,0:T(8,128)} collective-permute-done((f32[6,4,64,128]{3,2,1,0:T(8,128)}, f32[6,4,64,128]{3,2,1,0:T(8,128)}, u32[]{:S(2)}, u32[]{:S(2)}) %collective-permute-start.3) | collective-permute-done | bytes 786464 | tf_op jit(solution)/shard_map/ppermute | solution.py:128
  58.5 2.0 collective-permute-start.11
  61.6 3.1 pack_tiles.12
  64.7 1.6 collective-permute-start.5
  68.3 12.4 %collective-permute-done.4.refs_3_ = f32[6,4,64,128]{3,2,1,0:T(8,128)} collective-permute-done((f32[6,4,64,128]{3,2,1,0:T(8,128)}, f32[6,4,64,128]{3,2,1,0:T(8,128)}, u32[]{:S(2)}, u32[]{:S(2)}) %collective-permute-start.4) | collective-permute-done | bytes 786464 | tf_op jit(solution)/shard_map/ppermute | solution.py:128
  81.3 1.9 broadcast_in_dim.47.b_ref
  83.1 1.8 broadcast_in_dim.45.a_ref
  84.9 2.5 collective-permute-start.16
  87.4 7.1 %drift_chunk.11 = (f32[8,4,64,128]{3,2,1,0:T(8,128)}, f32[8,4,64,128]{3,2,1,0:T(8,128)}, f32[8,128]{1,0:T(8,128)}) custom-call(s32[1,4,16]{2,1,0:T(4,128)} %sec_ref.39, s32[1,4,16]{2,1,0:T(4,128)} %til_ref.39, bf16[16,256,256]{2,1,0:T(8,128)(2,1)} %split_weights.1.w_ref, f32[16,64,2048]{2,1,0:T(8,128)} %refs_0_.19, ...), custom_call_target="tpu_custom_call" | custom-call | bytes 1024 | tf_op jit(solution)/shard_map/drift_chunk/pallas_call | solution.py:202
  94.5 3.1 collective-permute-done.5.refs_2_.refs_1_
  98.0 1.3 collective-permute-start.19
  100.3 2.9 pack_tiles.13
  104.3 15.5 %collective-permute-done.6.refs_3_ = f32[6,4,64,128]{3,2,1,0:T(8,128)} collective-permute-done((f32[6,4,64,128]{3,2,1,0:T(8,128)}, f32[6,4,64,128]{3,2,1,0:T(8,128)}, u32[]{:S(2)}, u32[]{:S(2)}) %collective-permute-start.6) | collective-permute-done | bytes 786464 | tf_op jit(solution)/shard_map/ppermute | solution.py:128
  119.8 7.1 %drift_chunk.12 = (f32[8,4,64,128]{3,2,1,0:T(8,128)}, f32[8,4,64,128]{3,2,1,0:T(8,128)}, f32[8,128]{1,0:T(8,128)}) custom-call(s32[1,4,16]{2,1,0:T(4,128)} %sec_ref.39, s32[1,4,16]{2,1,0:T(4,128)} %til_ref.39, bf16[16,256,256]{2,1,0:T(8,128)(2,1)} %split_weights.1.w_ref, f32[16,64,2048]{2,1,0:T(8,128)} %refs_0_.19, ...), custom_call_target="tpu_custom_call" | custom-call | bytes 1024 | tf_op jit(solution)/shard_map/drift_chunk/pallas_call | solution.py:202
  127.0 4.8 %collective-permute-start.17 = (f32[8,4,64,128]{3,2,1,0:T(8,128)}, f32[8,4,64,128]{3,2,1,0:T(8,128)}, u32[]{:S(2)}, u32[]{:S(2)}) collective-permute-start(f32[8,4,64,128]{3,2,1,0:T(8,128)} %get-tuple-element.204.refs_1_), channel_id=1, source_target_pairs={{1,3},{2,0},{3,5},{4,2},{5,7},{6,4},{9,11},{10,8},{11,13},{12,10},... | collective-permute-start | bytes 3145736 | tf_op jit(solution)/shard_map/ppermute | solution.py:528
  131.8 1.3 collective-permute-start.20
  133.1 1.4 collective-permute-start.8
  134.4 2.9 pack_tiles.14
  138.5 6.4 %collective-permute-done.8.refs_3_ = f32[6,2,64,128]{3,2,1,0:T(8,128)} collective-permute-done((f32[6,2,64,128]{3,2,1,0:T(8,128)}, f32[6,2,64,128]{3,2,1,0:T(8,128)}, u32[]{:S(2)}, u32[]{:S(2)}) %collective-permute-start.8) | collective-permute-done | bytes 393248 | tf_op jit(solution)/shard_map/ppermute | solution.py:128
  144.9 6.7 %drift_chunk.13 = (f32[8,2,64,128]{3,2,1,0:T(8,128)}, f32[8,2,64,128]{3,2,1,0:T(8,128)}, f32[8,128]{1,0:T(8,128)}) custom-call(s32[1,4,16]{2,1,0:T(4,128)} %sec_ref.39, s32[1,4,16]{2,1,0:T(4,128)} %til_ref.39, bf16[16,256,256]{2,1,0:T(8,128)(2,1)} %split_weights.1.w_ref, f32[16,64,2048]{2,1,0:T(8,128)} %refs_0_.19, ...), custom_call_target="tpu_custom_call" | custom-call | bytes 1024 | tf_op jit(solution)/shard_map/drift_chunk/pallas_call | solution.py:202
  151.6 2.0 collective-permute-done.9.refs_2_
  153.6 5.0 %collective-permute-start.18 = (f32[8,4,64,128]{3,2,1,0:T(8,128)}, f32[8,4,64,128]{3,2,1,0:T(8,128)}, u32[]{:S(2)}, u32[]{:S(2)}) collective-permute-start(f32[8,4,64,128]{3,2,1,0:T(8,128)} %get-tuple-element.206.refs_2_), channel_id=1, source_target_pairs={{1,3},{2,0},{3,5},{4,2},{5,7},{6,4},{9,11},{10,8},{11,13},{12,10},... | collective-permute-start | bytes 3145736 | tf_op jit(solution)/shard_map/ppermute | solution.py:528
  158.6 1.3 collective-permute-start.21
  159.9 2.1 collective-permute-start.10
  162.0 10.0 %collective-permute-done.10.refs_3_ = f32[6,2,64,128]{3,2,1,0:T(8,128)} collective-permute-done((f32[6,2,64,128]{3,2,1,0:T(8,128)}, f32[6,2,64,128]{3,2,1,0:T(8,128)}, u32[]{:S(2)}, u32[]{:S(2)}) %collective-permute-start.10) | collective-permute-done | bytes 393248 | tf_op jit(solution)/shard_map/ppermute | solution.py:128
  172.0 6.7 %drift_chunk.14 = (f32[8,2,64,128]{3,2,1,0:T(8,128)}, f32[8,2,64,128]{3,2,1,0:T(8,128)}, f32[8,128]{1,0:T(8,128)}) custom-call(s32[1,4,16]{2,1,0:T(4,128)} %sec_ref.39, s32[1,4,16]{2,1,0:T(4,128)} %til_ref.39, bf16[16,256,256]{2,1,0:T(8,128)(2,1)} %split_weights.1.w_ref, f32[16,64,2048]{2,1,0:T(8,128)} %refs_0_.19, ...), custom_call_target="tpu_custom_call" | custom-call | bytes 1024 | tf_op jit(solution)/shard_map/drift_chunk/pallas_call | solution.py:202
  178.7 3.3 collective-permute-start.15
  182.0 12.5 %collective-permute-done.15.refs_9_ = f32[8,2,64,128]{3,2,1,0:T(8,128)} collective-permute-done((f32[8,2,64,128]{3,2,1,0:T(8,128)}, f32[8,2,64,128]{3,2,1,0:T(8,128)}, u32[]{:S(2)}, u32[]{:S(2)}) %collective-permute-start.15) | collective-permute-done | bytes 524320 | tf_op jit(solution)/shard_map/ppermute | solution.py:519
  194.5 52.4 %diffuse_tiles.1 = (f32[8,16,64,128]{3,2,1,0:T(8,128)}, f32[8,2,64,128]{3,2,1,0:T(8,128)}, f32[8,4,64,128]{3,2,1,0:T(8,128)}, f32[8,4,64,128]{3,2,1,0:T(8,128)},...) custom-call(f32[8,8,128]{2,1,0:T(8,128)} %broadcast_in_dim.43.rate_ref, f32[56,64,128]{2,1,0:T(8,128)} %broadcast_in_dim.45.a_ref, ...), custom_call_target="tpu_custom_call" | custom-call | bytes 1024 | tf_op jit(solution)/shard_map/diffuse_tiles/pallas_call | solution.py:377
  246.9 1.3 collective-permute-start.22
  248.2 11.8 %collective-permute-done.22.refs_1_ = f32[8,2,64,128]{3,2,1,0:T(8,128)} collective-permute-done((f32[8,2,64,128]{3,2,1,0:T(8,128)}, f32[8,2,64,128]{3,2,1,0:T(8,128)}, u32[]{:S(2)}, u32[]{:S(2)}) %collective-permute-start.22) | collective-permute-done | bytes 524320 | tf_op jit(solution)/shard_map/ppermute | solution.py:557
  261.0 3.6 pack_tiles.16
  264.7 3.7 collective-permute-start.25
  268.3 15.1 %collective-permute-done.23.refs_1_ = f32[8,4,64,128]{3,2,1,0:T(8,128)} collective-permute-done((f32[8,4,64,128]{3,2,1,0:T(8,128)}, f32[8,4,64,128]{3,2,1,0:T(8,128)}, u32[]{:S(2)}, u32[]{:S(2)}) %collective-permute-start.23) | collective-permute-done | bytes 1048608 | tf_op jit(solution)/shard_map/ppermute | solution.py:559
  283.4 3.8 pack_tiles.15
  288.0 4.8 %collective-permute-start.29 = (f32[6,4,64,128]{3,2,1,0:T(8,128)}, f32[6,4,64,128]{3,2,1,0:T(8,128)}, u32[]{:S(2)}, u32[]{:S(2)}) collective-permute-start(f32[6,4,64,128]{3,2,1,0:T(8,128)} %get-tuple-element.234), channel_id=1, source_target_pairs={{0,24},{8,16},{16,8},{24,0},{1,25},{9,17},{17,9},{25,1},{2,26},{10... | collective-permute-start | bytes 2359304 | tf_op jit(solution)/shard_map/ppermute | solution.py:128
  293.2 1.6 collective-permute-done.27.refs_2_
  294.8 6.7 %drift_chunk.15 = (f32[16,64,2048]{2,1,0:T(8,128)}, f32[8,128]{1,0:T(8,128)}) custom-call(s32[1,4,16]{2,1,0:T(4,128)} %sec_ref.39, s32[1,4,16]{2,1,0:T(4,128)} %til_ref.39, bf16[16,256,256]{2,1,0:T(8,128)(2,1)} %split_weights.1.w_ref, f32[8,16,64,128]{3,2,1,0:T(8,128)} %get-tuple-element.211.refs_0_, f32[8,2,64,128]{3,2,1,0:T(8,128)} %collective-permute-done.22.refs_1_, ...), custom_call_target="tpu_custom_call" | custom-call | bytes 1024 | tf_op jit(solution)/shard_map/drift_chunk/pallas_call | solution.py:202
  301.5 8.3 %collective-permute-done.26.refs_1_ = f32[8,4,64,128]{3,2,1,0:T(8,128)} collective-permute-done((f32[8,4,64,128]{3,2,1,0:T(8,128)}, f32[8,4,64,128]{3,2,1,0:T(8,128)}, u32[]{:S(2)}, u32[]{:S(2)}) %collective-permute-start.26) | collective-permute-done | bytes 1048608 | tf_op jit(solution)/shard_map/ppermute | solution.py:572
  309.8 3.8 pack_tiles.17
  313.6 10.8 %collective-permute-done.29.refs_4_ = f32[6,4,64,128]{3,2,1,0:T(8,128)} collective-permute-done((f32[6,4,64,128]{3,2,1,0:T(8,128)}, f32[6,4,64,128]{3,2,1,0:T(8,128)}, u32[]{:S(2)}, u32[]{:S(2)}) %collective-permute-start.29) | collective-permute-done | bytes 786464 | tf_op jit(solution)/shard_map/ppermute | solution.py:128
  325.6 1.5 collective-permute-start.35
  327.1 7.2 %drift_chunk.16 = (f32[16,64,2048]{2,1,0:T(8,128)}, f32[8,128]{1,0:T(8,128)}) custom-call(s32[1,4,16]{2,1,0:T(4,128)} %sec_ref.39, s32[1,4,16]{2,1,0:T(4,128)} %til_ref.39, bf16[16,256,256]{2,1,0:T(8,128)(2,1)} %split_weights.1.w_ref, f32[8,16,64,128]{3,2,1,0:T(8,128)} %get-tuple-element.211.refs_0_, ...), custom_call_target="tpu_custom_call", output_to_operand_aliasing={{0}: (9, {})} | custom-call | bytes 1024 | tf_op jit(solution)/shard_map/drift_chunk/pallas_call | solution.py:202
  334.2 9.0 %collective-permute-done.30.refs_1_ = f32[8,3,64,128]{3,2,1,0:T(8,128)} collective-permute-done((f32[8,3,64,128]{3,2,1,0:T(8,128)}, f32[8,3,64,128]{3,2,1,0:T(8,128)}, u32[]{:S(2)}, u32[]{:S(2)}) %collective-permute-start.30) | collective-permute-done | bytes 786464 | tf_op jit(solution)/shard_map/ppermute | solution.py:572
  343.2 3.7 pack_tiles.18
  347.0 13.4 %collective-permute-done.33.refs_4_ = f32[6,4,64,128]{3,2,1,0:T(8,128)} collective-permute-done((f32[6,4,64,128]{3,2,1,0:T(8,128)}, f32[6,4,64,128]{3,2,1,0:T(8,128)}, u32[]{:S(2)}, u32[]{:S(2)}) %collective-permute-start.33) | collective-permute-done | bytes 786464 | tf_op jit(solution)/shard_map/ppermute | solution.py:128
  361.1 1.2 collective-permute-start.37
  362.3 1.8 collective-permute-start.39
  364.1 7.2 %drift_chunk.17 = (f32[16,64,2048]{2,1,0:T(8,128)}, f32[8,128]{1,0:T(8,128)}) custom-call(s32[1,4,16]{2,1,0:T(4,128)} %sec_ref.39, s32[1,4,16]{2,1,0:T(4,128)} %til_ref.39, bf16[16,256,256]{2,1,0:T(8,128)(2,1)} %split_weights.1.w_ref, f32[8,16,64,128]{3,2,1,0:T(8,128)} %get-tuple-element.211.refs_0_, ...), custom_call_target="tpu_custom_call", output_to_operand_aliasing={{0}: (9, {})} | custom-call | bytes 1024 | tf_op jit(solution)/shard_map/drift_chunk/pallas_call | solution.py:202
  371.3 7.3 %collective-permute-done.34.refs_1_ = f32[8,3,64,128]{3,2,1,0:T(8,128)} collective-permute-done((f32[8,3,64,128]{3,2,1,0:T(8,128)}, f32[8,3,64,128]{3,2,1,0:T(8,128)}, u32[]{:S(2)}, u32[]{:S(2)}) %collective-permute-start.34) | collective-permute-done | bytes 786464 | tf_op jit(solution)/shard_map/ppermute | solution.py:572
  378.6 3.7 pack_tiles.19
  382.4 6.7 %collective-permute-done.39.refs_4_ = f32[6,3,64,128]{3,2,1,0:T(8,128)} collective-permute-done((f32[6,3,64,128]{3,2,1,0:T(8,128)}, f32[6,3,64,128]{3,2,1,0:T(8,128)}, u32[]{:S(2)}, u32[]{:S(2)}) %collective-permute-start.39) | collective-permute-done | bytes 589856 | tf_op jit(solution)/shard_map/ppermute | solution.py:128
  391.2 7.0 %drift_chunk.18 = (f32[16,64,2048]{2,1,0:T(8,128)}, f32[8,128]{1,0:T(8,128)}) custom-call(s32[1,4,16]{2,1,0:T(4,128)} %sec_ref.39, s32[1,4,16]{2,1,0:T(4,128)} %til_ref.39, bf16[16,256,256]{2,1,0:T(8,128)(2,1)} %split_weights.1.w_ref, f32[8,16,64,128]{3,2,1,0:T(8,128)} %get-tuple-element.211.refs_0_, ...), custom_call_target="tpu_custom_call", output_to_operand_aliasing={{0}: (9, {})} | custom-call | bytes 1024 | tf_op jit(solution)/shard_map/drift_chunk/pallas_call | solution.py:202
  398.3 6.8 %collective-permute-done.40.refs_4_ = f32[6,3,64,128]{3,2,1,0:T(8,128)} collective-permute-done((f32[6,3,64,128]{3,2,1,0:T(8,128)}, f32[6,3,64,128]{3,2,1,0:T(8,128)}, u32[]{:S(2)}, u32[]{:S(2)}) %collective-permute-start.40) | collective-permute-done | bytes 589856 | tf_op jit(solution)/shard_map/ppermute | solution.py:128
  405.0 11.3 %collective-permute-done.38.refs_3_ = f32[6,3,64,128]{3,2,1,0:T(8,128)} collective-permute-done((f32[6,3,64,128]{3,2,1,0:T(8,128)}, f32[6,3,64,128]{3,2,1,0:T(8,128)}, u32[]{:S(2)}, u32[]{:S(2)}) %collective-permute-start.38) | collective-permute-done | bytes 589856 | tf_op jit(solution)/shard_map/ppermute | solution.py:128
  416.4 7.0 %drift_chunk.19 = (f32[16,64,2048]{2,1,0:T(8,128)}, f32[8,128]{1,0:T(8,128)}) custom-call(s32[1,4,16]{2,1,0:T(4,128)} %sec_ref.39, s32[1,4,16]{2,1,0:T(4,128)} %til_ref.39, bf16[16,256,256]{2,1,0:T(8,128)(2,1)} %split_weights.1.w_ref, f32[8,16,64,128]{3,2,1,0:T(8,128)} %get-tuple-element.211.refs_0_, ...), custom_call_target="tpu_custom_call", output_to_operand_aliasing={{0}: (9, {})} | custom-call | bytes 1024 | tf_op jit(solution)/shard_map/drift_chunk/pallas_call | solution.py:202
  (58 shorter events, 13.8 us)
Async XLA Ops:
  4.8 37.4 %collective-permute-start.1 = (f32[6,16,64,128]{3,2,1,0:T(8,128)}, f32[6,16,64,128]{3,2,1,0:T(8,128)}, u32[]{:S(2)}, u32[]{:S(2)}) collective-permute-start(f32[6,16,64,128]{3,2,1,0:T(8,128)} %get-tuple-element.142), channel_id=1, source_target_pairs={{0,8},{8,0},{16,24},{24,16},{1,9},{9,1},{17,25},{25,17},{2,10},{10... | collective-permute-start | bytes 9437192 | tf_op jit(solution)/shard_map/ppermute | solution.py:128
  4.9 19.9 %collective-permute-start = (f32[6,4,64,128]{3,2,1,0:T(8,128)}, f32[6,4,64,128]{3,2,1,0:T(8,128)}, u32[]{:S(2)}, u32[]{:S(2)}) collective-permute-start(f32[6,4,64,128]{3,2,1,0:T(8,128)} %get-tuple-element.138.refs_1_), channel_id=1, source_target_pairs={{0,16},{8,24},{16,0},{24,8},{1,17},{9,25},{17,1},{25,9},{2,18},{10... | collective-permute-start | bytes 2359304 | tf_op jit(solution)/shard_map/ppermute | solution.py:128
  6.8 35.4 %collective-permute-start.2 = (f32[6,4,64,128]{3,2,1,0:T(8,128)}, f32[6,4,64,128]{3,2,1,0:T(8,128)}, u32[]{:S(2)}, u32[]{:S(2)}) collective-permute-start(f32[6,4,64,128]{3,2,1,0:T(8,128)} %get-tuple-element.144), channel_id=1, source_target_pairs={{0,24},{8,16},{16,8},{24,0},{1,25},{9,17},{17,9},{25,1},{2,26},{10... | collective-permute-start | bytes 2359304 | tf_op jit(solution)/shard_map/ppermute | solution.py:128
  24.8 33.7 %collective-permute-start.3 = (f32[6,4,64,128]{3,2,1,0:T(8,128)}, f32[6,4,64,128]{3,2,1,0:T(8,128)}, u32[]{:S(2)}, u32[]{:S(2)}) collective-permute-start(f32[6,4,64,128]{3,2,1,0:T(8,128)} %get-tuple-element.148), channel_id=1, source_target_pairs={{0,16},{8,24},{16,0},{24,8},{1,17},{9,25},{17,1},{25,9},{2,18},{10... | collective-permute-start | bytes 2359304 | tf_op jit(solution)/shard_map/ppermute | solution.py:128
  58.5 8.6 %copy-start = (f32[128,64]{0,1:T(8,128)S(1)}, f32[128,64]{0,1:T(8,128)}, u32[]{:S(2)}) copy-start(f32[128,64]{0,1:T(8,128)} %param.16) | copy-start | bytes 98308
  58.5 8.6 %copy-start.1 = (f32[128,64]{0,1:T(8,128)S(1)}, f32[128,64]{0,1:T(8,128)}, u32[]{:S(2)}) copy-start(f32[128,64]{0,1:T(8,128)} %param.17) | copy-start | bytes 98308
  58.5 39.1 %collective-permute-start.11 = (f32[8,4,64,128]{3,2,1,0:T(8,128)}, f32[8,4,64,128]{3,2,1,0:T(8,128)}, u32[]{:S(2)}, u32[]{:S(2)}) collective-permute-start(f32[8,4,64,128]{3,2,1,0:T(8,128)} %get-tuple-element.188), channel_id=1, source_target_pairs={{0,1},{1,0},{2,3},{3,2},{4,5},{5,4},{6,7},{7,6},{8,9},{9,8},{10,11... | collective-permute-start | bytes 3145736 | tf_op jit(solution)/shard_map/ppermute | solution.py:519
  60.6 20.1 %collective-permute-start.4 = (f32[6,4,64,128]{3,2,1,0:T(8,128)}, f32[6,4,64,128]{3,2,1,0:T(8,128)}, u32[]{:S(2)}, u32[]{:S(2)}) collective-permute-start(f32[6,4,64,128]{3,2,1,0:T(8,128)} %get-tuple-element.152), channel_id=1, source_target_pairs={{0,24},{8,16},{16,8},{24,0},{1,25},{9,17},{17,9},{25,1},{2,26},{10... | collective-permute-start | bytes 2359304 | tf_op jit(solution)/shard_map/ppermute | solution.py:128
  64.7 32.9 %collective-permute-start.5 = (f32[6,4,64,128]{3,2,1,0:T(8,128)}, f32[6,4,64,128]{3,2,1,0:T(8,128)}, u32[]{:S(2)}, u32[]{:S(2)}) collective-permute-start(f32[6,4,64,128]{3,2,1,0:T(8,128)} %get-tuple-element.163), channel_id=1, source_target_pairs={{0,16},{8,24},{16,0},{24,8},{1,17},{9,25},{17,1},{25,9},{2,18},{10... | collective-permute-start | bytes 2359304 | tf_op jit(solution)/shard_map/ppermute | solution.py:128
  84.9 42.1 %collective-permute-start.16 = (f32[8,4,64,128]{3,2,1,0:T(8,128)}, f32[8,4,64,128]{3,2,1,0:T(8,128)}, u32[]{:S(2)}, u32[]{:S(2)}) collective-permute-start(f32[8,4,64,128]{3,2,1,0:T(8,128)} %get-tuple-element.201.refs_0_), channel_id=1, source_target_pairs={{1,3},{2,0},{3,5},{4,2},{5,7},{6,4},{9,11},{10,8},{11,13},{12,10},... | collective-permute-start | bytes 3145736 | tf_op jit(solution)/shard_map/ppermute | solution.py:528
  97.6 34.2 %collective-permute-start.12 = (f32[8,4,64,128]{3,2,1,0:T(8,128)}, f32[8,4,64,128]{3,2,1,0:T(8,128)}, u32[]{:S(2)}, u32[]{:S(2)}) collective-permute-start(f32[8,4,64,128]{3,2,1,0:T(8,128)} %get-tuple-element.191), channel_id=1, source_target_pairs={{0,1},{1,0},{2,3},{3,2},{4,5},{5,4},{6,7},{7,6},{8,9},{9,8},{10,11... | collective-permute-start | bytes 3145736 | tf_op jit(solution)/shard_map/ppermute | solution.py:519
  98.0 33.8 %collective-permute-start.19 = (f32[8,4,64,128]{3,2,1,0:T(8,128)}, f32[8,4,64,128]{3,2,1,0:T(8,128)}, u32[]{:S(2)}, u32[]{:S(2)}) collective-permute-start(f32[8,4,64,128]{3,2,1,0:T(8,128)} %collective-permute-done.11.refs_5_), channel_id=1, source_target_pairs={{0,2},{2,4},{3,1},{4,6},{5,3},{7,5},{8,10},{10,12},{11,9},{12,14},... | collective-permute-start | bytes 3145736 | tf_op jit(solution)/shard_map/ppermute | solution.py:524
  99.3 20.5 %collective-permute-start.6 = (f32[6,4,64,128]{3,2,1,0:T(8,128)}, f32[6,4,64,128]{3,2,1,0:T(8,128)}, u32[]{:S(2)}, u32[]{:S(2)}) collective-permute-start(f32[6,4,64,128]{3,2,1,0:T(8,128)} %get-tuple-element.167), channel_id=1, source_target_pairs={{0,24},{8,16},{16,8},{24,0},{1,25},{9,17},{17,9},{25,1},{2,26},{10... | collective-permute-start | bytes 2359304 | tf_op jit(solution)/shard_map/ppermute | solution.py:128
  103.2 28.5 %collective-permute-start.7 = (f32[6,2,64,128]{3,2,1,0:T(8,128)}, f32[6,2,64,128]{3,2,1,0:T(8,128)}, u32[]{:S(2)}, u32[]{:S(2)}) collective-permute-start(f32[6,2,64,128]{3,2,1,0:T(8,128)} %get-tuple-element.173), channel_id=1, source_target_pairs={{0,16},{8,24},{16,0},{24,8},{1,17},{9,25},{17,1},{25,9},{2,18},{10... | collective-permute-start | bytes 1179656 | tf_op jit(solution)/shard_map/ppermute | solution.py:128
  127.0 26.6 %collective-permute-start.17 = (f32[8,4,64,128]{3,2,1,0:T(8,128)}, f32[8,4,64,128]{3,2,1,0:T(8,128)}, u32[]{:S(2)}, u32[]{:S(2)}) collective-permute-start(f32[8,4,64,128]{3,2,1,0:T(8,128)} %get-tuple-element.204.refs_1_), channel_id=1, source_target_pairs={{1,3},{2,0},{3,5},{4,2},{5,7},{6,4},{9,11},{10,8},{11,13},{12,10},... | collective-permute-start | bytes 3145736 | tf_op jit(solution)/shard_map/ppermute | solution.py:528
  131.8 26.8 %collective-permute-start.13 = (f32[8,4,64,128]{3,2,1,0:T(8,128)}, f32[8,4,64,128]{3,2,1,0:T(8,128)}, u32[]{:S(2)}, u32[]{:S(2)}) collective-permute-start(f32[8,4,64,128]{3,2,1,0:T(8,128)} %get-tuple-element.194), channel_id=1, source_target_pairs={{0,1},{1,0},{2,3},{3,2},{4,5},{5,4},{6,7},{7,6},{8,9},{9,8},{10,11... | collective-permute-start | bytes 3145736 | tf_op jit(solution)/shard_map/ppermute | solution.py:519
  131.8 26.8 %collective-permute-start.20 = (f32[8,4,64,128]{3,2,1,0:T(8,128)}, f32[8,4,64,128]{3,2,1,0:T(8,128)}, u32[]{:S(2)}, u32[]{:S(2)}) collective-permute-start(f32[8,4,64,128]{3,2,1,0:T(8,128)} %collective-permute-done.12.refs_6_), channel_id=1, source_target_pairs={{0,2},{2,4},{3,1},{4,6},{5,3},{7,5},{8,10},{10,12},{11,9},{12,14},... | collective-permute-start | bytes 3145736 | tf_op jit(solution)/shard_map/ppermute | solution.py:524
  133.1 11.8 %collective-permute-start.8 = (f32[6,2,64,128]{3,2,1,0:T(8,128)}, f32[6,2,64,128]{3,2,1,0:T(8,128)}, u32[]{:S(2)}, u32[]{:S(2)}) collective-permute-start(f32[6,2,64,128]{3,2,1,0:T(8,128)} %get-tuple-element.177), channel_id=1, source_target_pairs={{0,24},{8,16},{16,8},{24,0},{1,25},{9,17},{17,9},{25,1},{2,26},{10... | collective-permute-start | bytes 1179656 | tf_op jit(solution)/shard_map/ppermute | solution.py:128
  137.4 16.2 %collective-permute-start.9 = (f32[6,2,64,128]{3,2,1,0:T(8,128)}, f32[6,2,64,128]{3,2,1,0:T(8,128)}, u32[]{:S(2)}, u32[]{:S(2)}) collective-permute-start(f32[6,2,64,128]{3,2,1,0:T(8,128)} %get-tuple-element.182), channel_id=1, source_target_pairs={{0,16},{8,24},{16,0},{24,8},{1,17},{9,25},{17,1},{25,9},{2,18},{10... | collective-permute-start | bytes 1179656 | tf_op jit(solution)/shard_map/ppermute | solution.py:128
  153.6 28.4 %collective-permute-start.18 = (f32[8,4,64,128]{3,2,1,0:T(8,128)}, f32[8,4,64,128]{3,2,1,0:T(8,128)}, u32[]{:S(2)}, u32[]{:S(2)}) collective-permute-start(f32[8,4,64,128]{3,2,1,0:T(8,128)} %get-tuple-element.206.refs_2_), channel_id=1, source_target_pairs={{1,3},{2,0},{3,5},{4,2},{5,7},{6,4},{9,11},{10,8},{11,13},{12,10},... | collective-permute-start | bytes 3145736 | tf_op jit(solution)/shard_map/ppermute | solution.py:528
  158.6 20.1 %collective-permute-start.14 = (f32[8,2,64,128]{3,2,1,0:T(8,128)}, f32[8,2,64,128]{3,2,1,0:T(8,128)}, u32[]{:S(2)}, u32[]{:S(2)}) collective-permute-start(f32[8,2,64,128]{3,2,1,0:T(8,128)} %get-tuple-element.197), channel_id=1, source_target_pairs={{0,1},{1,0},{2,3},{3,2},{4,5},{5,4},{6,7},{7,6},{8,9},{9,8},{10,11... | collective-permute-start | bytes 1572872 | tf_op jit(solution)/shard_map/ppermute | solution.py:519
  158.6 35.9 %collective-permute-start.21 = (f32[8,4,64,128]{3,2,1,0:T(8,128)}, f32[8,4,64,128]{3,2,1,0:T(8,128)}, u32[]{:S(2)}, u32[]{:S(2)}) collective-permute-start(f32[8,4,64,128]{3,2,1,0:T(8,128)} %collective-permute-done.13.refs_7_), channel_id=1, source_target_pairs={{0,2},{2,4},{3,1},{4,6},{5,3},{7,5},{8,10},{10,12},{11,9},{12,14},... | collective-permute-start | bytes 3145736 | tf_op jit(solution)/shard_map/ppermute | solution.py:524
  159.9 12.1 %collective-permute-start.10 = (f32[6,2,64,128]{3,2,1,0:T(8,128)}, f32[6,2,64,128]{3,2,1,0:T(8,128)}, u32[]{:S(2)}, u32[]{:S(2)}) collective-permute-start(f32[6,2,64,128]{3,2,1,0:T(8,128)} %get-tuple-element.184), channel_id=1, source_target_pairs={{0,24},{8,16},{16,8},{24,0},{1,25},{9,17},{17,9},{25,1},{2,26},{10... | collective-permute-start | bytes 1179656 | tf_op jit(solution)/shard_map/ppermute | solution.py:128
  178.7 15.8 %collective-permute-start.15 = (f32[8,2,64,128]{3,2,1,0:T(8,128)}, f32[8,2,64,128]{3,2,1,0:T(8,128)}, u32[]{:S(2)}, u32[]{:S(2)}) collective-permute-start(f32[8,2,64,128]{3,2,1,0:T(8,128)} %get-tuple-element.199), channel_id=1, source_target_pairs={{0,1},{1,0},{2,3},{3,2},{4,5},{5,4},{6,7},{7,6},{8,9},{9,8},{10,11... | collective-permute-start | bytes 1572872 | tf_op jit(solution)/shard_map/ppermute | solution.py:519
  246.9 13.1 %collective-permute-start.22 = (f32[8,2,64,128]{3,2,1,0:T(8,128)}, f32[8,2,64,128]{3,2,1,0:T(8,128)}, u32[]{:S(2)}, u32[]{:S(2)}) collective-permute-start(f32[8,2,64,128]{3,2,1,0:T(8,128)} %get-tuple-element.216), channel_id=1, source_target_pairs={{0,1},{1,0},{2,3},{3,2},{4,5},{5,4},{6,7},{7,6},{8,9},{9,8},{10,11... | collective-permute-start | bytes 1572872 | tf_op jit(solution)/shard_map/ppermute | solution.py:557
  260.0 23.4 %collective-permute-start.23 = (f32[8,4,64,128]{3,2,1,0:T(8,128)}, f32[8,4,64,128]{3,2,1,0:T(8,128)}, u32[]{:S(2)}, u32[]{:S(2)}) collective-permute-start(f32[8,4,64,128]{3,2,1,0:T(8,128)} %get-tuple-element.217), channel_id=1, source_target_pairs={{0,1},{1,0},{2,3},{3,2},{4,5},{5,4},{6,7},{7,6},{8,9},{9,8},{10,11... | collective-permute-start | bytes 3145736 | tf_op jit(solution)/shard_map/ppermute | solution.py:559
  264.6 22.6 %collective-permute-start.24 = (f32[6,2,64,128]{3,2,1,0:T(8,128)}, f32[6,2,64,128]{3,2,1,0:T(8,128)}, u32[]{:S(2)}, u32[]{:S(2)}) collective-permute-start(f32[6,2,64,128]{3,2,1,0:T(8,128)} %get-tuple-element.220), channel_id=1, source_target_pairs={{0,16},{8,24},{16,0},{24,8},{1,17},{9,25},{17,1},{25,9},{2,18},{10... | collective-permute-start | bytes 1179656 | tf_op jit(solution)/shard_map/ppermute | solution.py:128
  264.7 22.6 %collective-permute-start.25 = (f32[6,2,64,128]{3,2,1,0:T(8,128)}, f32[6,2,64,128]{3,2,1,0:T(8,128)}, u32[]{:S(2)}, u32[]{:S(2)}) collective-permute-start(f32[6,2,64,128]{3,2,1,0:T(8,128)} %get-tuple-element.223), channel_id=1, source_target_pairs={{0,24},{8,16},{16,8},{24,0},{1,25},{9,17},{17,9},{25,1},{2,26},{10... | collective-permute-start | bytes 1179656 | tf_op jit(solution)/shard_map/ppermute | solution.py:128
  287.2 22.6 %collective-permute-start.26 = (f32[8,4,64,128]{3,2,1,0:T(8,128)}, f32[8,4,64,128]{3,2,1,0:T(8,128)}, u32[]{:S(2)}, u32[]{:S(2)}) collective-permute-start(f32[8,4,64,128]{3,2,1,0:T(8,128)} %get-tuple-element.225), channel_id=1, source_target_pairs={{0,1},{1,0},{2,3},{3,2},{4,5},{5,4},{6,7},{7,6},{8,9},{9,8},{10,11... | collective-permute-start | bytes 3145736 | tf_op jit(solution)/shard_map/ppermute | solution.py:572
  288.0 25.6 %collective-permute-start.28 = (f32[6,4,64,128]{3,2,1,0:T(8,128)}, f32[6,4,64,128]{3,2,1,0:T(8,128)}, u32[]{:S(2)}, u32[]{:S(2)}) collective-permute-start(f32[6,4,64,128]{3,2,1,0:T(8,128)} %get-tuple-element.231), channel_id=1, source_target_pairs={{0,16},{8,24},{16,0},{24,8},{1,17},{9,25},{17,1},{25,9},{2,18},{10... | collective-permute-start | bytes 2359304 | tf_op jit(solution)/shard_map/ppermute | solution.py:128
  288.0 36.4 %collective-permute-start.29 = (f32[6,4,64,128]{3,2,1,0:T(8,128)}, f32[6,4,64,128]{3,2,1,0:T(8,128)}, u32[]{:S(2)}, u32[]{:S(2)}) collective-permute-start(f32[6,4,64,128]{3,2,1,0:T(8,128)} %get-tuple-element.234), channel_id=1, source_target_pairs={{0,24},{8,16},{16,8},{24,0},{1,25},{9,17},{17,9},{25,1},{2,26},{10... | collective-permute-start | bytes 2359304 | tf_op jit(solution)/shard_map/ppermute | solution.py:128
  292.7 2.1 collective-permute-start.27
  292.7 34.3 %collective-permute-start.31 = (f32[6,4,64,128]{3,2,1,0:T(8,128)}, f32[6,4,64,128]{3,2,1,0:T(8,128)}, u32[]{:S(2)}, u32[]{:S(2)}) collective-permute-start(f32[6,4,64,128]{3,2,1,0:T(8,128)} %get-tuple-element.238), channel_id=1, source_target_pairs={{0,8},{8,0},{16,24},{24,16},{1,9},{9,1},{17,25},{25,17},{2,10},{10... | collective-permute-start | bytes 2359304 | tf_op jit(solution)/shard_map/ppermute | solution.py:128
  324.4 18.8 %collective-permute-start.30 = (f32[8,3,64,128]{3,2,1,0:T(8,128)}, f32[8,3,64,128]{3,2,1,0:T(8,128)}, u32[]{:S(2)}, u32[]{:S(2)}) collective-permute-start(f32[8,3,64,128]{3,2,1,0:T(8,128)} %get-tuple-element.236), channel_id=1, source_target_pairs={{0,1},{1,0},{2,3},{3,2},{4,5},{5,4},{6,7},{7,6},{8,9},{9,8},{10,11... | collective-permute-start | bytes 2359304 | tf_op jit(solution)/shard_map/ppermute | solution.py:572
  325.2 21.8 %collective-permute-start.32 = (f32[6,4,64,128]{3,2,1,0:T(8,128)}, f32[6,4,64,128]{3,2,1,0:T(8,128)}, u32[]{:S(2)}, u32[]{:S(2)}) collective-permute-start(f32[6,4,64,128]{3,2,1,0:T(8,128)} %get-tuple-element.244), channel_id=1, source_target_pairs={{0,16},{8,24},{16,0},{24,8},{1,17},{9,25},{17,1},{25,9},{2,18},{10... | collective-permute-start | bytes 2359304 | tf_op jit(solution)/shard_map/ppermute | solution.py:128
  325.2 35.2 %collective-permute-start.33 = (f32[6,4,64,128]{3,2,1,0:T(8,128)}, f32[6,4,64,128]{3,2,1,0:T(8,128)}, u32[]{:S(2)}, u32[]{:S(2)}) collective-permute-start(f32[6,4,64,128]{3,2,1,0:T(8,128)} %get-tuple-element.247), channel_id=1, source_target_pairs={{0,24},{8,16},{16,8},{24,0},{1,25},{9,17},{17,9},{25,1},{2,26},{10... | collective-permute-start | bytes 2359304 | tf_op jit(solution)/shard_map/ppermute | solution.py:128
  325.6 38.5 %collective-permute-start.35 = (f32[6,4,64,128]{3,2,1,0:T(8,128)}, f32[6,4,64,128]{3,2,1,0:T(8,128)}, u32[]{:S(2)}, u32[]{:S(2)}) collective-permute-start(f32[6,4,64,128]{3,2,1,0:T(8,128)} %get-tuple-element.251), channel_id=1, source_target_pairs={{0,8},{8,0},{16,24},{24,16},{1,9},{9,1},{17,25},{25,17},{2,10},{10... | collective-permute-start | bytes 2359304 | tf_op jit(solution)/shard_map/ppermute | solution.py:128
  360.4 18.2 %collective-permute-start.34 = (f32[8,3,64,128]{3,2,1,0:T(8,128)}, f32[8,3,64,128]{3,2,1,0:T(8,128)}, u32[]{:S(2)}, u32[]{:S(2)}) collective-permute-start(f32[8,3,64,128]{3,2,1,0:T(8,128)} %get-tuple-element.249), channel_id=1, source_target_pairs={{0,1},{1,0},{2,3},{3,2},{4,5},{5,4},{6,7},{7,6},{8,9},{9,8},{10,11... | collective-permute-start | bytes 2359304 | tf_op jit(solution)/shard_map/ppermute | solution.py:572
  361.1 21.3 %collective-permute-start.37 = (f32[6,3,64,128]{3,2,1,0:T(8,128)}, f32[6,3,64,128]{3,2,1,0:T(8,128)}, u32[]{:S(2)}, u32[]{:S(2)}) collective-permute-start(f32[6,3,64,128]{3,2,1,0:T(8,128)} %get-tuple-element.258), channel_id=1, source_target_pairs={{0,16},{8,24},{16,0},{24,8},{1,17},{9,25},{17,1},{25,9},{2,18},{10... | collective-permute-start | bytes 1769480 | tf_op jit(solution)/shard_map/ppermute | solution.py:128
  362.3 26.8 %collective-permute-start.39 = (f32[6,3,64,128]{3,2,1,0:T(8,128)}, f32[6,3,64,128]{3,2,1,0:T(8,128)}, u32[]{:S(2)}, u32[]{:S(2)}) collective-permute-start(f32[6,3,64,128]{3,2,1,0:T(8,128)} %get-tuple-element.261), channel_id=1, source_target_pairs={{0,24},{8,16},{16,8},{24,0},{1,25},{9,17},{17,9},{25,1},{2,26},{10... | collective-permute-start | bytes 1769480 | tf_op jit(solution)/shard_map/ppermute | solution.py:128
  364.1 27.1 %collective-permute-start.41 = (f32[6,3,64,128]{3,2,1,0:T(8,128)}, f32[6,3,64,128]{3,2,1,0:T(8,128)}, u32[]{:S(2)}, u32[]{:S(2)}) collective-permute-start(f32[6,3,64,128]{3,2,1,0:T(8,128)} %get-tuple-element.264), channel_id=1, source_target_pairs={{0,8},{8,0},{16,24},{24,16},{1,9},{9,1},{17,25},{25,17},{2,10},{10... | collective-permute-start | bytes 1769480 | tf_op jit(solution)/shard_map/ppermute | solution.py:128
  389.1 15.9 %collective-permute-start.40 = (f32[6,3,64,128]{3,2,1,0:T(8,128)}, f32[6,3,64,128]{3,2,1,0:T(8,128)}, u32[]{:S(2)}, u32[]{:S(2)}) collective-permute-start(f32[6,3,64,128]{3,2,1,0:T(8,128)} %get-tuple-element.262), channel_id=1, source_target_pairs={{0,24},{8,16},{16,8},{24,0},{1,25},{9,17},{17,9},{25,1},{2,26},{10... | collective-permute-start | bytes 1769480 | tf_op jit(solution)/shard_map/ppermute | solution.py:128
  390.1 26.2 %collective-permute-start.38 = (f32[6,3,64,128]{3,2,1,0:T(8,128)}, f32[6,3,64,128]{3,2,1,0:T(8,128)}, u32[]{:S(2)}, u32[]{:S(2)}) collective-permute-start(f32[6,3,64,128]{3,2,1,0:T(8,128)} %get-tuple-element.259), channel_id=1, source_target_pairs={{0,16},{8,24},{16,0},{24,8},{1,17},{9,25},{17,1},{25,9},{2,18},{10... | collective-permute-start | bytes 1769480 | tf_op jit(solution)/shard_map/ppermute | solution.py:128
  390.4 26.0 %collective-permute-start.36 = (f32[6,3,64,128]{3,2,1,0:T(8,128)}, f32[6,3,64,128]{3,2,1,0:T(8,128)}, u32[]{:S(2)}, u32[]{:S(2)}) collective-permute-start(f32[6,3,64,128]{3,2,1,0:T(8,128)} %get-tuple-element.256), channel_id=1, source_target_pairs={{0,8},{8,0},{16,24},{24,16},{1,9},{9,1},{17,25},{25,17},{2,10},{10... | collective-permute-start | bytes 1769480 | tf_op jit(solution)/shard_map/ppermute | solution.py:128

commit v6 on v5

--- a/solution.py
+++ b/solution.py
@@ -64,9 +64,12 @@
     )(matrix_id, cubic_weights)
 
 
-def pack_kernel(offsets, finds, n_arrays, sec_ref, til_ref, *refs):
+def pack_kernel(offsets, finds, n_far, n_arrays, sec_ref, til_ref, *refs):
     tiles, n = sec_ref.shape[2], len(offsets)
-    sends, rooms = refs[-2 * n - 2 : -n - 2], refs[-n - 2 : -2]
+    near = n - n_far
+    sends, rooms = refs[-n - 2 - (near + (n_far > 0)) : -n - 2], refs[-n - 2 : -2]
+    if n_far:
+        sends = [sends[0].at[i] for i in range(n_far)] + list(sends[1:])
     in_sems, out_sems = refs[-2:]
     me = lax.axis_index("sector")
     counts = []
@@ -106,11 +109,13 @@
 def pack(groups, cap, tables, arrays, after=()):
     n = len(groups)
     offsets, finds, shapes = zip(*groups)
+    n_far = sum(d > 1 for d in offsets)
+    outs = [(n_far, cap) + shapes[0]] * (n_far > 0) + [(cap,) + shape for shape in shapes[n_far:]]
     return pl.pallas_call(
-        functools.partial(pack_kernel, offsets, finds, len(arrays)),
-        out_shape=[jax.ShapeDtypeStruct((cap,) + shape, F32) for shape in shapes],
+        functools.partial(pack_kernel, offsets, finds, n_far, len(arrays)),
+        out_shape=[jax.ShapeDtypeStruct(out, F32) for out in outs],
         in_specs=[SMEM, SMEM] + [ANY] * (len(arrays) + len(after)),
-        out_specs=[ANY] * n,
+        out_specs=[ANY] * len(outs),
         scratch_shapes=[
             *[pltpu.VMEM((cap,) + shape, F32) for shape in shapes],
             pltpu.SemaphoreType.DMA((n, cap)),
@@ -130,11 +135,12 @@
     ]
 
 
-def queue(came, sends, offsets):
-    sends = list(sends)
-    for i, send in enumerate(sends):
-        (sends[i],), (came[-1][i],) = in_turn([send], [came[-1][i]])
-    came.append(sector_exchange(sends, offsets))
+def far_queue(came, send):
+    if len(came) > 1:
+        (send,), (came[-2][0],) = in_turn([send], [came[-2][0]])
+    sectors = lax.axis_size("sector")
+    whole = lax.ppermute(send, "sector", [(s, s ^ 2) for s in range(sectors)])
+    came.append([whole, lax.ppermute(whole[1], "sector", [(s, s ^ 1) for s in range(sectors)])])
 
 
 def in_turn(later, earlier):
@@ -175,7 +181,7 @@
 
     lax.fori_loop(0, tiles, fetch, (jnp.int32(0),) * (sectors - 1))
 
-    @pl.loop(0, tiles)
+    @pl.loop(0, tiles, unroll=4)
     def _(t):
         pltpu.make_async_copy(taken.at[t], taken.at[t], in_sems.at[t]).wait()
         value = taken[t].reshape(rows, side)
@@ -422,9 +428,10 @@
     tiles = cell_count // side
     half = tiles // 2
     quarter = block // 4
+    first_steps = (quarter, quarter, quarter, quarter // 2, quarter - quarter // 2)
     halo_chunks = PASSES // quarter
-    first_steps = (quarter, quarter, quarter, quarter // 2, quarter - quarter // 2)
-    last_steps = (quarter // 2, quarter, quarter, quarter - quarter // 4, block - 3 * quarter - quarter // 2 + quarter // 4)
+    less = quarter - quarter // 4
+    last_steps = (less, quarter, block - quarter - 2 * less, less)
     cap = slots(tiles, sectors)
     tables = (source_sector, source_tile)
     near, far = [1], list(range(2, sectors))
@@ -475,6 +482,8 @@
             return lambda t: [(t >= 0, lambda: field.at[:, :, at_lanes(t)])]
 
         def receive(came, other, slot, first_of=first_of, step=step):
+            if other == 2:
+                return came.at[0, slot]
             return came.at[slot, pl.ds(first_of(), step)] if other == 1 else came.at[slot]
 
         def place(kept, sent):
@@ -497,23 +506,23 @@
 
     sends = pack_first(0, ())
     beside = sector_exchange(sends[-1:], near)
-    came = [sector_exchange(sends[:-1], far)]
-    after_pack, token = sends[0], None
+    came = []
+    far_queue(came, sends[0])
+    token, tokens = None, []
     for k, (start, step, find, receive, place) in enumerate(packed):
         if k + 1 < len(packed):
-            queue(came, pack_first(k + 1, (after_pack,)), far)
-            after_pack = came[k][0]
+            before = tokens[k - 1] if k else sends[0]
+            far_queue(came, pack_first(k + 1, (before,))[0])
         if k == 1:
             came[k], (rate, a, b) = in_turn(came[k], [rate, a, b])
         part = jax.ShapeDtypeStruct((half, step, pitches, side), F32)
         piece = (step, pitches, side)
-        after = () if token is None else (token,)
+        after = [] if token is None else [token]
         kept, sent, token = drift(
             find, place, receive, tables, weights, [density], beside + came[k], [part, part], piece, after
         )
+        tokens.append(token)
         own.append(kept)
-        if k + 1 < len(packed):
-            (sent, kept), (came[k + 1][0],) = in_turn([sent, kept], [came[k + 1][0]])
         if k > 0:
             (sent,), (got[k - 1],) = in_turn([sent], [got[k - 1]])
         got.append(lax.ppermute(sent, "inner", swap))
@@ -546,29 +555,30 @@
         start += step
 
     def receive_slot(came, other, slot):
-        return came.at[slot]
+        return came.at[0, slot] if other == 2 else came.at[slot]
 
     def pack_last(k, after):
         find, _, piece = ready[k]
-        sends = pack([(d, find, piece) for d in near + far], cap, tables, [kept, backs[k]], after)
-        return sends[:1], sends[1:]
+        sends = pack([(d, find, piece) for d in far + near], cap, tables, [kept, backs[k]], after)
+        return sends[1:], sends[0]
 
     whole = [jax.ShapeDtypeStruct(density.shape, F32)]
     backs = [lax.ppermute(returns[0], "inner", swap)]
     (last,), (backs[0],) = in_turn([returns[1]], [backs[0]])
     backs.append(lax.ppermute(last, "inner", swap))
     sends, far_sends = pack_last(0, ())
-    came = [sector_exchange(far_sends, far)]
+    came = []
+    far_queue(came, far_sends)
     beside = sector_exchange(sends, near)
     token = None
     for k, (find, place, piece) in enumerate(ready):
         after = [] if token is None else [token]
         if k + 1 < len(ready):
             sends, far_sends = pack_last(k + 1, after)
-            queue(came, far_sends, far)
+            far_queue(came, far_sends)
             beside_next = sector_exchange(sends, near)
         if k + 2 < len(ready):
-            (last,), (backs[k + 1], *came[k]) = in_turn([returns[k + 2]], [backs[k + 1], *came[k]])
+            (last,), (backs[k + 1], came[k][0]) = in_turn([returns[k + 2]], [backs[k + 1], came[k][0]])
             backs.append(lax.ppermute(last, "inner", swap))
         *out, token = drift(
             find, place, receive_slot, tables, weights, [kept, backs[k]], beside + came[k], whole, piece, after, out
@@ -677,9 +687,9 @@
     block = energies // inner
     tiles = cells // sectors // side
     return (
-        sectors & (sectors - 1) == 0
+        sectors == 4
         and inner % 2 == 0
-        and tiles % 2 == 0
+        and tiles % 4 == 0
         and pitches % 16 == 0
         and side % 128 == 0
         and block % 16 == 0

time: 427 us -> 426 us (level)
  local copies, waits for them, and re-layouts: 4.51 us -> 18.2 us
  Pallas kernels: 162 us -> 156 us
  starting transfers between devices: 55.4 us -> 49.7 us
    ppermute x26 -> x5, waiting for transfers between devices: 135 us -> 0.01 us  [sector_exchange(): lax.ppermute(send, 'sector', [(s, s ^ d) for s in range(sectors)])]
    ppermute x0 -> x18, waiting for transfers between devices: none -> 115 us  [the longest x9 110 us: far_queue(): whole = lax.ppermute(send, 'sector', [(s, s ^ 2) for s in range(sectors)])]
    ppermute x26 -> x5, starting transfers between devices: 29.1 us -> 8.57 us  [sector_exchange(): lax.ppermute(send, 'sector', [(s, s ^ d) for s in range(sectors)])]
    ppermute x0 -> x18, starting transfers between devices: none -> 15.2 us  [the longest x9 12.1 us: far_queue(): lax.ppermute(whole[1], 'sector', [(s, s ^ 1) for s in range(sectors)])]
    squeeze x0 -> x9, local copies, waits for them, and re-layouts: none -> 12 us  [far_queue(): whole[1]]
    ppermute x3, waiting for transfers between devices: 0.01 us -> 9.63 us  [paired_shards(): got_halo.append(lax.ppermute(forward, 'inner', got_pairs))]
    ppermute x4 -> x3, waiting for transfers between devices: 39.7 us -> 47.5 us  [paired_shards(): backs.append(lax.ppermute(last, 'inner', swap))]
    ppermute x5, waiting for transfers between devices: 12.5 us -> 4.81 us  [paired_shards(): got.append(lax.ppermute(sent, 'inner', swap))]
  transfers between devices with their start and end apart: 42 -> 38, of which waited for: 21 -> 20; matrix products, arithmetic and copies ran while one was open for 1% -> 4% of each run, Pallas kernels for 23% -> 21%
where the time goes in v6:
time: 426 us; the launch traced here: 423 us
  waiting for transfers between devices  198 us (46%)
  Pallas kernels  156 us (37%)
  starting transfers between devices  49.7 us (12%)
  local copies, waits for them, and re-layouts  18.2 us (4%)
    ppermute x9, waiting for transfers between devices, far_queue(): whole = lax.ppermute(send, 'sector', [(s, s ^ 2) for s in range(sectors)])  110 us
    pallas_call x9, Pallas kernels, drift(): pl.pallas_call(functools.partial(drift_kernel, find, place, receive, n_lo...  66.7 us
    pallas_call x1, Pallas kernels, diffuse(): pl.pallas_call(functools.partial(diffusion_kernel, len(own), len(own_halo...  52.3 us
    ppermute x3, waiting for transfers between devices, paired_shards(): backs.append(lax.ppermute(last, 'inner', swap))  47.5 us
    pallas_call x9, Pallas kernels, pack(): pl.pallas_call(functools.partial(pack_kernel, offsets, finds, n_far, len(...  32.7 us
    ppermute x1, waiting for transfers between devices, paired_shards(): backs = [lax.ppermute(returns[0], 'inner', swap)]  17.3 us
    ppermute x9, starting transfers between devices, far_queue(): lax.ppermute(whole[1], 'sector', [(s, s ^ 1) for s in range(sectors)])  12.1 us
    squeeze x9, local copies, waits for them, and re-layouts, far_queue(): whole[1]  12 us
  transfers between devices with their start and end apart: 38, of which 20 were waited for; matrix products, arithmetic and copies ran while one was open for 4% of the time, Pallas kernels for 21%

profile of v6, /device:TPU:25, one launch (start us, length us, event | category | flops | bytes accessed | tf_op | source)
XLA Modules:
  0.0 422.8 jit_solution(5980126012611944162)
XLA Ops:
  0.0 5.4 %pack_tiles.9 = (f32[2,6,4,64,128]{4,3,2,1,0:T(8,128)}, f32[6,16,64,128]{3,2,1,0:T(8,128)}) custom-call(s32[1,4,16]{2,1,0:T(4,128)} %sec_ref.35, s32[1,4,16]{2,1,0:T(4,128)} %til_ref.35, f32[16,64,2048]{2,1,0:T(8,128)} %refs_0_.19), custom_call_target="tpu_custom_call" | custom-call | bytes 1024 | tf_op jit(solution)/shard_map/pack_tiles/pallas_call | solution.py:114
  6.4 3.1 pack_tiles.10
  10.2 31.3 %collective-permute-done.3.refs_2_ = f32[2,6,4,64,128]{4,3,2,1,0:T(8,128)} collective-permute-done((f32[2,6,4,64,128]{4,3,2,1,0:T(8,128)}, f32[2,6,4,64,128]{4,3,2,1,0:T(8,128)}, u32[]{:S(2)}, u32[]{:S(2)}) %collective-permute-start.3) | collective-permute-done | bytes 1572896 | tf_op jit(solution)/shard_map/ppermute | solution.py:142
  41.4 2.1 slice_bitcast_fusion.3
  43.5 2.1 collective-permute-start.4
  45.7 4.7 %split_weights.1.w_ref = bf16[16,256,256]{2,1,0:T(8,128)(2,1)} custom-call(s32[1,4,16]{2,1,0:T(4,128)} %mid_ref.1, f32[32,128,128]{2,1,0:T(8,128)} %w_ref.1), custom_call_target="tpu_custom_call" | custom-call | bytes 1024 | tf_op jit(solution)/shard_map/split_weights/pallas_call | solution.py:52
  50.4 7.6 %drift_chunk.9 = (f32[8,4,64,128]{3,2,1,0:T(8,128)}, f32[8,4,64,128]{3,2,1,0:T(8,128)}, f32[8,128]{1,0:T(8,128)}) custom-call(s32[1,4,16]{2,1,0:T(4,128)} %sec_ref.35, s32[1,4,16]{2,1,0:T(4,128)} %til_ref.35, bf16[16,256,256]{2,1,0:T(8,128)(2,1)} %split_weights.1.w_ref, f32[16,64,2048]{2,1,0:T(8,128)} %refs_0_.19, ...), custom_call_target="tpu_custom_call" | custom-call | bytes 1024 | tf_op jit(solution)/shard_map/drift_chunk/pallas_call | solution.py:208
  58.0 3.1 pack_tiles.11
  61.5 2.3 collective-permute-start.11
  63.8 11.3 %collective-permute-done.refs_2_ = f32[2,6,4,64,128]{4,3,2,1,0:T(8,128)} collective-permute-done((f32[2,6,4,64,128]{4,3,2,1,0:T(8,128)}, f32[2,6,4,64,128]{4,3,2,1,0:T(8,128)}, u32[]{:S(2)}, u32[]{:S(2)}) %collective-permute-start) | collective-permute-done | bytes 1572896 | tf_op jit(solution)/shard_map/ppermute | solution.py:142
  76.3 2.2 collective-permute-start.1
  79.2 1.2 collective-permute-done.1.refs_3_
  81.1 1.8 broadcast_in_dim.47.b_ref
  82.9 1.8 broadcast_in_dim.45.a_ref
  84.7 2.9 collective-permute-start.16
  87.6 7.5 %drift_chunk.10 = (f32[8,4,64,128]{3,2,1,0:T(8,128)}, f32[8,4,64,128]{3,2,1,0:T(8,128)}, f32[8,128]{1,0:T(8,128)}) custom-call(s32[1,4,16]{2,1,0:T(4,128)} %sec_ref.35, s32[1,4,16]{2,1,0:T(4,128)} %til_ref.35, bf16[16,256,256]{2,1,0:T(8,128)(2,1)} %split_weights.1.w_ref, f32[16,64,2048]{2,1,0:T(8,128)} %refs_0_.19, ...), custom_call_target="tpu_custom_call" | custom-call | bytes 1024 | tf_op jit(solution)/shard_map/drift_chunk/pallas_call | solution.py:208
  95.2 1.3 collective-permute-start.19
  96.5 12.3 %collective-permute-done.5.refs_2_ = f32[2,6,4,64,128]{4,3,2,1,0:T(8,128)} collective-permute-done((f32[2,6,4,64,128]{4,3,2,1,0:T(8,128)}, f32[2,6,4,64,128]{4,3,2,1,0:T(8,128)}, u32[]{:S(2)}, u32[]{:S(2)}) %collective-permute-start.5) | collective-permute-done | bytes 1572896 | tf_op jit(solution)/shard_map/ppermute | solution.py:142
  108.8 2.1 slice_bitcast_fusion.2
  110.9 1.3 collective-permute-start.6
  112.2 2.9 pack_tiles.12
  116.0 2.5 collective-permute-start.17
  118.5 7.6 %drift_chunk.11 = (f32[8,4,64,128]{3,2,1,0:T(8,128)}, f32[8,4,64,128]{3,2,1,0:T(8,128)}, f32[8,128]{1,0:T(8,128)}) custom-call(s32[1,4,16]{2,1,0:T(4,128)} %sec_ref.35, s32[1,4,16]{2,1,0:T(4,128)} %til_ref.35, bf16[16,256,256]{2,1,0:T(8,128)(2,1)} %split_weights.1.w_ref, f32[16,64,2048]{2,1,0:T(8,128)} %refs_0_.19, ...), custom_call_target="tpu_custom_call" | custom-call | bytes 1024 | tf_op jit(solution)/shard_map/drift_chunk/pallas_call | solution.py:208
  127.2 1.3 collective-permute-start.20
  128.5 3.0 pack_tiles.13
  131.6 3.1 collective-permute-done.7.refs_2_
  135.7 1.3 collective-permute-start.8
  137.0 3.1 collective-permute-done.17.refs_11_
  140.1 5.1 %collective-permute-start.18 = (f32[8,4,64,128]{3,2,1,0:T(8,128)}, f32[8,4,64,128]{3,2,1,0:T(8,128)}, u32[]{:S(2)}, u32[]{:S(2)}) collective-permute-start(f32[8,4,64,128]{3,2,1,0:T(8,128)} %get-tuple-element.110.refs_2_), channel_id=1, source_target_pairs={{1,3},{2,0},{3,5},{4,2},{5,7},{6,4},{9,11},{10,8},{11,13},{12,10},... | collective-permute-start | bytes 3145736 | tf_op jit(solution)/shard_map/ppermute | solution.py:537
  145.2 6.9 %drift_chunk.12 = (f32[8,2,64,128]{3,2,1,0:T(8,128)}, f32[8,2,64,128]{3,2,1,0:T(8,128)}, f32[8,128]{1,0:T(8,128)}) custom-call(s32[1,4,16]{2,1,0:T(4,128)} %sec_ref.35, s32[1,4,16]{2,1,0:T(4,128)} %til_ref.35, bf16[16,256,256]{2,1,0:T(8,128)(2,1)} %split_weights.1.w_ref, f32[16,64,2048]{2,1,0:T(8,128)} %refs_0_.19, ...), custom_call_target="tpu_custom_call" | custom-call | bytes 1024 | tf_op jit(solution)/shard_map/drift_chunk/pallas_call | solution.py:208
  152.1 2.1 collective-permute-done.20.refs_14_
  154.2 1.3 collective-permute-start.21
  156.6 1.5 collective-permute-start.10
  158.0 1.3 collective-permute-done.10.refs_3_
  160.1 6.9 %drift_chunk.13 = (f32[8,2,64,128]{3,2,1,0:T(8,128)}, f32[8,2,64,128]{3,2,1,0:T(8,128)}, f32[8,128]{1,0:T(8,128)}) custom-call(s32[1,4,16]{2,1,0:T(4,128)} %sec_ref.35, s32[1,4,16]{2,1,0:T(4,128)} %til_ref.35, bf16[16,256,256]{2,1,0:T(8,128)(2,1)} %split_weights.1.w_ref, f32[16,64,2048]{2,1,0:T(8,128)} %refs_0_.19, ...), custom_call_target="tpu_custom_call" | custom-call | bytes 1024 | tf_op jit(solution)/shard_map/drift_chunk/pallas_call | solution.py:208
  167.1 5.1 %collective-permute-start.15 = (f32[8,2,64,128]{3,2,1,0:T(8,128)}, f32[8,2,64,128]{3,2,1,0:T(8,128)}, u32[]{:S(2)}, u32[]{:S(2)}) collective-permute-start(f32[8,2,64,128]{3,2,1,0:T(8,128)} %get-tuple-element.106), channel_id=1, source_target_pairs={{0,1},{1,0},{2,3},{3,2},{4,5},{5,4},{6,7},{7,6},{8,9},{9,8},{10,11... | collective-permute-start | bytes 1572872 | tf_op jit(solution)/shard_map/ppermute | solution.py:528
  172.2 7.5 %collective-permute-done.21.refs_15_ = f32[8,4,64,128]{3,2,1,0:T(8,128)} collective-permute-done((f32[8,4,64,128]{3,2,1,0:T(8,128)}, f32[8,4,64,128]{3,2,1,0:T(8,128)}, u32[]{:S(2)}, u32[]{:S(2)}) %collective-permute-start.21) | collective-permute-done | bytes 1048608 | tf_op jit(solution)/shard_map/ppermute | solution.py:533
  179.7 4.8 %collective-permute-done.15.refs_9_ = f32[8,2,64,128]{3,2,1,0:T(8,128)} collective-permute-done((f32[8,2,64,128]{3,2,1,0:T(8,128)}, f32[8,2,64,128]{3,2,1,0:T(8,128)}, u32[]{:S(2)}, u32[]{:S(2)}) %collective-permute-start.15) | collective-permute-done | bytes 524320 | tf_op jit(solution)/shard_map/ppermute | solution.py:528
  184.5 52.3 %diffuse_tiles.1 = (f32[8,16,64,128]{3,2,1,0:T(8,128)}, f32[8,3,64,128]{3,2,1,0:T(8,128)}, f32[8,4,64,128]{3,2,1,0:T(8,128)}, f32[8,6,64,128]{3,2,1,0:T(8,128)}, f32[8,3,64,128]{3,2,1,0:T(8,128)}) custom-call(f32[8,8,128]{2,1,0:T(8,128)} %broadcast_in_dim.43.rate_ref, f32[56,64,128]{2,1,0:T(8,128)} %broadcast_in_dim.45.a_ref, ...), custom_call_target="tpu_custom_call" | custom-call | bytes 1024 | tf_op jit(solution)/shard_map/diffuse_tiles/pallas_call | solution.py:383
  236.8 1.2 collective-permute-start.22
  238.0 17.3 %collective-permute-done.22.refs_1_ = f32[8,3,64,128]{3,2,1,0:T(8,128)} collective-permute-done((f32[8,3,64,128]{3,2,1,0:T(8,128)}, f32[8,3,64,128]{3,2,1,0:T(8,128)}, u32[]{:S(2)}, u32[]{:S(2)}) %collective-permute-start.22) | collective-permute-done | bytes 786464 | tf_op jit(solution)/shard_map/ppermute | solution.py:566
  255.3 3.7 pack_tiles.14
  259.9 22.3 %collective-permute-done.23.refs_1_ = f32[8,4,64,128]{3,2,1,0:T(8,128)} collective-permute-done((f32[8,4,64,128]{3,2,1,0:T(8,128)}, f32[8,4,64,128]{3,2,1,0:T(8,128)}, u32[]{:S(2)}, u32[]{:S(2)}) %collective-permute-start.23) | collective-permute-done | bytes 1048608 | tf_op jit(solution)/shard_map/ppermute | solution.py:568
  282.1 2.9 collective-permute-done.24.refs_3_
  285.3 3.4 collective-permute-start.30
  288.8 3.8 pack_tiles.15
  294.1 1.8 collective-permute-done.31.refs_4_
  295.9 7.3 %drift_chunk.14 = (f32[16,64,2048]{2,1,0:T(8,128)}, f32[8,128]{1,0:T(8,128)}) custom-call(s32[1,4,16]{2,1,0:T(4,128)} %sec_ref.35, s32[1,4,16]{2,1,0:T(4,128)} %til_ref.35, bf16[16,256,256]{2,1,0:T(8,128)(2,1)} %split_weights.1.w_ref, f32[8,16,64,128]{3,2,1,0:T(8,128)} %get-tuple-element.115.refs_0_, f32[8,3,64,128]{3,2,1,0:T(8,128)} %collective-permute-done.22.refs_1_, ...), custom_call_target="tpu_custom_call" | custom-call | bytes 1024 | tf_op jit(solution)/shard_map/drift_chunk/pallas_call | solution.py:208
  303.2 15.4 %collective-permute-done.25.refs_1_ = f32[8,6,64,128]{3,2,1,0:T(8,128)} collective-permute-done((f32[8,6,64,128]{3,2,1,0:T(8,128)}, f32[8,6,64,128]{3,2,1,0:T(8,128)}, u32[]{:S(2)}, u32[]{:S(2)}) %collective-permute-start.25) | collective-permute-done | bytes 1572896 | tf_op jit(solution)/shard_map/ppermute | solution.py:582
  318.6 4.0 pack_tiles.17
  322.6 3.8 collective-permute-start.28
  326.4 2.5 collective-permute-done.26.refs_3_
  330.1 1.2 collective-permute-start.29
  332.1 1.3 collective-permute-done.29.refs_4_
  333.4 7.6 %drift_chunk.15 = (f32[16,64,2048]{2,1,0:T(8,128)}, f32[8,128]{1,0:T(8,128)}) custom-call(s32[1,4,16]{2,1,0:T(4,128)} %sec_ref.35, s32[1,4,16]{2,1,0:T(4,128)} %til_ref.35, bf16[16,256,256]{2,1,0:T(8,128)(2,1)} %split_weights.1.w_ref, f32[8,16,64,128]{3,2,1,0:T(8,128)} %get-tuple-element.115.refs_0_, ...), custom_call_target="tpu_custom_call", output_to_operand_aliasing={{0}: (9, {})} | custom-call | bytes 1024 | tf_op jit(solution)/shard_map/drift_chunk/pallas_call | solution.py:208
  341.0 9.8 %collective-permute-done.27.refs_1_ = f32[8,3,64,128]{3,2,1,0:T(8,128)} collective-permute-done((f32[8,3,64,128]{3,2,1,0:T(8,128)}, f32[8,3,64,128]{3,2,1,0:T(8,128)}, u32[]{:S(2)}, u32[]{:S(2)}) %collective-permute-start.27) | collective-permute-done | bytes 786464 | tf_op jit(solution)/shard_map/ppermute | solution.py:582
  350.8 3.7 pack_tiles.16
  354.6 1.2 collective-permute-start.35
  355.8 23.7 %collective-permute-done.36.refs_3_ = f32[2,6,6,64,128]{4,3,2,1,0:T(8,128)} collective-permute-done((f32[2,6,6,64,128]{4,3,2,1,0:T(8,128)}, f32[2,6,6,64,128]{4,3,2,1,0:T(8,128)}, u32[]{:S(2)}, u32[]{:S(2)}) %collective-permute-start.36) | collective-permute-done | bytes 2359328 | tf_op jit(solution)/shard_map/ppermute | solution.py:142
  379.5 1.4 slice_bitcast_fusion
  380.9 1.2 collective-permute-start.37
  382.2 22.5 %collective-permute-done.33.refs_3_ = f32[2,6,3,64,128]{4,3,2,1,0:T(8,128)S(1)} collective-permute-done((f32[2,6,3,64,128]{4,3,2,1,0:T(8,128)}, f32[2,6,3,64,128]{4,3,2,1,0:T(8,128)S(1)}, u32[]{:S(2)}, u32[]{:S(2)}) %collective-permute-start.33) | collective-permute-done | bytes 1179680 | tf_op jit(solution)/shard_map/ppermute | solution.py:142
  407.4 8.1 %drift_chunk.16 = (f32[16,64,2048]{2,1,0:T(8,128)}, f32[8,128]{1,0:T(8,128)}) custom-call(s32[1,4,16]{2,1,0:T(4,128)} %sec_ref.35, s32[1,4,16]{2,1,0:T(4,128)} %til_ref.35, bf16[16,256,256]{2,1,0:T(8,128)(2,1)} %split_weights.1.w_ref, f32[8,16,64,128]{3,2,1,0:T(8,128)} %get-tuple-element.115.refs_0_, ...), custom_call_target="tpu_custom_call", output_to_operand_aliasing={{0}: (9, {})} | custom-call | bytes 1024 | tf_op jit(solution)/shard_map/drift_chunk/pallas_call | solution.py:208
  415.5 7.3 %drift_chunk.17 = (f32[16,64,2048]{2,1,0:T(8,128)}, f32[8,128]{1,0:T(8,128)}) custom-call(s32[1,4,16]{2,1,0:T(4,128)} %sec_ref.35, s32[1,4,16]{2,1,0:T(4,128)} %til_ref.35, bf16[16,256,256]{2,1,0:T(8,128)(2,1)} %split_weights.1.w_ref, f32[8,16,64,128]{3,2,1,0:T(8,128)} %get-tuple-element.115.refs_0_, ...), custom_call_target="tpu_custom_call", output_to_operand_aliasing={{0}: (9, {})} | custom-call | bytes 1024 | tf_op jit(solution)/shard_map/drift_chunk/pallas_call | solution.py:208
  (67 shorter events, 16.9 us)
Async XLA Ops:
  5.4 45.0 %collective-permute-start.2 = (f32[6,16,64,128]{3,2,1,0:T(8,128)}, f32[6,16,64,128]{3,2,1,0:T(8,128)}, u32[]{:S(2)}, u32[]{:S(2)}) collective-permute-start(f32[6,16,64,128]{3,2,1,0:T(8,128)} %get-tuple-element.79), channel_id=1, source_target_pairs={{0,8},{8,0},{16,24},{24,16},{1,9},{9,1},{17,25},{25,17},{2,10},{10... | collective-permute-start | bytes 9437192 | tf_op jit(solution)/shard_map/ppermute | solution.py:133
  5.5 35.9 %collective-permute-start.3 = (f32[2,6,4,64,128]{4,3,2,1,0:T(8,128)}, f32[2,6,4,64,128]{4,3,2,1,0:T(8,128)}, u32[]{:S(2)}, u32[]{:S(2)}) collective-permute-start(f32[2,6,4,64,128]{4,3,2,1,0:T(8,128)} %get-tuple-element.75.refs_1_), channel_id=1, source_target_pairs={{0,16},{8,24},{16,0},{24,8},{1,17},{9,25},{17,1},{25,9},{2,18},{10... | collective-permute-start | bytes 4718600 | tf_op jit(solution)/shard_map/ppermute | solution.py:142
  9.5 65.6 %collective-permute-start = (f32[2,6,4,64,128]{4,3,2,1,0:T(8,128)}, f32[2,6,4,64,128]{4,3,2,1,0:T(8,128)}, u32[]{:S(2)}, u32[]{:S(2)}) collective-permute-start(f32[2,6,4,64,128]{4,3,2,1,0:T(8,128)} %pack_tiles.10), channel_id=1, source_target_pairs={{0,16},{8,24},{16,0},{24,8},{1,17},{9,25},{17,1},{25,9},{2,18},{10... | collective-permute-start | bytes 4718600 | tf_op jit(solution)/shard_map/ppermute | solution.py:142
  43.5 6.9 %collective-permute-start.4 = (f32[6,4,64,128]{3,2,1,0:T(8,128)}, f32[6,4,64,128]{3,2,1,0:T(8,128)}, u32[]{:S(2)}, u32[]{:S(2)}) collective-permute-start(f32[6,4,64,128]{3,2,1,0:T(8,128)} %slice_bitcast_fusion.3), channel_id=1, source_target_pairs={{0,8},{8,0},{16,24},{24,16},{1,9},{9,1},{17,25},{25,17},{2,10},{10... | collective-permute-start | bytes 2359304 | tf_op jit(solution)/shard_map/ppermute | solution.py:143
  61.1 17.5 %copy-start.6 = (s32[1,8]{1,0:T(1,128)S(1)}, s32[1,8]{1,0:T(1,128)}, u32[]{:S(2)}) copy-start(s32[1,8]{1,0:T(1,128)} %param.14) | copy-start | bytes 100
  61.1 17.6 %copy-start.3 = (f32[128,64]{0,1:T(8,128)S(1)}, f32[128,64]{0,1:T(8,128)}, u32[]{:S(2)}) copy-start(f32[128,64]{0,1:T(8,128)} %param.16) | copy-start | bytes 98308
  61.1 17.6 %copy-start.4 = (f32[128,64]{0,1:T(8,128)S(1)}, f32[128,64]{0,1:T(8,128)}, u32[]{:S(2)}) copy-start(f32[128,64]{0,1:T(8,128)} %param.17) | copy-start | bytes 98308
  61.1 18.0 %copy-start.5 = (f32[1,8]{1,0:T(1,128)S(1)}, f32[1,8]{1,0:T(1,128)}, u32[]{:S(2)}) copy-start(f32[1,8]{1,0:T(1,128)} %param.15) | copy-start | bytes 100
  61.1 47.7 %collective-permute-start.5 = (f32[2,6,4,64,128]{4,3,2,1,0:T(8,128)}, f32[2,6,4,64,128]{4,3,2,1,0:T(8,128)}, u32[]{:S(2)}, u32[]{:S(2)}) collective-permute-start(f32[2,6,4,64,128]{4,3,2,1,0:T(8,128)} %pack_tiles.11), channel_id=1, source_target_pairs={{0,16},{8,24},{16,0},{24,8},{1,17},{9,25},{17,1},{25,9},{2,18},{10... | collective-permute-start | bytes 4718600 | tf_op jit(solution)/shard_map/ppermute | solution.py:142
  61.5 33.6 %collective-permute-start.11 = (f32[8,4,64,128]{3,2,1,0:T(8,128)}, f32[8,4,64,128]{3,2,1,0:T(8,128)}, u32[]{:S(2)}, u32[]{:S(2)}) collective-permute-start(f32[8,4,64,128]{3,2,1,0:T(8,128)} %get-tuple-element.95), channel_id=1, source_target_pairs={{0,1},{1,0},{2,3},{3,2},{4,5},{5,4},{6,7},{7,6},{8,9},{9,8},{10,11... | collective-permute-start | bytes 3145736 | tf_op jit(solution)/shard_map/ppermute | solution.py:528
  76.3 4.1 collective-permute-start.1
  80.4 4.2 copy-start.1
  84.7 31.4 %collective-permute-start.16 = (f32[8,4,64,128]{3,2,1,0:T(8,128)}, f32[8,4,64,128]{3,2,1,0:T(8,128)}, u32[]{:S(2)}, u32[]{:S(2)}) collective-permute-start(f32[8,4,64,128]{3,2,1,0:T(8,128)} %get-tuple-element.80.refs_0_), channel_id=1, source_target_pairs={{1,3},{2,0},{3,5},{4,2},{5,7},{6,4},{9,11},{10,8},{11,13},{12,10},... | collective-permute-start | bytes 3145736 | tf_op jit(solution)/shard_map/ppermute | solution.py:537
  95.1 30.9 %collective-permute-start.12 = (f32[8,4,64,128]{3,2,1,0:T(8,128)}, f32[8,4,64,128]{3,2,1,0:T(8,128)}, u32[]{:S(2)}, u32[]{:S(2)}) collective-permute-start(f32[8,4,64,128]{3,2,1,0:T(8,128)} %get-tuple-element.98), channel_id=1, source_target_pairs={{0,1},{1,0},{2,3},{3,2},{4,5},{5,4},{6,7},{7,6},{8,9},{9,8},{10,11... | collective-permute-start | bytes 3145736 | tf_op jit(solution)/shard_map/ppermute | solution.py:528
  95.2 32.0 %collective-permute-start.19 = (f32[8,4,64,128]{3,2,1,0:T(8,128)}, f32[8,4,64,128]{3,2,1,0:T(8,128)}, u32[]{:S(2)}, u32[]{:S(2)}) collective-permute-start(f32[8,4,64,128]{3,2,1,0:T(8,128)} %collective-permute-done.11.refs_5_), channel_id=1, source_target_pairs={{0,2},{2,4},{3,1},{4,6},{5,3},{7,5},{8,10},{10,12},{11,9},{12,14},... | collective-permute-start | bytes 3145736 | tf_op jit(solution)/shard_map/ppermute | solution.py:533
  110.9 7.5 %collective-permute-start.6 = (f32[6,4,64,128]{3,2,1,0:T(8,128)}, f32[6,4,64,128]{3,2,1,0:T(8,128)}, u32[]{:S(2)}, u32[]{:S(2)}) collective-permute-start(f32[6,4,64,128]{3,2,1,0:T(8,128)} %slice_bitcast_fusion.2), channel_id=1, source_target_pairs={{0,8},{8,0},{16,24},{24,16},{1,9},{9,1},{17,25},{25,17},{2,10},{10... | collective-permute-start | bytes 2359304 | tf_op jit(solution)/shard_map/ppermute | solution.py:143
  115.2 19.5 %collective-permute-start.7 = (f32[2,6,2,64,128]{4,3,2,1,0:T(8,128)}, f32[2,6,2,64,128]{4,3,2,1,0:T(8,128)}, u32[]{:S(2)}, u32[]{:S(2)}) collective-permute-start(f32[2,6,2,64,128]{4,3,2,1,0:T(8,128)} %pack_tiles.12), channel_id=1, source_target_pairs={{0,16},{8,24},{16,0},{24,8},{1,17},{9,25},{17,1},{25,9},{2,18},{10... | collective-permute-start | bytes 2359304 | tf_op jit(solution)/shard_map/ppermute | solution.py:142
  116.0 24.1 %collective-permute-start.17 = (f32[8,4,64,128]{3,2,1,0:T(8,128)}, f32[8,4,64,128]{3,2,1,0:T(8,128)}, u32[]{:S(2)}, u32[]{:S(2)}) collective-permute-start(f32[8,4,64,128]{3,2,1,0:T(8,128)} %get-tuple-element.108.refs_1_), channel_id=1, source_target_pairs={{1,3},{2,0},{3,5},{4,2},{5,7},{6,4},{9,11},{10,8},{11,13},{12,10},... | collective-permute-start | bytes 3145736 | tf_op jit(solution)/shard_map/ppermute | solution.py:537
  126.1 26.0 %collective-permute-start.13 = (f32[8,4,64,128]{3,2,1,0:T(8,128)}, f32[8,4,64,128]{3,2,1,0:T(8,128)}, u32[]{:S(2)}, u32[]{:S(2)}) collective-permute-start(f32[8,4,64,128]{3,2,1,0:T(8,128)} %get-tuple-element.101), channel_id=1, source_target_pairs={{0,1},{1,0},{2,3},{3,2},{4,5},{5,4},{6,7},{7,6},{8,9},{9,8},{10,11... | collective-permute-start | bytes 3145736 | tf_op jit(solution)/shard_map/ppermute | solution.py:528
  127.2 27.0 %collective-permute-start.20 = (f32[8,4,64,128]{3,2,1,0:T(8,128)}, f32[8,4,64,128]{3,2,1,0:T(8,128)}, u32[]{:S(2)}, u32[]{:S(2)}) collective-permute-start(f32[8,4,64,128]{3,2,1,0:T(8,128)} %collective-permute-done.12.refs_6_), channel_id=1, source_target_pairs={{0,2},{2,4},{3,1},{4,6},{5,3},{7,5},{8,10},{10,12},{11,9},{12,14},... | collective-permute-start | bytes 3145736 | tf_op jit(solution)/shard_map/ppermute | solution.py:533
  131.5 24.0 %collective-permute-start.9 = (f32[2,6,2,64,128]{4,3,2,1,0:T(8,128)}, f32[2,6,2,64,128]{4,3,2,1,0:T(8,128)}, u32[]{:S(2)}, u32[]{:S(2)}) collective-permute-start(f32[2,6,2,64,128]{4,3,2,1,0:T(8,128)} %pack_tiles.13), channel_id=1, source_target_pairs={{0,16},{8,24},{16,0},{24,8},{1,17},{9,25},{17,1},{25,9},{2,18},{10... | collective-permute-start | bytes 2359304 | tf_op jit(solution)/shard_map/ppermute | solution.py:142
  135.7 9.5 %collective-permute-start.8 = (f32[6,2,64,128]{3,2,1,0:T(8,128)S(1)}, f32[6,2,64,128]{3,2,1,0:T(8,128)}, u32[]{:S(2)}, u32[]{:S(2)}) collective-permute-start(f32[6,2,64,128]{3,2,1,0:T(8,128)S(1)} %slice_bitcast_fusion.8), channel_id=1, source_target_pairs={{0,8},{8,0},{16,24},{24,16},{1,9},{9,1},{17,25},{25,17},{2,10},{10... | collective-permute-start | bytes 1179656 | tf_op jit(solution)/shard_map/ppermute | solution.py:143
  140.1 32.1 %collective-permute-start.18 = (f32[8,4,64,128]{3,2,1,0:T(8,128)}, f32[8,4,64,128]{3,2,1,0:T(8,128)}, u32[]{:S(2)}, u32[]{:S(2)}) collective-permute-start(f32[8,4,64,128]{3,2,1,0:T(8,128)} %get-tuple-element.110.refs_2_), channel_id=1, source_target_pairs={{1,3},{2,0},{3,5},{4,2},{5,7},{6,4},{9,11},{10,8},{11,13},{12,10},... | collective-permute-start | bytes 3145736 | tf_op jit(solution)/shard_map/ppermute | solution.py:537
  154.2 12.8 %collective-permute-start.14 = (f32[8,2,64,128]{3,2,1,0:T(8,128)}, f32[8,2,64,128]{3,2,1,0:T(8,128)}, u32[]{:S(2)}, u32[]{:S(2)}) collective-permute-start(f32[8,2,64,128]{3,2,1,0:T(8,128)} %get-tuple-element.104), channel_id=1, source_target_pairs={{0,1},{1,0},{2,3},{3,2},{4,5},{5,4},{6,7},{7,6},{8,9},{9,8},{10,11... | collective-permute-start | bytes 1572872 | tf_op jit(solution)/shard_map/ppermute | solution.py:528
  154.2 25.5 %collective-permute-start.21 = (f32[8,4,64,128]{3,2,1,0:T(8,128)}, f32[8,4,64,128]{3,2,1,0:T(8,128)}, u32[]{:S(2)}, u32[]{:S(2)}) collective-permute-start(f32[8,4,64,128]{3,2,1,0:T(8,128)} %collective-permute-done.13.refs_7_), channel_id=1, source_target_pairs={{0,2},{2,4},{3,1},{4,6},{5,3},{7,5},{8,10},{10,12},{11,9},{12,14},... | collective-permute-start | bytes 3145736 | tf_op jit(solution)/shard_map/ppermute | solution.py:533
  156.6 2.8 collective-permute-start.10
  159.4 0.8 copy-start.2
  167.1 17.4 %collective-permute-start.15 = (f32[8,2,64,128]{3,2,1,0:T(8,128)}, f32[8,2,64,128]{3,2,1,0:T(8,128)}, u32[]{:S(2)}, u32[]{:S(2)}) collective-permute-start(f32[8,2,64,128]{3,2,1,0:T(8,128)} %get-tuple-element.106), channel_id=1, source_target_pairs={{0,1},{1,0},{2,3},{3,2},{4,5},{5,4},{6,7},{7,6},{8,9},{9,8},{10,11... | collective-permute-start | bytes 1572872 | tf_op jit(solution)/shard_map/ppermute | solution.py:528
  236.8 18.6 %collective-permute-start.22 = (f32[8,3,64,128]{3,2,1,0:T(8,128)}, f32[8,3,64,128]{3,2,1,0:T(8,128)}, u32[]{:S(2)}, u32[]{:S(2)}) collective-permute-start(f32[8,3,64,128]{3,2,1,0:T(8,128)} %get-tuple-element.119), channel_id=1, source_target_pairs={{0,1},{1,0},{2,3},{3,2},{4,5},{5,4},{6,7},{7,6},{8,9},{9,8},{10,11... | collective-permute-start | bytes 2359304 | tf_op jit(solution)/shard_map/ppermute | solution.py:566
  259.0 26.0 %collective-permute-start.24 = (f32[2,6,3,64,128]{4,3,2,1,0:T(8,128)}, f32[2,6,3,64,128]{4,3,2,1,0:T(8,128)}, u32[]{:S(2)}, u32[]{:S(2)}) collective-permute-start(f32[2,6,3,64,128]{4,3,2,1,0:T(8,128)} %get-tuple-element.122), channel_id=1, source_target_pairs={{0,16},{8,24},{16,0},{24,8},{1,17},{9,25},{17,1},{25,9},{2,18},{10... | collective-permute-start | bytes 3538952 | tf_op jit(solution)/shard_map/ppermute | solution.py:142
  259.1 23.0 %collective-permute-start.23 = (f32[8,4,64,128]{3,2,1,0:T(8,128)}, f32[8,4,64,128]{3,2,1,0:T(8,128)}, u32[]{:S(2)}, u32[]{:S(2)}) collective-permute-start(f32[8,4,64,128]{3,2,1,0:T(8,128)} %get-tuple-element.120), channel_id=1, source_target_pairs={{0,1},{1,0},{2,3},{3,2},{4,5},{5,4},{6,7},{7,6},{8,9},{9,8},{10,11... | collective-permute-start | bytes 3145736 | tf_op jit(solution)/shard_map/ppermute | solution.py:568
  285.1 33.5 %collective-permute-start.25 = (f32[8,6,64,128]{3,2,1,0:T(8,128)}, f32[8,6,64,128]{3,2,1,0:T(8,128)}, u32[]{:S(2)}, u32[]{:S(2)}) collective-permute-start(f32[8,6,64,128]{3,2,1,0:T(8,128)} %get-tuple-element.123), channel_id=1, source_target_pairs={{0,1},{1,0},{2,3},{3,2},{4,5},{5,4},{6,7},{7,6},{8,9},{9,8},{10,11... | collective-permute-start | bytes 4718600 | tf_op jit(solution)/shard_map/ppermute | solution.py:582
  285.3 8.8 %collective-permute-start.30 = (f32[6,3,64,128]{3,2,1,0:T(8,128)}, f32[6,3,64,128]{3,2,1,0:T(8,128)}, u32[]{:S(2)}, u32[]{:S(2)}) collective-permute-start(f32[6,3,64,128]{3,2,1,0:T(8,128)} %get-tuple-element.129), channel_id=1, source_target_pairs={{0,8},{8,0},{16,24},{24,16},{1,9},{9,1},{17,25},{25,17},{2,10},{10... | collective-permute-start | bytes 1769480 | tf_op jit(solution)/shard_map/ppermute | solution.py:133
  292.5 36.4 %collective-permute-start.26 = (f32[2,6,4,64,128]{4,3,2,1,0:T(8,128)}, f32[2,6,4,64,128]{4,3,2,1,0:T(8,128)}, u32[]{:S(2)}, u32[]{:S(2)}) collective-permute-start(f32[2,6,4,64,128]{4,3,2,1,0:T(8,128)} %get-tuple-element.124), channel_id=1, source_target_pairs={{0,16},{8,24},{16,0},{24,8},{1,17},{9,25},{17,1},{25,9},{2,18},{10... | collective-permute-start | bytes 4718600 | tf_op jit(solution)/shard_map/ppermute | solution.py:142
  293.7 2.2 collective-permute-start.31
  322.6 56.9 %collective-permute-start.36 = (f32[2,6,6,64,128]{4,3,2,1,0:T(8,128)}, f32[2,6,6,64,128]{4,3,2,1,0:T(8,128)}, u32[]{:S(2)}, u32[]{:S(2)}) collective-permute-start(f32[2,6,6,64,128]{4,3,2,1,0:T(8,128)} %get-tuple-element.140), channel_id=1, source_target_pairs={{0,16},{8,24},{16,0},{24,8},{1,17},{9,25},{17,1},{25,9},{2,18},{10... | collective-permute-start | bytes 7077896 | tf_op jit(solution)/shard_map/ppermute | solution.py:142
  322.6 9.5 %collective-permute-start.28 = (f32[6,4,64,128]{3,2,1,0:T(8,128)}, f32[6,4,64,128]{3,2,1,0:T(8,128)}, u32[]{:S(2)}, u32[]{:S(2)}) collective-permute-start(f32[6,4,64,128]{3,2,1,0:T(8,128)} %get-tuple-element.127), channel_id=1, source_target_pairs={{0,8},{8,0},{16,24},{24,16},{1,9},{9,1},{17,25},{25,17},{2,10},{10... | collective-permute-start | bytes 2359304 | tf_op jit(solution)/shard_map/ppermute | solution.py:133
  330.1 3.3 collective-permute-start.29
  331.4 19.4 %collective-permute-start.27 = (f32[8,3,64,128]{3,2,1,0:T(8,128)}, f32[8,3,64,128]{3,2,1,0:T(8,128)}, u32[]{:S(2)}, u32[]{:S(2)}) collective-permute-start(f32[8,3,64,128]{3,2,1,0:T(8,128)} %get-tuple-element.125), channel_id=1, source_target_pairs={{0,1},{1,0},{2,3},{3,2},{4,5},{5,4},{6,7},{7,6},{8,9},{9,8},{10,11... | collective-permute-start | bytes 2359304 | tf_op jit(solution)/shard_map/ppermute | solution.py:582
  354.5 50.1 %collective-permute-start.33 = (f32[2,6,3,64,128]{4,3,2,1,0:T(8,128)}, f32[2,6,3,64,128]{4,3,2,1,0:T(8,128)S(1)}, u32[]{:S(2)}, u32[]{:S(2)}) collective-permute-start(f32[2,6,3,64,128]{4,3,2,1,0:T(8,128)} %get-tuple-element.136), channel_id=1, source_target_pairs={{0,16},{8,24},{16,0},{24,8},{1,17},{9,25},{17,1},{25,9},{2,18},{10... | collective-permute-start | bytes 3538952 | tf_op jit(solution)/shard_map/ppermute | solution.py:142
  354.6 52.7 %collective-permute-start.35 = (f32[6,6,64,128]{3,2,1,0:T(8,128)}, f32[6,6,64,128]{3,2,1,0:T(8,128)}, u32[]{:S(2)}, u32[]{:S(2)}) collective-permute-start(f32[6,6,64,128]{3,2,1,0:T(8,128)} %get-tuple-element.138), channel_id=1, source_target_pairs={{0,8},{8,0},{16,24},{24,16},{1,9},{9,1},{17,25},{25,17},{2,10},{10... | collective-permute-start | bytes 3538952 | tf_op jit(solution)/shard_map/ppermute | solution.py:133
  380.9 26.5 %collective-permute-start.37 = (f32[6,6,64,128]{3,2,1,0:T(8,128)S(1)}, f32[6,6,64,128]{3,2,1,0:T(8,128)}, u32[]{:S(2)}, u32[]{:S(2)}) collective-permute-start(f32[6,6,64,128]{3,2,1,0:T(8,128)S(1)} %slice_bitcast_fusion), channel_id=1, source_target_pairs={{0,8},{8,0},{16,24},{24,16},{1,9},{9,1},{17,25},{25,17},{2,10},{10... | collective-permute-start | bytes 3538952 | tf_op jit(solution)/shard_map/ppermute | solution.py:143
  382.1 33.4 %collective-permute-start.32 = (f32[6,3,64,128]{3,2,1,0:T(8,128)}, f32[6,3,64,128]{3,2,1,0:T(8,128)}, u32[]{:S(2)}, u32[]{:S(2)}) collective-permute-start(f32[6,3,64,128]{3,2,1,0:T(8,128)} %get-tuple-element.134), channel_id=1, source_target_pairs={{0,8},{8,0},{16,24},{24,16},{1,9},{9,1},{17,25},{25,17},{2,10},{10... | collective-permute-start | bytes 1769480 | tf_op jit(solution)/shard_map/ppermute | solution.py:133
  404.7 1.0 copy-start
  406.6 9.0 %collective-permute-start.34 = (f32[6,3,64,128]{3,2,1,0:T(8,128)}, f32[6,3,64,128]{3,2,1,0:T(8,128)}, u32[]{:S(2)}, u32[]{:S(2)}) collective-permute-start(f32[6,3,64,128]{3,2,1,0:T(8,128)} %slice_bitcast_fusion.5), channel_id=1, source_target_pairs={{0,8},{8,0},{16,24},{24,16},{1,9},{9,1},{17,25},{25,17},{2,10},{10... | collective-permute-start | bytes 1769480 | tf_op jit(solution)/shard_map/ppermute | solution.py:143

commit v7 on v6

--- a/solution.py
+++ b/solution.py
@@ -226,9 +226,9 @@
 def diffusion_kernel(n_own, n_halo, n_send, rate_ref, a_ref, b_ref, *refs):
     n_in = 2 * n_own + 2 * n_halo
     ins, keep, sends = refs[:n_in], refs[n_in], refs[n_in + 1 : n_in + 1 + n_send]
-    field, work, ra_ref, rb_ref, done, in_sems, out_sems = refs[n_in + 1 + n_send :]
+    field, work, done, in_sems, out_sems = refs[n_in + 1 + n_send :]
     tiles, block = keep.shape[0], keep.shape[1]
-    frame, pitches, side = work.shape
+    pair, frame, pitches, side = work.shape
     halo = (frame - 2 * block) // 2
     vregs = pitches // 8
     flip = lax.axis_index("inner") % 2
@@ -248,15 +248,20 @@
             at = jnp.where(flip == 0, place, frame - place - step)
             copies.append(
                 pltpu.make_async_copy(
-                    ins[i].at[g], field.at[slot, pl.ds(at, step)], in_sems.at[slot, i]
+                    ins[i].at[pl.ds(pair * g, pair)],
+                    field.at[slot, :, pl.ds(at, step)],
+                    in_sems.at[slot, i],
                 )
             )
         return copies
 
     def store(g, slot):
+        these = pl.ds(pair * g, pair)
         copies = [
             pltpu.make_async_copy(
-                done.at[slot, pl.ds(flip * block, block)], keep.at[g], out_sems.at[slot, n_send]
+                done.at[slot, :, pl.ds(flip * block, block)],
+                keep.at[these],
+                out_sems.at[slot, n_send],
             )
         ]
         first = (1 - flip) * block
@@ -264,20 +269,22 @@
             step = sends[k].shape[1]
             copies.append(
                 pltpu.make_async_copy(
-                    done.at[slot, pl.ds(first, step)], sends[k].at[g], out_sems.at[slot, k]
+                    done.at[slot, :, pl.ds(first, step)], sends[k].at[these], out_sems.at[slot, k]
                 )
             )
             first = first + step
         return copies
 
+    rounds = tiles // pair
+    both = range(pair)
     for copy in fetch(0, 0):
         copy.start()
 
-    @pl.loop(0, tiles)
+    @pl.loop(0, rounds)
     def _(g):
         slot = g % 2
 
-        @pl.when(g + 1 < tiles)
+        @pl.when(g + 1 < rounds)
         def _():
             for copy in fetch(g + 1, 1 - slot):
                 copy.start()
@@ -290,87 +297,73 @@
             for copy in store(g - 2, slot):
                 copy.wait()
 
-        rate = rate_ref[g]
-
-        def rows_of(ref, e):
-            return [ref[e, 8 * v : 8 * v + 8, :] for v in range(vregs)]
-
-        def write_work(e, rows):
-            for v in range(vregs):
-                work[e, 8 * v : 8 * v + 8, :] = rows[v]
-
-        def read_work(e):
-            return rows_of(work, e)
-
-        def read_field(e):
-            return [field[slot, e, pl.ds(v, 8, stride=vregs), :] for v in range(vregs)]
-
-        def write_done(e, rows):
-            for v in range(vregs):
-                done[slot, e - halo, pl.ds(v, 8, stride=vregs), :] = rows[v]
-
-        def scaled(e):
-            ra = [rate * x for x in rows_of(a_ref, e)]
-            rb = [rate * x for x in rows_of(b_ref, e)]
-            for v in range(vregs):
-                ra_ref[e, 8 * v : 8 * v + 8, :] = ra[v]
-                rb_ref[e, 8 * v : 8 * v + 8, :] = rb[v]
-            return ra, rb
-
-        def ready(e):
-            return rows_of(ra_ref, e), rows_of(rb_ref, e)
-
-        def sweep(first, count, read, write, rates, wide):
+        rate = [rate_ref[pair * g + i] for i in both]
+
+        def read_work(i, e, v):
+            return work[i, e, 8 * v : 8 * v + 8, :]
+
+        def write_work(i, e, v, value):
+            work[i, e, 8 * v : 8 * v + 8, :] = value
+
+        def read_field(i, e, v):
+            return field[slot, i, e, pl.ds(v, 8, stride=vregs), :]
+
+        def write_done(i, e, v, value):
+            done[slot, i, e - halo, pl.ds(v, 8, stride=vregs), :] = value
+
+        def sweep(first, count, read, write):
             def energy(e, here, below):
-                after = read(e + 1)
-                ra, rb = rates(e)
-                above = [ra[v] * (after[v] - here[v]) for v in range(vregs)]
-                nearby = here[1:] + [pltpu.roll(here[0], 7, 0)]
-                pitch = [rb[v] * (nearby[v] - here[v]) for v in range(vregs)]
-                before = [pltpu.roll(pitch[-1], 1, 0)] + pitch[:-1]
-                write(
-                    e,
-                    [
-                        here[v] + ((above[v] - below[v]) + (pitch[v] - before[v]))
-                        for v in range(vregs)
-                    ],
-                )
+                after = [[None] * vregs for _ in both]
+                above = [[None] * vregs for _ in both]
+                pitch = [[None] * vregs for _ in both]
+                turned = [pltpu.roll(here[i][0], 7, 0) for i in both]
+                for v in reversed(range(vregs)):
+                    a_rate = a_ref[e, 8 * v : 8 * v + 8, :]
+                    b_rate = b_ref[e, 8 * v : 8 * v + 8, :]
+                    for i in both:
+                        after[i][v] = read(i, e + 1, v)
+                        above[i][v] = a_rate * (after[i][v] - here[i][v])
+                        nearby = here[i][v + 1] if v + 1 < vregs else turned[i]
+                        pitch[i][v] = b_rate * (nearby - here[i][v])
+                        if v + 1 < vregs:
+                            change = (above[i][v + 1] - below[i][v + 1]) + (pitch[i][v + 1] - pitch[i][v])
+                            write(i, e, v + 1, here[i][v + 1] + rate[i] * change)
+                for i in both:
+                    before = pltpu.roll(pitch[i][-1], 1, 0)
+                    change = (above[i][0] - below[i][0]) + (pitch[i][0] - before)
+                    write(i, e, 0, here[i][0] + rate[i] * change)
                 return after, above
 
-            def several(e, carry, n):
-                here, below = list(carry[:vregs]), list(carry[vregs:])
-                for i in range(n):
-                    here, below = energy(e + i, here, below)
-                return (*here, *below)
-
-            edge = read(first - 1)
-            here = read(first)
-            ra = rates(first - 1)[0]
-            below = [ra[v] * (here[v] - edge[v]) for v in range(vregs)]
-            carry = lax.fori_loop(
-                0,
-                count // wide,
-                lambda i, carry: several(first + wide * i, carry, wide),
-                (*here, *below),
-            )
-            for left in range(2, wide, 2):
-
-                @pl.when(count % wide == left)
-                def _(left=left):
-                    several(first + count - left, carry, left)
-
-        sweep(1, frame - 2, read_field, write_work, scaled, 2)
+            def two(j, carry):
+                rows = [list(carry[vregs * i : vregs * (i + 1)]) for i in range(2 * pair)]
+                here, below = rows[:pair], rows[pair:]
+                e = first + 2 * j
+                here, below = energy(e, here, below)
+                here, below = energy(e + 1, here, below)
+                return tuple(x for row in here + below for x in row)
+
+            here = [[read(i, first, v) for v in range(vregs)] for i in both]
+            below = [
+                [
+                    a_ref[first - 1, 8 * v : 8 * v + 8, :] * (here[i][v] - read(i, first - 1, v))
+                    for v in range(vregs)
+                ]
+                for i in both
+            ]
+            lax.fori_loop(0, count // 2, two, tuple(x for row in here + below for x in row))
+
+        sweep(1, frame - 2, read_field, write_work)
 
         @pl.loop(1, PASSES - 1)
         def _(n):
-            sweep(n + 1, frame - 2 - 2 * n, read_work, write_work, ready, 4)
-
-        sweep(PASSES, frame - 2 * PASSES, read_work, write_done, ready, 4)
+            sweep(n + 1, frame - 2 - 2 * n, read_work, write_work)
+
+        sweep(PASSES, frame - 2 * PASSES, read_work, write_done)
 
         for copy in store(g, slot):
             copy.start()
 
-    for g in range(max(0, tiles - 2), tiles):
+    for g in range(max(0, rounds - 2), rounds):
         for copy in store(g, g % 2):
             copy.wait()
 
@@ -388,11 +381,9 @@
         in_specs=[VMEM] * 3 + [ANY] * len(ins),
         out_specs=[ANY] * (1 + len(steps)),
         scratch_shapes=[
+            pltpu.VMEM((2, 2, frame, pitches, side), F32),
             pltpu.VMEM((2, frame, pitches, side), F32),
-            pltpu.VMEM((frame, pitches, side), F32),
-            pltpu.VMEM((frame, pitches, side), F32),
-            pltpu.VMEM((frame, pitches, side), F32),
-            pltpu.VMEM((2, 2 * block, pitches, side), F32),
+            pltpu.VMEM((2, 2, 2 * block, pitches, side), F32),
             pltpu.SemaphoreType.DMA((2, len(ins))),
             pltpu.SemaphoreType.DMA((2, len(steps) + 1)),
         ],

time: 426 us -> 430 us (level)
    ppermute x9, starting transfers between devices: 3.13 us -> 8.17 us  [far_queue(): whole = lax.ppermute(send, 'sector', [(s, s ^ 2) for s in range(sectors)])]
    pallas_call x1, Pallas kernels: 52.3 us -> 56.9 us  [diffuse(): pl.pallas_call(functools.partial(diffusion_kernel, len(own), len(own_halo...]
  transfers between devices with their start and end apart: 38 -> 38, of which waited for: 20 -> 21; matrix products, arithmetic and copies ran while one was open for 4% -> 4% of each run, Pallas kernels for 21% -> 20%
where the time goes in v7:
time: 430 us; the launch traced here: 426 us
  waiting for transfers between devices  198 us (46%)
  Pallas kernels  158 us (37%)
  starting transfers between devices  51 us (12%)
  local copies, waits for them, and re-layouts  18.2 us (4%)
    ppermute x9, waiting for transfers between devices, far_queue(): whole = lax.ppermute(send, 'sector', [(s, s ^ 2) for s in range(sectors)])  111 us
    pallas_call x9, Pallas kernels, drift(): pl.pallas_call(functools.partial(drift_kernel, find, place, receive, n_lo...  66.7 us
    pallas_call x1, Pallas kernels, diffuse(): pl.pallas_call(functools.partial(diffusion_kernel, len(own), len(own_halo...  56.9 us
    ppermute x3, waiting for transfers between devices, paired_shards(): backs.append(lax.ppermute(last, 'inner', swap))  46.3 us
    pallas_call x9, Pallas kernels, pack(): pl.pallas_call(functools.partial(pack_kernel, offsets, finds, n_far, len(...  29.4 us
    ppermute x1, waiting for transfers between devices, paired_shards(): backs = [lax.ppermute(returns[0], 'inner', swap)]  17.3 us
    squeeze x9, local copies, waits for them, and re-layouts, far_queue(): whole[1]  11.9 us
    ppermute x5, starting transfers between devices, sector_exchange(): lax.ppermute(send, 'sector', [(s, s ^ d) for s in range(sectors)])  10.4 us
  transfers between devices with their start and end apart: 38, of which 21 were waited for; matrix products, arithmetic and copies ran while one was open for 4% of the time, Pallas kernels for 20%

profile of v7, /device:TPU:25, one launch (start us, length us, event | category | flops | bytes accessed | tf_op | source)
XLA Modules:
  0.0 426.0 jit_solution(12179049371981612086)
XLA Ops:
  0.0 3.6 pack_tiles.9
  3.6 1.6 collective-permute-start.2
  5.2 2.4 collective-permute-start.3
  7.6 3.0 pack_tiles.10
  10.7 31.9 %collective-permute-done.3.refs_2_ = f32[2,6,4,64,128]{4,3,2,1,0:T(8,128)} collective-permute-done((f32[2,6,4,64,128]{4,3,2,1,0:T(8,128)}, f32[2,6,4,64,128]{4,3,2,1,0:T(8,128)}, u32[]{:S(2)}, u32[]{:S(2)}) %collective-permute-start.3) | collective-permute-done | bytes 1572896 | tf_op jit(solution)/shard_map/ppermute | solution.py:142
  42.6 2.1 slice_bitcast_fusion.3
  45.6 4.7 %split_weights.1.w_ref = bf16[16,256,256]{2,1,0:T(8,128)(2,1)} custom-call(s32[1,4,16]{2,1,0:T(4,128)} %mid_ref.1, f32[32,128,128]{2,1,0:T(8,128)} %w_ref.1), custom_call_target="tpu_custom_call" | custom-call | bytes 1024 | tf_op jit(solution)/shard_map/split_weights/pallas_call | solution.py:52
  50.4 7.6 %drift_chunk.9 = (f32[8,4,64,128]{3,2,1,0:T(8,128)}, f32[8,4,64,128]{3,2,1,0:T(8,128)}, f32[8,128]{1,0:T(8,128)}) custom-call(s32[1,4,16]{2,1,0:T(4,128)} %sec_ref.35, s32[1,4,16]{2,1,0:T(4,128)} %til_ref.35, bf16[16,256,256]{2,1,0:T(8,128)(2,1)} %split_weights.1.w_ref, f32[16,64,2048]{2,1,0:T(8,128)} %refs_0_.19, ...), custom_call_target="tpu_custom_call" | custom-call | bytes 1024 | tf_op jit(solution)/shard_map/drift_chunk/pallas_call | solution.py:208
  57.9 3.0 pack_tiles.11
  61.0 1.8 collective-permute-start.5
  62.7 13.6 %collective-permute-done.refs_2_ = f32[2,6,4,64,128]{4,3,2,1,0:T(8,128)} collective-permute-done((f32[2,6,4,64,128]{4,3,2,1,0:T(8,128)}, f32[2,6,4,64,128]{4,3,2,1,0:T(8,128)}, u32[]{:S(2)}, u32[]{:S(2)}) %collective-permute-start) | collective-permute-done | bytes 1572896 | tf_op jit(solution)/shard_map/ppermute | solution.py:142
  76.3 1.2 slice_bitcast_fusion.4
  79.1 1.2 collective-permute-done.1.refs_3_
  81.1 1.8 broadcast_in_dim.47.b_ref
  82.8 1.8 broadcast_in_dim.45.a_ref
  84.6 3.0 collective-permute-start.16
  87.6 7.5 %drift_chunk.10 = (f32[8,4,64,128]{3,2,1,0:T(8,128)}, f32[8,4,64,128]{3,2,1,0:T(8,128)}, f32[8,128]{1,0:T(8,128)}) custom-call(s32[1,4,16]{2,1,0:T(4,128)} %sec_ref.35, s32[1,4,16]{2,1,0:T(4,128)} %til_ref.35, bf16[16,256,256]{2,1,0:T(8,128)(2,1)} %split_weights.1.w_ref, f32[16,64,2048]{2,1,0:T(8,128)} %refs_0_.19, ...), custom_call_target="tpu_custom_call" | custom-call | bytes 1024 | tf_op jit(solution)/shard_map/drift_chunk/pallas_call | solution.py:208
  95.3 1.3 collective-permute-start.19
  96.6 13.5 %collective-permute-done.5.refs_2_ = f32[2,6,4,64,128]{4,3,2,1,0:T(8,128)} collective-permute-done((f32[2,6,4,64,128]{4,3,2,1,0:T(8,128)}, f32[2,6,4,64,128]{4,3,2,1,0:T(8,128)}, u32[]{:S(2)}, u32[]{:S(2)}) %collective-permute-start.5) | collective-permute-done | bytes 1572896 | tf_op jit(solution)/shard_map/ppermute | solution.py:142
  110.0 2.1 slice_bitcast_fusion.2
  112.8 2.9 pack_tiles.12
  115.7 1.6 collective-permute-start.7
  117.2 2.3 collective-permute-start.17
  119.5 7.6 %drift_chunk.11 = (f32[8,4,64,128]{3,2,1,0:T(8,128)}, f32[8,4,64,128]{3,2,1,0:T(8,128)}, f32[8,128]{1,0:T(8,128)}) custom-call(s32[1,4,16]{2,1,0:T(4,128)} %sec_ref.35, s32[1,4,16]{2,1,0:T(4,128)} %til_ref.35, bf16[16,256,256]{2,1,0:T(8,128)(2,1)} %split_weights.1.w_ref, f32[16,64,2048]{2,1,0:T(8,128)} %refs_0_.19, ...), custom_call_target="tpu_custom_call" | custom-call | bytes 1024 | tf_op jit(solution)/shard_map/drift_chunk/pallas_call | solution.py:208
  127.2 1.3 collective-permute-start.20
  128.5 2.9 pack_tiles.13
  132.0 3.3 collective-permute-done.7.refs_2_
  137.4 4.0 collective-permute-done.17.refs_11_
  141.4 5.1 %collective-permute-start.18 = (f32[8,4,64,128]{3,2,1,0:T(8,128)}, f32[8,4,64,128]{3,2,1,0:T(8,128)}, u32[]{:S(2)}, u32[]{:S(2)}) collective-permute-start(f32[8,4,64,128]{3,2,1,0:T(8,128)} %get-tuple-element.110.refs_2_), channel_id=1, source_target_pairs={{1,3},{2,0},{3,5},{4,2},{5,7},{6,4},{9,11},{10,8},{11,13},{12,10},... | collective-permute-start | bytes 3145736 | tf_op jit(solution)/shard_map/ppermute | solution.py:528
  146.5 6.9 %drift_chunk.12 = (f32[8,2,64,128]{3,2,1,0:T(8,128)}, f32[8,2,64,128]{3,2,1,0:T(8,128)}, f32[8,128]{1,0:T(8,128)}) custom-call(s32[1,4,16]{2,1,0:T(4,128)} %sec_ref.35, s32[1,4,16]{2,1,0:T(4,128)} %til_ref.35, bf16[16,256,256]{2,1,0:T(8,128)(2,1)} %split_weights.1.w_ref, f32[16,64,2048]{2,1,0:T(8,128)} %refs_0_.19, ...), custom_call_target="tpu_custom_call" | custom-call | bytes 1024 | tf_op jit(solution)/shard_map/drift_chunk/pallas_call | solution.py:208
  153.9 1.3 collective-permute-start.21
  157.4 1.3 collective-permute-done.10.refs_3_
  159.5 6.9 %drift_chunk.13 = (f32[8,2,64,128]{3,2,1,0:T(8,128)}, f32[8,2,64,128]{3,2,1,0:T(8,128)}, f32[8,128]{1,0:T(8,128)}) custom-call(s32[1,4,16]{2,1,0:T(4,128)} %sec_ref.35, s32[1,4,16]{2,1,0:T(4,128)} %til_ref.35, bf16[16,256,256]{2,1,0:T(8,128)(2,1)} %split_weights.1.w_ref, f32[16,64,2048]{2,1,0:T(8,128)} %refs_0_.19, ...), custom_call_target="tpu_custom_call" | custom-call | bytes 1024 | tf_op jit(solution)/shard_map/drift_chunk/pallas_call | solution.py:208
  166.5 4.3 %collective-permute-start.15 = (f32[8,2,64,128]{3,2,1,0:T(8,128)}, f32[8,2,64,128]{3,2,1,0:T(8,128)}, u32[]{:S(2)}, u32[]{:S(2)}) collective-permute-start(f32[8,2,64,128]{3,2,1,0:T(8,128)} %get-tuple-element.106), channel_id=1, source_target_pairs={{0,1},{1,0},{2,3},{3,2},{4,5},{5,4},{6,7},{7,6},{8,9},{9,8},{10,11... | collective-permute-start | bytes 1572872 | tf_op jit(solution)/shard_map/ppermute | solution.py:519
  170.8 8.8 %collective-permute-done.21.refs_15_ = f32[8,4,64,128]{3,2,1,0:T(8,128)} collective-permute-done((f32[8,4,64,128]{3,2,1,0:T(8,128)}, f32[8,4,64,128]{3,2,1,0:T(8,128)}, u32[]{:S(2)}, u32[]{:S(2)}) %collective-permute-start.21) | collective-permute-done | bytes 1048608 | tf_op jit(solution)/shard_map/ppermute | solution.py:524
  179.6 3.5 collective-permute-done.15.refs_9_
  183.1 56.9 %diffuse_tiles.1 = (f32[8,16,64,128]{3,2,1,0:T(8,128)}, f32[8,3,64,128]{3,2,1,0:T(8,128)}, f32[8,4,64,128]{3,2,1,0:T(8,128)}, f32[8,6,64,128]{3,2,1,0:T(8,128)}, f32[8,3,64,128]{3,2,1,0:T(8,128)}) custom-call(f32[8,8,128]{2,1,0:T(8,128)} %broadcast_in_dim.43.rate_ref, f32[56,64,128]{2,1,0:T(8,128)} %broadcast_in_dim.45.a_ref, ...), custom_call_target="tpu_custom_call" | custom-call | bytes 1024 | tf_op jit(solution)/shard_map/diffuse_tiles/pallas_call | solution.py:376
  240.1 1.2 collective-permute-start.22
  241.3 17.3 %collective-permute-done.22.refs_1_ = f32[8,3,64,128]{3,2,1,0:T(8,128)} collective-permute-done((f32[8,3,64,128]{3,2,1,0:T(8,128)}, f32[8,3,64,128]{3,2,1,0:T(8,128)}, u32[]{:S(2)}, u32[]{:S(2)}) %collective-permute-start.22) | collective-permute-done | bytes 786464 | tf_op jit(solution)/shard_map/ppermute | solution.py:557
  258.6 3.4 pack_tiles.14
  263.3 21.9 %collective-permute-done.23.refs_1_ = f32[8,4,64,128]{3,2,1,0:T(8,128)} collective-permute-done((f32[8,4,64,128]{3,2,1,0:T(8,128)}, f32[8,4,64,128]{3,2,1,0:T(8,128)}, u32[]{:S(2)}, u32[]{:S(2)}) %collective-permute-start.23) | collective-permute-done | bytes 1048608 | tf_op jit(solution)/shard_map/ppermute | solution.py:559
  285.2 2.7 collective-permute-done.24.refs_3_
  287.9 1.5 collective-permute-start.25
  289.4 2.8 collective-permute-start.30
  292.2 3.5 pack_tiles.15
  297.6 1.8 collective-permute-done.31.refs_4_
  299.4 7.3 %drift_chunk.14 = (f32[16,64,2048]{2,1,0:T(8,128)}, f32[8,128]{1,0:T(8,128)}) custom-call(s32[1,4,16]{2,1,0:T(4,128)} %sec_ref.35, s32[1,4,16]{2,1,0:T(4,128)} %til_ref.35, bf16[16,256,256]{2,1,0:T(8,128)(2,1)} %split_weights.1.w_ref, f32[8,16,64,128]{3,2,1,0:T(8,128)} %get-tuple-element.115.refs_0_, f32[8,3,64,128]{3,2,1,0:T(8,128)} %collective-permute-done.22.refs_1_, ...), custom_call_target="tpu_custom_call" | custom-call | bytes 1024 | tf_op jit(solution)/shard_map/drift_chunk/pallas_call | solution.py:208
  306.6 14.6 %collective-permute-done.25.refs_1_ = f32[8,6,64,128]{3,2,1,0:T(8,128)} collective-permute-done((f32[8,6,64,128]{3,2,1,0:T(8,128)}, f32[8,6,64,128]{3,2,1,0:T(8,128)}, u32[]{:S(2)}, u32[]{:S(2)}) %collective-permute-start.25) | collective-permute-done | bytes 1572896 | tf_op jit(solution)/shard_map/ppermute | solution.py:573
  321.2 3.6 pack_tiles.17
  325.6 4.7 %collective-permute-start.28 = (f32[6,4,64,128]{3,2,1,0:T(8,128)}, f32[6,4,64,128]{3,2,1,0:T(8,128)}, u32[]{:S(2)}, u32[]{:S(2)}) collective-permute-start(f32[6,4,64,128]{3,2,1,0:T(8,128)} %get-tuple-element.127), channel_id=1, source_target_pairs={{0,8},{8,0},{16,24},{24,16},{1,9},{9,1},{17,25},{25,17},{2,10},{10... | collective-permute-start | bytes 2359304 | tf_op jit(solution)/shard_map/ppermute | solution.py:133
  330.3 1.5 collective-permute-done.26.refs_3_
  331.8 1.2 slice_bitcast_fusion.1
  333.0 1.9 collective-permute-start.29
  334.9 2.0 collective-permute-done.29.refs_4_
  336.9 7.6 %drift_chunk.15 = (f32[16,64,2048]{2,1,0:T(8,128)}, f32[8,128]{1,0:T(8,128)}) custom-call(s32[1,4,16]{2,1,0:T(4,128)} %sec_ref.35, s32[1,4,16]{2,1,0:T(4,128)} %til_ref.35, bf16[16,256,256]{2,1,0:T(8,128)(2,1)} %split_weights.1.w_ref, f32[8,16,64,128]{3,2,1,0:T(8,128)} %get-tuple-element.115.refs_0_, ...), custom_call_target="tpu_custom_call", output_to_operand_aliasing={{0}: (9, {})} | custom-call | bytes 1024 | tf_op jit(solution)/shard_map/drift_chunk/pallas_call | solution.py:208
  344.5 9.8 %collective-permute-done.27.refs_1_ = f32[8,3,64,128]{3,2,1,0:T(8,128)} collective-permute-done((f32[8,3,64,128]{3,2,1,0:T(8,128)}, f32[8,3,64,128]{3,2,1,0:T(8,128)}, u32[]{:S(2)}, u32[]{:S(2)}) %collective-permute-start.27) | collective-permute-done | bytes 786464 | tf_op jit(solution)/shard_map/ppermute | solution.py:573
  354.3 3.5 pack_tiles.16
  358.1 1.2 collective-permute-start.35
  359.3 23.1 %collective-permute-done.36.refs_3_ = f32[2,6,6,64,128]{4,3,2,1,0:T(8,128)} collective-permute-done((f32[2,6,6,64,128]{4,3,2,1,0:T(8,128)}, f32[2,6,6,64,128]{4,3,2,1,0:T(8,128)}, u32[]{:S(2)}, u32[]{:S(2)}) %collective-permute-start.36) | collective-permute-done | bytes 2359328 | tf_op jit(solution)/shard_map/ppermute | solution.py:142
  382.4 1.4 slice_bitcast_fusion
  383.8 1.9 collective-permute-start.37
  385.7 21.8 %collective-permute-done.33.refs_3_ = f32[2,6,3,64,128]{4,3,2,1,0:T(8,128)S(1)} collective-permute-done((f32[2,6,3,64,128]{4,3,2,1,0:T(8,128)}, f32[2,6,3,64,128]{4,3,2,1,0:T(8,128)S(1)}, u32[]{:S(2)}, u32[]{:S(2)}) %collective-permute-start.33) | collective-permute-done | bytes 1179680 | tf_op jit(solution)/shard_map/ppermute | solution.py:142
  410.6 8.1 %drift_chunk.16 = (f32[16,64,2048]{2,1,0:T(8,128)}, f32[8,128]{1,0:T(8,128)}) custom-call(s32[1,4,16]{2,1,0:T(4,128)} %sec_ref.35, s32[1,4,16]{2,1,0:T(4,128)} %til_ref.35, bf16[16,256,256]{2,1,0:T(8,128)(2,1)} %split_weights.1.w_ref, f32[8,16,64,128]{3,2,1,0:T(8,128)} %get-tuple-element.115.refs_0_, ...), custom_call_target="tpu_custom_call", output_to_operand_aliasing={{0}: (9, {})} | custom-call | bytes 1024 | tf_op jit(solution)/shard_map/drift_chunk/pallas_call | solution.py:208
  418.7 7.3 %drift_chunk.17 = (f32[16,64,2048]{2,1,0:T(8,128)}, f32[8,128]{1,0:T(8,128)}) custom-call(s32[1,4,16]{2,1,0:T(4,128)} %sec_ref.35, s32[1,4,16]{2,1,0:T(4,128)} %til_ref.35, bf16[16,256,256]{2,1,0:T(8,128)(2,1)} %split_weights.1.w_ref, f32[8,16,64,128]{3,2,1,0:T(8,128)} %get-tuple-element.115.refs_0_, ...), custom_call_target="tpu_custom_call", output_to_operand_aliasing={{0}: (9, {})} | custom-call | bytes 1024 | tf_op jit(solution)/shard_map/drift_chunk/pallas_call | solution.py:208
  (67 shorter events, 17.6 us)
Async XLA Ops:
  3.6 46.7 %collective-permute-start.2 = (f32[6,16,64,128]{3,2,1,0:T(8,128)}, f32[6,16,64,128]{3,2,1,0:T(8,128)}, u32[]{:S(2)}, u32[]{:S(2)}) collective-permute-start(f32[6,16,64,128]{3,2,1,0:T(8,128)} %get-tuple-element.79), channel_id=1, source_target_pairs={{0,8},{8,0},{16,24},{24,16},{1,9},{9,1},{17,25},{25,17},{2,10},{10... | collective-permute-start | bytes 9437192 | tf_op jit(solution)/shard_map/ppermute | solution.py:133
  5.2 37.4 %collective-permute-start.3 = (f32[2,6,4,64,128]{4,3,2,1,0:T(8,128)}, f32[2,6,4,64,128]{4,3,2,1,0:T(8,128)}, u32[]{:S(2)}, u32[]{:S(2)}) collective-permute-start(f32[2,6,4,64,128]{4,3,2,1,0:T(8,128)} %get-tuple-element.75.refs_1_), channel_id=1, source_target_pairs={{0,16},{8,24},{16,0},{24,8},{1,17},{9,25},{17,1},{25,9},{2,18},{10... | collective-permute-start | bytes 4718600 | tf_op jit(solution)/shard_map/ppermute | solution.py:142
  10.6 65.7 %collective-permute-start = (f32[2,6,4,64,128]{4,3,2,1,0:T(8,128)}, f32[2,6,4,64,128]{4,3,2,1,0:T(8,128)}, u32[]{:S(2)}, u32[]{:S(2)}) collective-permute-start(f32[2,6,4,64,128]{4,3,2,1,0:T(8,128)} %pack_tiles.10), channel_id=1, source_target_pairs={{0,16},{8,24},{16,0},{24,8},{1,17},{9,25},{17,1},{25,9},{2,18},{10... | collective-permute-start | bytes 4718600 | tf_op jit(solution)/shard_map/ppermute | solution.py:142
  44.7 5.6 %collective-permute-start.4 = (f32[6,4,64,128]{3,2,1,0:T(8,128)}, f32[6,4,64,128]{3,2,1,0:T(8,128)}, u32[]{:S(2)}, u32[]{:S(2)}) collective-permute-start(f32[6,4,64,128]{3,2,1,0:T(8,128)} %slice_bitcast_fusion.3), channel_id=1, source_target_pairs={{0,8},{8,0},{16,24},{24,16},{1,9},{9,1},{17,25},{25,17},{2,10},{10... | collective-permute-start | bytes 2359304 | tf_op jit(solution)/shard_map/ppermute | solution.py:143
  60.9 17.5 %copy-start.6 = (s32[1,8]{1,0:T(1,128)S(1)}, s32[1,8]{1,0:T(1,128)}, u32[]{:S(2)}) copy-start(s32[1,8]{1,0:T(1,128)} %param.14) | copy-start | bytes 100
  61.0 17.7 %copy-start.3 = (f32[128,64]{0,1:T(8,128)S(1)}, f32[128,64]{0,1:T(8,128)}, u32[]{:S(2)}) copy-start(f32[128,64]{0,1:T(8,128)} %param.16) | copy-start | bytes 98308
  61.0 17.7 %copy-start.4 = (f32[128,64]{0,1:T(8,128)S(1)}, f32[128,64]{0,1:T(8,128)}, u32[]{:S(2)}) copy-start(f32[128,64]{0,1:T(8,128)} %param.17) | copy-start | bytes 98308
  61.0 18.1 %copy-start.5 = (f32[1,8]{1,0:T(1,128)S(1)}, f32[1,8]{1,0:T(1,128)}, u32[]{:S(2)}) copy-start(f32[1,8]{1,0:T(1,128)} %param.15) | copy-start | bytes 100
  61.0 49.0 %collective-permute-start.5 = (f32[2,6,4,64,128]{4,3,2,1,0:T(8,128)}, f32[2,6,4,64,128]{4,3,2,1,0:T(8,128)}, u32[]{:S(2)}, u32[]{:S(2)}) collective-permute-start(f32[2,6,4,64,128]{4,3,2,1,0:T(8,128)} %pack_tiles.11), channel_id=1, source_target_pairs={{0,16},{8,24},{16,0},{24,8},{1,17},{9,25},{17,1},{25,9},{2,18},{10... | collective-permute-start | bytes 4718600 | tf_op jit(solution)/shard_map/ppermute | solution.py:142
  62.7 32.4 %collective-permute-start.11 = (f32[8,4,64,128]{3,2,1,0:T(8,128)}, f32[8,4,64,128]{3,2,1,0:T(8,128)}, u32[]{:S(2)}, u32[]{:S(2)}) collective-permute-start(f32[8,4,64,128]{3,2,1,0:T(8,128)} %get-tuple-element.95), channel_id=1, source_target_pairs={{0,1},{1,0},{2,3},{3,2},{4,5},{5,4},{6,7},{7,6},{8,9},{9,8},{10,11... | collective-permute-start | bytes 3145736 | tf_op jit(solution)/shard_map/ppermute | solution.py:519
  77.5 2.9 collective-permute-start.1
  80.4 4.2 copy-start.1
  84.6 32.6 %collective-permute-start.16 = (f32[8,4,64,128]{3,2,1,0:T(8,128)}, f32[8,4,64,128]{3,2,1,0:T(8,128)}, u32[]{:S(2)}, u32[]{:S(2)}) collective-permute-start(f32[8,4,64,128]{3,2,1,0:T(8,128)} %get-tuple-element.80.refs_0_), channel_id=1, source_target_pairs={{1,3},{2,0},{3,5},{4,2},{5,7},{6,4},{9,11},{10,8},{11,13},{12,10},... | collective-permute-start | bytes 3145736 | tf_op jit(solution)/shard_map/ppermute | solution.py:528
  95.2 31.9 %collective-permute-start.12 = (f32[8,4,64,128]{3,2,1,0:T(8,128)}, f32[8,4,64,128]{3,2,1,0:T(8,128)}, u32[]{:S(2)}, u32[]{:S(2)}) collective-permute-start(f32[8,4,64,128]{3,2,1,0:T(8,128)} %get-tuple-element.98), channel_id=1, source_target_pairs={{0,1},{1,0},{2,3},{3,2},{4,5},{5,4},{6,7},{7,6},{8,9},{9,8},{10,11... | collective-permute-start | bytes 3145736 | tf_op jit(solution)/shard_map/ppermute | solution.py:519
  95.3 31.9 %collective-permute-start.19 = (f32[8,4,64,128]{3,2,1,0:T(8,128)}, f32[8,4,64,128]{3,2,1,0:T(8,128)}, u32[]{:S(2)}, u32[]{:S(2)}) collective-permute-start(f32[8,4,64,128]{3,2,1,0:T(8,128)} %collective-permute-done.11.refs_5_), channel_id=1, source_target_pairs={{0,2},{2,4},{3,1},{4,6},{5,3},{7,5},{8,10},{10,12},{11,9},{12,14},... | collective-permute-start | bytes 3145736 | tf_op jit(solution)/shard_map/ppermute | solution.py:524
  112.1 7.4 %collective-permute-start.6 = (f32[6,4,64,128]{3,2,1,0:T(8,128)}, f32[6,4,64,128]{3,2,1,0:T(8,128)}, u32[]{:S(2)}, u32[]{:S(2)}) collective-permute-start(f32[6,4,64,128]{3,2,1,0:T(8,128)} %slice_bitcast_fusion.2), channel_id=1, source_target_pairs={{0,8},{8,0},{16,24},{24,16},{1,9},{9,1},{17,25},{25,17},{2,10},{10... | collective-permute-start | bytes 2359304 | tf_op jit(solution)/shard_map/ppermute | solution.py:143
  115.7 19.7 %collective-permute-start.7 = (f32[2,6,2,64,128]{4,3,2,1,0:T(8,128)}, f32[2,6,2,64,128]{4,3,2,1,0:T(8,128)}, u32[]{:S(2)}, u32[]{:S(2)}) collective-permute-start(f32[2,6,2,64,128]{4,3,2,1,0:T(8,128)} %pack_tiles.12), channel_id=1, source_target_pairs={{0,16},{8,24},{16,0},{24,8},{1,17},{9,25},{17,1},{25,9},{2,18},{10... | collective-permute-start | bytes 2359304 | tf_op jit(solution)/shard_map/ppermute | solution.py:142
  117.2 24.2 %collective-permute-start.17 = (f32[8,4,64,128]{3,2,1,0:T(8,128)}, f32[8,4,64,128]{3,2,1,0:T(8,128)}, u32[]{:S(2)}, u32[]{:S(2)}) collective-permute-start(f32[8,4,64,128]{3,2,1,0:T(8,128)} %get-tuple-element.108.refs_1_), channel_id=1, source_target_pairs={{1,3},{2,0},{3,5},{4,2},{5,7},{6,4},{9,11},{10,8},{11,13},{12,10},... | collective-permute-start | bytes 3145736 | tf_op jit(solution)/shard_map/ppermute | solution.py:528
  127.1 26.4 %collective-permute-start.13 = (f32[8,4,64,128]{3,2,1,0:T(8,128)}, f32[8,4,64,128]{3,2,1,0:T(8,128)}, u32[]{:S(2)}, u32[]{:S(2)}) collective-permute-start(f32[8,4,64,128]{3,2,1,0:T(8,128)} %get-tuple-element.101), channel_id=1, source_target_pairs={{0,1},{1,0},{2,3},{3,2},{4,5},{5,4},{6,7},{7,6},{8,9},{9,8},{10,11... | collective-permute-start | bytes 3145736 | tf_op jit(solution)/shard_map/ppermute | solution.py:519
  127.2 26.7 %collective-permute-start.20 = (f32[8,4,64,128]{3,2,1,0:T(8,128)}, f32[8,4,64,128]{3,2,1,0:T(8,128)}, u32[]{:S(2)}, u32[]{:S(2)}) collective-permute-start(f32[8,4,64,128]{3,2,1,0:T(8,128)} %collective-permute-done.12.refs_6_), channel_id=1, source_target_pairs={{0,2},{2,4},{3,1},{4,6},{5,3},{7,5},{8,10},{10,12},{11,9},{12,14},... | collective-permute-start | bytes 3145736 | tf_op jit(solution)/shard_map/ppermute | solution.py:524
  131.4 23.8 %collective-permute-start.9 = (f32[2,6,2,64,128]{4,3,2,1,0:T(8,128)}, f32[2,6,2,64,128]{4,3,2,1,0:T(8,128)}, u32[]{:S(2)}, u32[]{:S(2)}) collective-permute-start(f32[2,6,2,64,128]{4,3,2,1,0:T(8,128)} %pack_tiles.13), channel_id=1, source_target_pairs={{0,16},{8,24},{16,0},{24,8},{1,17},{9,25},{17,1},{25,9},{2,18},{10... | collective-permute-start | bytes 2359304 | tf_op jit(solution)/shard_map/ppermute | solution.py:142
  136.4 10.1 %collective-permute-start.8 = (f32[6,2,64,128]{3,2,1,0:T(8,128)S(1)}, f32[6,2,64,128]{3,2,1,0:T(8,128)}, u32[]{:S(2)}, u32[]{:S(2)}) collective-permute-start(f32[6,2,64,128]{3,2,1,0:T(8,128)S(1)} %slice_bitcast_fusion.8), channel_id=1, source_target_pairs={{0,8},{8,0},{16,24},{24,16},{1,9},{9,1},{17,25},{25,17},{2,10},{10... | collective-permute-start | bytes 1179656 | tf_op jit(solution)/shard_map/ppermute | solution.py:143
  141.4 29.4 %collective-permute-start.18 = (f32[8,4,64,128]{3,2,1,0:T(8,128)}, f32[8,4,64,128]{3,2,1,0:T(8,128)}, u32[]{:S(2)}, u32[]{:S(2)}) collective-permute-start(f32[8,4,64,128]{3,2,1,0:T(8,128)} %get-tuple-element.110.refs_2_), channel_id=1, source_target_pairs={{1,3},{2,0},{3,5},{4,2},{5,7},{6,4},{9,11},{10,8},{11,13},{12,10},... | collective-permute-start | bytes 3145736 | tf_op jit(solution)/shard_map/ppermute | solution.py:528
  153.9 12.6 %collective-permute-start.14 = (f32[8,2,64,128]{3,2,1,0:T(8,128)}, f32[8,2,64,128]{3,2,1,0:T(8,128)}, u32[]{:S(2)}, u32[]{:S(2)}) collective-permute-start(f32[8,2,64,128]{3,2,1,0:T(8,128)} %get-tuple-element.104), channel_id=1, source_target_pairs={{0,1},{1,0},{2,3},{3,2},{4,5},{5,4},{6,7},{7,6},{8,9},{9,8},{10,11... | collective-permute-start | bytes 1572872 | tf_op jit(solution)/shard_map/ppermute | solution.py:519
  153.9 25.8 %collective-permute-start.21 = (f32[8,4,64,128]{3,2,1,0:T(8,128)}, f32[8,4,64,128]{3,2,1,0:T(8,128)}, u32[]{:S(2)}, u32[]{:S(2)}) collective-permute-start(f32[8,4,64,128]{3,2,1,0:T(8,128)} %collective-permute-done.13.refs_7_), channel_id=1, source_target_pairs={{0,2},{2,4},{3,1},{4,6},{5,3},{7,5},{8,10},{10,12},{11,9},{12,14},... | collective-permute-start | bytes 3145736 | tf_op jit(solution)/shard_map/ppermute | solution.py:524
  156.2 2.5 collective-permute-start.10
  158.7 0.8 copy-start.2
  166.5 16.6 %collective-permute-start.15 = (f32[8,2,64,128]{3,2,1,0:T(8,128)}, f32[8,2,64,128]{3,2,1,0:T(8,128)}, u32[]{:S(2)}, u32[]{:S(2)}) collective-permute-start(f32[8,2,64,128]{3,2,1,0:T(8,128)} %get-tuple-element.106), channel_id=1, source_target_pairs={{0,1},{1,0},{2,3},{3,2},{4,5},{5,4},{6,7},{7,6},{8,9},{9,8},{10,11... | collective-permute-start | bytes 1572872 | tf_op jit(solution)/shard_map/ppermute | solution.py:519
  240.1 18.5 %collective-permute-start.22 = (f32[8,3,64,128]{3,2,1,0:T(8,128)}, f32[8,3,64,128]{3,2,1,0:T(8,128)}, u32[]{:S(2)}, u32[]{:S(2)}) collective-permute-start(f32[8,3,64,128]{3,2,1,0:T(8,128)} %get-tuple-element.119), channel_id=1, source_target_pairs={{0,1},{1,0},{2,3},{3,2},{4,5},{5,4},{6,7},{7,6},{8,9},{9,8},{10,11... | collective-permute-start | bytes 2359304 | tf_op jit(solution)/shard_map/ppermute | solution.py:557
  262.1 25.8 %collective-permute-start.24 = (f32[2,6,3,64,128]{4,3,2,1,0:T(8,128)}, f32[2,6,3,64,128]{4,3,2,1,0:T(8,128)}, u32[]{:S(2)}, u32[]{:S(2)}) collective-permute-start(f32[2,6,3,64,128]{4,3,2,1,0:T(8,128)} %get-tuple-element.122), channel_id=1, source_target_pairs={{0,16},{8,24},{16,0},{24,8},{1,17},{9,25},{17,1},{25,9},{2,18},{10... | collective-permute-start | bytes 3538952 | tf_op jit(solution)/shard_map/ppermute | solution.py:142
  262.4 22.8 %collective-permute-start.23 = (f32[8,4,64,128]{3,2,1,0:T(8,128)}, f32[8,4,64,128]{3,2,1,0:T(8,128)}, u32[]{:S(2)}, u32[]{:S(2)}) collective-permute-start(f32[8,4,64,128]{3,2,1,0:T(8,128)} %get-tuple-element.120), channel_id=1, source_target_pairs={{0,1},{1,0},{2,3},{3,2},{4,5},{5,4},{6,7},{7,6},{8,9},{9,8},{10,11... | collective-permute-start | bytes 3145736 | tf_op jit(solution)/shard_map/ppermute | solution.py:559
  287.9 33.3 %collective-permute-start.25 = (f32[8,6,64,128]{3,2,1,0:T(8,128)}, f32[8,6,64,128]{3,2,1,0:T(8,128)}, u32[]{:S(2)}, u32[]{:S(2)}) collective-permute-start(f32[8,6,64,128]{3,2,1,0:T(8,128)} %get-tuple-element.123), channel_id=1, source_target_pairs={{0,1},{1,0},{2,3},{3,2},{4,5},{5,4},{6,7},{7,6},{8,9},{9,8},{10,11... | collective-permute-start | bytes 4718600 | tf_op jit(solution)/shard_map/ppermute | solution.py:573
  289.4 8.2 %collective-permute-start.30 = (f32[6,3,64,128]{3,2,1,0:T(8,128)}, f32[6,3,64,128]{3,2,1,0:T(8,128)}, u32[]{:S(2)}, u32[]{:S(2)}) collective-permute-start(f32[6,3,64,128]{3,2,1,0:T(8,128)} %get-tuple-element.129), channel_id=1, source_target_pairs={{0,8},{8,0},{16,24},{24,16},{1,9},{9,1},{17,25},{25,17},{2,10},{10... | collective-permute-start | bytes 1769480 | tf_op jit(solution)/shard_map/ppermute | solution.py:133
  295.7 36.1 %collective-permute-start.26 = (f32[2,6,4,64,128]{4,3,2,1,0:T(8,128)}, f32[2,6,4,64,128]{4,3,2,1,0:T(8,128)}, u32[]{:S(2)}, u32[]{:S(2)}) collective-permute-start(f32[2,6,4,64,128]{4,3,2,1,0:T(8,128)} %get-tuple-element.124), channel_id=1, source_target_pairs={{0,16},{8,24},{16,0},{24,8},{1,17},{9,25},{17,1},{25,9},{2,18},{10... | collective-permute-start | bytes 4718600 | tf_op jit(solution)/shard_map/ppermute | solution.py:142
  297.2 2.2 collective-permute-start.31
  324.8 57.6 %collective-permute-start.36 = (f32[2,6,6,64,128]{4,3,2,1,0:T(8,128)}, f32[2,6,6,64,128]{4,3,2,1,0:T(8,128)}, u32[]{:S(2)}, u32[]{:S(2)}) collective-permute-start(f32[2,6,6,64,128]{4,3,2,1,0:T(8,128)} %get-tuple-element.140), channel_id=1, source_target_pairs={{0,16},{8,24},{16,0},{24,8},{1,17},{9,25},{17,1},{25,9},{2,18},{10... | collective-permute-start | bytes 7077896 | tf_op jit(solution)/shard_map/ppermute | solution.py:142
  325.6 9.3 %collective-permute-start.28 = (f32[6,4,64,128]{3,2,1,0:T(8,128)}, f32[6,4,64,128]{3,2,1,0:T(8,128)}, u32[]{:S(2)}, u32[]{:S(2)}) collective-permute-start(f32[6,4,64,128]{3,2,1,0:T(8,128)} %get-tuple-element.127), channel_id=1, source_target_pairs={{0,8},{8,0},{16,24},{24,16},{1,9},{9,1},{17,25},{25,17},{2,10},{10... | collective-permute-start | bytes 2359304 | tf_op jit(solution)/shard_map/ppermute | solution.py:133
  333.0 3.9 collective-permute-start.29
  334.9 19.4 %collective-permute-start.27 = (f32[8,3,64,128]{3,2,1,0:T(8,128)}, f32[8,3,64,128]{3,2,1,0:T(8,128)}, u32[]{:S(2)}, u32[]{:S(2)}) collective-permute-start(f32[8,3,64,128]{3,2,1,0:T(8,128)} %get-tuple-element.125), channel_id=1, source_target_pairs={{0,1},{1,0},{2,3},{3,2},{4,5},{5,4},{6,7},{7,6},{8,9},{9,8},{10,11... | collective-permute-start | bytes 2359304 | tf_op jit(solution)/shard_map/ppermute | solution.py:573
  357.8 49.7 %collective-permute-start.33 = (f32[2,6,3,64,128]{4,3,2,1,0:T(8,128)}, f32[2,6,3,64,128]{4,3,2,1,0:T(8,128)S(1)}, u32[]{:S(2)}, u32[]{:S(2)}) collective-permute-start(f32[2,6,3,64,128]{4,3,2,1,0:T(8,128)} %get-tuple-element.136), channel_id=1, source_target_pairs={{0,16},{8,24},{16,0},{24,8},{1,17},{9,25},{17,1},{25,9},{2,18},{10... | collective-permute-start | bytes 3538952 | tf_op jit(solution)/shard_map/ppermute | solution.py:142
  358.1 52.5 %collective-permute-start.35 = (f32[6,6,64,128]{3,2,1,0:T(8,128)}, f32[6,6,64,128]{3,2,1,0:T(8,128)}, u32[]{:S(2)}, u32[]{:S(2)}) collective-permute-start(f32[6,6,64,128]{3,2,1,0:T(8,128)} %get-tuple-element.138), channel_id=1, source_target_pairs={{0,8},{8,0},{16,24},{24,16},{1,9},{9,1},{17,25},{25,17},{2,10},{10... | collective-permute-start | bytes 3538952 | tf_op jit(solution)/shard_map/ppermute | solution.py:133
  383.8 26.8 %collective-permute-start.37 = (f32[6,6,64,128]{3,2,1,0:T(8,128)S(1)}, f32[6,6,64,128]{3,2,1,0:T(8,128)}, u32[]{:S(2)}, u32[]{:S(2)}) collective-permute-start(f32[6,6,64,128]{3,2,1,0:T(8,128)S(1)} %slice_bitcast_fusion), channel_id=1, source_target_pairs={{0,8},{8,0},{16,24},{24,16},{1,9},{9,1},{17,25},{25,17},{2,10},{10... | collective-permute-start | bytes 3538952 | tf_op jit(solution)/shard_map/ppermute | solution.py:143
  385.7 33.1 %collective-permute-start.32 = (f32[6,3,64,128]{3,2,1,0:T(8,128)}, f32[6,3,64,128]{3,2,1,0:T(8,128)}, u32[]{:S(2)}, u32[]{:S(2)}) collective-permute-start(f32[6,3,64,128]{3,2,1,0:T(8,128)} %get-tuple-element.134), channel_id=1, source_target_pairs={{0,8},{8,0},{16,24},{24,16},{1,9},{9,1},{17,25},{25,17},{2,10},{10... | collective-permute-start | bytes 1769480 | tf_op jit(solution)/shard_map/ppermute | solution.py:133
  407.6 1.0 copy-start
  409.5 9.3 %collective-permute-start.34 = (f32[6,3,64,128]{3,2,1,0:T(8,128)}, f32[6,3,64,128]{3,2,1,0:T(8,128)}, u32[]{:S(2)}, u32[]{:S(2)}) collective-permute-start(f32[6,3,64,128]{3,2,1,0:T(8,128)} %slice_bitcast_fusion.5), channel_id=1, source_target_pairs={{0,8},{8,0},{16,24},{24,16},{1,9},{9,1},{17,25},{25,17},{2,10},{10... | collective-permute-start | bytes 1769480 | tf_op jit(solution)/shard_map/ppermute | solution.py:143

commit v8 on v6

--- a/solution.py
+++ b/solution.py
@@ -223,7 +223,7 @@
     )(*ins)
 
 
-def diffusion_kernel(n_own, n_halo, n_send, rate_ref, a_ref, b_ref, *refs):
+def diffusion_kernel(n_own, n_halo, n_send, first_tile, rate_ref, a_ref, b_ref, *refs):
     n_in = 2 * n_own + 2 * n_halo
     ins, keep, sends = refs[:n_in], refs[n_in], refs[n_in + 1 : n_in + 1 + n_send]
     field, work, ra_ref, rb_ref, done, in_sems, out_sems = refs[n_in + 1 + n_send :]
@@ -248,7 +248,7 @@
             at = jnp.where(flip == 0, place, frame - place - step)
             copies.append(
                 pltpu.make_async_copy(
-                    ins[i].at[g], field.at[slot, pl.ds(at, step)], in_sems.at[slot, i]
+                    ins[i].at[first_tile + g], field.at[slot, pl.ds(at, step)], in_sems.at[slot, i]
                 )
             )
         return copies
@@ -290,7 +290,7 @@
             for copy in store(g - 2, slot):
                 copy.wait()
 
-        rate = rate_ref[g]
+        rate = rate_ref[first_tile + g]
 
         def rows_of(ref, e):
             return [ref[e, 8 * v : 8 * v + 8, :] for v in range(vregs)]
@@ -375,13 +375,13 @@
             copy.wait()
 
 
-def diffuse(rate, a, b, own, got, own_halo, got_halo, steps):
-    tiles, _, pitches, side = own[0].shape
+def diffuse(rate, a, b, own, got, own_halo, got_halo, steps, first_tile, tiles):
+    pitches, side = own[0].shape[2:]
     frame = a.shape[0]
     block = sum(steps)
     ins = [*own, *got, *own_halo, *got_halo]
     out = pl.pallas_call(
-        functools.partial(diffusion_kernel, len(own), len(own_halo), len(steps)),
+        functools.partial(diffusion_kernel, len(own), len(own_halo), len(steps), first_tile),
         out_shape=[
             jax.ShapeDtypeStruct((tiles, step, pitches, side), F32) for step in (block, *steps)
         ],
@@ -431,7 +431,8 @@
     first_steps = (quarter, quarter, quarter, quarter // 2, quarter - quarter // 2)
     halo_chunks = PASSES // quarter
     less = quarter - quarter // 4
-    last_steps = (less, quarter, block - quarter - 2 * less, less)
+    more = block // 2 - less
+    last_steps = (less, more, more, less)
     cap = slots(tiles, sectors)
     tables = (source_sector, source_tile)
     near, far = [1], list(range(2, sectors))
@@ -536,17 +537,31 @@
                 (kept,), (own_halo[k - 1],) = in_turn([kept], [own_halo[k - 1]])
             own_halo.append(lax.ppermute(kept, "inner", own_pairs))
 
-    kept, sends = diffuse(rate, a, b, own, got, own_halo, got_halo, last_steps)
-
-    returns, ready, out, start = sends, [], (), 0
+    fields = (rate, a, b, own, got, own_halo, got_halo)
+    quad = half // 2
+    kept_low, low = diffuse(*fields, (last_steps[0] + last_steps[1], *last_steps[2:]), 0, quad)
+    kept_high, high = diffuse(*fields, last_steps, quad, quad)
+
+    ready, out, start = [], (), 0
     for k, step in enumerate(last_steps):
 
-        def find(mine, theirs, start=start, step=step):
-            here = side_here()
-            return lambda t: [
-                ((t // half) == here, lambda: mine.at[t % half, pl.ds(start, step)]),
-                ((t // half) != here, lambda: theirs.at[t % half]),
-            ]
+        def find(mine_low, mine_high, their_low, their_high, k=k, start=start, step=step):
+            here, there = pl.ds(start, step), pl.ds(start if k < 2 else 0, step)
+
+            def pieces(t):
+                ours = (t // half) == side_here()
+                rank = t % half
+                lower = rank < quad
+                both, theirs = jnp.logical_and, jnp.logical_not(ours)
+                upper = jnp.logical_not(lower)
+                return [
+                    (both(ours, lower), lambda: mine_low.at[rank % quad, here]),
+                    (both(ours, upper), lambda: mine_high.at[rank % quad, here]),
+                    (both(theirs, lower), lambda: their_low.at[rank % quad, there]),
+                    (both(theirs, upper), lambda: their_high.at[rank % quad]),
+                ]
+
+            return pieces
 
         def place(result, start=start, step=step):
             return lambda t: [(t >= 0, lambda: result.at[pl.ds(start, step), :, at_lanes(t)])]
@@ -559,13 +574,16 @@
 
     def pack_last(k, after):
         find, _, piece = ready[k]
-        sends = pack([(d, find, piece) for d in far + near], cap, tables, [kept, backs[k]], after)
+        local = [kept_low, kept_high, backs_low[k], backs_high[k]]
+        sends = pack([(d, find, piece) for d in far + near], cap, tables, local, after)
         return sends[1:], sends[0]
 
     whole = [jax.ShapeDtypeStruct(density.shape, F32)]
-    backs = [lax.ppermute(returns[0], "inner", swap)]
-    (last,), (backs[0],) = in_turn([returns[1]], [backs[0]])
-    backs.append(lax.ppermute(last, "inner", swap))
+    early = lax.ppermute(low[0], "inner", swap)
+    (last,), (early,) = in_turn([high[0]], [early])
+    backs_low, backs_high = [early, early], [lax.ppermute(last, "inner", swap)]
+    (last,), (backs_high[0],) = in_turn([high[1]], [backs_high[0]])
+    backs_high.append(lax.ppermute(last, "inner", swap))
     sends, far_sends = pack_last(0, ())
     came = []
     far_queue(came, far_sends)
@@ -578,10 +596,14 @@
             far_queue(came, far_sends)
             beside_next = sector_exchange(sends, near)
         if k + 2 < len(ready):
-            (last,), (backs[k + 1], came[k][0]) = in_turn([returns[k + 2]], [backs[k + 1], came[k][0]])
-            backs.append(lax.ppermute(last, "inner", swap))
+            pair, (backs_high[k + 1], came[k][0]) = in_turn(
+                [low[k + 1], high[k + 2]], [backs_high[k + 1], came[k][0]]
+            )
+            backs_low.append(lax.ppermute(pair[0], "inner", swap))
+            backs_high.append(lax.ppermute(pair[1], "inner", swap))
+        local = [kept_low, kept_high, backs_low[k], backs_high[k]]
         *out, token = drift(
-            find, place, receive_slot, tables, weights, [kept, backs[k]], beside + came[k], whole, piece, after, out
+            find, place, receive_slot, tables, weights, local, beside + came[k], whole, piece, after, out
         )
         beside = beside_next
     return out[0]

time: 426 us -> 415 us (0.974)
  waiting for transfers between devices: 198 us -> 161 us
  starting transfers between devices: 49.7 us -> 71.3 us
    ppermute x4 -> x7, waiting for transfers between devices: 64.8 us -> 32.9 us  [the longest x1 9.29 us: paired_shards(): backs_high.append(lax.ppermute(last, 'inner', swap))]
    ppermute x9, starting transfers between devices: 12.1 us -> 29.8 us  [far_queue(): lax.ppermute(whole[1], 'sector', [(s, s ^ 1) for s in range(sectors)])]
    pallas_call x1 -> x2, Pallas kernels: 52.3 us -> 57.1 us  [diffuse(): pl.pallas_call(functools.partial(diffusion_kernel, len(own), len(own_halo...]
    ppermute x9, waiting for transfers between devices: 110 us -> 105 us  [far_queue(): whole = lax.ppermute(send, 'sector', [(s, s ^ 2) for s in range(sectors)])]
  transfers between devices with their start and end apart: 38 -> 41, of which waited for: 20 -> 21; matrix products, arithmetic and copies ran while one was open for 4% -> 4% of each run, Pallas kernels for 21% -> 29%
where the time goes in v8:
time: 415 us; the launch traced here: 412 us
  waiting for transfers between devices  161 us (39%)
  Pallas kernels  160 us (39%)
  starting transfers between devices  71.3 us (17%)
  local copies, waits for them, and re-layouts  18.3 us (4%)
    ppermute x9, waiting for transfers between devices, far_queue(): whole = lax.ppermute(send, 'sector', [(s, s ^ 2) for s in range(sectors)])  105 us
    pallas_call x9, Pallas kernels, drift(): pl.pallas_call(functools.partial(drift_kernel, find, place, receive, n_lo...  66.7 us
    pallas_call x2, Pallas kernels, diffuse(): pl.pallas_call(functools.partial(diffusion_kernel, len(own), len(own_halo...  57.1 us
    pallas_call x9, Pallas kernels, pack(): pl.pallas_call(functools.partial(pack_kernel, offsets, finds, n_far, len(...  31.9 us
    ppermute x9, starting transfers between devices, far_queue(): lax.ppermute(whole[1], 'sector', [(s, s ^ 1) for s in range(sectors)])  29.8 us
    ppermute x3, starting transfers between devices, paired_shards(): own_halo.append(lax.ppermute(kept, 'inner', own_pairs))  12.9 us
    squeeze x9, local copies, waits for them, and re-layouts, far_queue(): whole[1]  12 us
    ppermute x1, waiting for transfers between devices, paired_shards(): backs_high.append(lax.ppermute(last, 'inner', swap))  9.29 us
  transfers between devices with their start and end apart: 41, of which 21 were waited for; matrix products, arithmetic and copies ran while one was open for 4% of the time, Pallas kernels for 29%

profile of v8, /device:TPU:25, one launch (start us, length us, event | category | flops | bytes accessed | tf_op | source)
XLA Modules:
  0.0 412.2 jit_solution(4751752577286113453)
XLA Ops:
  0.0 3.8 pack_tiles.9
  3.8 1.8 collective-permute-start.2
  6.1 3.1 pack_tiles.10
  10.3 31.5 %collective-permute-done.3.refs_2_ = f32[2,6,4,64,128]{4,3,2,1,0:T(8,128)} collective-permute-done((f32[2,6,4,64,128]{4,3,2,1,0:T(8,128)}, f32[2,6,4,64,128]{4,3,2,1,0:T(8,128)}, u32[]{:S(2)}, u32[]{:S(2)}) %collective-permute-start.3) | collective-permute-done | bytes 1572896 | tf_op jit(solution)/shard_map/ppermute | solution.py:142
  41.9 2.1 slice_bitcast_fusion.3
  44.0 1.3 collective-permute-start.4
  45.3 4.7 %split_weights.1.w_ref = bf16[16,256,256]{2,1,0:T(8,128)(2,1)} custom-call(s32[1,4,16]{2,1,0:T(4,128)} %mid_ref.1, f32[32,128,128]{2,1,0:T(8,128)} %w_ref.1), custom_call_target="tpu_custom_call" | custom-call | bytes 1024 | tf_op jit(solution)/shard_map/split_weights/pallas_call | solution.py:52
  50.0 7.5 %drift_chunk.9 = (f32[8,4,64,128]{3,2,1,0:T(8,128)}, f32[8,4,64,128]{3,2,1,0:T(8,128)}, f32[8,128]{1,0:T(8,128)}) custom-call(s32[1,4,16]{2,1,0:T(4,128)} %sec_ref.35, s32[1,4,16]{2,1,0:T(4,128)} %til_ref.35, bf16[16,256,256]{2,1,0:T(8,128)(2,1)} %split_weights.1.w_ref, f32[16,64,2048]{2,1,0:T(8,128)} %refs_0_.19, ...), custom_call_target="tpu_custom_call" | custom-call | bytes 1024 | tf_op jit(solution)/shard_map/drift_chunk/pallas_call | solution.py:208
  57.6 3.2 pack_tiles.11
  61.7 2.3 collective-permute-start.11
  63.9 11.6 %collective-permute-done.refs_2_ = f32[2,6,4,64,128]{4,3,2,1,0:T(8,128)} collective-permute-done((f32[2,6,4,64,128]{4,3,2,1,0:T(8,128)}, f32[2,6,4,64,128]{4,3,2,1,0:T(8,128)}, u32[]{:S(2)}, u32[]{:S(2)}) %collective-permute-start) | collective-permute-done | bytes 1572896 | tf_op jit(solution)/shard_map/ppermute | solution.py:142
  75.6 1.2 slice_bitcast_fusion.4
  76.8 1.4 collective-permute-start.1
  80.8 1.9 broadcast_in_dim.47.b_ref
  82.7 1.8 broadcast_in_dim.45.a_ref
  84.4 3.4 collective-permute-start.16
  87.8 7.5 %drift_chunk.10 = (f32[8,4,64,128]{3,2,1,0:T(8,128)}, f32[8,4,64,128]{3,2,1,0:T(8,128)}, f32[8,128]{1,0:T(8,128)}) custom-call(s32[1,4,16]{2,1,0:T(4,128)} %sec_ref.35, s32[1,4,16]{2,1,0:T(4,128)} %til_ref.35, bf16[16,256,256]{2,1,0:T(8,128)(2,1)} %split_weights.1.w_ref, f32[16,64,2048]{2,1,0:T(8,128)} %refs_0_.19, ...), custom_call_target="tpu_custom_call" | custom-call | bytes 1024 | tf_op jit(solution)/shard_map/drift_chunk/pallas_call | solution.py:208
  95.5 1.3 collective-permute-start.19
  96.8 12.5 %collective-permute-done.5.refs_2_ = f32[2,6,4,64,128]{4,3,2,1,0:T(8,128)} collective-permute-done((f32[2,6,4,64,128]{4,3,2,1,0:T(8,128)}, f32[2,6,4,64,128]{4,3,2,1,0:T(8,128)}, u32[]{:S(2)}, u32[]{:S(2)}) %collective-permute-start.5) | collective-permute-done | bytes 1572896 | tf_op jit(solution)/shard_map/ppermute | solution.py:142
  109.3 2.1 slice_bitcast_fusion.2
  112.3 2.9 pack_tiles.12
  115.8 4.5 %collective-permute-start.17 = (f32[8,4,64,128]{3,2,1,0:T(8,128)}, f32[8,4,64,128]{3,2,1,0:T(8,128)}, u32[]{:S(2)}, u32[]{:S(2)}) collective-permute-start(f32[8,4,64,128]{3,2,1,0:T(8,128)} %get-tuple-element.116.refs_1_), channel_id=1, source_target_pairs={{1,3},{2,0},{3,5},{4,2},{5,7},{6,4},{9,11},{10,8},{11,13},{12,10},... | collective-permute-start | bytes 3145736 | tf_op jit(solution)/shard_map/ppermute | solution.py:538
  120.3 7.6 %drift_chunk.11 = (f32[8,4,64,128]{3,2,1,0:T(8,128)}, f32[8,4,64,128]{3,2,1,0:T(8,128)}, f32[8,128]{1,0:T(8,128)}) custom-call(s32[1,4,16]{2,1,0:T(4,128)} %sec_ref.35, s32[1,4,16]{2,1,0:T(4,128)} %til_ref.35, bf16[16,256,256]{2,1,0:T(8,128)(2,1)} %split_weights.1.w_ref, f32[16,64,2048]{2,1,0:T(8,128)} %refs_0_.19, ...), custom_call_target="tpu_custom_call" | custom-call | bytes 1024 | tf_op jit(solution)/shard_map/drift_chunk/pallas_call | solution.py:208
  128.0 1.3 collective-permute-start.20
  129.3 2.9 pack_tiles.13
  132.4 2.2 collective-permute-done.7.refs_2_
  136.6 5.3 %collective-permute-done.17.refs_11_ = f32[8,4,64,128]{3,2,1,0:T(8,128)} collective-permute-done((f32[8,4,64,128]{3,2,1,0:T(8,128)}, f32[8,4,64,128]{3,2,1,0:T(8,128)}, u32[]{:S(2)}, u32[]{:S(2)}) %collective-permute-start.17) | collective-permute-done | bytes 1048608 | tf_op jit(solution)/shard_map/ppermute | solution.py:538
  141.9 5.1 %collective-permute-start.18 = (f32[8,4,64,128]{3,2,1,0:T(8,128)}, f32[8,4,64,128]{3,2,1,0:T(8,128)}, u32[]{:S(2)}, u32[]{:S(2)}) collective-permute-start(f32[8,4,64,128]{3,2,1,0:T(8,128)} %get-tuple-element.118.refs_2_), channel_id=1, source_target_pairs={{1,3},{2,0},{3,5},{4,2},{5,7},{6,4},{9,11},{10,8},{11,13},{12,10},... | collective-permute-start | bytes 3145736 | tf_op jit(solution)/shard_map/ppermute | solution.py:538
  147.0 6.9 %drift_chunk.12 = (f32[8,2,64,128]{3,2,1,0:T(8,128)}, f32[8,2,64,128]{3,2,1,0:T(8,128)}, f32[8,128]{1,0:T(8,128)}) custom-call(s32[1,4,16]{2,1,0:T(4,128)} %sec_ref.35, s32[1,4,16]{2,1,0:T(4,128)} %til_ref.35, bf16[16,256,256]{2,1,0:T(8,128)(2,1)} %split_weights.1.w_ref, f32[16,64,2048]{2,1,0:T(8,128)} %refs_0_.19, ...), custom_call_target="tpu_custom_call" | custom-call | bytes 1024 | tf_op jit(solution)/shard_map/drift_chunk/pallas_call | solution.py:208
  154.4 1.3 collective-permute-start.21
  156.7 1.5 collective-permute-start.10
  158.2 1.3 collective-permute-done.10.refs_3_
  160.3 6.9 %drift_chunk.13 = (f32[8,2,64,128]{3,2,1,0:T(8,128)}, f32[8,2,64,128]{3,2,1,0:T(8,128)}, f32[8,128]{1,0:T(8,128)}) custom-call(s32[1,4,16]{2,1,0:T(4,128)} %sec_ref.35, s32[1,4,16]{2,1,0:T(4,128)} %til_ref.35, bf16[16,256,256]{2,1,0:T(8,128)(2,1)} %split_weights.1.w_ref, f32[16,64,2048]{2,1,0:T(8,128)} %refs_0_.19, ...), custom_call_target="tpu_custom_call" | custom-call | bytes 1024 | tf_op jit(solution)/shard_map/drift_chunk/pallas_call | solution.py:208
  167.2 5.1 %collective-permute-start.15 = (f32[8,2,64,128]{3,2,1,0:T(8,128)}, f32[8,2,64,128]{3,2,1,0:T(8,128)}, u32[]{:S(2)}, u32[]{:S(2)}) collective-permute-start(f32[8,2,64,128]{3,2,1,0:T(8,128)} %get-tuple-element.114), channel_id=1, source_target_pairs={{0,1},{1,0},{2,3},{3,2},{4,5},{5,4},{6,7},{7,6},{8,9},{9,8},{10,11... | collective-permute-start | bytes 1572872 | tf_op jit(solution)/shard_map/ppermute | solution.py:529
  172.3 7.5 %collective-permute-done.21.refs_15_ = f32[8,4,64,128]{3,2,1,0:T(8,128)} collective-permute-done((f32[8,4,64,128]{3,2,1,0:T(8,128)}, f32[8,4,64,128]{3,2,1,0:T(8,128)}, u32[]{:S(2)}, u32[]{:S(2)}) %collective-permute-start.21) | collective-permute-done | bytes 1048608 | tf_op jit(solution)/shard_map/ppermute | solution.py:534
  179.8 4.8 %collective-permute-done.15.refs_9_ = f32[8,2,64,128]{3,2,1,0:T(8,128)} collective-permute-done((f32[8,2,64,128]{3,2,1,0:T(8,128)}, f32[8,2,64,128]{3,2,1,0:T(8,128)}, u32[]{:S(2)}, u32[]{:S(2)}) %collective-permute-start.15) | collective-permute-done | bytes 524320 | tf_op jit(solution)/shard_map/ppermute | solution.py:529
  184.6 28.5 %diffuse_tiles.2 = (f32[4,16,64,128]{3,2,1,0:T(8,128)}, f32[4,8,64,128]{3,2,1,0:T(8,128)}, f32[4,5,64,128]{3,2,1,0:T(8,128)}, f32[4,3,64,128]{3,2,1,0:T(8,128)}) custom-call(f32[8,8,128]{2,1,0:T(8,128)} %broadcast_in_dim.43.rate_ref, f32[56,64,128]{2,1,0:T(8,128)} %broadcast_in_dim.45.a_ref, f32[56,64,128]{2,1,0:T(8,128)} %broadcast_in_dim.47.b_ref, ...), custom_call_target="tpu_custom_call" | custom-call | bytes 1024 | tf_op jit(solution)/shard_map/diffuse_tiles/pallas_call | solution.py:383
  213.1 1.2 collective-permute-start.22
  214.3 28.6 %diffuse_tiles.3 = (f32[4,16,64,128]{3,2,1,0:T(8,128)}, f32[4,3,64,128]{3,2,1,0:T(8,128)}, f32[4,5,64,128]{3,2,1,0:T(8,128)}, f32[4,5,64,128]{3,2,1,0:T(8,128)}, f32[4,3,64,128]{3,2,1,0:T(8,128)}) custom-call(f32[8,8,128]{2,1,0:T(8,128)} %broadcast_in_dim.43.rate_ref, f32[56,64,128]{2,1,0:T(8,128)} %broadcast_in_dim.45.a_ref, ...), custom_call_target="tpu_custom_call" | custom-call | bytes 1024 | tf_op jit(solution)/shard_map/diffuse_tiles/pallas_call | solution.py:383
  243.3 9.1 %collective-permute-done.23.refs_3_ = f32[4,3,64,128]{3,2,1,0:T(8,128)} collective-permute-done((f32[4,3,64,128]{3,2,1,0:T(8,128)}, f32[4,3,64,128]{3,2,1,0:T(8,128)}, u32[]{:S(2)}, u32[]{:S(2)}) %collective-permute-start.23) | collective-permute-done | bytes 393248 | tf_op jit(solution)/shard_map/ppermute | solution.py:584
  253.0 3.9 pack_tiles.14
  257.2 9.3 %collective-permute-done.24.refs_3_ = f32[4,5,64,128]{3,2,1,0:T(8,128)} collective-permute-done((f32[4,5,64,128]{3,2,1,0:T(8,128)}, f32[4,5,64,128]{3,2,1,0:T(8,128)}, u32[]{:S(2)}, u32[]{:S(2)}) %collective-permute-start.24) | collective-permute-done | bytes 655392 | tf_op jit(solution)/shard_map/ppermute | solution.py:586
  266.5 4.0 pack_tiles.15
  270.9 3.7 collective-permute-start.32
  274.5 7.7 %collective-permute-done.25.refs_5_ = f32[2,6,3,64,128]{4,3,2,1,0:T(8,128)} collective-permute-done((f32[2,6,3,64,128]{4,3,2,1,0:T(8,128)}, f32[2,6,3,64,128]{4,3,2,1,0:T(8,128)}, u32[]{:S(2)}, u32[]{:S(2)}) %collective-permute-start.25) | collective-permute-done | bytes 1179680 | tf_op jit(solution)/shard_map/ppermute | solution.py:142
  284.8 7.2 %collective-permute-start.33 = (f32[6,3,64,128]{3,2,1,0:T(8,128)S(1)}, f32[6,3,64,128]{3,2,1,0:T(8,128)}, u32[]{:S(2)}, u32[]{:S(2)}) collective-permute-start(f32[6,3,64,128]{3,2,1,0:T(8,128)S(1)} %slice_bitcast_fusion.6), channel_id=1, source_target_pairs={{0,8},{8,0},{16,24},{24,16},{1,9},{9,1},{17,25},{25,17},{2,10},{10... | collective-permute-start | bytes 1769480 | tf_op jit(solution)/shard_map/ppermute | solution.py:143
  292.1 1.7 collective-permute-done.33.refs_6_
  293.8 7.2 %drift_chunk.14 = (f32[16,64,2048]{2,1,0:T(8,128)}, f32[8,128]{1,0:T(8,128)}) custom-call(s32[1,4,16]{2,1,0:T(4,128)} %sec_ref.35, s32[1,4,16]{2,1,0:T(4,128)} %til_ref.35, bf16[16,256,256]{2,1,0:T(8,128)(2,1)} %split_weights.1.w_ref, f32[4,16,64,128]{3,2,1,0:T(8,128)} %get-tuple-element.123.refs_0_, f32[4,16,64,128]{3,2,1,0:T(8,128)} %get-tuple-element.124.refs_1_, ...), custom_call_target="tpu_custom_call" | custom-call | bytes 1024 | tf_op jit(solution)/shard_map/drift_chunk/pallas_call | solution.py:208
  301.1 5.2 %collective-permute-done.37.refs_2_ = f32[4,5,64,128]{3,2,1,0:T(8,128)} collective-permute-done((f32[4,5,64,128]{3,2,1,0:T(8,128)}, f32[4,5,64,128]{3,2,1,0:T(8,128)}, u32[]{:S(2)}, u32[]{:S(2)}) %collective-permute-start.37) | collective-permute-done | bytes 655392 | tf_op jit(solution)/shard_map/ppermute | solution.py:602
  306.3 4.1 pack_tiles.17
  311.3 13.1 %collective-permute-done.27.refs_5_ = f32[2,6,5,64,128]{4,3,2,1,0:T(8,128)} collective-permute-done((f32[2,6,5,64,128]{4,3,2,1,0:T(8,128)}, f32[2,6,5,64,128]{4,3,2,1,0:T(8,128)}, u32[]{:S(2)}, u32[]{:S(2)}) %collective-permute-start.27) | collective-permute-done | bytes 1966112 | tf_op jit(solution)/shard_map/ppermute | solution.py:142
  324.4 1.3 slice_bitcast_fusion.1
  325.7 6.6 %collective-permute-start.31 = (f32[6,5,64,128]{3,2,1,0:T(8,128)S(1)}, f32[6,5,64,128]{3,2,1,0:T(8,128)}, u32[]{:S(2)}, u32[]{:S(2)}) collective-permute-start(f32[6,5,64,128]{3,2,1,0:T(8,128)S(1)} %slice_bitcast_fusion.1), channel_id=1, source_target_pairs={{0,8},{8,0},{16,24},{24,16},{1,9},{9,1},{17,25},{25,17},{2,10},{10... | collective-permute-start | bytes 2949128 | tf_op jit(solution)/shard_map/ppermute | solution.py:143
  334.6 7.9 %drift_chunk.15 = (f32[16,64,2048]{2,1,0:T(8,128)}, f32[8,128]{1,0:T(8,128)}) custom-call(s32[1,4,16]{2,1,0:T(4,128)} %sec_ref.35, s32[1,4,16]{2,1,0:T(4,128)} %til_ref.35, bf16[16,256,256]{2,1,0:T(8,128)(2,1)} %split_weights.1.w_ref, f32[4,16,64,128]{3,2,1,0:T(8,128)} %get-tuple-element.123.refs_0_, ...), custom_call_target="tpu_custom_call", output_to_operand_aliasing={{0}: (11, {})} | custom-call | bytes 1024 | tf_op jit(solution)/shard_map/drift_chunk/pallas_call | solution.py:208
  343.3 8.4 %collective-permute-done.29.refs_3_ = f32[4,3,64,128]{3,2,1,0:T(8,128)} collective-permute-done((f32[4,3,64,128]{3,2,1,0:T(8,128)}, f32[4,3,64,128]{3,2,1,0:T(8,128)}, u32[]{:S(2)}, u32[]{:S(2)}) %collective-permute-start.29) | collective-permute-done | bytes 393248 | tf_op jit(solution)/shard_map/ppermute | solution.py:603
  351.8 4.0 pack_tiles.16
  356.1 1.2 collective-permute-start.38
  357.3 9.3 %collective-permute-done.39.refs_5_ = f32[2,6,5,64,128]{4,3,2,1,0:T(8,128)} collective-permute-done((f32[2,6,5,64,128]{4,3,2,1,0:T(8,128)}, f32[2,6,5,64,128]{4,3,2,1,0:T(8,128)}, u32[]{:S(2)}, u32[]{:S(2)}) %collective-permute-start.39) | collective-permute-done | bytes 1966112 | tf_op jit(solution)/shard_map/ppermute | solution.py:142
  366.5 1.3 slice_bitcast_fusion
  367.8 6.6 %collective-permute-start.40 = (f32[6,5,64,128]{3,2,1,0:T(8,128)S(1)}, f32[6,5,64,128]{3,2,1,0:T(8,128)}, u32[]{:S(2)}, u32[]{:S(2)}) collective-permute-start(f32[6,5,64,128]{3,2,1,0:T(8,128)S(1)} %slice_bitcast_fusion), channel_id=1, source_target_pairs={{0,8},{8,0},{16,24},{24,16},{1,9},{9,1},{17,25},{25,17},{2,10},{10... | collective-permute-start | bytes 2949128 | tf_op jit(solution)/shard_map/ppermute | solution.py:143
  374.5 17.2 %collective-permute-done.35.refs_5_ = f32[2,6,3,64,128]{4,3,2,1,0:T(8,128)S(1)} collective-permute-done((f32[2,6,3,64,128]{4,3,2,1,0:T(8,128)}, f32[2,6,3,64,128]{4,3,2,1,0:T(8,128)S(1)}, u32[]{:S(2)}, u32[]{:S(2)}) %collective-permute-start.35) | collective-permute-done | bytes 1179680 | tf_op jit(solution)/shard_map/ppermute | solution.py:142
  393.6 3.5 collective-permute-start.36
  397.1 7.9 %drift_chunk.16 = (f32[16,64,2048]{2,1,0:T(8,128)}, f32[8,128]{1,0:T(8,128)}) custom-call(s32[1,4,16]{2,1,0:T(4,128)} %sec_ref.35, s32[1,4,16]{2,1,0:T(4,128)} %til_ref.35, bf16[16,256,256]{2,1,0:T(8,128)(2,1)} %split_weights.1.w_ref, f32[4,16,64,128]{3,2,1,0:T(8,128)} %get-tuple-element.123.refs_0_, ...), custom_call_target="tpu_custom_call", output_to_operand_aliasing={{0}: (11, {})} | custom-call | bytes 1024 | tf_op jit(solution)/shard_map/drift_chunk/pallas_call | solution.py:208
  405.0 7.3 %drift_chunk.17 = (f32[16,64,2048]{2,1,0:T(8,128)}, f32[8,128]{1,0:T(8,128)}) custom-call(s32[1,4,16]{2,1,0:T(4,128)} %sec_ref.35, s32[1,4,16]{2,1,0:T(4,128)} %til_ref.35, bf16[16,256,256]{2,1,0:T(8,128)(2,1)} %split_weights.1.w_ref, f32[4,16,64,128]{3,2,1,0:T(8,128)} %get-tuple-element.123.refs_0_, ...), custom_call_target="tpu_custom_call", output_to_operand_aliasing={{0}: (11, {})} | custom-call | bytes 1024 | tf_op jit(solution)/shard_map/drift_chunk/pallas_call | solution.py:208
  (70 shorter events, 21.9 us)
Async XLA Ops:
  3.8 46.2 %collective-permute-start.2 = (f32[6,16,64,128]{3,2,1,0:T(8,128)}, f32[6,16,64,128]{3,2,1,0:T(8,128)}, u32[]{:S(2)}, u32[]{:S(2)}) collective-permute-start(f32[6,16,64,128]{3,2,1,0:T(8,128)} %get-tuple-element.87), channel_id=1, source_target_pairs={{0,8},{8,0},{16,24},{24,16},{1,9},{9,1},{17,25},{25,17},{2,10},{10... | collective-permute-start | bytes 9437192 | tf_op jit(solution)/shard_map/ppermute | solution.py:133
  5.6 36.3 %collective-permute-start.3 = (f32[2,6,4,64,128]{4,3,2,1,0:T(8,128)}, f32[2,6,4,64,128]{4,3,2,1,0:T(8,128)}, u32[]{:S(2)}, u32[]{:S(2)}) collective-permute-start(f32[2,6,4,64,128]{4,3,2,1,0:T(8,128)} %get-tuple-element.83.refs_1_), channel_id=1, source_target_pairs={{0,16},{8,24},{16,0},{24,8},{1,17},{9,25},{17,1},{25,9},{2,18},{10... | collective-permute-start | bytes 4718600 | tf_op jit(solution)/shard_map/ppermute | solution.py:142
  9.2 66.4 %collective-permute-start = (f32[2,6,4,64,128]{4,3,2,1,0:T(8,128)}, f32[2,6,4,64,128]{4,3,2,1,0:T(8,128)}, u32[]{:S(2)}, u32[]{:S(2)}) collective-permute-start(f32[2,6,4,64,128]{4,3,2,1,0:T(8,128)} %pack_tiles.10), channel_id=1, source_target_pairs={{0,16},{8,24},{16,0},{24,8},{1,17},{9,25},{17,1},{25,9},{2,18},{10... | collective-permute-start | bytes 4718600 | tf_op jit(solution)/shard_map/ppermute | solution.py:142
  44.0 6.0 %collective-permute-start.4 = (f32[6,4,64,128]{3,2,1,0:T(8,128)}, f32[6,4,64,128]{3,2,1,0:T(8,128)}, u32[]{:S(2)}, u32[]{:S(2)}) collective-permute-start(f32[6,4,64,128]{3,2,1,0:T(8,128)} %slice_bitcast_fusion.3), channel_id=1, source_target_pairs={{0,8},{8,0},{16,24},{24,16},{1,9},{9,1},{17,25},{25,17},{2,10},{10... | collective-permute-start | bytes 2359304 | tf_op jit(solution)/shard_map/ppermute | solution.py:143
  57.6 21.4 %copy-start.2 = (f32[128,64]{0,1:T(8,128)S(1)}, f32[128,64]{0,1:T(8,128)}, u32[]{:S(2)}) copy-start(f32[128,64]{0,1:T(8,128)} %param.16) | copy-start | bytes 98308
  57.6 21.4 %copy-start.3 = (f32[128,64]{0,1:T(8,128)S(1)}, f32[128,64]{0,1:T(8,128)}, u32[]{:S(2)}) copy-start(f32[128,64]{0,1:T(8,128)} %param.17) | copy-start | bytes 98308
  60.8 18.5 %copy-start.4 = (f32[1,8]{1,0:T(1,128)S(1)}, f32[1,8]{1,0:T(1,128)}, u32[]{:S(2)}) copy-start(f32[1,8]{1,0:T(1,128)} %param.15) | copy-start | bytes 100
  60.8 48.5 %collective-permute-start.5 = (f32[2,6,4,64,128]{4,3,2,1,0:T(8,128)}, f32[2,6,4,64,128]{4,3,2,1,0:T(8,128)}, u32[]{:S(2)}, u32[]{:S(2)}) collective-permute-start(f32[2,6,4,64,128]{4,3,2,1,0:T(8,128)} %pack_tiles.11), channel_id=1, source_target_pairs={{0,16},{8,24},{16,0},{24,8},{1,17},{9,25},{17,1},{25,9},{2,18},{10... | collective-permute-start | bytes 4718600 | tf_op jit(solution)/shard_map/ppermute | solution.py:142
  61.7 33.7 %collective-permute-start.11 = (f32[8,4,64,128]{3,2,1,0:T(8,128)}, f32[8,4,64,128]{3,2,1,0:T(8,128)}, u32[]{:S(2)}, u32[]{:S(2)}) collective-permute-start(f32[8,4,64,128]{3,2,1,0:T(8,128)} %get-tuple-element.103), channel_id=1, source_target_pairs={{0,1},{1,0},{2,3},{3,2},{4,5},{5,4},{6,7},{7,6},{8,9},{9,8},{10,11... | collective-permute-start | bytes 3145736 | tf_op jit(solution)/shard_map/ppermute | solution.py:529
  76.8 3.4 collective-permute-start.1
  84.4 31.4 %collective-permute-start.16 = (f32[8,4,64,128]{3,2,1,0:T(8,128)}, f32[8,4,64,128]{3,2,1,0:T(8,128)}, u32[]{:S(2)}, u32[]{:S(2)}) collective-permute-start(f32[8,4,64,128]{3,2,1,0:T(8,128)} %get-tuple-element.88.refs_0_), channel_id=1, source_target_pairs={{1,3},{2,0},{3,5},{4,2},{5,7},{6,4},{9,11},{10,8},{11,13},{12,10},... | collective-permute-start | bytes 3145736 | tf_op jit(solution)/shard_map/ppermute | solution.py:538
  95.4 32.5 %collective-permute-start.12 = (f32[8,4,64,128]{3,2,1,0:T(8,128)}, f32[8,4,64,128]{3,2,1,0:T(8,128)}, u32[]{:S(2)}, u32[]{:S(2)}) collective-permute-start(f32[8,4,64,128]{3,2,1,0:T(8,128)} %get-tuple-element.106), channel_id=1, source_target_pairs={{0,1},{1,0},{2,3},{3,2},{4,5},{5,4},{6,7},{7,6},{8,9},{9,8},{10,11... | collective-permute-start | bytes 3145736 | tf_op jit(solution)/shard_map/ppermute | solution.py:529
  95.5 32.5 %collective-permute-start.19 = (f32[8,4,64,128]{3,2,1,0:T(8,128)}, f32[8,4,64,128]{3,2,1,0:T(8,128)}, u32[]{:S(2)}, u32[]{:S(2)}) collective-permute-start(f32[8,4,64,128]{3,2,1,0:T(8,128)} %collective-permute-done.11.refs_5_), channel_id=1, source_target_pairs={{0,2},{2,4},{3,1},{4,6},{5,3},{7,5},{8,10},{10,12},{11,9},{12,14},... | collective-permute-start | bytes 3145736 | tf_op jit(solution)/shard_map/ppermute | solution.py:534
  111.4 8.9 %collective-permute-start.6 = (f32[6,4,64,128]{3,2,1,0:T(8,128)}, f32[6,4,64,128]{3,2,1,0:T(8,128)}, u32[]{:S(2)}, u32[]{:S(2)}) collective-permute-start(f32[6,4,64,128]{3,2,1,0:T(8,128)} %slice_bitcast_fusion.2), channel_id=1, source_target_pairs={{0,8},{8,0},{16,24},{24,16},{1,9},{9,1},{17,25},{25,17},{2,10},{10... | collective-permute-start | bytes 2359304 | tf_op jit(solution)/shard_map/ppermute | solution.py:143
  115.1 19.5 %collective-permute-start.7 = (f32[2,6,2,64,128]{4,3,2,1,0:T(8,128)}, f32[2,6,2,64,128]{4,3,2,1,0:T(8,128)}, u32[]{:S(2)}, u32[]{:S(2)}) collective-permute-start(f32[2,6,2,64,128]{4,3,2,1,0:T(8,128)} %pack_tiles.12), channel_id=1, source_target_pairs={{0,16},{8,24},{16,0},{24,8},{1,17},{9,25},{17,1},{25,9},{2,18},{10... | collective-permute-start | bytes 2359304 | tf_op jit(solution)/shard_map/ppermute | solution.py:142
  115.8 26.1 %collective-permute-start.17 = (f32[8,4,64,128]{3,2,1,0:T(8,128)}, f32[8,4,64,128]{3,2,1,0:T(8,128)}, u32[]{:S(2)}, u32[]{:S(2)}) collective-permute-start(f32[8,4,64,128]{3,2,1,0:T(8,128)} %get-tuple-element.116.refs_1_), channel_id=1, source_target_pairs={{1,3},{2,0},{3,5},{4,2},{5,7},{6,4},{9,11},{10,8},{11,13},{12,10},... | collective-permute-start | bytes 3145736 | tf_op jit(solution)/shard_map/ppermute | solution.py:538
  127.9 26.0 %collective-permute-start.13 = (f32[8,4,64,128]{3,2,1,0:T(8,128)}, f32[8,4,64,128]{3,2,1,0:T(8,128)}, u32[]{:S(2)}, u32[]{:S(2)}) collective-permute-start(f32[8,4,64,128]{3,2,1,0:T(8,128)} %get-tuple-element.109), channel_id=1, source_target_pairs={{0,1},{1,0},{2,3},{3,2},{4,5},{5,4},{6,7},{7,6},{8,9},{9,8},{10,11... | collective-permute-start | bytes 3145736 | tf_op jit(solution)/shard_map/ppermute | solution.py:529
  128.0 26.4 %collective-permute-start.20 = (f32[8,4,64,128]{3,2,1,0:T(8,128)}, f32[8,4,64,128]{3,2,1,0:T(8,128)}, u32[]{:S(2)}, u32[]{:S(2)}) collective-permute-start(f32[8,4,64,128]{3,2,1,0:T(8,128)} %collective-permute-done.12.refs_6_), channel_id=1, source_target_pairs={{0,2},{2,4},{3,1},{4,6},{5,3},{7,5},{8,10},{10,12},{11,9},{12,14},... | collective-permute-start | bytes 3145736 | tf_op jit(solution)/shard_map/ppermute | solution.py:534
  132.1 23.5 %collective-permute-start.9 = (f32[2,6,2,64,128]{4,3,2,1,0:T(8,128)}, f32[2,6,2,64,128]{4,3,2,1,0:T(8,128)}, u32[]{:S(2)}, u32[]{:S(2)}) collective-permute-start(f32[2,6,2,64,128]{4,3,2,1,0:T(8,128)} %pack_tiles.13), channel_id=1, source_target_pairs={{0,16},{8,24},{16,0},{24,8},{1,17},{9,25},{17,1},{25,9},{2,18},{10... | collective-permute-start | bytes 2359304 | tf_op jit(solution)/shard_map/ppermute | solution.py:142
  135.6 11.4 %collective-permute-start.8 = (f32[6,2,64,128]{3,2,1,0:T(8,128)S(1)}, f32[6,2,64,128]{3,2,1,0:T(8,128)}, u32[]{:S(2)}, u32[]{:S(2)}) collective-permute-start(f32[6,2,64,128]{3,2,1,0:T(8,128)S(1)} %slice_bitcast_fusion.8), channel_id=1, source_target_pairs={{0,8},{8,0},{16,24},{24,16},{1,9},{9,1},{17,25},{25,17},{2,10},{10... | collective-permute-start | bytes 1179656 | tf_op jit(solution)/shard_map/ppermute | solution.py:143
  141.9 30.4 %collective-permute-start.18 = (f32[8,4,64,128]{3,2,1,0:T(8,128)}, f32[8,4,64,128]{3,2,1,0:T(8,128)}, u32[]{:S(2)}, u32[]{:S(2)}) collective-permute-start(f32[8,4,64,128]{3,2,1,0:T(8,128)} %get-tuple-element.118.refs_2_), channel_id=1, source_target_pairs={{1,3},{2,0},{3,5},{4,2},{5,7},{6,4},{9,11},{10,8},{11,13},{12,10},... | collective-permute-start | bytes 3145736 | tf_op jit(solution)/shard_map/ppermute | solution.py:538
  154.4 12.8 %collective-permute-start.14 = (f32[8,2,64,128]{3,2,1,0:T(8,128)}, f32[8,2,64,128]{3,2,1,0:T(8,128)}, u32[]{:S(2)}, u32[]{:S(2)}) collective-permute-start(f32[8,2,64,128]{3,2,1,0:T(8,128)} %get-tuple-element.112), channel_id=1, source_target_pairs={{0,1},{1,0},{2,3},{3,2},{4,5},{5,4},{6,7},{7,6},{8,9},{9,8},{10,11... | collective-permute-start | bytes 1572872 | tf_op jit(solution)/shard_map/ppermute | solution.py:529
  154.4 25.4 %collective-permute-start.21 = (f32[8,4,64,128]{3,2,1,0:T(8,128)}, f32[8,4,64,128]{3,2,1,0:T(8,128)}, u32[]{:S(2)}, u32[]{:S(2)}) collective-permute-start(f32[8,4,64,128]{3,2,1,0:T(8,128)} %collective-permute-done.13.refs_7_), channel_id=1, source_target_pairs={{0,2},{2,4},{3,1},{4,6},{5,3},{7,5},{8,10},{10,12},{11,9},{12,14},... | collective-permute-start | bytes 3145736 | tf_op jit(solution)/shard_map/ppermute | solution.py:534
  156.7 2.8 collective-permute-start.10
  159.5 0.8 copy-start.1
  167.2 17.4 %collective-permute-start.15 = (f32[8,2,64,128]{3,2,1,0:T(8,128)}, f32[8,2,64,128]{3,2,1,0:T(8,128)}, u32[]{:S(2)}, u32[]{:S(2)}) collective-permute-start(f32[8,2,64,128]{3,2,1,0:T(8,128)} %get-tuple-element.114), channel_id=1, source_target_pairs={{0,1},{1,0},{2,3},{3,2},{4,5},{5,4},{6,7},{7,6},{8,9},{9,8},{10,11... | collective-permute-start | bytes 1572872 | tf_op jit(solution)/shard_map/ppermute | solution.py:529
  213.1 29.8 %collective-permute-start.22 = (f32[4,8,64,128]{3,2,1,0:T(8,128)}, f32[4,8,64,128]{3,2,1,0:T(8,128)}, u32[]{:S(2)}, u32[]{:S(2)}) collective-permute-start(f32[4,8,64,128]{3,2,1,0:T(8,128)} %get-tuple-element.131), channel_id=1, source_target_pairs={{0,1},{1,0},{2,3},{3,2},{4,5},{5,4},{6,7},{7,6},{8,9},{9,8},{10,11... | collective-permute-start | bytes 3145736 | tf_op jit(solution)/shard_map/ppermute | solution.py:582
  242.9 9.5 %collective-permute-start.23 = (f32[4,3,64,128]{3,2,1,0:T(8,128)}, f32[4,3,64,128]{3,2,1,0:T(8,128)}, u32[]{:S(2)}, u32[]{:S(2)}) collective-permute-start(f32[4,3,64,128]{3,2,1,0:T(8,128)} %get-tuple-element.132), channel_id=1, source_target_pairs={{0,1},{1,0},{2,3},{3,2},{4,5},{5,4},{6,7},{7,6},{8,9},{9,8},{10,11... | collective-permute-start | bytes 1179656 | tf_op jit(solution)/shard_map/ppermute | solution.py:584
  252.4 14.1 %collective-permute-start.24 = (f32[4,5,64,128]{3,2,1,0:T(8,128)}, f32[4,5,64,128]{3,2,1,0:T(8,128)}, u32[]{:S(2)}, u32[]{:S(2)}) collective-permute-start(f32[4,5,64,128]{3,2,1,0:T(8,128)} %get-tuple-element.133), channel_id=1, source_target_pairs={{0,1},{1,0},{2,3},{3,2},{4,5},{5,4},{6,7},{7,6},{8,9},{9,8},{10,11... | collective-permute-start | bytes 1966088 | tf_op jit(solution)/shard_map/ppermute | solution.py:586
  257.0 25.3 %collective-permute-start.25 = (f32[2,6,3,64,128]{4,3,2,1,0:T(8,128)}, f32[2,6,3,64,128]{4,3,2,1,0:T(8,128)}, u32[]{:S(2)}, u32[]{:S(2)}) collective-permute-start(f32[2,6,3,64,128]{4,3,2,1,0:T(8,128)} %get-tuple-element.136), channel_id=1, source_target_pairs={{0,16},{8,24},{16,0},{24,8},{1,17},{9,25},{17,1},{25,9},{2,18},{10... | collective-permute-start | bytes 3538952 | tf_op jit(solution)/shard_map/ppermute | solution.py:142
  270.6 53.8 %collective-permute-start.27 = (f32[2,6,5,64,128]{4,3,2,1,0:T(8,128)}, f32[2,6,5,64,128]{4,3,2,1,0:T(8,128)}, u32[]{:S(2)}, u32[]{:S(2)}) collective-permute-start(f32[2,6,5,64,128]{4,3,2,1,0:T(8,128)} %get-tuple-element.138), channel_id=1, source_target_pairs={{0,16},{8,24},{16,0},{24,8},{1,17},{9,25},{17,1},{25,9},{2,18},{10... | collective-permute-start | bytes 5898248 | tf_op jit(solution)/shard_map/ppermute | solution.py:142
  270.9 21.2 %collective-permute-start.32 = (f32[6,3,64,128]{3,2,1,0:T(8,128)}, f32[6,3,64,128]{3,2,1,0:T(8,128)}, u32[]{:S(2)}, u32[]{:S(2)}) collective-permute-start(f32[6,3,64,128]{3,2,1,0:T(8,128)} %get-tuple-element.144), channel_id=1, source_target_pairs={{0,8},{8,0},{16,24},{24,16},{1,9},{9,1},{17,25},{25,17},{2,10},{10... | collective-permute-start | bytes 1769480 | tf_op jit(solution)/shard_map/ppermute | solution.py:133
  282.3 18.8 %collective-permute-start.26 = (f32[4,5,64,128]{3,2,1,0:T(8,128)}, f32[4,5,64,128]{3,2,1,0:T(8,128)}, u32[]{:S(2)}, u32[]{:S(2)}) collective-permute-start(f32[4,5,64,128]{3,2,1,0:T(8,128)} %get-tuple-element.137), channel_id=1, source_target_pairs={{0,1},{1,0},{2,3},{3,2},{4,5},{5,4},{6,7},{7,6},{8,9},{9,8},{10,11... | collective-permute-start | bytes 1966088 | tf_op jit(solution)/shard_map/ppermute | solution.py:603
  283.1 23.2 %collective-permute-start.37 = (f32[4,5,64,128]{3,2,1,0:T(8,128)}, f32[4,5,64,128]{3,2,1,0:T(8,128)}, u32[]{:S(2)}, u32[]{:S(2)}) collective-permute-start(f32[4,5,64,128]{3,2,1,0:T(8,128)} %get-tuple-element.152), channel_id=1, source_target_pairs={{0,1},{1,0},{2,3},{3,2},{4,5},{5,4},{6,7},{7,6},{8,9},{9,8},{10,11... | collective-permute-start | bytes 1966088 | tf_op jit(solution)/shard_map/ppermute | solution.py:602
  284.8 8.9 %collective-permute-start.33 = (f32[6,3,64,128]{3,2,1,0:T(8,128)S(1)}, f32[6,3,64,128]{3,2,1,0:T(8,128)}, u32[]{:S(2)}, u32[]{:S(2)}) collective-permute-start(f32[6,3,64,128]{3,2,1,0:T(8,128)S(1)} %slice_bitcast_fusion.6), channel_id=1, source_target_pairs={{0,8},{8,0},{16,24},{24,16},{1,9},{9,1},{17,25},{25,17},{2,10},{10... | collective-permute-start | bytes 1769480 | tf_op jit(solution)/shard_map/ppermute | solution.py:143
  292.0 41.8 %collective-permute-start.30 = (f32[6,5,64,128]{3,2,1,0:T(8,128)}, f32[6,5,64,128]{3,2,1,0:T(8,128)}, u32[]{:S(2)}, u32[]{:S(2)}) collective-permute-start(f32[6,5,64,128]{3,2,1,0:T(8,128)} %get-tuple-element.142), channel_id=1, source_target_pairs={{0,8},{8,0},{16,24},{24,16},{1,9},{9,1},{17,25},{25,17},{2,10},{10... | collective-permute-start | bytes 2949128 | tf_op jit(solution)/shard_map/ppermute | solution.py:133
  310.4 56.2 %collective-permute-start.39 = (f32[2,6,5,64,128]{4,3,2,1,0:T(8,128)}, f32[2,6,5,64,128]{4,3,2,1,0:T(8,128)}, u32[]{:S(2)}, u32[]{:S(2)}) collective-permute-start(f32[2,6,5,64,128]{4,3,2,1,0:T(8,128)} %get-tuple-element.156), channel_id=1, source_target_pairs={{0,16},{8,24},{16,0},{24,8},{1,17},{9,25},{17,1},{25,9},{2,18},{10... | collective-permute-start | bytes 5898248 | tf_op jit(solution)/shard_map/ppermute | solution.py:142
  325.7 8.9 %collective-permute-start.31 = (f32[6,5,64,128]{3,2,1,0:T(8,128)S(1)}, f32[6,5,64,128]{3,2,1,0:T(8,128)}, u32[]{:S(2)}, u32[]{:S(2)}) collective-permute-start(f32[6,5,64,128]{3,2,1,0:T(8,128)S(1)} %slice_bitcast_fusion.1), channel_id=1, source_target_pairs={{0,8},{8,0},{16,24},{24,16},{1,9},{9,1},{17,25},{25,17},{2,10},{10... | collective-permute-start | bytes 2949128 | tf_op jit(solution)/shard_map/ppermute | solution.py:143
  332.3 11.0 %collective-permute-start.28 = (f32[4,3,64,128]{3,2,1,0:T(8,128)}, f32[4,3,64,128]{3,2,1,0:T(8,128)}, u32[]{:S(2)}, u32[]{:S(2)}) collective-permute-start(f32[4,3,64,128]{3,2,1,0:T(8,128)} %get-tuple-element.139), channel_id=1, source_target_pairs={{0,1},{1,0},{2,3},{3,2},{4,5},{5,4},{6,7},{7,6},{8,9},{9,8},{10,11... | collective-permute-start | bytes 1179656 | tf_op jit(solution)/shard_map/ppermute | solution.py:602
  333.4 18.4 %collective-permute-start.29 = (f32[4,3,64,128]{3,2,1,0:T(8,128)}, f32[4,3,64,128]{3,2,1,0:T(8,128)}, u32[]{:S(2)}, u32[]{:S(2)}) collective-permute-start(f32[4,3,64,128]{3,2,1,0:T(8,128)} %get-tuple-element.140), channel_id=1, source_target_pairs={{0,1},{1,0},{2,3},{3,2},{4,5},{5,4},{6,7},{7,6},{8,9},{9,8},{10,11... | collective-permute-start | bytes 1179656 | tf_op jit(solution)/shard_map/ppermute | solution.py:603
  355.8 35.9 %collective-permute-start.35 = (f32[2,6,3,64,128]{4,3,2,1,0:T(8,128)}, f32[2,6,3,64,128]{4,3,2,1,0:T(8,128)S(1)}, u32[]{:S(2)}, u32[]{:S(2)}) collective-permute-start(f32[2,6,3,64,128]{4,3,2,1,0:T(8,128)} %get-tuple-element.151), channel_id=1, source_target_pairs={{0,16},{8,24},{16,0},{24,8},{1,17},{9,25},{17,1},{25,9},{2,18},{10... | collective-permute-start | bytes 3538952 | tf_op jit(solution)/shard_map/ppermute | solution.py:142
  356.1 41.0 %collective-permute-start.38 = (f32[6,5,64,128]{3,2,1,0:T(8,128)}, f32[6,5,64,128]{3,2,1,0:T(8,128)}, u32[]{:S(2)}, u32[]{:S(2)}) collective-permute-start(f32[6,5,64,128]{3,2,1,0:T(8,128)} %get-tuple-element.154), channel_id=1, source_target_pairs={{0,8},{8,0},{16,24},{24,16},{1,9},{9,1},{17,25},{25,17},{2,10},{10... | collective-permute-start | bytes 2949128 | tf_op jit(solution)/shard_map/ppermute | solution.py:133
  367.8 29.3 %collective-permute-start.40 = (f32[6,5,64,128]{3,2,1,0:T(8,128)S(1)}, f32[6,5,64,128]{3,2,1,0:T(8,128)}, u32[]{:S(2)}, u32[]{:S(2)}) collective-permute-start(f32[6,5,64,128]{3,2,1,0:T(8,128)S(1)} %slice_bitcast_fusion), channel_id=1, source_target_pairs={{0,8},{8,0},{16,24},{24,16},{1,9},{9,1},{17,25},{25,17},{2,10},{10... | collective-permute-start | bytes 2949128 | tf_op jit(solution)/shard_map/ppermute | solution.py:143
  374.5 30.5 %collective-permute-start.34 = (f32[6,3,64,128]{3,2,1,0:T(8,128)}, f32[6,3,64,128]{3,2,1,0:T(8,128)}, u32[]{:S(2)}, u32[]{:S(2)}) collective-permute-start(f32[6,3,64,128]{3,2,1,0:T(8,128)} %get-tuple-element.149), channel_id=1, source_target_pairs={{0,8},{8,0},{16,24},{24,16},{1,9},{9,1},{17,25},{25,17},{2,10},{10... | collective-permute-start | bytes 1769480 | tf_op jit(solution)/shard_map/ppermute | solution.py:133
  391.7 1.0 copy-start
  393.6 11.4 %collective-permute-start.36 = (f32[6,3,64,128]{3,2,1,0:T(8,128)}, f32[6,3,64,128]{3,2,1,0:T(8,128)}, u32[]{:S(2)}, u32[]{:S(2)}) collective-permute-start(f32[6,3,64,128]{3,2,1,0:T(8,128)} %slice_bitcast_fusion.5), channel_id=1, source_target_pairs={{0,8},{8,0},{16,24},{24,16},{1,9},{9,1},{17,25},{25,17},{2,10},{10... | collective-permute-start | bytes 1769480 | tf_op jit(solution)/shard_map/ppermute | solution.py:143

commit v9 on v8

--- a/solution.py
+++ b/solution.py
@@ -151,15 +151,19 @@
 def drift_kernel(find, place, receive, n_local, n_extra, sec_ref, til_ref, w_ref, *refs):
     sectors, tiles = sec_ref.shape[1], sec_ref.shape[2]
     local, recvs = refs[:n_local], refs[n_local : n_local + sectors - 1]
-    outs = refs[n_local + sectors - 1 + n_extra : -5]
-    token, taken, made, in_sems, out_sems = refs[-5:]
+    outs = refs[n_local + sectors - 1 + n_extra : -7]
+    token, taken, made, w_room, in_sems, out_sems, w_sems = refs[-7:]
     pieces = find(*local)
     put = place(*outs)
     me = lax.axis_index("sector")
     rows, side = taken.shape[1] * taken.shape[2], taken.shape[3]
     token[...] = jnp.zeros(token.shape, F32)
 
+    def matrix(t):
+        return pltpu.make_async_copy(w_ref.at[t], w_room.at[t], w_sems.at[t])
+
     def fetch(t, counts):
+        matrix(t).start()
         d = sec_ref[0, me, t] ^ me
 
         @pl.when(d == 0)
@@ -183,11 +187,12 @@
 
     @pl.loop(0, tiles, unroll=4)
     def _(t):
+        matrix(t).wait()
         pltpu.make_async_copy(taken.at[t], taken.at[t], in_sems.at[t]).wait()
         value = taken[t].reshape(rows, side)
         high = value.astype(BF16)
         low = (value - high.astype(F32)).astype(BF16)
-        both = jnp.dot(jnp.concatenate([high, low], axis=1), w_ref[t], preferred_element_type=F32)
+        both = jnp.dot(jnp.concatenate([high, low], axis=1), w_room[t], preferred_element_type=F32)
         made[t] = (both[:, :side] + both[:, side:]).reshape(taken.shape[1:])
         for guard, there in put(t):
 
@@ -208,11 +213,13 @@
     return pl.pallas_call(
         functools.partial(drift_kernel, find, place, receive, n_local, n_extra),
         out_shape=[*outs, jax.ShapeDtypeStruct((8, 128), F32)],
-        in_specs=[SMEM, SMEM, VMEM] + [ANY] * (len(ins) - 3),
+        in_specs=[SMEM, SMEM] + [ANY] * (len(ins) - 2),
         out_specs=[ANY] * len(outs) + [VMEM],
         scratch_shapes=[
             pltpu.VMEM((tiles,) + piece, F32),
             pltpu.VMEM((tiles,) + piece, F32),
+            pltpu.VMEM(weights.shape, BF16),
+            pltpu.SemaphoreType.DMA((tiles,)),
             pltpu.SemaphoreType.DMA((tiles,)),
             pltpu.SemaphoreType.DMA((tiles,)),
         ],
@@ -518,7 +525,7 @@
             came[k], (rate, a, b) = in_turn(came[k], [rate, a, b])
         part = jax.ShapeDtypeStruct((half, step, pitches, side), F32)
         piece = (step, pitches, side)
-        after = [] if token is None else [token]
+        after = ([] if token is None else [token]) + own_halo * (k == 1)
         kept, sent, token = drift(
             find, place, receive, tables, weights, [density], beside + came[k], [part, part], piece, after
         )

time: 415 us -> 412 us (level)
    pallas_call x9, Pallas kernels: 66.7 us -> 60.9 us  [drift(): pl.pallas_call(functools.partial(drift_kernel, find, place, receive, n_lo...]
  transfers between devices with their start and end apart: 41 -> 41, of which waited for: 21 -> 22; matrix products, arithmetic and copies ran while one was open for 4% -> 4% of each run, Pallas kernels for 29% -> 28%
where the time goes in v9:
time: 412 us; the launch traced here: 409 us
  waiting for transfers between devices  160 us (39%)
  Pallas kernels  157 us (38%)
  starting transfers between devices  71.5 us (17%)
  local copies, waits for them, and re-layouts  19.1 us (5%)
    ppermute x9, waiting for transfers between devices, far_queue(): whole = lax.ppermute(send, 'sector', [(s, s ^ 2) for s in range(sectors)])  102 us
    pallas_call x9, Pallas kernels, drift(): pl.pallas_call(functools.partial(drift_kernel, find, place, receive, n_lo...  60.9 us
    pallas_call x2, Pallas kernels, diffuse(): pl.pallas_call(functools.partial(diffusion_kernel, len(own), len(own_halo...  57 us
    pallas_call x9, Pallas kernels, pack(): pl.pallas_call(functools.partial(pack_kernel, offsets, finds, n_far, len(...  34 us
    ppermute x9, starting transfers between devices, far_queue(): lax.ppermute(whole[1], 'sector', [(s, s ^ 1) for s in range(sectors)])  30.5 us
    squeeze x9, local copies, waits for them, and re-layouts, far_queue(): whole[1]  12 us
    ppermute x3, starting transfers between devices, paired_shards(): own_halo.append(lax.ppermute(kept, 'inner', own_pairs))  11.7 us
    ppermute x5, starting transfers between devices, paired_shards(): got.append(lax.ppermute(sent, 'inner', swap))  9.87 us
  transfers between devices with their start and end apart: 41, of which 22 were waited for; matrix products, arithmetic and copies ran while one was open for 4% of the time, Pallas kernels for 28%

profile of v9, /device:TPU:25, one launch (start us, length us, event | category | flops | bytes accessed | tf_op | source)
XLA Modules:
  0.0 409.1 jit_solution(5559855939480034149)
XLA Ops:
  0.0 5.0 %pack_tiles.9 = (f32[2,6,4,64,128]{4,3,2,1,0:T(8,128)}, f32[6,16,64,128]{3,2,1,0:T(8,128)}) custom-call(s32[1,4,16]{2,1,0:T(4,128)} %sec_ref.35, s32[1,4,16]{2,1,0:T(4,128)} %til_ref.35, f32[16,64,2048]{2,1,0:T(8,128)} %refs_0_.19), custom_call_target="tpu_custom_call" | custom-call | bytes 1024 | tf_op jit(solution)/shard_map/pack_tiles/pallas_call | solution.py:114
  5.9 3.0 pack_tiles.10
  9.8 31.2 %collective-permute-done.3.refs_2_ = f32[2,6,4,64,128]{4,3,2,1,0:T(8,128)} collective-permute-done((f32[2,6,4,64,128]{4,3,2,1,0:T(8,128)}, f32[2,6,4,64,128]{4,3,2,1,0:T(8,128)}, u32[]{:S(2)}, u32[]{:S(2)}) %collective-permute-start.3) | collective-permute-done | bytes 1572896 | tf_op jit(solution)/shard_map/ppermute | solution.py:142
  41.0 2.1 slice_bitcast_fusion.3
  43.1 2.1 collective-permute-start.4
  45.2 4.7 %split_weights.1.w_ref = bf16[16,256,256]{2,1,0:T(8,128)(2,1)} custom-call(s32[1,4,16]{2,1,0:T(4,128)} %mid_ref.1, f32[32,128,128]{2,1,0:T(8,128)} %w_ref.1), custom_call_target="tpu_custom_call" | custom-call | bytes 1024 | tf_op jit(solution)/shard_map/split_weights/pallas_call | solution.py:52
  50.0 6.9 %drift_chunk.9 = (f32[8,4,64,128]{3,2,1,0:T(8,128)}, f32[8,4,64,128]{3,2,1,0:T(8,128)}, f32[8,128]{1,0:T(8,128)}) custom-call(s32[1,4,16]{2,1,0:T(4,128)} %sec_ref.35, s32[1,4,16]{2,1,0:T(4,128)} %til_ref.35, bf16[16,256,256]{2,1,0:T(8,128)(2,1)} %split_weights.1.w_ref, f32[16,64,2048]{2,1,0:T(8,128)} %refs_0_.19, ...), custom_call_target="tpu_custom_call" | custom-call | bytes 1024 | tf_op jit(solution)/shard_map/drift_chunk/pallas_call | solution.py:213
  56.9 3.2 pack_tiles.11
  61.0 2.1 collective-permute-start.12
  63.0 2.3 collective-permute-start.5
  65.3 9.4 %collective-permute-done.refs_2_ = f32[2,6,4,64,128]{4,3,2,1,0:T(8,128)} collective-permute-done((f32[2,6,4,64,128]{4,3,2,1,0:T(8,128)}, f32[2,6,4,64,128]{4,3,2,1,0:T(8,128)}, u32[]{:S(2)}, u32[]{:S(2)}) %collective-permute-start) | collective-permute-done | bytes 1572896 | tf_op jit(solution)/shard_map/ppermute | solution.py:142
  75.9 2.2 collective-permute-start.1
  81.5 1.8 broadcast_in_dim.47.b_ref
  83.4 1.8 broadcast_in_dim.45.a_ref
  85.1 1.8 collective-permute-done.5.refs_5_.refs_10_
  86.9 6.9 %drift_chunk.10 = (f32[8,4,64,128]{3,2,1,0:T(8,128)}, f32[8,4,64,128]{3,2,1,0:T(8,128)}, f32[8,128]{1,0:T(8,128)}) custom-call(s32[1,4,16]{2,1,0:T(4,128)} %sec_ref.35, s32[1,4,16]{2,1,0:T(4,128)} %til_ref.35, bf16[16,256,256]{2,1,0:T(8,128)(2,1)} %split_weights.1.w_ref, f32[16,64,2048]{2,1,0:T(8,128)} %refs_0_.19, ...), custom_call_target="tpu_custom_call" | custom-call | bytes 1024 | tf_op jit(solution)/shard_map/drift_chunk/pallas_call | solution.py:213
  93.8 3.0 collective-permute-start.13
  96.8 1.3 collective-permute-start.19
  98.1 10.3 %collective-permute-done.6.refs_2_ = f32[2,6,4,64,128]{4,3,2,1,0:T(8,128)} collective-permute-done((f32[2,6,4,64,128]{4,3,2,1,0:T(8,128)}, f32[2,6,4,64,128]{4,3,2,1,0:T(8,128)}, u32[]{:S(2)}, u32[]{:S(2)}) %collective-permute-start.6) | collective-permute-done | bytes 1572896 | tf_op jit(solution)/shard_map/ppermute | solution.py:142
  108.4 2.1 slice_bitcast_fusion.2
  110.5 1.3 collective-permute-start.7
  111.8 2.9 pack_tiles.12
  115.6 4.3 %collective-permute-start.17 = (f32[8,4,64,128]{3,2,1,0:T(8,128)}, f32[8,4,64,128]{3,2,1,0:T(8,128)}, u32[]{:S(2)}, u32[]{:S(2)}) collective-permute-start(f32[8,4,64,128]{3,2,1,0:T(8,128)} %get-tuple-element.116.refs_1_), channel_id=1, source_target_pairs={{1,3},{2,0},{3,5},{4,2},{5,7},{6,4},{9,11},{10,8},{11,13},{12,10},... | collective-permute-start | bytes 3145736 | tf_op jit(solution)/shard_map/ppermute | solution.py:545
  119.9 6.9 %drift_chunk.11 = (f32[8,4,64,128]{3,2,1,0:T(8,128)}, f32[8,4,64,128]{3,2,1,0:T(8,128)}, f32[8,128]{1,0:T(8,128)}) custom-call(s32[1,4,16]{2,1,0:T(4,128)} %sec_ref.35, s32[1,4,16]{2,1,0:T(4,128)} %til_ref.35, bf16[16,256,256]{2,1,0:T(8,128)(2,1)} %split_weights.1.w_ref, f32[16,64,2048]{2,1,0:T(8,128)} %refs_0_.19, ...), custom_call_target="tpu_custom_call" | custom-call | bytes 1024 | tf_op jit(solution)/shard_map/drift_chunk/pallas_call | solution.py:213
  126.9 1.3 collective-permute-start.20
  128.2 2.9 pack_tiles.13
  131.3 2.9 collective-permute-done.8.refs_2_
  136.5 5.0 %collective-permute-done.17.refs_11_ = f32[8,4,64,128]{3,2,1,0:T(8,128)} collective-permute-done((f32[8,4,64,128]{3,2,1,0:T(8,128)}, f32[8,4,64,128]{3,2,1,0:T(8,128)}, u32[]{:S(2)}, u32[]{:S(2)}) %collective-permute-start.17) | collective-permute-done | bytes 1048608 | tf_op jit(solution)/shard_map/ppermute | solution.py:545
  141.5 5.1 %collective-permute-start.18 = (f32[8,4,64,128]{3,2,1,0:T(8,128)}, f32[8,4,64,128]{3,2,1,0:T(8,128)}, u32[]{:S(2)}, u32[]{:S(2)}) collective-permute-start(f32[8,4,64,128]{3,2,1,0:T(8,128)} %get-tuple-element.118.refs_2_), channel_id=1, source_target_pairs={{1,3},{2,0},{3,5},{4,2},{5,7},{6,4},{9,11},{10,8},{11,13},{12,10},... | collective-permute-start | bytes 3145736 | tf_op jit(solution)/shard_map/ppermute | solution.py:545
  146.6 6.3 %drift_chunk.12 = (f32[8,2,64,128]{3,2,1,0:T(8,128)}, f32[8,2,64,128]{3,2,1,0:T(8,128)}, f32[8,128]{1,0:T(8,128)}) custom-call(s32[1,4,16]{2,1,0:T(4,128)} %sec_ref.35, s32[1,4,16]{2,1,0:T(4,128)} %til_ref.35, bf16[16,256,256]{2,1,0:T(8,128)(2,1)} %split_weights.1.w_ref, f32[16,64,2048]{2,1,0:T(8,128)} %refs_0_.19, ...), custom_call_target="tpu_custom_call" | custom-call | bytes 1024 | tf_op jit(solution)/shard_map/drift_chunk/pallas_call | solution.py:213
  153.2 1.3 collective-permute-start.21
  155.6 1.5 collective-permute-start.11
  157.1 1.3 collective-permute-done.11.refs_3_
  159.2 6.3 %drift_chunk.13 = (f32[8,2,64,128]{3,2,1,0:T(8,128)}, f32[8,2,64,128]{3,2,1,0:T(8,128)}, f32[8,128]{1,0:T(8,128)}) custom-call(s32[1,4,16]{2,1,0:T(4,128)} %sec_ref.35, s32[1,4,16]{2,1,0:T(4,128)} %til_ref.35, bf16[16,256,256]{2,1,0:T(8,128)(2,1)} %split_weights.1.w_ref, f32[16,64,2048]{2,1,0:T(8,128)} %refs_0_.19, ...), custom_call_target="tpu_custom_call" | custom-call | bytes 1024 | tf_op jit(solution)/shard_map/drift_chunk/pallas_call | solution.py:213
  165.5 4.7 %collective-permute-start.16 = (f32[8,2,64,128]{3,2,1,0:T(8,128)}, f32[8,2,64,128]{3,2,1,0:T(8,128)}, u32[]{:S(2)}, u32[]{:S(2)}) collective-permute-start(f32[8,2,64,128]{3,2,1,0:T(8,128)} %get-tuple-element.114), channel_id=1, source_target_pairs={{0,1},{1,0},{2,3},{3,2},{4,5},{5,4},{6,7},{7,6},{8,9},{9,8},{10,11... | collective-permute-start | bytes 1572872 | tf_op jit(solution)/shard_map/ppermute | solution.py:536
  170.2 8.4 %collective-permute-done.21.refs_15_ = f32[8,4,64,128]{3,2,1,0:T(8,128)} collective-permute-done((f32[8,4,64,128]{3,2,1,0:T(8,128)}, f32[8,4,64,128]{3,2,1,0:T(8,128)}, u32[]{:S(2)}, u32[]{:S(2)}) %collective-permute-start.21) | collective-permute-done | bytes 1048608 | tf_op jit(solution)/shard_map/ppermute | solution.py:541
  178.6 3.9 collective-permute-done.16.refs_9_
  182.5 28.5 %diffuse_tiles.2 = (f32[4,16,64,128]{3,2,1,0:T(8,128)}, f32[4,8,64,128]{3,2,1,0:T(8,128)}, f32[4,5,64,128]{3,2,1,0:T(8,128)}, f32[4,3,64,128]{3,2,1,0:T(8,128)}) custom-call(f32[8,8,128]{2,1,0:T(8,128)} %broadcast_in_dim.43.rate_ref, f32[56,64,128]{2,1,0:T(8,128)} %broadcast_in_dim.45.a_ref, f32[56,64,128]{2,1,0:T(8,128)} %broadcast_in_dim.47.b_ref, ...), custom_call_target="tpu_custom_call" | custom-call | bytes 1024 | tf_op jit(solution)/shard_map/diffuse_tiles/pallas_call | solution.py:390
  212.3 28.5 %diffuse_tiles.3 = (f32[4,16,64,128]{3,2,1,0:T(8,128)}, f32[4,3,64,128]{3,2,1,0:T(8,128)}, f32[4,5,64,128]{3,2,1,0:T(8,128)}, f32[4,5,64,128]{3,2,1,0:T(8,128)}, f32[4,3,64,128]{3,2,1,0:T(8,128)}) custom-call(f32[8,8,128]{2,1,0:T(8,128)} %broadcast_in_dim.43.rate_ref, f32[56,64,128]{2,1,0:T(8,128)} %broadcast_in_dim.45.a_ref, ...), custom_call_target="tpu_custom_call" | custom-call | bytes 1024 | tf_op jit(solution)/shard_map/diffuse_tiles/pallas_call | solution.py:390
  241.2 9.1 %collective-permute-done.23.refs_3_ = f32[4,3,64,128]{3,2,1,0:T(8,128)} collective-permute-done((f32[4,3,64,128]{3,2,1,0:T(8,128)}, f32[4,3,64,128]{3,2,1,0:T(8,128)}, u32[]{:S(2)}, u32[]{:S(2)}) %collective-permute-start.23) | collective-permute-done | bytes 393248 | tf_op jit(solution)/shard_map/ppermute | solution.py:591
  251.0 4.1 %pack_tiles.14 = (f32[2,6,3,64,128]{4,3,2,1,0:T(8,128)}, f32[6,3,64,128]{3,2,1,0:T(8,128)}) custom-call(s32[1,4,16]{2,1,0:T(4,128)} %sec_ref.35, s32[1,4,16]{2,1,0:T(4,128)} %til_ref.35, f32[4,16,64,128]{3,2,1,0:T(8,128)} %get-tuple-element.123.refs_0_, f32[4,16,64,128]{3,2,1,0:T(8,128)} %get-tuple-element.124.refs_1_, ...), custom_call_target="tpu_custom_call" | custom-call | bytes 1024 | tf_op jit(solution)/shard_map/pack_tiles/pallas_call | solution.py:114
  255.6 8.9 %collective-permute-done.24.refs_3_ = f32[4,5,64,128]{3,2,1,0:T(8,128)} collective-permute-done((f32[4,5,64,128]{3,2,1,0:T(8,128)}, f32[4,5,64,128]{3,2,1,0:T(8,128)}, u32[]{:S(2)}, u32[]{:S(2)}) %collective-permute-start.24) | collective-permute-done | bytes 655392 | tf_op jit(solution)/shard_map/ppermute | solution.py:593
  264.5 4.3 %pack_tiles.15 = (f32[2,6,5,64,128]{4,3,2,1,0:T(8,128)}, f32[6,5,64,128]{3,2,1,0:T(8,128)}) custom-call(s32[1,4,16]{2,1,0:T(4,128)} %sec_ref.35, s32[1,4,16]{2,1,0:T(4,128)} %til_ref.35, f32[4,16,64,128]{3,2,1,0:T(8,128)} %get-tuple-element.123.refs_0_, f32[4,16,64,128]{3,2,1,0:T(8,128)} %get-tuple-element.124.refs_1_, ...), custom_call_target="tpu_custom_call" | custom-call | bytes 1024 | tf_op jit(solution)/shard_map/pack_tiles/pallas_call | solution.py:114
  269.2 3.4 collective-permute-start.32
  272.6 8.0 %collective-permute-done.25.refs_5_ = f32[2,6,3,64,128]{4,3,2,1,0:T(8,128)} collective-permute-done((f32[2,6,3,64,128]{4,3,2,1,0:T(8,128)}, f32[2,6,3,64,128]{4,3,2,1,0:T(8,128)}, u32[]{:S(2)}, u32[]{:S(2)}) %collective-permute-start.25) | collective-permute-done | bytes 1179680 | tf_op jit(solution)/shard_map/ppermute | solution.py:142
  283.2 6.7 %collective-permute-start.33 = (f32[6,3,64,128]{3,2,1,0:T(8,128)S(1)}, f32[6,3,64,128]{3,2,1,0:T(8,128)}, u32[]{:S(2)}, u32[]{:S(2)}) collective-permute-start(f32[6,3,64,128]{3,2,1,0:T(8,128)S(1)} %slice_bitcast_fusion.6), channel_id=1, source_target_pairs={{0,8},{8,0},{16,24},{24,16},{1,9},{9,1},{17,25},{25,17},{2,10},{10... | collective-permute-start | bytes 1769480 | tf_op jit(solution)/shard_map/ppermute | solution.py:143
  290.0 1.7 collective-permute-done.33.refs_6_
  291.6 6.6 %drift_chunk.14 = (f32[16,64,2048]{2,1,0:T(8,128)}, f32[8,128]{1,0:T(8,128)}) custom-call(s32[1,4,16]{2,1,0:T(4,128)} %sec_ref.35, s32[1,4,16]{2,1,0:T(4,128)} %til_ref.35, bf16[16,256,256]{2,1,0:T(8,128)(2,1)} %split_weights.1.w_ref, f32[4,16,64,128]{3,2,1,0:T(8,128)} %get-tuple-element.123.refs_0_, f32[4,16,64,128]{3,2,1,0:T(8,128)} %get-tuple-element.124.refs_1_, ...), custom_call_target="tpu_custom_call" | custom-call | bytes 1024 | tf_op jit(solution)/shard_map/drift_chunk/pallas_call | solution.py:213
  298.3 6.9 %collective-permute-done.37.refs_2_ = f32[4,5,64,128]{3,2,1,0:T(8,128)} collective-permute-done((f32[4,5,64,128]{3,2,1,0:T(8,128)}, f32[4,5,64,128]{3,2,1,0:T(8,128)}, u32[]{:S(2)}, u32[]{:S(2)}) %collective-permute-start.37) | collective-permute-done | bytes 655392 | tf_op jit(solution)/shard_map/ppermute | solution.py:609
  305.2 4.4 %pack_tiles.17 = (f32[2,6,5,64,128]{4,3,2,1,0:T(8,128)}, f32[6,5,64,128]{3,2,1,0:T(8,128)}) custom-call(s32[1,4,16]{2,1,0:T(4,128)} %sec_ref.35, s32[1,4,16]{2,1,0:T(4,128)} %til_ref.35, f32[4,16,64,128]{3,2,1,0:T(8,128)} %get-tuple-element.123.refs_0_, f32[4,16,64,128]{3,2,1,0:T(8,128)} %get-tuple-element.124.refs_1_, ...), custom_call_target="tpu_custom_call" | custom-call | bytes 1024 | tf_op jit(solution)/shard_map/pack_tiles/pallas_call | solution.py:114
  310.3 12.4 %collective-permute-done.27.refs_5_ = f32[2,6,5,64,128]{4,3,2,1,0:T(8,128)} collective-permute-done((f32[2,6,5,64,128]{4,3,2,1,0:T(8,128)}, f32[2,6,5,64,128]{4,3,2,1,0:T(8,128)}, u32[]{:S(2)}, u32[]{:S(2)}) %collective-permute-start.27) | collective-permute-done | bytes 1966112 | tf_op jit(solution)/shard_map/ppermute | solution.py:142
  322.8 1.3 slice_bitcast_fusion.1
  324.1 6.1 %collective-permute-start.31 = (f32[6,5,64,128]{3,2,1,0:T(8,128)S(1)}, f32[6,5,64,128]{3,2,1,0:T(8,128)}, u32[]{:S(2)}, u32[]{:S(2)}) collective-permute-start(f32[6,5,64,128]{3,2,1,0:T(8,128)S(1)} %slice_bitcast_fusion.1), channel_id=1, source_target_pairs={{0,8},{8,0},{16,24},{24,16},{1,9},{9,1},{17,25},{25,17},{2,10},{10... | collective-permute-start | bytes 2949128 | tf_op jit(solution)/shard_map/ppermute | solution.py:143
  332.5 7.2 %drift_chunk.15 = (f32[16,64,2048]{2,1,0:T(8,128)}, f32[8,128]{1,0:T(8,128)}) custom-call(s32[1,4,16]{2,1,0:T(4,128)} %sec_ref.35, s32[1,4,16]{2,1,0:T(4,128)} %til_ref.35, bf16[16,256,256]{2,1,0:T(8,128)(2,1)} %split_weights.1.w_ref, f32[4,16,64,128]{3,2,1,0:T(8,128)} %get-tuple-element.123.refs_0_, ...), custom_call_target="tpu_custom_call", output_to_operand_aliasing={{0}: (11, {})} | custom-call | bytes 1024 | tf_op jit(solution)/shard_map/drift_chunk/pallas_call | solution.py:213
  339.7 1.5 collective-permute-done.28.refs_2_
  341.2 8.4 %collective-permute-done.29.refs_3_ = f32[4,3,64,128]{3,2,1,0:T(8,128)} collective-permute-done((f32[4,3,64,128]{3,2,1,0:T(8,128)}, f32[4,3,64,128]{3,2,1,0:T(8,128)}, u32[]{:S(2)}, u32[]{:S(2)}) %collective-permute-start.29) | collective-permute-done | bytes 393248 | tf_op jit(solution)/shard_map/ppermute | solution.py:610
  349.6 4.2 %pack_tiles.16 = (f32[2,6,3,64,128]{4,3,2,1,0:T(8,128)}, f32[6,3,64,128]{3,2,1,0:T(8,128)}) custom-call(s32[1,4,16]{2,1,0:T(4,128)} %sec_ref.35, s32[1,4,16]{2,1,0:T(4,128)} %til_ref.35, f32[4,16,64,128]{3,2,1,0:T(8,128)} %get-tuple-element.123.refs_0_, f32[4,16,64,128]{3,2,1,0:T(8,128)} %get-tuple-element.124.refs_1_, ...), custom_call_target="tpu_custom_call" | custom-call | bytes 1024 | tf_op jit(solution)/shard_map/pack_tiles/pallas_call | solution.py:114
  355.2 9.7 %collective-permute-done.39.refs_5_ = f32[2,6,5,64,128]{4,3,2,1,0:T(8,128)} collective-permute-done((f32[2,6,5,64,128]{4,3,2,1,0:T(8,128)}, f32[2,6,5,64,128]{4,3,2,1,0:T(8,128)}, u32[]{:S(2)}, u32[]{:S(2)}) %collective-permute-start.39) | collective-permute-done | bytes 1966112 | tf_op jit(solution)/shard_map/ppermute | solution.py:142
  364.9 1.3 slice_bitcast_fusion
  366.2 6.1 %collective-permute-start.40 = (f32[6,5,64,128]{3,2,1,0:T(8,128)S(1)}, f32[6,5,64,128]{3,2,1,0:T(8,128)}, u32[]{:S(2)}, u32[]{:S(2)}) collective-permute-start(f32[6,5,64,128]{3,2,1,0:T(8,128)S(1)} %slice_bitcast_fusion), channel_id=1, source_target_pairs={{0,8},{8,0},{16,24},{24,16},{1,9},{9,1},{17,25},{25,17},{2,10},{10... | collective-permute-start | bytes 2949128 | tf_op jit(solution)/shard_map/ppermute | solution.py:143
  372.4 17.7 %collective-permute-done.35.refs_5_ = f32[2,6,3,64,128]{4,3,2,1,0:T(8,128)S(1)} collective-permute-done((f32[2,6,3,64,128]{4,3,2,1,0:T(8,128)}, f32[2,6,3,64,128]{4,3,2,1,0:T(8,128)S(1)}, u32[]{:S(2)}, u32[]{:S(2)}) %collective-permute-start.35) | collective-permute-done | bytes 1179680 | tf_op jit(solution)/shard_map/ppermute | solution.py:142
  392.0 3.2 collective-permute-start.36
  395.2 7.2 %drift_chunk.16 = (f32[16,64,2048]{2,1,0:T(8,128)}, f32[8,128]{1,0:T(8,128)}) custom-call(s32[1,4,16]{2,1,0:T(4,128)} %sec_ref.35, s32[1,4,16]{2,1,0:T(4,128)} %til_ref.35, bf16[16,256,256]{2,1,0:T(8,128)(2,1)} %split_weights.1.w_ref, f32[4,16,64,128]{3,2,1,0:T(8,128)} %get-tuple-element.123.refs_0_, ...), custom_call_target="tpu_custom_call", output_to_operand_aliasing={{0}: (11, {})} | custom-call | bytes 1024 | tf_op jit(solution)/shard_map/drift_chunk/pallas_call | solution.py:213
  402.4 6.6 %drift_chunk.17 = (f32[16,64,2048]{2,1,0:T(8,128)}, f32[8,128]{1,0:T(8,128)}) custom-call(s32[1,4,16]{2,1,0:T(4,128)} %sec_ref.35, s32[1,4,16]{2,1,0:T(4,128)} %til_ref.35, bf16[16,256,256]{2,1,0:T(8,128)(2,1)} %split_weights.1.w_ref, f32[4,16,64,128]{3,2,1,0:T(8,128)} %get-tuple-element.123.refs_0_, ...), custom_call_target="tpu_custom_call", output_to_operand_aliasing={{0}: (11, {})} | custom-call | bytes 1024 | tf_op jit(solution)/shard_map/drift_chunk/pallas_call | solution.py:213
  (72 shorter events, 25.1 us)
Async XLA Ops:
  5.0 45.0 %collective-permute-start.2 = (f32[6,16,64,128]{3,2,1,0:T(8,128)}, f32[6,16,64,128]{3,2,1,0:T(8,128)}, u32[]{:S(2)}, u32[]{:S(2)}) collective-permute-start(f32[6,16,64,128]{3,2,1,0:T(8,128)} %get-tuple-element.87), channel_id=1, source_target_pairs={{0,8},{8,0},{16,24},{24,16},{1,9},{9,1},{17,25},{25,17},{2,10},{10... | collective-permute-start | bytes 9437192 | tf_op jit(solution)/shard_map/ppermute | solution.py:133
  5.1 35.9 %collective-permute-start.3 = (f32[2,6,4,64,128]{4,3,2,1,0:T(8,128)}, f32[2,6,4,64,128]{4,3,2,1,0:T(8,128)}, u32[]{:S(2)}, u32[]{:S(2)}) collective-permute-start(f32[2,6,4,64,128]{4,3,2,1,0:T(8,128)} %get-tuple-element.83.refs_1_), channel_id=1, source_target_pairs={{0,16},{8,24},{16,0},{24,8},{1,17},{9,25},{17,1},{25,9},{2,18},{10... | collective-permute-start | bytes 4718600 | tf_op jit(solution)/shard_map/ppermute | solution.py:142
  9.0 65.7 %collective-permute-start = (f32[2,6,4,64,128]{4,3,2,1,0:T(8,128)}, f32[2,6,4,64,128]{4,3,2,1,0:T(8,128)}, u32[]{:S(2)}, u32[]{:S(2)}) collective-permute-start(f32[2,6,4,64,128]{4,3,2,1,0:T(8,128)} %pack_tiles.10), channel_id=1, source_target_pairs={{0,16},{8,24},{16,0},{24,8},{1,17},{9,25},{17,1},{25,9},{2,18},{10... | collective-permute-start | bytes 4718600 | tf_op jit(solution)/shard_map/ppermute | solution.py:142
  43.1 6.9 %collective-permute-start.4 = (f32[6,4,64,128]{3,2,1,0:T(8,128)}, f32[6,4,64,128]{3,2,1,0:T(8,128)}, u32[]{:S(2)}, u32[]{:S(2)}) collective-permute-start(f32[6,4,64,128]{3,2,1,0:T(8,128)} %slice_bitcast_fusion.3), channel_id=1, source_target_pairs={{0,8},{8,0},{16,24},{24,16},{1,9},{9,1},{17,25},{25,17},{2,10},{10... | collective-permute-start | bytes 2359304 | tf_op jit(solution)/shard_map/ppermute | solution.py:143
  56.9 22.1 %copy-start.3 = (f32[128,64]{0,1:T(8,128)S(1)}, f32[128,64]{0,1:T(8,128)}, u32[]{:S(2)}) copy-start(f32[128,64]{0,1:T(8,128)} %param.16) | copy-start | bytes 98308
  56.9 22.1 %copy-start.4 = (f32[128,64]{0,1:T(8,128)S(1)}, f32[128,64]{0,1:T(8,128)}, u32[]{:S(2)}) copy-start(f32[128,64]{0,1:T(8,128)} %param.17) | copy-start | bytes 98308
  60.1 19.2 %copy-start.5 = (f32[1,8]{1,0:T(1,128)S(1)}, f32[1,8]{1,0:T(1,128)}, u32[]{:S(2)}) copy-start(f32[1,8]{1,0:T(1,128)} %param.15) | copy-start | bytes 100
  60.1 48.3 %collective-permute-start.6 = (f32[2,6,4,64,128]{4,3,2,1,0:T(8,128)}, f32[2,6,4,64,128]{4,3,2,1,0:T(8,128)}, u32[]{:S(2)}, u32[]{:S(2)}) collective-permute-start(f32[2,6,4,64,128]{4,3,2,1,0:T(8,128)} %pack_tiles.11), channel_id=1, source_target_pairs={{0,16},{8,24},{16,0},{24,8},{1,17},{9,25},{17,1},{25,9},{2,18},{10... | collective-permute-start | bytes 4718600 | tf_op jit(solution)/shard_map/ppermute | solution.py:142
  61.0 32.8 %collective-permute-start.12 = (f32[8,4,64,128]{3,2,1,0:T(8,128)}, f32[8,4,64,128]{3,2,1,0:T(8,128)}, u32[]{:S(2)}, u32[]{:S(2)}) collective-permute-start(f32[8,4,64,128]{3,2,1,0:T(8,128)} %get-tuple-element.103), channel_id=1, source_target_pairs={{0,1},{1,0},{2,3},{3,2},{4,5},{5,4},{6,7},{7,6},{8,9},{9,8},{10,11... | collective-permute-start | bytes 3145736 | tf_op jit(solution)/shard_map/ppermute | solution.py:536
  63.0 23.9 %collective-permute-start.5 = (f32[8,4,64,128]{3,2,1,0:T(8,128)}, f32[8,4,64,128]{3,2,1,0:T(8,128)}, u32[]{:S(2)}, u32[]{:S(2)}) collective-permute-start(f32[8,4,64,128]{3,2,1,0:T(8,128)} %get-tuple-element.88.refs_0_), channel_id=1, source_target_pairs={{1,3},{2,0},{3,5},{4,2},{5,7},{6,4},{9,11},{10,8},{11,13},{12,10},... | collective-permute-start | bytes 3145736 | tf_op jit(solution)/shard_map/ppermute | solution.py:545
  75.9 4.1 %collective-permute-start.1 = (f32[6,4,64,128]{3,2,1,0:T(8,128)S(1)}, f32[6,4,64,128]{3,2,1,0:T(8,128)S(1)}, u32[]{:S(2)}, u32[]{:S(2)}) collective-permute-start(f32[6,4,64,128]{3,2,1,0:T(8,128)S(1)} %slice_bitcast_fusion.4), channel_id=1, source_target_pairs={{0,8},{8,0},{16,24},{24,16},{1,9},{9,1},{17,25},{25,17},{2,10},{10... | collective-permute-start | bytes 2359304 | tf_op jit(solution)/shard_map/ppermute | solution.py:143
  80.0 0.9 copy-start.1
  93.8 33.0 %collective-permute-start.13 = (f32[8,4,64,128]{3,2,1,0:T(8,128)}, f32[8,4,64,128]{3,2,1,0:T(8,128)}, u32[]{:S(2)}, u32[]{:S(2)}) collective-permute-start(f32[8,4,64,128]{3,2,1,0:T(8,128)} %get-tuple-element.106), channel_id=1, source_target_pairs={{0,1},{1,0},{2,3},{3,2},{4,5},{5,4},{6,7},{7,6},{8,9},{9,8},{10,11... | collective-permute-start | bytes 3145736 | tf_op jit(solution)/shard_map/ppermute | solution.py:536
  96.8 30.1 %collective-permute-start.19 = (f32[8,4,64,128]{3,2,1,0:T(8,128)}, f32[8,4,64,128]{3,2,1,0:T(8,128)}, u32[]{:S(2)}, u32[]{:S(2)}) collective-permute-start(f32[8,4,64,128]{3,2,1,0:T(8,128)} %collective-permute-done.12.refs_5_), channel_id=1, source_target_pairs={{0,2},{2,4},{3,1},{4,6},{5,3},{7,5},{8,10},{10,12},{11,9},{12,14},... | collective-permute-start | bytes 3145736 | tf_op jit(solution)/shard_map/ppermute | solution.py:541
  110.5 9.4 %collective-permute-start.7 = (f32[6,4,64,128]{3,2,1,0:T(8,128)}, f32[6,4,64,128]{3,2,1,0:T(8,128)}, u32[]{:S(2)}, u32[]{:S(2)}) collective-permute-start(f32[6,4,64,128]{3,2,1,0:T(8,128)} %slice_bitcast_fusion.2), channel_id=1, source_target_pairs={{0,8},{8,0},{16,24},{24,16},{1,9},{9,1},{17,25},{25,17},{2,10},{10... | collective-permute-start | bytes 2359304 | tf_op jit(solution)/shard_map/ppermute | solution.py:143
  114.7 19.5 %collective-permute-start.8 = (f32[2,6,2,64,128]{4,3,2,1,0:T(8,128)}, f32[2,6,2,64,128]{4,3,2,1,0:T(8,128)}, u32[]{:S(2)}, u32[]{:S(2)}) collective-permute-start(f32[2,6,2,64,128]{4,3,2,1,0:T(8,128)} %pack_tiles.12), channel_id=1, source_target_pairs={{0,16},{8,24},{16,0},{24,8},{1,17},{9,25},{17,1},{25,9},{2,18},{10... | collective-permute-start | bytes 2359304 | tf_op jit(solution)/shard_map/ppermute | solution.py:142
  115.6 25.9 %collective-permute-start.17 = (f32[8,4,64,128]{3,2,1,0:T(8,128)}, f32[8,4,64,128]{3,2,1,0:T(8,128)}, u32[]{:S(2)}, u32[]{:S(2)}) collective-permute-start(f32[8,4,64,128]{3,2,1,0:T(8,128)} %get-tuple-element.116.refs_1_), channel_id=1, source_target_pairs={{1,3},{2,0},{3,5},{4,2},{5,7},{6,4},{9,11},{10,8},{11,13},{12,10},... | collective-permute-start | bytes 3145736 | tf_op jit(solution)/shard_map/ppermute | solution.py:545
  126.8 26.0 %collective-permute-start.14 = (f32[8,4,64,128]{3,2,1,0:T(8,128)}, f32[8,4,64,128]{3,2,1,0:T(8,128)}, u32[]{:S(2)}, u32[]{:S(2)}) collective-permute-start(f32[8,4,64,128]{3,2,1,0:T(8,128)} %get-tuple-element.109), channel_id=1, source_target_pairs={{0,1},{1,0},{2,3},{3,2},{4,5},{5,4},{6,7},{7,6},{8,9},{9,8},{10,11... | collective-permute-start | bytes 3145736 | tf_op jit(solution)/shard_map/ppermute | solution.py:536
  126.9 26.3 %collective-permute-start.20 = (f32[8,4,64,128]{3,2,1,0:T(8,128)}, f32[8,4,64,128]{3,2,1,0:T(8,128)}, u32[]{:S(2)}, u32[]{:S(2)}) collective-permute-start(f32[8,4,64,128]{3,2,1,0:T(8,128)} %collective-permute-done.13.refs_6_), channel_id=1, source_target_pairs={{0,2},{2,4},{3,1},{4,6},{5,3},{7,5},{8,10},{10,12},{11,9},{12,14},... | collective-permute-start | bytes 3145736 | tf_op jit(solution)/shard_map/ppermute | solution.py:541
  131.1 23.4 %collective-permute-start.10 = (f32[2,6,2,64,128]{4,3,2,1,0:T(8,128)}, f32[2,6,2,64,128]{4,3,2,1,0:T(8,128)}, u32[]{:S(2)}, u32[]{:S(2)}) collective-permute-start(f32[2,6,2,64,128]{4,3,2,1,0:T(8,128)} %pack_tiles.13), channel_id=1, source_target_pairs={{0,16},{8,24},{16,0},{24,8},{1,17},{9,25},{17,1},{25,9},{2,18},{10... | collective-permute-start | bytes 2359304 | tf_op jit(solution)/shard_map/ppermute | solution.py:142
  135.2 11.3 %collective-permute-start.9 = (f32[6,2,64,128]{3,2,1,0:T(8,128)S(1)}, f32[6,2,64,128]{3,2,1,0:T(8,128)}, u32[]{:S(2)}, u32[]{:S(2)}) collective-permute-start(f32[6,2,64,128]{3,2,1,0:T(8,128)S(1)} %slice_bitcast_fusion.8), channel_id=1, source_target_pairs={{0,8},{8,0},{16,24},{24,16},{1,9},{9,1},{17,25},{25,17},{2,10},{10... | collective-permute-start | bytes 1179656 | tf_op jit(solution)/shard_map/ppermute | solution.py:143
  141.5 28.8 %collective-permute-start.18 = (f32[8,4,64,128]{3,2,1,0:T(8,128)}, f32[8,4,64,128]{3,2,1,0:T(8,128)}, u32[]{:S(2)}, u32[]{:S(2)}) collective-permute-start(f32[8,4,64,128]{3,2,1,0:T(8,128)} %get-tuple-element.118.refs_2_), channel_id=1, source_target_pairs={{1,3},{2,0},{3,5},{4,2},{5,7},{6,4},{9,11},{10,8},{11,13},{12,10},... | collective-permute-start | bytes 3145736 | tf_op jit(solution)/shard_map/ppermute | solution.py:545
  153.2 12.3 %collective-permute-start.15 = (f32[8,2,64,128]{3,2,1,0:T(8,128)}, f32[8,2,64,128]{3,2,1,0:T(8,128)}, u32[]{:S(2)}, u32[]{:S(2)}) collective-permute-start(f32[8,2,64,128]{3,2,1,0:T(8,128)} %get-tuple-element.112), channel_id=1, source_target_pairs={{0,1},{1,0},{2,3},{3,2},{4,5},{5,4},{6,7},{7,6},{8,9},{9,8},{10,11... | collective-permute-start | bytes 1572872 | tf_op jit(solution)/shard_map/ppermute | solution.py:536
  153.2 25.4 %collective-permute-start.21 = (f32[8,4,64,128]{3,2,1,0:T(8,128)}, f32[8,4,64,128]{3,2,1,0:T(8,128)}, u32[]{:S(2)}, u32[]{:S(2)}) collective-permute-start(f32[8,4,64,128]{3,2,1,0:T(8,128)} %collective-permute-done.14.refs_7_), channel_id=1, source_target_pairs={{0,2},{2,4},{3,1},{4,6},{5,3},{7,5},{8,10},{10,12},{11,9},{12,14},... | collective-permute-start | bytes 3145736 | tf_op jit(solution)/shard_map/ppermute | solution.py:541
  155.6 2.9 collective-permute-start.11
  158.5 0.8 copy-start.2
  165.5 17.0 %collective-permute-start.16 = (f32[8,2,64,128]{3,2,1,0:T(8,128)}, f32[8,2,64,128]{3,2,1,0:T(8,128)}, u32[]{:S(2)}, u32[]{:S(2)}) collective-permute-start(f32[8,2,64,128]{3,2,1,0:T(8,128)} %get-tuple-element.114), channel_id=1, source_target_pairs={{0,1},{1,0},{2,3},{3,2},{4,5},{5,4},{6,7},{7,6},{8,9},{9,8},{10,11... | collective-permute-start | bytes 1572872 | tf_op jit(solution)/shard_map/ppermute | solution.py:536
  211.1 29.8 %collective-permute-start.22 = (f32[4,8,64,128]{3,2,1,0:T(8,128)}, f32[4,8,64,128]{3,2,1,0:T(8,128)}, u32[]{:S(2)}, u32[]{:S(2)}) collective-permute-start(f32[4,8,64,128]{3,2,1,0:T(8,128)} %get-tuple-element.131), channel_id=1, source_target_pairs={{0,1},{1,0},{2,3},{3,2},{4,5},{5,4},{6,7},{7,6},{8,9},{9,8},{10,11... | collective-permute-start | bytes 3145736 | tf_op jit(solution)/shard_map/ppermute | solution.py:589
  240.8 9.5 %collective-permute-start.23 = (f32[4,3,64,128]{3,2,1,0:T(8,128)}, f32[4,3,64,128]{3,2,1,0:T(8,128)}, u32[]{:S(2)}, u32[]{:S(2)}) collective-permute-start(f32[4,3,64,128]{3,2,1,0:T(8,128)} %get-tuple-element.132), channel_id=1, source_target_pairs={{0,1},{1,0},{2,3},{3,2},{4,5},{5,4},{6,7},{7,6},{8,9},{9,8},{10,11... | collective-permute-start | bytes 1179656 | tf_op jit(solution)/shard_map/ppermute | solution.py:591
  250.3 14.1 %collective-permute-start.24 = (f32[4,5,64,128]{3,2,1,0:T(8,128)}, f32[4,5,64,128]{3,2,1,0:T(8,128)}, u32[]{:S(2)}, u32[]{:S(2)}) collective-permute-start(f32[4,5,64,128]{3,2,1,0:T(8,128)} %get-tuple-element.133), channel_id=1, source_target_pairs={{0,1},{1,0},{2,3},{3,2},{4,5},{5,4},{6,7},{7,6},{8,9},{9,8},{10,11... | collective-permute-start | bytes 1966088 | tf_op jit(solution)/shard_map/ppermute | solution.py:593
  255.1 25.5 %collective-permute-start.25 = (f32[2,6,3,64,128]{4,3,2,1,0:T(8,128)}, f32[2,6,3,64,128]{4,3,2,1,0:T(8,128)}, u32[]{:S(2)}, u32[]{:S(2)}) collective-permute-start(f32[2,6,3,64,128]{4,3,2,1,0:T(8,128)} %get-tuple-element.136), channel_id=1, source_target_pairs={{0,16},{8,24},{16,0},{24,8},{1,17},{9,25},{17,1},{25,9},{2,18},{10... | collective-permute-start | bytes 3538952 | tf_op jit(solution)/shard_map/ppermute | solution.py:142
  268.8 54.0 %collective-permute-start.27 = (f32[2,6,5,64,128]{4,3,2,1,0:T(8,128)}, f32[2,6,5,64,128]{4,3,2,1,0:T(8,128)}, u32[]{:S(2)}, u32[]{:S(2)}) collective-permute-start(f32[2,6,5,64,128]{4,3,2,1,0:T(8,128)} %get-tuple-element.138), channel_id=1, source_target_pairs={{0,16},{8,24},{16,0},{24,8},{1,17},{9,25},{17,1},{25,9},{2,18},{10... | collective-permute-start | bytes 5898248 | tf_op jit(solution)/shard_map/ppermute | solution.py:142
  269.2 20.7 %collective-permute-start.32 = (f32[6,3,64,128]{3,2,1,0:T(8,128)}, f32[6,3,64,128]{3,2,1,0:T(8,128)}, u32[]{:S(2)}, u32[]{:S(2)}) collective-permute-start(f32[6,3,64,128]{3,2,1,0:T(8,128)} %get-tuple-element.144), channel_id=1, source_target_pairs={{0,8},{8,0},{16,24},{24,16},{1,9},{9,1},{17,25},{25,17},{2,10},{10... | collective-permute-start | bytes 1769480 | tf_op jit(solution)/shard_map/ppermute | solution.py:133
  280.6 17.6 %collective-permute-start.26 = (f32[4,5,64,128]{3,2,1,0:T(8,128)}, f32[4,5,64,128]{3,2,1,0:T(8,128)}, u32[]{:S(2)}, u32[]{:S(2)}) collective-permute-start(f32[4,5,64,128]{3,2,1,0:T(8,128)} %get-tuple-element.137), channel_id=1, source_target_pairs={{0,1},{1,0},{2,3},{3,2},{4,5},{5,4},{6,7},{7,6},{8,9},{9,8},{10,11... | collective-permute-start | bytes 1966088 | tf_op jit(solution)/shard_map/ppermute | solution.py:610
  281.1 24.1 %collective-permute-start.37 = (f32[4,5,64,128]{3,2,1,0:T(8,128)}, f32[4,5,64,128]{3,2,1,0:T(8,128)}, u32[]{:S(2)}, u32[]{:S(2)}) collective-permute-start(f32[4,5,64,128]{3,2,1,0:T(8,128)} %get-tuple-element.152), channel_id=1, source_target_pairs={{0,1},{1,0},{2,3},{3,2},{4,5},{5,4},{6,7},{7,6},{8,9},{9,8},{10,11... | collective-permute-start | bytes 1966088 | tf_op jit(solution)/shard_map/ppermute | solution.py:609
  283.2 8.4 %collective-permute-start.33 = (f32[6,3,64,128]{3,2,1,0:T(8,128)S(1)}, f32[6,3,64,128]{3,2,1,0:T(8,128)}, u32[]{:S(2)}, u32[]{:S(2)}) collective-permute-start(f32[6,3,64,128]{3,2,1,0:T(8,128)S(1)} %slice_bitcast_fusion.6), channel_id=1, source_target_pairs={{0,8},{8,0},{16,24},{24,16},{1,9},{9,1},{17,25},{25,17},{2,10},{10... | collective-permute-start | bytes 1769480 | tf_op jit(solution)/shard_map/ppermute | solution.py:143
  289.9 41.8 %collective-permute-start.30 = (f32[6,5,64,128]{3,2,1,0:T(8,128)}, f32[6,5,64,128]{3,2,1,0:T(8,128)}, u32[]{:S(2)}, u32[]{:S(2)}) collective-permute-start(f32[6,5,64,128]{3,2,1,0:T(8,128)} %get-tuple-element.142), channel_id=1, source_target_pairs={{0,8},{8,0},{16,24},{24,16},{1,9},{9,1},{17,25},{25,17},{2,10},{10... | collective-permute-start | bytes 2949128 | tf_op jit(solution)/shard_map/ppermute | solution.py:133
  309.5 55.4 %collective-permute-start.39 = (f32[2,6,5,64,128]{4,3,2,1,0:T(8,128)}, f32[2,6,5,64,128]{4,3,2,1,0:T(8,128)}, u32[]{:S(2)}, u32[]{:S(2)}) collective-permute-start(f32[2,6,5,64,128]{4,3,2,1,0:T(8,128)} %get-tuple-element.156), channel_id=1, source_target_pairs={{0,16},{8,24},{16,0},{24,8},{1,17},{9,25},{17,1},{25,9},{2,18},{10... | collective-permute-start | bytes 5898248 | tf_op jit(solution)/shard_map/ppermute | solution.py:142
  324.1 8.4 %collective-permute-start.31 = (f32[6,5,64,128]{3,2,1,0:T(8,128)S(1)}, f32[6,5,64,128]{3,2,1,0:T(8,128)}, u32[]{:S(2)}, u32[]{:S(2)}) collective-permute-start(f32[6,5,64,128]{3,2,1,0:T(8,128)S(1)} %slice_bitcast_fusion.1), channel_id=1, source_target_pairs={{0,8},{8,0},{16,24},{24,16},{1,9},{9,1},{17,25},{25,17},{2,10},{10... | collective-permute-start | bytes 2949128 | tf_op jit(solution)/shard_map/ppermute | solution.py:143
  330.2 11.0 %collective-permute-start.28 = (f32[4,3,64,128]{3,2,1,0:T(8,128)}, f32[4,3,64,128]{3,2,1,0:T(8,128)}, u32[]{:S(2)}, u32[]{:S(2)}) collective-permute-start(f32[4,3,64,128]{3,2,1,0:T(8,128)} %get-tuple-element.139), channel_id=1, source_target_pairs={{0,1},{1,0},{2,3},{3,2},{4,5},{5,4},{6,7},{7,6},{8,9},{9,8},{10,11... | collective-permute-start | bytes 1179656 | tf_op jit(solution)/shard_map/ppermute | solution.py:609
  331.4 18.2 %collective-permute-start.29 = (f32[4,3,64,128]{3,2,1,0:T(8,128)}, f32[4,3,64,128]{3,2,1,0:T(8,128)}, u32[]{:S(2)}, u32[]{:S(2)}) collective-permute-start(f32[4,3,64,128]{3,2,1,0:T(8,128)} %get-tuple-element.140), channel_id=1, source_target_pairs={{0,1},{1,0},{2,3},{3,2},{4,5},{5,4},{6,7},{7,6},{8,9},{9,8},{10,11... | collective-permute-start | bytes 1179656 | tf_op jit(solution)/shard_map/ppermute | solution.py:610
  353.9 36.2 %collective-permute-start.35 = (f32[2,6,3,64,128]{4,3,2,1,0:T(8,128)}, f32[2,6,3,64,128]{4,3,2,1,0:T(8,128)S(1)}, u32[]{:S(2)}, u32[]{:S(2)}) collective-permute-start(f32[2,6,3,64,128]{4,3,2,1,0:T(8,128)} %get-tuple-element.151), channel_id=1, source_target_pairs={{0,16},{8,24},{16,0},{24,8},{1,17},{9,25},{17,1},{25,9},{2,18},{10... | collective-permute-start | bytes 3538952 | tf_op jit(solution)/shard_map/ppermute | solution.py:142
  354.3 40.9 %collective-permute-start.38 = (f32[6,5,64,128]{3,2,1,0:T(8,128)}, f32[6,5,64,128]{3,2,1,0:T(8,128)}, u32[]{:S(2)}, u32[]{:S(2)}) collective-permute-start(f32[6,5,64,128]{3,2,1,0:T(8,128)} %get-tuple-element.154), channel_id=1, source_target_pairs={{0,8},{8,0},{16,24},{24,16},{1,9},{9,1},{17,25},{25,17},{2,10},{10... | collective-permute-start | bytes 2949128 | tf_op jit(solution)/shard_map/ppermute | solution.py:133
  366.2 29.0 %collective-permute-start.40 = (f32[6,5,64,128]{3,2,1,0:T(8,128)S(1)}, f32[6,5,64,128]{3,2,1,0:T(8,128)}, u32[]{:S(2)}, u32[]{:S(2)}) collective-permute-start(f32[6,5,64,128]{3,2,1,0:T(8,128)S(1)} %slice_bitcast_fusion), channel_id=1, source_target_pairs={{0,8},{8,0},{16,24},{24,16},{1,9},{9,1},{17,25},{25,17},{2,10},{10... | collective-permute-start | bytes 2949128 | tf_op jit(solution)/shard_map/ppermute | solution.py:143
  372.3 30.1 %collective-permute-start.34 = (f32[6,3,64,128]{3,2,1,0:T(8,128)}, f32[6,3,64,128]{3,2,1,0:T(8,128)}, u32[]{:S(2)}, u32[]{:S(2)}) collective-permute-start(f32[6,3,64,128]{3,2,1,0:T(8,128)} %get-tuple-element.149), channel_id=1, source_target_pairs={{0,8},{8,0},{16,24},{24,16},{1,9},{9,1},{17,25},{25,17},{2,10},{10... | collective-permute-start | bytes 1769480 | tf_op jit(solution)/shard_map/ppermute | solution.py:133
  390.1 1.0 copy-start
  392.0 10.5 %collective-permute-start.36 = (f32[6,3,64,128]{3,2,1,0:T(8,128)}, f32[6,3,64,128]{3,2,1,0:T(8,128)}, u32[]{:S(2)}, u32[]{:S(2)}) collective-permute-start(f32[6,3,64,128]{3,2,1,0:T(8,128)} %slice_bitcast_fusion.5), channel_id=1, source_target_pairs={{0,8},{8,0},{16,24},{24,16},{1,9},{9,1},{17,25},{25,17},{2,10},{10... | collective-permute-start | bytes 1769480 | tf_op jit(solution)/shard_map/ppermute | solution.py:143

commit v10 on v9

--- a/solution.py
+++ b/solution.py
@@ -435,7 +435,7 @@
     tiles = cell_count // side
     half = tiles // 2
     quarter = block // 4
-    first_steps = (quarter, quarter, quarter, quarter // 2, quarter - quarter // 2)
+    first_steps = (quarter, quarter, quarter, quarter - quarter // 4, quarter // 4)
     halo_chunks = PASSES // quarter
     less = quarter - quarter // 4
     more = block // 2 - less

time: 412 us -> 407 us (0.988)
    ppermute x5, starting transfers between devices: 9.87 us -> 4.16 us  [paired_shards(): got.append(lax.ppermute(sent, 'inner', swap))]
    ppermute x3, waiting for transfers between devices: 6.77 us -> 2.06 us  [paired_shards(): own_halo.append(lax.ppermute(kept, 'inner', own_pairs))]
    ppermute x5, waiting for transfers between devices: 3.97 us -> 8.53 us  [paired_shards(): got.append(lax.ppermute(sent, 'inner', swap))]
    ppermute x9, waiting for transfers between devices: 102 us -> 106 us  [far_queue(): whole = lax.ppermute(send, 'sector', [(s, s ^ 2) for s in range(sectors)])]
  transfers between devices with their start and end apart: 41 -> 41, of which waited for: 22 -> 20; matrix products, arithmetic and copies ran while one was open for 4% -> 4% of each run, Pallas kernels for 28% -> 29%
where the time goes in v10:
time: 407 us; the launch traced here: 403 us
  Pallas kernels  157 us (39%)
  waiting for transfers between devices  157 us (39%)
  starting transfers between devices  69.9 us (17%)
  local copies, waits for them, and re-layouts  17.4 us (4%)
    ppermute x9, waiting for transfers between devices, far_queue(): whole = lax.ppermute(send, 'sector', [(s, s ^ 2) for s in range(sectors)])  106 us
    pallas_call x9, Pallas kernels, drift(): pl.pallas_call(functools.partial(drift_kernel, find, place, receive, n_lo...  60.9 us
    pallas_call x2, Pallas kernels, diffuse(): pl.pallas_call(functools.partial(diffusion_kernel, len(own), len(own_halo...  57.1 us
    pallas_call x9, Pallas kernels, pack(): pl.pallas_call(functools.partial(pack_kernel, offsets, finds, n_far, len(...  34.7 us
    ppermute x9, starting transfers between devices, far_queue(): lax.ppermute(whole[1], 'sector', [(s, s ^ 1) for s in range(sectors)])  32.2 us
    squeeze x9, local copies, waits for them, and re-layouts, far_queue(): whole[1]  11.9 us
    ppermute x3, starting transfers between devices, paired_shards(): own_halo.append(lax.ppermute(kept, 'inner', own_pairs))  9.24 us
    ppermute x5, waiting for transfers between devices, paired_shards(): got.append(lax.ppermute(sent, 'inner', swap))  8.53 us
  transfers between devices with their start and end apart: 41, of which 20 were waited for; matrix products, arithmetic and copies ran while one was open for 4% of the time, Pallas kernels for 29%

profile of v10, /device:TPU:25, one launch (start us, length us, event | category | flops | bytes accessed | tf_op | source)
XLA Modules:
  0.0 402.9 jit_solution(14926612184386547516)
XLA Ops:
  0.0 5.4 %pack_tiles.9 = (f32[2,6,4,64,128]{4,3,2,1,0:T(8,128)}, f32[6,16,64,128]{3,2,1,0:T(8,128)}) custom-call(s32[1,4,16]{2,1,0:T(4,128)} %sec_ref.35, s32[1,4,16]{2,1,0:T(4,128)} %til_ref.35, f32[16,64,2048]{2,1,0:T(8,128)} %refs_0_.19), custom_call_target="tpu_custom_call" | custom-call | bytes 1024 | tf_op jit(solution)/shard_map/pack_tiles/pallas_call | solution.py:114
  6.1 3.1 pack_tiles.10
  9.3 1.5 collective-permute-start
  10.8 31.7 %collective-permute-done.3.refs_2_ = f32[2,6,4,64,128]{4,3,2,1,0:T(8,128)} collective-permute-done((f32[2,6,4,64,128]{4,3,2,1,0:T(8,128)}, f32[2,6,4,64,128]{4,3,2,1,0:T(8,128)}, u32[]{:S(2)}, u32[]{:S(2)}) %collective-permute-start.3) | collective-permute-done | bytes 1572896 | tf_op jit(solution)/shard_map/ppermute | solution.py:142
  42.4 2.1 slice_bitcast_fusion.3
  44.5 1.3 collective-permute-start.4
  45.8 4.7 %split_weights.1.w_ref = bf16[16,256,256]{2,1,0:T(8,128)(2,1)} custom-call(s32[1,4,16]{2,1,0:T(4,128)} %mid_ref.1, f32[32,128,128]{2,1,0:T(8,128)} %w_ref.1), custom_call_target="tpu_custom_call" | custom-call | bytes 1024 | tf_op jit(solution)/shard_map/split_weights/pallas_call | solution.py:52
  50.6 6.9 %drift_chunk.9 = (f32[8,4,64,128]{3,2,1,0:T(8,128)}, f32[8,4,64,128]{3,2,1,0:T(8,128)}, f32[8,128]{1,0:T(8,128)}) custom-call(s32[1,4,16]{2,1,0:T(4,128)} %sec_ref.35, s32[1,4,16]{2,1,0:T(4,128)} %til_ref.35, bf16[16,256,256]{2,1,0:T(8,128)(2,1)} %split_weights.1.w_ref, f32[16,64,2048]{2,1,0:T(8,128)} %refs_0_.19, ...), custom_call_target="tpu_custom_call" | custom-call | bytes 1024 | tf_op jit(solution)/shard_map/drift_chunk/pallas_call | solution.py:213
  57.5 3.3 pack_tiles.11
  62.1 3.3 collective-permute-start.5
  65.4 10.7 %collective-permute-done.refs_2_ = f32[2,6,4,64,128]{4,3,2,1,0:T(8,128)} collective-permute-done((f32[2,6,4,64,128]{4,3,2,1,0:T(8,128)}, f32[2,6,4,64,128]{4,3,2,1,0:T(8,128)}, u32[]{:S(2)}, u32[]{:S(2)}) %collective-permute-start) | collective-permute-done | bytes 1572896 | tf_op jit(solution)/shard_map/ppermute | solution.py:142
  77.3 1.4 collective-permute-start.1
  81.3 1.8 broadcast_in_dim.47.b_ref
  83.0 1.8 broadcast_in_dim.45.a_ref
  84.8 2.1 collective-permute-done.5.refs_5_.refs_10_
  86.9 6.9 %drift_chunk.10 = (f32[8,4,64,128]{3,2,1,0:T(8,128)}, f32[8,4,64,128]{3,2,1,0:T(8,128)}, f32[8,128]{1,0:T(8,128)}) custom-call(s32[1,4,16]{2,1,0:T(4,128)} %sec_ref.35, s32[1,4,16]{2,1,0:T(4,128)} %til_ref.35, bf16[16,256,256]{2,1,0:T(8,128)(2,1)} %split_weights.1.w_ref, f32[16,64,2048]{2,1,0:T(8,128)} %refs_0_.19, ...), custom_call_target="tpu_custom_call" | custom-call | bytes 1024 | tf_op jit(solution)/shard_map/drift_chunk/pallas_call | solution.py:213
  93.8 2.3 collective-permute-start.13
  97.3 3.1 pack_tiles.12
  101.5 8.3 %collective-permute-done.6.refs_2_ = f32[2,6,4,64,128]{4,3,2,1,0:T(8,128)} collective-permute-done((f32[2,6,4,64,128]{4,3,2,1,0:T(8,128)}, f32[2,6,4,64,128]{4,3,2,1,0:T(8,128)}, u32[]{:S(2)}, u32[]{:S(2)}) %collective-permute-start.6) | collective-permute-done | bytes 1572896 | tf_op jit(solution)/shard_map/ppermute | solution.py:142
  111.0 1.4 collective-permute-start.7
  112.4 3.0 collective-permute-start.17
  115.4 6.9 %drift_chunk.11 = (f32[8,4,64,128]{3,2,1,0:T(8,128)}, f32[8,4,64,128]{3,2,1,0:T(8,128)}, f32[8,128]{1,0:T(8,128)}) custom-call(s32[1,4,16]{2,1,0:T(4,128)} %sec_ref.35, s32[1,4,16]{2,1,0:T(4,128)} %til_ref.35, bf16[16,256,256]{2,1,0:T(8,128)(2,1)} %split_weights.1.w_ref, f32[16,64,2048]{2,1,0:T(8,128)} %refs_0_.19, ...), custom_call_target="tpu_custom_call" | custom-call | bytes 1024 | tf_op jit(solution)/shard_map/drift_chunk/pallas_call | solution.py:213
  123.9 11.2 %collective-permute-done.8.refs_2_ = f32[2,6,3,64,128]{4,3,2,1,0:T(8,128)} collective-permute-done((f32[2,6,3,64,128]{4,3,2,1,0:T(8,128)}, f32[2,6,3,64,128]{4,3,2,1,0:T(8,128)}, u32[]{:S(2)}, u32[]{:S(2)}) %collective-permute-start.8) | collective-permute-done | bytes 1179680 | tf_op jit(solution)/shard_map/ppermute | solution.py:142
  135.1 1.9 slice_bitcast_fusion.7
  137.9 2.8 pack_tiles.13
  140.8 2.9 collective-permute-start.18
  143.8 6.6 %drift_chunk.12 = (f32[8,3,64,128]{3,2,1,0:T(8,128)}, f32[8,3,64,128]{3,2,1,0:T(8,128)}, f32[8,128]{1,0:T(8,128)}) custom-call(s32[1,4,16]{2,1,0:T(4,128)} %sec_ref.35, s32[1,4,16]{2,1,0:T(4,128)} %til_ref.35, bf16[16,256,256]{2,1,0:T(8,128)(2,1)} %split_weights.1.w_ref, f32[16,64,2048]{2,1,0:T(8,128)} %refs_0_.19, ...), custom_call_target="tpu_custom_call" | custom-call | bytes 1024 | tf_op jit(solution)/shard_map/drift_chunk/pallas_call | solution.py:213
  150.5 1.3 collective-permute-start.21
  154.9 5.9 %drift_chunk.13 = (f32[8,1,64,128]{3,2,1,0:T(8,128)}, f32[8,1,64,128]{3,2,1,0:T(8,128)}, f32[8,128]{1,0:T(8,128)}) custom-call(s32[1,4,16]{2,1,0:T(4,128)} %sec_ref.35, s32[1,4,16]{2,1,0:T(4,128)} %til_ref.35, bf16[16,256,256]{2,1,0:T(8,128)(2,1)} %split_weights.1.w_ref, f32[16,64,2048]{2,1,0:T(8,128)} %refs_0_.19, ...), custom_call_target="tpu_custom_call" | custom-call | bytes 1024 | tf_op jit(solution)/shard_map/drift_chunk/pallas_call | solution.py:213
  160.8 8.5 %collective-permute-done.15.refs_8_ = f32[8,3,64,128]{3,2,1,0:T(8,128)} collective-permute-done((f32[8,3,64,128]{3,2,1,0:T(8,128)}, f32[8,3,64,128]{3,2,1,0:T(8,128)}, u32[]{:S(2)}, u32[]{:S(2)}) %collective-permute-start.15) | collective-permute-done | bytes 786464 | tf_op jit(solution)/shard_map/ppermute | solution.py:536
  169.6 7.3 %collective-permute-done.21.refs_15_ = f32[8,4,64,128]{3,2,1,0:T(8,128)} collective-permute-done((f32[8,4,64,128]{3,2,1,0:T(8,128)}, f32[8,4,64,128]{3,2,1,0:T(8,128)}, u32[]{:S(2)}, u32[]{:S(2)}) %collective-permute-start.21) | collective-permute-done | bytes 1048608 | tf_op jit(solution)/shard_map/ppermute | solution.py:541
  176.9 28.5 %diffuse_tiles.2 = (f32[4,16,64,128]{3,2,1,0:T(8,128)}, f32[4,8,64,128]{3,2,1,0:T(8,128)}, f32[4,5,64,128]{3,2,1,0:T(8,128)}, f32[4,3,64,128]{3,2,1,0:T(8,128)}) custom-call(f32[8,8,128]{2,1,0:T(8,128)} %broadcast_in_dim.43.rate_ref, f32[56,64,128]{2,1,0:T(8,128)} %broadcast_in_dim.45.a_ref, f32[56,64,128]{2,1,0:T(8,128)} %broadcast_in_dim.47.b_ref, ...), custom_call_target="tpu_custom_call" | custom-call | bytes 1024 | tf_op jit(solution)/shard_map/diffuse_tiles/pallas_call | solution.py:390
  205.5 28.6 %diffuse_tiles.3 = (f32[4,16,64,128]{3,2,1,0:T(8,128)}, f32[4,3,64,128]{3,2,1,0:T(8,128)}, f32[4,5,64,128]{3,2,1,0:T(8,128)}, f32[4,5,64,128]{3,2,1,0:T(8,128)}, f32[4,3,64,128]{3,2,1,0:T(8,128)}) custom-call(f32[8,8,128]{2,1,0:T(8,128)} %broadcast_in_dim.43.rate_ref, f32[56,64,128]{2,1,0:T(8,128)} %broadcast_in_dim.45.a_ref, ...), custom_call_target="tpu_custom_call" | custom-call | bytes 1024 | tf_op jit(solution)/shard_map/diffuse_tiles/pallas_call | solution.py:390
  234.1 1.5 collective-permute-start.23
  235.6 7.5 %collective-permute-done.23.refs_3_ = f32[4,3,64,128]{3,2,1,0:T(8,128)} collective-permute-done((f32[4,3,64,128]{3,2,1,0:T(8,128)}, f32[4,3,64,128]{3,2,1,0:T(8,128)}, u32[]{:S(2)}, u32[]{:S(2)}) %collective-permute-start.23) | collective-permute-done | bytes 393248 | tf_op jit(solution)/shard_map/ppermute | solution.py:591
  243.1 1.7 collective-permute-start.24
  244.8 4.1 %pack_tiles.14 = (f32[2,6,3,64,128]{4,3,2,1,0:T(8,128)}, f32[6,3,64,128]{3,2,1,0:T(8,128)}) custom-call(s32[1,4,16]{2,1,0:T(4,128)} %sec_ref.35, s32[1,4,16]{2,1,0:T(4,128)} %til_ref.35, f32[4,16,64,128]{3,2,1,0:T(8,128)} %get-tuple-element.123.refs_0_, f32[4,16,64,128]{3,2,1,0:T(8,128)} %get-tuple-element.124.refs_1_, ...), custom_call_target="tpu_custom_call" | custom-call | bytes 1024 | tf_op jit(solution)/shard_map/pack_tiles/pallas_call | solution.py:114
  248.9 1.4 collective-permute-start.25
  250.3 6.9 %collective-permute-done.24.refs_3_ = f32[4,5,64,128]{3,2,1,0:T(8,128)} collective-permute-done((f32[4,5,64,128]{3,2,1,0:T(8,128)}, f32[4,5,64,128]{3,2,1,0:T(8,128)}, u32[]{:S(2)}, u32[]{:S(2)}) %collective-permute-start.24) | collective-permute-done | bytes 655392 | tf_op jit(solution)/shard_map/ppermute | solution.py:593
  257.2 4.3 %pack_tiles.15 = (f32[2,6,5,64,128]{4,3,2,1,0:T(8,128)}, f32[6,5,64,128]{3,2,1,0:T(8,128)}) custom-call(s32[1,4,16]{2,1,0:T(4,128)} %sec_ref.35, s32[1,4,16]{2,1,0:T(4,128)} %til_ref.35, f32[4,16,64,128]{3,2,1,0:T(8,128)} %get-tuple-element.123.refs_0_, f32[4,16,64,128]{3,2,1,0:T(8,128)} %get-tuple-element.124.refs_1_, ...), custom_call_target="tpu_custom_call" | custom-call | bytes 1024 | tf_op jit(solution)/shard_map/pack_tiles/pallas_call | solution.py:114
  261.5 1.7 collective-permute-start.27
  263.2 3.9 collective-permute-start.32
  267.1 6.8 %collective-permute-done.25.refs_5_ = f32[2,6,3,64,128]{4,3,2,1,0:T(8,128)} collective-permute-done((f32[2,6,3,64,128]{4,3,2,1,0:T(8,128)}, f32[2,6,3,64,128]{4,3,2,1,0:T(8,128)}, u32[]{:S(2)}, u32[]{:S(2)}) %collective-permute-start.25) | collective-permute-done | bytes 1179680 | tf_op jit(solution)/shard_map/ppermute | solution.py:142
  274.0 1.3 collective-permute-start.37
  276.4 7.9 %collective-permute-start.33 = (f32[6,3,64,128]{3,2,1,0:T(8,128)S(1)}, f32[6,3,64,128]{3,2,1,0:T(8,128)}, u32[]{:S(2)}, u32[]{:S(2)}) collective-permute-start(f32[6,3,64,128]{3,2,1,0:T(8,128)S(1)} %slice_bitcast_fusion.6), channel_id=1, source_target_pairs={{0,8},{8,0},{16,24},{24,16},{1,9},{9,1},{17,25},{25,17},{2,10},{10... | collective-permute-start | bytes 1769480 | tf_op jit(solution)/shard_map/ppermute | solution.py:143
  284.4 1.7 collective-permute-done.33.refs_6_
  286.1 6.6 %drift_chunk.14 = (f32[16,64,2048]{2,1,0:T(8,128)}, f32[8,128]{1,0:T(8,128)}) custom-call(s32[1,4,16]{2,1,0:T(4,128)} %sec_ref.35, s32[1,4,16]{2,1,0:T(4,128)} %til_ref.35, bf16[16,256,256]{2,1,0:T(8,128)(2,1)} %split_weights.1.w_ref, f32[4,16,64,128]{3,2,1,0:T(8,128)} %get-tuple-element.123.refs_0_, f32[4,16,64,128]{3,2,1,0:T(8,128)} %get-tuple-element.124.refs_1_, ...), custom_call_target="tpu_custom_call" | custom-call | bytes 1024 | tf_op jit(solution)/shard_map/drift_chunk/pallas_call | solution.py:213
  292.7 4.5 %collective-permute-done.37.refs_2_ = f32[4,5,64,128]{3,2,1,0:T(8,128)} collective-permute-done((f32[4,5,64,128]{3,2,1,0:T(8,128)}, f32[4,5,64,128]{3,2,1,0:T(8,128)}, u32[]{:S(2)}, u32[]{:S(2)}) %collective-permute-start.37) | collective-permute-done | bytes 655392 | tf_op jit(solution)/shard_map/ppermute | solution.py:609
  297.2 4.4 %pack_tiles.17 = (f32[2,6,5,64,128]{4,3,2,1,0:T(8,128)}, f32[6,5,64,128]{3,2,1,0:T(8,128)}) custom-call(s32[1,4,16]{2,1,0:T(4,128)} %sec_ref.35, s32[1,4,16]{2,1,0:T(4,128)} %til_ref.35, f32[4,16,64,128]{3,2,1,0:T(8,128)} %get-tuple-element.123.refs_0_, f32[4,16,64,128]{3,2,1,0:T(8,128)} %get-tuple-element.124.refs_1_, ...), custom_call_target="tpu_custom_call" | custom-call | bytes 1024 | tf_op jit(solution)/shard_map/pack_tiles/pallas_call | solution.py:114
  302.6 13.4 %collective-permute-done.27.refs_5_ = f32[2,6,5,64,128]{4,3,2,1,0:T(8,128)} collective-permute-done((f32[2,6,5,64,128]{4,3,2,1,0:T(8,128)}, f32[2,6,5,64,128]{4,3,2,1,0:T(8,128)}, u32[]{:S(2)}, u32[]{:S(2)}) %collective-permute-start.27) | collective-permute-done | bytes 1966112 | tf_op jit(solution)/shard_map/ppermute | solution.py:142
  316.0 1.3 slice_bitcast_fusion.1
  317.3 7.3 %collective-permute-start.31 = (f32[6,5,64,128]{3,2,1,0:T(8,128)S(1)}, f32[6,5,64,128]{3,2,1,0:T(8,128)}, u32[]{:S(2)}, u32[]{:S(2)}) collective-permute-start(f32[6,5,64,128]{3,2,1,0:T(8,128)S(1)} %slice_bitcast_fusion.1), channel_id=1, source_target_pairs={{0,8},{8,0},{16,24},{24,16},{1,9},{9,1},{17,25},{25,17},{2,10},{10... | collective-permute-start | bytes 2949128 | tf_op jit(solution)/shard_map/ppermute | solution.py:143
  324.6 1.5 collective-permute-start.29
  327.0 7.2 %drift_chunk.15 = (f32[16,64,2048]{2,1,0:T(8,128)}, f32[8,128]{1,0:T(8,128)}) custom-call(s32[1,4,16]{2,1,0:T(4,128)} %sec_ref.35, s32[1,4,16]{2,1,0:T(4,128)} %til_ref.35, bf16[16,256,256]{2,1,0:T(8,128)(2,1)} %split_weights.1.w_ref, f32[4,16,64,128]{3,2,1,0:T(8,128)} %get-tuple-element.123.refs_0_, ...), custom_call_target="tpu_custom_call", output_to_operand_aliasing={{0}: (11, {})} | custom-call | bytes 1024 | tf_op jit(solution)/shard_map/drift_chunk/pallas_call | solution.py:213
  334.2 1.5 collective-permute-done.28.refs_2_
  335.6 8.4 %collective-permute-done.29.refs_3_ = f32[4,3,64,128]{3,2,1,0:T(8,128)} collective-permute-done((f32[4,3,64,128]{3,2,1,0:T(8,128)}, f32[4,3,64,128]{3,2,1,0:T(8,128)}, u32[]{:S(2)}, u32[]{:S(2)}) %collective-permute-start.29) | collective-permute-done | bytes 393248 | tf_op jit(solution)/shard_map/ppermute | solution.py:610
  344.1 4.2 %pack_tiles.16 = (f32[2,6,3,64,128]{4,3,2,1,0:T(8,128)}, f32[6,3,64,128]{3,2,1,0:T(8,128)}) custom-call(s32[1,4,16]{2,1,0:T(4,128)} %sec_ref.35, s32[1,4,16]{2,1,0:T(4,128)} %til_ref.35, f32[4,16,64,128]{3,2,1,0:T(8,128)} %get-tuple-element.123.refs_0_, f32[4,16,64,128]{3,2,1,0:T(8,128)} %get-tuple-element.124.refs_1_, ...), custom_call_target="tpu_custom_call" | custom-call | bytes 1024 | tf_op jit(solution)/shard_map/pack_tiles/pallas_call | solution.py:114
  348.3 1.4 collective-permute-start.35
  350.9 7.2 %collective-permute-done.39.refs_5_ = f32[2,6,5,64,128]{4,3,2,1,0:T(8,128)} collective-permute-done((f32[2,6,5,64,128]{4,3,2,1,0:T(8,128)}, f32[2,6,5,64,128]{4,3,2,1,0:T(8,128)}, u32[]{:S(2)}, u32[]{:S(2)}) %collective-permute-start.39) | collective-permute-done | bytes 1966112 | tf_op jit(solution)/shard_map/ppermute | solution.py:142
  359.4 7.3 %collective-permute-start.40 = (f32[6,5,64,128]{3,2,1,0:T(8,128)S(1)}, f32[6,5,64,128]{3,2,1,0:T(8,128)}, u32[]{:S(2)}, u32[]{:S(2)}) collective-permute-start(f32[6,5,64,128]{3,2,1,0:T(8,128)S(1)} %slice_bitcast_fusion), channel_id=1, source_target_pairs={{0,8},{8,0},{16,24},{24,16},{1,9},{9,1},{17,25},{25,17},{2,10},{10... | collective-permute-start | bytes 2949128 | tf_op jit(solution)/shard_map/ppermute | solution.py:143
  366.8 16.5 %collective-permute-done.35.refs_5_ = f32[2,6,3,64,128]{4,3,2,1,0:T(8,128)S(1)} collective-permute-done((f32[2,6,3,64,128]{4,3,2,1,0:T(8,128)}, f32[2,6,3,64,128]{4,3,2,1,0:T(8,128)S(1)}, u32[]{:S(2)}, u32[]{:S(2)}) %collective-permute-start.35) | collective-permute-done | bytes 1179680 | tf_op jit(solution)/shard_map/ppermute | solution.py:142
  385.2 3.8 collective-permute-start.36
  389.1 7.2 %drift_chunk.16 = (f32[16,64,2048]{2,1,0:T(8,128)}, f32[8,128]{1,0:T(8,128)}) custom-call(s32[1,4,16]{2,1,0:T(4,128)} %sec_ref.35, s32[1,4,16]{2,1,0:T(4,128)} %til_ref.35, bf16[16,256,256]{2,1,0:T(8,128)(2,1)} %split_weights.1.w_ref, f32[4,16,64,128]{3,2,1,0:T(8,128)} %get-tuple-element.123.refs_0_, ...), custom_call_target="tpu_custom_call", output_to_operand_aliasing={{0}: (11, {})} | custom-call | bytes 1024 | tf_op jit(solution)/shard_map/drift_chunk/pallas_call | solution.py:213
  396.3 6.6 %drift_chunk.17 = (f32[16,64,2048]{2,1,0:T(8,128)}, f32[8,128]{1,0:T(8,128)}) custom-call(s32[1,4,16]{2,1,0:T(4,128)} %sec_ref.35, s32[1,4,16]{2,1,0:T(4,128)} %til_ref.35, bf16[16,256,256]{2,1,0:T(8,128)(2,1)} %split_weights.1.w_ref, f32[4,16,64,128]{3,2,1,0:T(8,128)} %get-tuple-element.123.refs_0_, ...), custom_call_target="tpu_custom_call", output_to_operand_aliasing={{0}: (11, {})} | custom-call | bytes 1024 | tf_op jit(solution)/shard_map/drift_chunk/pallas_call | solution.py:213
  (70 shorter events, 23.1 us)
Async XLA Ops:
  5.5 45.1 %collective-permute-start.2 = (f32[6,16,64,128]{3,2,1,0:T(8,128)}, f32[6,16,64,128]{3,2,1,0:T(8,128)}, u32[]{:S(2)}, u32[]{:S(2)}) collective-permute-start(f32[6,16,64,128]{3,2,1,0:T(8,128)} %get-tuple-element.87), channel_id=1, source_target_pairs={{0,8},{8,0},{16,24},{24,16},{1,9},{9,1},{17,25},{25,17},{2,10},{10... | collective-permute-start | bytes 9437192 | tf_op jit(solution)/shard_map/ppermute | solution.py:133
  6.1 36.3 %collective-permute-start.3 = (f32[2,6,4,64,128]{4,3,2,1,0:T(8,128)}, f32[2,6,4,64,128]{4,3,2,1,0:T(8,128)}, u32[]{:S(2)}, u32[]{:S(2)}) collective-permute-start(f32[2,6,4,64,128]{4,3,2,1,0:T(8,128)} %get-tuple-element.83.refs_1_), channel_id=1, source_target_pairs={{0,16},{8,24},{16,0},{24,8},{1,17},{9,25},{17,1},{25,9},{2,18},{10... | collective-permute-start | bytes 4718600 | tf_op jit(solution)/shard_map/ppermute | solution.py:142
  9.3 66.9 %collective-permute-start = (f32[2,6,4,64,128]{4,3,2,1,0:T(8,128)}, f32[2,6,4,64,128]{4,3,2,1,0:T(8,128)}, u32[]{:S(2)}, u32[]{:S(2)}) collective-permute-start(f32[2,6,4,64,128]{4,3,2,1,0:T(8,128)} %pack_tiles.10), channel_id=1, source_target_pairs={{0,16},{8,24},{16,0},{24,8},{1,17},{9,25},{17,1},{25,9},{2,18},{10... | collective-permute-start | bytes 4718600 | tf_op jit(solution)/shard_map/ppermute | solution.py:142
  44.5 6.0 %collective-permute-start.4 = (f32[6,4,64,128]{3,2,1,0:T(8,128)}, f32[6,4,64,128]{3,2,1,0:T(8,128)}, u32[]{:S(2)}, u32[]{:S(2)}) collective-permute-start(f32[6,4,64,128]{3,2,1,0:T(8,128)} %slice_bitcast_fusion.3), channel_id=1, source_target_pairs={{0,8},{8,0},{16,24},{24,16},{1,9},{9,1},{17,25},{25,17},{2,10},{10... | collective-permute-start | bytes 2359304 | tf_op jit(solution)/shard_map/ppermute | solution.py:143
  57.5 22.0 %copy-start.2 = (f32[128,64]{0,1:T(8,128)S(1)}, f32[128,64]{0,1:T(8,128)}, u32[]{:S(2)}) copy-start(f32[128,64]{0,1:T(8,128)} %param.16) | copy-start | bytes 98308
  57.5 22.0 %copy-start.3 = (f32[128,64]{0,1:T(8,128)S(1)}, f32[128,64]{0,1:T(8,128)}, u32[]{:S(2)}) copy-start(f32[128,64]{0,1:T(8,128)} %param.17) | copy-start | bytes 98308
  60.8 19.1 %copy-start.4 = (f32[1,8]{1,0:T(1,128)S(1)}, f32[1,8]{1,0:T(1,128)}, u32[]{:S(2)}) copy-start(f32[1,8]{1,0:T(1,128)} %param.15) | copy-start | bytes 100
  60.8 49.0 %collective-permute-start.6 = (f32[2,6,4,64,128]{4,3,2,1,0:T(8,128)}, f32[2,6,4,64,128]{4,3,2,1,0:T(8,128)}, u32[]{:S(2)}, u32[]{:S(2)}) collective-permute-start(f32[2,6,4,64,128]{4,3,2,1,0:T(8,128)} %pack_tiles.11), channel_id=1, source_target_pairs={{0,16},{8,24},{16,0},{24,8},{1,17},{9,25},{17,1},{25,9},{2,18},{10... | collective-permute-start | bytes 4718600 | tf_op jit(solution)/shard_map/ppermute | solution.py:142
  60.9 32.9 %collective-permute-start.12 = (f32[8,4,64,128]{3,2,1,0:T(8,128)}, f32[8,4,64,128]{3,2,1,0:T(8,128)}, u32[]{:S(2)}, u32[]{:S(2)}) collective-permute-start(f32[8,4,64,128]{3,2,1,0:T(8,128)} %get-tuple-element.103), channel_id=1, source_target_pairs={{0,1},{1,0},{2,3},{3,2},{4,5},{5,4},{6,7},{7,6},{8,9},{9,8},{10,11... | collective-permute-start | bytes 3145736 | tf_op jit(solution)/shard_map/ppermute | solution.py:536
  62.1 24.8 %collective-permute-start.5 = (f32[8,4,64,128]{3,2,1,0:T(8,128)}, f32[8,4,64,128]{3,2,1,0:T(8,128)}, u32[]{:S(2)}, u32[]{:S(2)}) collective-permute-start(f32[8,4,64,128]{3,2,1,0:T(8,128)} %get-tuple-element.88.refs_0_), channel_id=1, source_target_pairs={{1,3},{2,0},{3,5},{4,2},{5,7},{6,4},{9,11},{10,8},{11,13},{12,10},... | collective-permute-start | bytes 3145736 | tf_op jit(solution)/shard_map/ppermute | solution.py:545
  77.3 3.3 collective-permute-start.1
  80.6 4.2 %copy-start.1 = (f32[6,4,64,128]{3,2,1,0:T(8,128)}, f32[6,4,64,128]{3,2,1,0:T(8,128)S(1)}, u32[]{:S(2)}) copy-start(f32[6,4,64,128]{3,2,1,0:T(8,128)S(1)} %collective-permute-done.1.refs_3_) | copy-start | bytes 2359300
  93.8 28.5 %collective-permute-start.13 = (f32[8,4,64,128]{3,2,1,0:T(8,128)}, f32[8,4,64,128]{3,2,1,0:T(8,128)}, u32[]{:S(2)}, u32[]{:S(2)}) collective-permute-start(f32[8,4,64,128]{3,2,1,0:T(8,128)} %get-tuple-element.106), channel_id=1, source_target_pairs={{0,1},{1,0},{2,3},{3,2},{4,5},{5,4},{6,7},{7,6},{8,9},{9,8},{10,11... | collective-permute-start | bytes 3145736 | tf_op jit(solution)/shard_map/ppermute | solution.py:536
  96.1 26.6 %collective-permute-start.19 = (f32[8,4,64,128]{3,2,1,0:T(8,128)}, f32[8,4,64,128]{3,2,1,0:T(8,128)}, u32[]{:S(2)}, u32[]{:S(2)}) collective-permute-start(f32[8,4,64,128]{3,2,1,0:T(8,128)} %collective-permute-done.12.refs_5_), channel_id=1, source_target_pairs={{0,2},{2,4},{3,1},{4,6},{5,3},{7,5},{8,10},{10,12},{11,9},{12,14},... | collective-permute-start | bytes 3145736 | tf_op jit(solution)/shard_map/ppermute | solution.py:541
  100.4 34.7 %collective-permute-start.8 = (f32[2,6,3,64,128]{4,3,2,1,0:T(8,128)}, f32[2,6,3,64,128]{4,3,2,1,0:T(8,128)}, u32[]{:S(2)}, u32[]{:S(2)}) collective-permute-start(f32[2,6,3,64,128]{4,3,2,1,0:T(8,128)} %pack_tiles.12), channel_id=1, source_target_pairs={{0,16},{8,24},{16,0},{24,8},{1,17},{9,25},{17,1},{25,9},{2,18},{10... | collective-permute-start | bytes 3538952 | tf_op jit(solution)/shard_map/ppermute | solution.py:142
  111.0 4.3 %collective-permute-start.7 = (f32[6,4,64,128]{3,2,1,0:T(8,128)S(1)}, f32[6,4,64,128]{3,2,1,0:T(8,128)}, u32[]{:S(2)}, u32[]{:S(2)}) collective-permute-start(f32[6,4,64,128]{3,2,1,0:T(8,128)S(1)} %slice_bitcast_fusion.2), channel_id=1, source_target_pairs={{0,8},{8,0},{16,24},{24,16},{1,9},{9,1},{17,25},{25,17},{2,10},{10... | collective-permute-start | bytes 2359304 | tf_op jit(solution)/shard_map/ppermute | solution.py:143
  112.4 28.4 %collective-permute-start.17 = (f32[8,4,64,128]{3,2,1,0:T(8,128)}, f32[8,4,64,128]{3,2,1,0:T(8,128)}, u32[]{:S(2)}, u32[]{:S(2)}) collective-permute-start(f32[8,4,64,128]{3,2,1,0:T(8,128)} %get-tuple-element.116.refs_1_), channel_id=1, source_target_pairs={{1,3},{2,0},{3,5},{4,2},{5,7},{6,4},{9,11},{10,8},{11,13},{12,10},... | collective-permute-start | bytes 3145736 | tf_op jit(solution)/shard_map/ppermute | solution.py:545
  122.3 28.1 %collective-permute-start.14 = (f32[8,4,64,128]{3,2,1,0:T(8,128)}, f32[8,4,64,128]{3,2,1,0:T(8,128)}, u32[]{:S(2)}, u32[]{:S(2)}) collective-permute-start(f32[8,4,64,128]{3,2,1,0:T(8,128)} %get-tuple-element.109), channel_id=1, source_target_pairs={{0,1},{1,0},{2,3},{3,2},{4,5},{5,4},{6,7},{7,6},{8,9},{9,8},{10,11... | collective-permute-start | bytes 3145736 | tf_op jit(solution)/shard_map/ppermute | solution.py:536
  122.6 27.8 %collective-permute-start.20 = (f32[8,4,64,128]{3,2,1,0:T(8,128)}, f32[8,4,64,128]{3,2,1,0:T(8,128)}, u32[]{:S(2)}, u32[]{:S(2)}) collective-permute-start(f32[8,4,64,128]{3,2,1,0:T(8,128)} %collective-permute-done.13.refs_6_), channel_id=1, source_target_pairs={{0,2},{2,4},{3,1},{4,6},{5,3},{7,5},{8,10},{10,12},{11,9},{12,14},... | collective-permute-start | bytes 3145736 | tf_op jit(solution)/shard_map/ppermute | solution.py:541
  137.1 6.7 %collective-permute-start.9 = (f32[6,3,64,128]{3,2,1,0:T(8,128)}, f32[6,3,64,128]{3,2,1,0:T(8,128)}, u32[]{:S(2)}, u32[]{:S(2)}) collective-permute-start(f32[6,3,64,128]{3,2,1,0:T(8,128)} %slice_bitcast_fusion.7), channel_id=1, source_target_pairs={{0,8},{8,0},{16,24},{24,16},{1,9},{9,1},{17,25},{25,17},{2,10},{10... | collective-permute-start | bytes 1769480 | tf_op jit(solution)/shard_map/ppermute | solution.py:143
  140.7 11.1 %collective-permute-start.10 = (f32[2,6,1,64,128]{4,3,1,2,0:T(8,128)}, f32[2,6,1,64,128]{4,3,1,2,0:T(8,128)}, u32[]{:S(2)}, u32[]{:S(2)}) collective-permute-start(f32[2,6,1,64,128]{4,3,1,2,0:T(8,128)} %bitcast.40), channel_id=1, source_target_pairs={{0,16},{8,24},{16,0},{24,8},{1,17},{9,25},{17,1},{25,9},{2,18},{10... | collective-permute-start | bytes 1179656 | tf_op jit(solution)/shard_map/ppermute | solution.py:142
  140.8 28.8 %collective-permute-start.18 = (f32[8,4,64,128]{3,2,1,0:T(8,128)}, f32[8,4,64,128]{3,2,1,0:T(8,128)}, u32[]{:S(2)}, u32[]{:S(2)}) collective-permute-start(f32[8,4,64,128]{3,2,1,0:T(8,128)} %get-tuple-element.118.refs_2_), channel_id=1, source_target_pairs={{1,3},{2,0},{3,5},{4,2},{5,7},{6,4},{9,11},{10,8},{11,13},{12,10},... | collective-permute-start | bytes 3145736 | tf_op jit(solution)/shard_map/ppermute | solution.py:545
  150.4 18.9 %collective-permute-start.15 = (f32[8,3,64,128]{3,2,1,0:T(8,128)}, f32[8,3,64,128]{3,2,1,0:T(8,128)}, u32[]{:S(2)}, u32[]{:S(2)}) collective-permute-start(f32[8,3,64,128]{3,2,1,0:T(8,128)} %get-tuple-element.112), channel_id=1, source_target_pairs={{0,1},{1,0},{2,3},{3,2},{4,5},{5,4},{6,7},{7,6},{8,9},{9,8},{10,11... | collective-permute-start | bytes 2359304 | tf_op jit(solution)/shard_map/ppermute | solution.py:536
  150.5 26.5 %collective-permute-start.21 = (f32[8,4,64,128]{3,2,1,0:T(8,128)}, f32[8,4,64,128]{3,2,1,0:T(8,128)}, u32[]{:S(2)}, u32[]{:S(2)}) collective-permute-start(f32[8,4,64,128]{3,2,1,0:T(8,128)} %collective-permute-done.14.refs_7_), channel_id=1, source_target_pairs={{0,2},{2,4},{3,1},{4,6},{5,3},{7,5},{8,10},{10,12},{11,9},{12,14},... | collective-permute-start | bytes 3145736 | tf_op jit(solution)/shard_map/ppermute | solution.py:541
  152.8 2.1 collective-permute-start.11
  169.3 7.6 %collective-permute-start.16 = (f32[8,1,64,128]{3,2,1,0:T(8,128)}, f32[8,1,64,128]{3,2,1,0:T(8,128)}, u32[]{:S(2)}, u32[]{:S(2)}) collective-permute-start(f32[8,1,64,128]{3,2,1,0:T(8,128)} %get-tuple-element.114), channel_id=1, source_target_pairs={{0,1},{1,0},{2,3},{3,2},{4,5},{5,4},{6,7},{7,6},{8,9},{9,8},{10,11... | collective-permute-start | bytes 786440 | tf_op jit(solution)/shard_map/ppermute | solution.py:536
  205.4 28.7 %collective-permute-start.22 = (f32[4,8,64,128]{3,2,1,0:T(8,128)}, f32[4,8,64,128]{3,2,1,0:T(8,128)}, u32[]{:S(2)}, u32[]{:S(2)}) collective-permute-start(f32[4,8,64,128]{3,2,1,0:T(8,128)} %get-tuple-element.131), channel_id=1, source_target_pairs={{0,1},{1,0},{2,3},{3,2},{4,5},{5,4},{6,7},{7,6},{8,9},{9,8},{10,11... | collective-permute-start | bytes 3145736 | tf_op jit(solution)/shard_map/ppermute | solution.py:589
  234.1 9.0 %collective-permute-start.23 = (f32[4,3,64,128]{3,2,1,0:T(8,128)}, f32[4,3,64,128]{3,2,1,0:T(8,128)}, u32[]{:S(2)}, u32[]{:S(2)}) collective-permute-start(f32[4,3,64,128]{3,2,1,0:T(8,128)} %get-tuple-element.132), channel_id=1, source_target_pairs={{0,1},{1,0},{2,3},{3,2},{4,5},{5,4},{6,7},{7,6},{8,9},{9,8},{10,11... | collective-permute-start | bytes 1179656 | tf_op jit(solution)/shard_map/ppermute | solution.py:591
  243.1 14.1 %collective-permute-start.24 = (f32[4,5,64,128]{3,2,1,0:T(8,128)}, f32[4,5,64,128]{3,2,1,0:T(8,128)}, u32[]{:S(2)}, u32[]{:S(2)}) collective-permute-start(f32[4,5,64,128]{3,2,1,0:T(8,128)} %get-tuple-element.133), channel_id=1, source_target_pairs={{0,1},{1,0},{2,3},{3,2},{4,5},{5,4},{6,7},{7,6},{8,9},{9,8},{10,11... | collective-permute-start | bytes 1966088 | tf_op jit(solution)/shard_map/ppermute | solution.py:593
  248.9 24.9 %collective-permute-start.25 = (f32[2,6,3,64,128]{4,3,2,1,0:T(8,128)}, f32[2,6,3,64,128]{4,3,2,1,0:T(8,128)}, u32[]{:S(2)}, u32[]{:S(2)}) collective-permute-start(f32[2,6,3,64,128]{4,3,2,1,0:T(8,128)} %get-tuple-element.136), channel_id=1, source_target_pairs={{0,16},{8,24},{16,0},{24,8},{1,17},{9,25},{17,1},{25,9},{2,18},{10... | collective-permute-start | bytes 3538952 | tf_op jit(solution)/shard_map/ppermute | solution.py:142
  261.5 54.5 %collective-permute-start.27 = (f32[2,6,5,64,128]{4,3,2,1,0:T(8,128)}, f32[2,6,5,64,128]{4,3,2,1,0:T(8,128)}, u32[]{:S(2)}, u32[]{:S(2)}) collective-permute-start(f32[2,6,5,64,128]{4,3,2,1,0:T(8,128)} %get-tuple-element.138), channel_id=1, source_target_pairs={{0,16},{8,24},{16,0},{24,8},{1,17},{9,25},{17,1},{25,9},{2,18},{10... | collective-permute-start | bytes 5898248 | tf_op jit(solution)/shard_map/ppermute | solution.py:142
  263.2 21.1 %collective-permute-start.32 = (f32[6,3,64,128]{3,2,1,0:T(8,128)}, f32[6,3,64,128]{3,2,1,0:T(8,128)}, u32[]{:S(2)}, u32[]{:S(2)}) collective-permute-start(f32[6,3,64,128]{3,2,1,0:T(8,128)} %get-tuple-element.144), channel_id=1, source_target_pairs={{0,8},{8,0},{16,24},{24,16},{1,9},{9,1},{17,25},{25,17},{2,10},{10... | collective-permute-start | bytes 1769480 | tf_op jit(solution)/shard_map/ppermute | solution.py:133
  273.9 18.8 %collective-permute-start.26 = (f32[4,5,64,128]{3,2,1,0:T(8,128)}, f32[4,5,64,128]{3,2,1,0:T(8,128)}, u32[]{:S(2)}, u32[]{:S(2)}) collective-permute-start(f32[4,5,64,128]{3,2,1,0:T(8,128)} %get-tuple-element.137), channel_id=1, source_target_pairs={{0,1},{1,0},{2,3},{3,2},{4,5},{5,4},{6,7},{7,6},{8,9},{9,8},{10,11... | collective-permute-start | bytes 1966088 | tf_op jit(solution)/shard_map/ppermute | solution.py:610
  274.0 23.1 %collective-permute-start.37 = (f32[4,5,64,128]{3,2,1,0:T(8,128)}, f32[4,5,64,128]{3,2,1,0:T(8,128)}, u32[]{:S(2)}, u32[]{:S(2)}) collective-permute-start(f32[4,5,64,128]{3,2,1,0:T(8,128)} %get-tuple-element.152), channel_id=1, source_target_pairs={{0,1},{1,0},{2,3},{3,2},{4,5},{5,4},{6,7},{7,6},{8,9},{9,8},{10,11... | collective-permute-start | bytes 1966088 | tf_op jit(solution)/shard_map/ppermute | solution.py:609
  276.4 9.7 %collective-permute-start.33 = (f32[6,3,64,128]{3,2,1,0:T(8,128)S(1)}, f32[6,3,64,128]{3,2,1,0:T(8,128)}, u32[]{:S(2)}, u32[]{:S(2)}) collective-permute-start(f32[6,3,64,128]{3,2,1,0:T(8,128)S(1)} %slice_bitcast_fusion.6), channel_id=1, source_target_pairs={{0,8},{8,0},{16,24},{24,16},{1,9},{9,1},{17,25},{25,17},{2,10},{10... | collective-permute-start | bytes 1769480 | tf_op jit(solution)/shard_map/ppermute | solution.py:143
  284.3 41.8 %collective-permute-start.30 = (f32[6,5,64,128]{3,2,1,0:T(8,128)}, f32[6,5,64,128]{3,2,1,0:T(8,128)}, u32[]{:S(2)}, u32[]{:S(2)}) collective-permute-start(f32[6,5,64,128]{3,2,1,0:T(8,128)} %get-tuple-element.142), channel_id=1, source_target_pairs={{0,8},{8,0},{16,24},{24,16},{1,9},{9,1},{17,25},{25,17},{2,10},{10... | collective-permute-start | bytes 2949128 | tf_op jit(solution)/shard_map/ppermute | solution.py:133
  301.5 56.6 %collective-permute-start.39 = (f32[2,6,5,64,128]{4,3,2,1,0:T(8,128)}, f32[2,6,5,64,128]{4,3,2,1,0:T(8,128)}, u32[]{:S(2)}, u32[]{:S(2)}) collective-permute-start(f32[2,6,5,64,128]{4,3,2,1,0:T(8,128)} %get-tuple-element.156), channel_id=1, source_target_pairs={{0,16},{8,24},{16,0},{24,8},{1,17},{9,25},{17,1},{25,9},{2,18},{10... | collective-permute-start | bytes 5898248 | tf_op jit(solution)/shard_map/ppermute | solution.py:142
  317.3 9.7 %collective-permute-start.31 = (f32[6,5,64,128]{3,2,1,0:T(8,128)S(1)}, f32[6,5,64,128]{3,2,1,0:T(8,128)}, u32[]{:S(2)}, u32[]{:S(2)}) collective-permute-start(f32[6,5,64,128]{3,2,1,0:T(8,128)S(1)} %slice_bitcast_fusion.1), channel_id=1, source_target_pairs={{0,8},{8,0},{16,24},{24,16},{1,9},{9,1},{17,25},{25,17},{2,10},{10... | collective-permute-start | bytes 2949128 | tf_op jit(solution)/shard_map/ppermute | solution.py:143
  324.6 11.0 %collective-permute-start.28 = (f32[4,3,64,128]{3,2,1,0:T(8,128)}, f32[4,3,64,128]{3,2,1,0:T(8,128)}, u32[]{:S(2)}, u32[]{:S(2)}) collective-permute-start(f32[4,3,64,128]{3,2,1,0:T(8,128)} %get-tuple-element.139), channel_id=1, source_target_pairs={{0,1},{1,0},{2,3},{3,2},{4,5},{5,4},{6,7},{7,6},{8,9},{9,8},{10,11... | collective-permute-start | bytes 1179656 | tf_op jit(solution)/shard_map/ppermute | solution.py:609
  324.6 19.4 %collective-permute-start.29 = (f32[4,3,64,128]{3,2,1,0:T(8,128)}, f32[4,3,64,128]{3,2,1,0:T(8,128)}, u32[]{:S(2)}, u32[]{:S(2)}) collective-permute-start(f32[4,3,64,128]{3,2,1,0:T(8,128)} %get-tuple-element.140), channel_id=1, source_target_pairs={{0,1},{1,0},{2,3},{3,2},{4,5},{5,4},{6,7},{7,6},{8,9},{9,8},{10,11... | collective-permute-start | bytes 1179656 | tf_op jit(solution)/shard_map/ppermute | solution.py:610
  348.3 35.0 %collective-permute-start.35 = (f32[2,6,3,64,128]{4,3,2,1,0:T(8,128)}, f32[2,6,3,64,128]{4,3,2,1,0:T(8,128)S(1)}, u32[]{:S(2)}, u32[]{:S(2)}) collective-permute-start(f32[2,6,3,64,128]{4,3,2,1,0:T(8,128)} %get-tuple-element.151), channel_id=1, source_target_pairs={{0,16},{8,24},{16,0},{24,8},{1,17},{9,25},{17,1},{25,9},{2,18},{10... | collective-permute-start | bytes 3538952 | tf_op jit(solution)/shard_map/ppermute | solution.py:142
  349.7 39.3 %collective-permute-start.38 = (f32[6,5,64,128]{3,2,1,0:T(8,128)}, f32[6,5,64,128]{3,2,1,0:T(8,128)}, u32[]{:S(2)}, u32[]{:S(2)}) collective-permute-start(f32[6,5,64,128]{3,2,1,0:T(8,128)} %get-tuple-element.154), channel_id=1, source_target_pairs={{0,8},{8,0},{16,24},{24,16},{1,9},{9,1},{17,25},{25,17},{2,10},{10... | collective-permute-start | bytes 2949128 | tf_op jit(solution)/shard_map/ppermute | solution.py:133
  359.4 29.6 %collective-permute-start.40 = (f32[6,5,64,128]{3,2,1,0:T(8,128)S(1)}, f32[6,5,64,128]{3,2,1,0:T(8,128)}, u32[]{:S(2)}, u32[]{:S(2)}) collective-permute-start(f32[6,5,64,128]{3,2,1,0:T(8,128)S(1)} %slice_bitcast_fusion), channel_id=1, source_target_pairs={{0,8},{8,0},{16,24},{24,16},{1,9},{9,1},{17,25},{25,17},{2,10},{10... | collective-permute-start | bytes 2949128 | tf_op jit(solution)/shard_map/ppermute | solution.py:143
  366.8 29.5 %collective-permute-start.34 = (f32[6,3,64,128]{3,2,1,0:T(8,128)}, f32[6,3,64,128]{3,2,1,0:T(8,128)}, u32[]{:S(2)}, u32[]{:S(2)}) collective-permute-start(f32[6,3,64,128]{3,2,1,0:T(8,128)} %get-tuple-element.149), channel_id=1, source_target_pairs={{0,8},{8,0},{16,24},{24,16},{1,9},{9,1},{17,25},{25,17},{2,10},{10... | collective-permute-start | bytes 1769480 | tf_op jit(solution)/shard_map/ppermute | solution.py:133
  383.3 1.0 copy-start
  385.2 11.1 %collective-permute-start.36 = (f32[6,3,64,128]{3,2,1,0:T(8,128)}, f32[6,3,64,128]{3,2,1,0:T(8,128)}, u32[]{:S(2)}, u32[]{:S(2)}) collective-permute-start(f32[6,3,64,128]{3,2,1,0:T(8,128)} %slice_bitcast_fusion.5), channel_id=1, source_target_pairs={{0,8},{8,0},{16,24},{24,16},{1,9},{9,1},{17,25},{25,17},{2,10},{10... | collective-permute-start | bytes 1769480 | tf_op jit(solution)/shard_map/ppermute | solution.py:143
